TPU v7x, 32 devices: a whole 2x2x4 slice. The times are simulated.
32 devices in a mesh: groups: 2 (over x), owner: 16 (over z, y, core).
Axes of the slice: x: 2, y: 2, z: 4, core: 2. Of those that a mesh axis runs over, the one named last changes fastest.
Arguments:
- embeddings: bfloat16 [65536, 768], P(('groups', 'owner')), parts along dimension 0, as said below
- cluster_ids: int32 [65536], P(('groups', 'owner')), parts along dimension 0, may hold values from 0 to 63, as said below
Outputs:
- neighbour_max: float32 [65536], P(('groups', 'owner')), parts along dimension 0
- centroid_gap: float32 [65536], P(('groups', 'owner')), parts along dimension 0
There are 2 independent parts, one for each index of `groups`. A program takes and returns all parts, laid end to end along the dimension named above; each array names one. Nothing has to cross between parts.
Inputs may be any that keep to these rules, and one draw needn't show every extreme that they name: `cluster_ids`: A fine cluster holds at most 64 of the 2048 rows of one device and at most 1024 rows in all; both bounds are reached in every draw. A fine cluster may hold no rows. `embeddings`: every row has a nonzero length.
All inputs are finite; a program needn't handle non-finite values.
Results may differ from a plain program's by a relative error of at most 0.00079.
Values may be sent and summed in bfloat16 or wider, within the bound.
No kernel may reach another device: no remote copies, remote signals or barrier semaphores. Data moves between devices by JAX's collectives and lax.ppermute only.
A program may use at most 64 MiB of HBM per device.

v0:
```python
import jax
import jax.numpy as jnp
from jax import lax
from jax.sharding import PartitionSpec as P

CL_DEV = 4


epsilon = 1e-06


def masked_max(left_rows, right_rows, live_count):
    scores = lax.dot_general(
        left_rows, right_rows, (((1,), (1,)), ((), ())), preferred_element_type=jnp.float32
    )
    row_number = jnp.arange(left_rows.shape[0], dtype=jnp.int32)[:, None]
    col_number = jnp.arange(right_rows.shape[0], dtype=jnp.int32)[None, :]
    allowed = (col_number < live_count) & (col_number != row_number)
    return jnp.max(jnp.where(allowed, scores, -1.0), axis=1)


def local(embeddings, cluster_ids):
    rows_here, feature_width = embeddings.shape
    owners = lax.axis_size("owner")
    my_index = lax.axis_index("owner")
    clusters = CL_DEV * owners
    row_limit = 2 * rows_here // clusters
    slot_rows = CL_DEV * row_limit
    cluster_cap = 2 * rows_here // CL_DEV
    widened = embeddings.astype(jnp.float32)
    unit_rows = (
        widened * lax.rsqrt(jnp.sum(widened * widened, axis=1, keepdims=True) + epsilon)
    ).astype(jnp.bfloat16)
    labels = jnp.arange(clusters, dtype=jnp.int32)
    member = cluster_ids[:, None] == labels[None, :]
    local_counts = jnp.sum(member.astype(jnp.int32), axis=0)
    counts = lax.psum(local_counts, "owner")
    row_place = jnp.sum(jnp.where(member, labels[None, :], 0), axis=1)
    destination = row_place // CL_DEV
    local_slot = row_place % CL_DEV
    dest_hot = (destination[:, None] == jnp.arange(owners, dtype=jnp.int32)[None, :]).astype(
        jnp.int32
    )
    before = jnp.cumsum(dest_hot, axis=0) - dest_hot
    position = jnp.sum(before * dest_hot, axis=1)
    flat_index = destination * slot_rows + position
    outgoing = (
        jnp.zeros((owners * slot_rows, feature_width), jnp.bfloat16).at[flat_index].set(unit_rows)
    )
    slot_tags = jnp.full((owners * slot_rows,), -1, jnp.int32).at[flat_index].set(local_slot)
    incoming, in_tags = (
        lax.all_to_all(
            outgoing.reshape(owners, slot_rows, feature_width),
            "owner",
            split_axis=0,
            concat_axis=0,
            tiled=True,
        ),
        lax.all_to_all(
            slot_tags.reshape(owners, slot_rows), "owner", split_axis=0, concat_axis=0, tiled=True
        ),
    )
    in_tags = in_tags.reshape(-1)
    incoming = incoming.reshape(owners * slot_rows, feature_width)
    tag_hot = (in_tags[:, None] == jnp.arange(CL_DEV, dtype=jnp.int32)[None, :]).astype(jnp.int32)
    earlier = jnp.cumsum(tag_hot, axis=0) - tag_hot
    rank_in = jnp.sum(earlier * tag_hot, axis=1)
    occupied = in_tags >= 0
    bucket_index = jnp.where(occupied, in_tags * cluster_cap + rank_in, CL_DEV * cluster_cap)
    gathered = (
        jnp.zeros((CL_DEV * cluster_cap, feature_width), jnp.bfloat16)
        .at[bucket_index]
        .set(incoming, mode="drop")
    )
    members = gathered.reshape(CL_DEV, cluster_cap, feature_width)
    group_sizes = jnp.sum(tag_hot, axis=0)
    best_match = jnp.stack(
        [masked_max(members[k], members[k], group_sizes[k]) for k in range(CL_DEV)]
    )
    flat_best = best_match.reshape(-1)
    answer = jnp.where(
        occupied, flat_best[jnp.minimum(bucket_index, CL_DEV * cluster_cap - 1)], 0.0
    )
    returned = lax.all_to_all(
        answer.reshape(owners, slot_rows), "owner", split_axis=0, concat_axis=0, tiled=True
    )
    neighbour_max = returned.reshape(-1)[flat_index]
    onehot = member.astype(jnp.bfloat16)
    cluster_sums = lax.psum_scatter(
        lax.dot_general(
            onehot, unit_rows, (((0,), (0,)), ((), ())), preferred_element_type=jnp.float32
        ),
        "owner",
        scatter_dimension=0,
        tiled=True,
    )
    own_counts = lax.dynamic_slice_in_dim(counts, my_index * CL_DEV, CL_DEV)
    centroids = (cluster_sums / jnp.maximum(own_counts, 1).astype(jnp.float32)[:, None]).astype(
        jnp.bfloat16
    )
    scores = lax.dot_general(
        unit_rows,
        lax.all_gather(centroids, "owner", axis=0, tiled=True),
        (((1,), (1,)), ((), ())),
        preferred_element_type=jnp.float32,
    )
    chosen = cluster_ids[:, None] == labels[None, :]
    centroid_gap = 1.0 - jnp.sum(jnp.where(chosen, scores, 0.0), axis=1)
    return (neighbour_max, centroid_gap)


def solution(mesh):
    return jax.shard_map(
        local,
        mesh=mesh,
        in_specs=(P(("groups", "owner"), None), P(("groups", "owner"))),
        out_specs=(P(("groups", "owner")), P(("groups", "owner"))),
        check_vma=False,
    )
```

profile of v0, /device:TPU:0, one launch (start us, length us, event | category | flops | bytes accessed | tf_op | source)
XLA Modules:
  0.0 355.0 jit_solution(8777527709405202834)
XLA Ops:
  7.2 1.1 convert_reduce_fusion
  8.3 4.5 %reduce-window.14 = s32[16,16,128]{2,1,0:T(8,128)S(1)} reduce-window(s32[16,16,128]{2,1,0:T(8,128)S(1)} %fusion.20, s32[]{:T(128)} %constant.26.clone.1), window={size=1x1x128 pad=0_0x0_0x127_0}, to_apply=%region_1.0 | reduce-window | flops 4161536 | bytes 262148 | tf_op jit(solution)/shard_map/reduce-window
  12.8 0.4 slice_reduce_fusion
  13.7 8.6 %scatter_custom_fusion = s32[4096]{0:T(1024)} fusion(s32[2048]{0:T(1024)S(1)} %bitcast.90, s32[2048]{0:T(1024)S(1)} %get-tuple-element.8, s32[]{:T(128)} %constant.25.clone.1), kind=kCustom, calls=%fused_computation.83 | custom fusion | bytes 16388 | tf_op jit(solution)/shard_map/scatter | solution.py:50
  22.3 7.4 %all-to-all-start = ((s32[16,1,256]{2,1,0:T(1,128)}), s32[16,1,256]{2,1,0:T(1,128)S(1)}, u32[]{:S(2)}, u32[]{:S(2)}) async-start(s32[16,1,256]{2,1,0:T(1,128)} %bitcast.5), calls=%async_computation | async-start | bytes 32768 | tf_op jit(solution)/shard_map/all_to_all | solution.py:59
  29.7 2.6 fusion
  32.3 14.2 %scatter_custom_fusion.1 = bf16[4096,768]{1,0:T(8,128)(2,1)} fusion(s32[2048]{0:T(1024)S(1)} %bitcast.91, bf16[]{:T(256)} %constant.59.clone.1, bf16[2048,768]{1,0:T(8,128)(2,1)S(1)} %copy-done, f32[2048]{0:T(1024)S(1)} %add_rsqrt_fusion), kind=kCustom, calls=%fused_computation.20 | custom fusion | flops 4718592 | bytes 9445378 | tf_op jit(solution)/shard_map/scatter | solution.py:48
  46.5 6.2 %all-to-all-start.1 = ((bf16[16,256,768]{2,1,0:T(8,128)(2,1)}), bf16[16,256,768]{2,1,0:T(8,128)(2,1)}, u32[]{:S(2)}, u32[]{:S(2)}) async-start(bf16[16,256,768]{2,1,0:T(8,128)(2,1)} %bitcast.79), calls=%async_computation.1 | async-start | bytes 12582912 | tf_op jit(solution)/shard_map/all_to_all | solution.py:52
  52.8 1.7 fusion.15
  54.5 0.6 dynamic-slice
  55.7 137.8 %psum.7 = s32[64]{0:T(128)S(1)} all-reduce(s32[64]{0:T(128)S(1)} %get-tuple-element.4), channel_id=1, replica_groups=mesh['groups'=2,'owner'=16] {'owner'}, use_global_device_ids=true, to_apply=%region_18.19 | all-reduce | flops 64 | bytes 512 | tf_op jit(solution)/shard_map/psum | solution.py:37
  193.6 1.2 reduce-window.16
  195.4 0.7 fusion.36
  196.1 0.6 iota_compare_fusion.10
  196.8 0.6 iota_compare_fusion.9
  197.4 0.7 iota_compare_fusion.8
  198.2 0.7 iota_compare_fusion.7
  198.9 41.1 %all-reduce.3.cloned.1.call-done = f32[64,768]{1,0:T(8,128)} async-done(((f32[64,768]{1,0:T(8,128)}), f32[64,768]{1,0:T(8,128)}) %all-reduce.3.cloned.1.call-update) | async-done | bytes 196624
  239.9 0.8 fusion.31
  240.7 19.8 %all-gather = bf16[16,4,768]{2,1,0:T(4,128)(2,1)S(1)} all-gather(bf16[1,4,768]{2,1,0:T(4,128)(2,1)S(1)} %fusion.31), channel_id=1, replica_groups=mesh['groups'=2,'owner'=16] {'owner'}, dimensions={0}, use_global_device_ids=true | all-gather | bytes 104448 | tf_op jit(solution)/shard_map/all_gather | solution.py:103
  260.6 1.2 fusion.14
  261.8 22.8 %scatter_custom_fusion.2 = bf16[4096,768]{1,0:T(8,128)(2,1)} fusion(s32[4096]{0:T(1024)S(1)} %bitcast.94, bf16[4096,768]{1,0:T(8,128)(2,1)} %bitcast.15, bf16[]{:T(256)} %constant.59.clone.1), kind=kCustom, calls=%fused_computation.18 | custom fusion | bytes 6291968 | tf_op jit(solution)/shard_map/scatter | solution.py:73
  284.6 3.9 %select_reduce_fusion.3 = f32[1024]{0:T(1024)S(1)} fusion(pred[1024]{0:T(1024)(128)(4,1)S(1)} %iota_compare_fusion.10, bf16[4096,768]{1,0:T(8,128)(2,1)} %scatter_custom_fusion.2), kind=kOutput, calls=%fused_computation.12 | convolution fusion | flops 1614806016 | bytes 1577984 | tf_op jit(solution)/shard_map/dot_general | solution.py:13
  288.4 1.8 select_reduce_fusion.2
  290.3 1.8 select_reduce_fusion.1
  292.1 1.8 select_reduce_fusion
  294.0 23.0 %gather_fusion = f32[4096]{0:T(1024)S(1)} fusion(f32[4096]{0:T(1024)S(1)} %bitcast.77, s32[4096]{0:T(1024)S(1)} %broadcast_clamp_fusion), kind=kCustom, calls=%fused_computation | custom fusion | bytes 49152 | tf_op jit(solution)/shard_map/gather | solution.py:82
  317.1 0.6 broadcast_select_fusion
  317.7 3.5 all-to-all-start.2
  321.2 0.6 broadcast_subtract_fusion
  321.8 5.9 %all-to-all-done.2 = f32[16,1,256]{2,1,0:T(1,128)S(1)} async-done(((f32[16,1,256]{2,1,0:T(1,128)}), f32[16,1,256]{2,1,0:T(1,128)S(1)}, u32[]{:S(2)}, u32[]{:S(2)}) %all-to-all-start.2) | async-done | bytes 16416 | tf_op jit(solution)/shard_map/all_to_all | solution.py:84
  327.6 20.5 %gather_fusion.1 = f32[2048]{0:T(1024)} fusion(f32[4096]{0:T(1024)S(1)} %bitcast.78, s32[2048]{0:T(1024)S(1)} %broadcast_clamp_fusion.1), kind=kCustom, calls=%fused_computation.1 | custom fusion | bytes 24576 | tf_op jit(solution)/shard_map/gather | solution.py:87
  (34 shorter events, 1.4 us)
Async XLA Ops:
  7.2 25.1 %copy-start = (bf16[2048,768]{1,0:T(8,128)(2,1)S(1)}, bf16[2048,768]{1,0:T(8,128)(2,1)}, u32[]{:S(2)}) copy-start(bf16[2048,768]{1,0:T(8,128)(2,1)} %param.2) | copy-start | bytes 9437188
  22.3 24.2 %all-to-all-start = ((s32[16,1,256]{2,1,0:T(1,128)}), s32[16,1,256]{2,1,0:T(1,128)S(1)}, u32[]{:S(2)}, u32[]{:S(2)}) async-start(s32[16,1,256]{2,1,0:T(1,128)} %bitcast.5), calls=%async_computation | async-start | bytes 32768 | tf_op jit(solution)/shard_map/all_to_all | solution.py:59
  46.5 6.2 %copy-start.2 = (s32[2048]{0:T(1024)S(1)}, s32[2048]{0:T(1024)}, u32[]{:S(2)}) copy-start(s32[2048]{0:T(1024)} %param.3) | copy-start | bytes 24580
  46.5 8.0 %copy-start.3 = (u32[32]{0:T(128)S(1)}, u32[32]{0:T(128)}, u32[]{:S(2)}) copy-start(u32[32]{0:T(128)} %constant.71) | copy-start | bytes 388
  46.5 215.2 %all-to-all-start.1 = ((bf16[16,256,768]{2,1,0:T(8,128)(2,1)}), bf16[16,256,768]{2,1,0:T(8,128)(2,1)}, u32[]{:S(2)}, u32[]{:S(2)}) async-start(bf16[16,256,768]{2,1,0:T(8,128)(2,1)} %bitcast.79), calls=%async_computation.1 | async-start | bytes 12582912 | tf_op jit(solution)/shard_map/all_to_all | solution.py:52
  52.7 187.2 %all-reduce.3.cloned.1.call-start = ((), (), s32[]{:S(2)}) async-start(), calls=%async_computation.3 | async-start | bytes 393216
  284.6 3.9 %copy-start.1 = (bf16[4096,768]{1,0:T(8,128)(2,1)S(1)}, bf16[4096,768]{1,0:T(8,128)(2,1)}, u32[]{:S(2)}) copy-start(bf16[4096,768]{1,0:T(8,128)(2,1)} %scatter_custom_fusion.2) | copy-start | bytes 18874372
  317.7 10.0 %all-to-all-start.2 = ((f32[16,1,256]{2,1,0:T(1,128)}), f32[16,1,256]{2,1,0:T(1,128)S(1)}, u32[]{:S(2)}, u32[]{:S(2)}) async-start(f32[16,1,256]{2,1,0:T(1,128)} %broadcast_select_fusion), calls=%async_computation.2 | async-start | bytes 32768 | tf_op jit(solution)/shard_map/all_to_all | solution.py:84
Sparse Core Ops, SparseCore 0:
  57.0 182.9 all-reduce.2
where the time goes:
time: 356 us; the launch traced here: 355 us
  blocking collectives  158 us (44%)
  local copies, waits for them, and re-layouts  76.9 us (22%)
  waiting for transfers between devices  46.9 us (13%)
  other arithmetic  29.3 us (8%)
  starting transfers between devices  17.1 us (5%)
  between operations  15 us (4%)
  matrix products  12.2 us (3%)
    psum x1, blocking collectives, local(): counts = lax.psum(local_counts, 'owner')  138 us
    unnamed x2, waiting for transfers between devices  41.1 us
    gather x1, local copies, waits for them, and re-layouts, local(): flat_best[jnp.minimum(bucket_index, CL_DEV * cluster_cap - 1)]  23 us
    scatter x1, local copies, waits for them, and re-layouts, local(): gathered = jnp.zeros((CL_DEV * cluster_cap, feature_width), jnp.bfloat16)...  22.8 us
    gather x1, local copies, waits for them, and re-layouts, local(): neighbour_max = returned.reshape(-1)[flat_index]  20.5 us
    all_gather x1, blocking collectives, local(): lax.all_gather(centroids, 'owner', axis=0, tiled=True)  19.8 us
    scatter x1, other arithmetic, local(): jnp.zeros((owners * slot_rows, feature_width), jnp.bfloat16).at[flat_index]  14.2 us
    dot_general x4, matrix products, masked_max(): lax.dot_general(left_rows, right_rows, (((1,), (1,)), ((), ())), preferre...  9.37 us
  transfers between devices with their start and end apart: 4, of which 2 were waited for; matrix products, arithmetic and copies ran while one was open for 8% of the time, Pallas kernels for 0%

commit v1 on v0

v1 whole, which is shorter than its diff:
```python
import functools

import jax
import jax.numpy as jnp
from jax import lax
from jax.experimental import pallas as pl
from jax.experimental.pallas import tpu as pltpu
from jax.sharding import PartitionSpec as P

CL_DEV = 4
VARIANTS = 8
STEP = 16
TILE = 256
MIB = 1 << 20

epsilon = 1e-06
f32 = jnp.float32
bf16 = jnp.bfloat16
i32 = jnp.int32


def iota(shape, axis):
    return lax.broadcasted_iota(i32, shape, axis)


def round_up(value, unit):
    return -(-value // unit) * unit


def nt_dot(a, b):
    return lax.dot_general(a, b, (((1,), (1,)), ((), ())), preferred_element_type=f32)


def mm(a, b):
    return jnp.dot(a, b, preferred_element_type=f32)


def sort_kernel(clusters, ids_ref, rows_ref, sorted_ref, rank_ref, unit_ref, pos_ref):
    rows = rows_ref.shape[0]
    blocks = rows // TILE
    label = iota((clusters, TILE), 0)
    upto = (iota((TILE, TILE), 0) <= iota((TILE, TILE), 1)).astype(bf16)
    total = jnp.zeros((clusters, 1), f32)
    for b in range(blocks):
        at = slice(b * TILE, (b + 1) * TILE)
        hot = ids_ref[:, at] == label
        hot16 = hot.astype(f32).astype(bf16)
        prefix = mm(hot16, upto)
        rank_ref[:, at] = jnp.sum(jnp.where(hot, prefix + total - 1.0, 0.0), axis=0, keepdims=True)
        total = total + prefix[:, TILE - 1 :]
    square = (clusters, clusters)
    total_row = jnp.sum(
        jnp.where(iota(square, 0) == iota(square, 1), total, 0.0), axis=0, keepdims=True
    )
    start = jnp.sum(
        jnp.where(iota(square, 1) < iota(square, 0), total_row, 0.0), axis=1, keepdims=True
    )
    for b in range(blocks):
        at = slice(b * TILE, (b + 1) * TILE)
        hot = ids_ref[:, at] == label
        first = jnp.sum(jnp.where(hot, start, 0.0), axis=0, keepdims=True)
        pos_ref[:, at] = (first + rank_ref[:, at]).astype(i32)

    def normalise(b, carry):
        at = pl.ds(pl.multiple_of(b * TILE, TILE), TILE)
        x = rows_ref[at, :].astype(f32)
        scale = lax.rsqrt(jnp.sum(x * x, axis=1, keepdims=True) + epsilon)
        unit_ref[at, :] = (x * scale).astype(bf16)
        return carry

    lax.fori_loop(0, blocks, normalise, 0)

    def arrange(b, carry):
        first = pl.multiple_of(b * TILE, TILE)
        take = (iota((TILE, rows), 0) + first) == pos_ref[...]
        sorted_ref[pl.ds(first, TILE), :] = mm(
            take.astype(f32).astype(bf16), unit_ref[...]
        ).astype(bf16)
        return carry

    lax.fori_loop(0, blocks, arrange, 0)
    tail = sorted_ref.shape[0] - rows
    sorted_ref[rows:, :] = jnp.zeros((tail, sorted_ref.shape[1]), bf16)


def sort_rows(embeddings, ids_row, clusters, tail):
    rows, width = embeddings.shape
    vmem = pl.BlockSpec(memory_space=pltpu.VMEM)
    return pl.pallas_call(
        functools.partial(sort_kernel, clusters),
        out_shape=(
            jax.ShapeDtypeStruct((rows + tail, width), bf16),
            jax.ShapeDtypeStruct((1, rows), f32),
        ),
        in_specs=[vmem, vmem],
        out_specs=(vmem, vmem),
        scratch_shapes=[pltpu.VMEM((rows, width), bf16), pltpu.VMEM((1, rows), i32)],
        compiler_params=pltpu.CompilerParams(vmem_limit_bytes=40 * MIB),
        cost_estimate=pl.CostEstimate(
            flops=2 * rows * rows * width, bytes_accessed=4 * rows * width, transcendentals=rows
        ),
        name="sort_rows",
    )(ids_row, embeddings)


def assign_kernel(owners, me_ref, counts_ref, tab_ref, bound_ref, bound_t_ref, place_ref):
    clusters = counts_ref.shape[1]
    shift = owners.bit_length() - 1
    me = me_ref[0]
    count = counts_ref[...].astype(f32)
    count16 = count.astype(bf16)
    square = (clusters, clusters)
    sub, lane = iota(square, 0), iota(square, 1)
    eye = sub == lane

    def to_col(row):
        return jnp.sum(jnp.where(eye, row, 0.0), axis=1, keepdims=True)

    total_row = jnp.sum(count, axis=0, keepdims=True)
    total_col = to_col(total_row)
    tie = total_row == total_col
    outranks_col = (total_row > total_col) | (tie & (lane < sub))
    outranks_row = (total_col > total_row) | (tie & (sub < lane))
    rank_col = jnp.sum(outranks_col.astype(f32), axis=1, keepdims=True).astype(i32)
    rank_row = jnp.sum(outranks_row.astype(f32), axis=0, keepdims=True).astype(i32)

    def owner_of(rank, variant):
        layer = rank >> shift
        within = rank & (owners - 1)
        flip = jnp.zeros_like(variant)
        for p in range(1, CL_DEV):
            flip = flip + jnp.where(layer == p, (variant >> (p - 1)) & 1, 0)
        within = within ^ flip
        return jnp.where((layer & 1) == 1, owners - 1 - within, within)

    wide = (clusters, VARIANTS * owners)
    variant = iota(wide, 1) >> shift
    tried = owner_of(rank_col, variant) == (iota(wide, 1) & (owners - 1))
    load = jnp.max(mm(count16, tried.astype(f32).astype(bf16)), axis=0, keepdims=True)
    by_variant = (VARIANTS, VARIANTS * owners)
    worst = jnp.max(
        jnp.where((iota(by_variant, 1) >> shift) == iota(by_variant, 0), load, 0.0),
        axis=1,
        keepdims=True,
    )
    best = jnp.min(worst, axis=0, keepdims=True)
    chosen = jnp.min(
        jnp.where(worst == best, iota((VARIANTS, 1), 0), VARIANTS), axis=0, keepdims=True
    )
    owner_col = owner_of(rank_col, chosen + jnp.zeros_like(rank_col))
    owner_row = owner_of(rank_row, chosen + jnp.zeros_like(rank_row))
    layer_col, layer_row = rank_col >> shift, rank_row >> shift

    mine_row = jnp.sum(
        jnp.where(iota(count.shape, 0) == me, count, 0.0), axis=0, keepdims=True
    )
    mine_col = to_col(mine_row)
    start_col = jnp.sum(jnp.where(lane < sub, mine_row, 0.0), axis=1, keepdims=True)
    earlier = (owner_row == owner_col) & (layer_row < layer_col)
    offset_col = jnp.sum(jnp.where(earlier, mine_row, 0.0), axis=1, keepdims=True)
    perm = lane == layer_col * owners + owner_col

    def by_slot(col):
        return jnp.sum(jnp.where(perm, col, 0.0), axis=0, keepdims=True).astype(i32)

    tab_ref[...] = jnp.zeros_like(tab_ref)
    tab_ref[0:1, 0:clusters] = by_slot(start_col)
    tab_ref[1:2, 0:clusters] = by_slot(mine_col)
    tab_ref[2:3, 0:clusters] = by_slot(offset_col)
    tab_ref[5:6, :] = jnp.broadcast_to(best, (1, tab_ref.shape[1])).astype(i32)

    select = (owner_col == me) & (layer_col <= iota((clusters, 128), 1))
    bound = mm(count16, select.astype(f32).astype(bf16))
    bound_ref[...] = bound
    select_t = (owner_row == me) & (layer_row <= iota((8, clusters), 0))
    bound_t_ref[...] = nt_dot(select_t.astype(f32).astype(bf16), count16)
    first = (iota((owners, 128), 1) * STEP).astype(f32)
    low = jnp.zeros((owners, 128), f32)
    high = jnp.zeros((owners, 128), f32)
    for k in range(CL_DEV):
        edge = bound[:, k : k + 1]
        low = low + (first >= edge).astype(f32)
        high = high + (first + (STEP - 1.0) >= edge).astype(f32)
    tab_ref[3:4, 0:128] = jnp.min(low, axis=0, keepdims=True).astype(i32)
    tab_ref[4:5, 0:128] = jnp.max(high, axis=0, keepdims=True).astype(i32)
    place_ref[...] = jnp.where(
        iota((clusters, 128), 1) == 0, owner_col.astype(f32), offset_col
    )


def assign(counts, me):
    owners, clusters = counts.shape
    vmem = pl.BlockSpec(memory_space=pltpu.VMEM)
    return pl.pallas_call(
        functools.partial(assign_kernel, owners),
        out_shape=(
            jax.ShapeDtypeStruct((8, max(clusters, 128)), i32),
            jax.ShapeDtypeStruct((owners, 128), f32),
            jax.ShapeDtypeStruct((8, owners), f32),
            jax.ShapeDtypeStruct((clusters, 128), f32),
        ),
        in_specs=[pl.BlockSpec(memory_space=pltpu.SMEM), vmem],
        out_specs=(vmem,) * 4,
        compiler_params=pltpu.CompilerParams(vmem_limit_bytes=24 * MIB),
        name="assign",
    )(me, counts)


def pack_kernel(owners, window, group, tab_ref, sorted_ref, out_ref):
    slots = out_ref.shape[1]
    slot = iota((slots, 1), 0)
    for g in range(group):
        owner = pl.program_id(0) * group + g
        runs = []
        source = jnp.full((slots, 1), -1, i32)
        for k in range(CL_DEV):
            start = tab_ref[0, k * owners + owner]
            size = tab_ref[1, k * owners + owner]
            offset = tab_ref[2, k * owners + owner]
            first = pl.multiple_of((start // STEP) * STEP, STEP)
            runs.append(sorted_ref[pl.ds(first, window), :])
            inside = (slot >= offset) & (slot < offset + size)
            source = jnp.where(inside, slot + (k * window + start - first - offset), source)
        take = iota((slots, CL_DEV * window), 1) == source
        out_ref[g] = mm(take.astype(f32).astype(bf16), jnp.concatenate(runs, axis=0)).astype(bf16)


def pack(sorted_rows, tab, owners, slots, window):
    total, width = sorted_rows.shape
    group = 4
    return pl.pallas_call(
        functools.partial(pack_kernel, owners, window, group),
        out_shape=jax.ShapeDtypeStruct((owners, slots, width), bf16),
        grid=(owners // group,),
        in_specs=[
            pl.BlockSpec(memory_space=pltpu.SMEM),
            pl.BlockSpec((total, width), lambda i: (0, 0)),
        ],
        out_specs=pl.BlockSpec((group, slots, width), lambda i: (i, 0, 0)),
        compiler_params=pltpu.CompilerParams(vmem_limit_bytes=40 * MIB),
        name="pack_rows",
    )(tab, sorted_rows)


def score_kernel(
    tab_ref, bound_ref, bound_t_ref, x_ref, out_ref, cid_col, cid_row, row_acc, col_acc
):
    owners, slots, width = x_ref.shape
    chunk = owners * STEP
    chunks = slots // STEP
    half = out_ref.shape[1] // 2

    def load(q):
        return x_ref[:, pl.ds(pl.multiple_of(q * STEP, STEP), STEP), :].reshape(chunk, width)

    spread = (iota((chunk, owners), 0) // STEP) == iota((chunk, owners), 1)
    edges = mm(spread.astype(f32).astype(bf16), bound_ref[...].astype(bf16))
    spread_t = (iota((owners, chunk), 1) // STEP) == iota((owners, chunk), 0)
    edges_t = mm(bound_t_ref[...].astype(bf16), spread_t.astype(f32).astype(bf16))
    in_col = (iota((chunk, 1), 0) % STEP).astype(f32)
    in_row = (iota((1, chunk), 1) % STEP).astype(f32)
    for q in range(chunks):
        col = jnp.zeros((chunk, 1), f32)
        row = jnp.zeros((1, chunk), f32)
        for k in range(CL_DEV):
            col = col + (in_col + q * STEP >= edges[:, k : k + 1]).astype(f32)
            row = row + (in_row + q * STEP >= edges_t[k : k + 1, :]).astype(f32)
        cid_col[q] = col
        cid_row[q] = row

    sums = jnp.zeros((8, width), f32)
    members = jnp.zeros((8, 1), f32)
    for q in range(chunks):
        hot = (cid_row[q] == iota((8, chunk), 0).astype(f32)).astype(f32)
        sums = sums + mm(hot.astype(bf16), load(q))
        members = members + jnp.sum(hot, axis=1, keepdims=True)
    centroid = (sums / jnp.maximum(members, 1.0)).astype(bf16)

    row_acc[...] = jnp.full(row_acc.shape, -1.0, f32)
    col_acc[...] = jnp.full(col_acc.shape, -1.0, f32)

    def lane_fold(m):
        r = m[:, 0:128]
        for i in range(1, chunk // 128):
            r = jnp.maximum(r, m[:, i * 128 : (i + 1) * 128])
        return r

    def sub_fold(m):
        return jnp.max(m.reshape(chunk // 8, 8, chunk), axis=0)

    def own(q1, carry):
        x1 = load(q1)
        same = (cid_col[q1] == cid_row[q1]) & (iota((chunk, chunk), 0) != iota((chunk, chunk), 1))
        m = jnp.where(same, nt_dot(x1, x1), -1.0)
        row_acc[q1] = jnp.maximum(row_acc[q1], lane_fold(m))

        def other(q2, inner):
            @pl.when(tab_ref[3, q2] <= jnp.minimum(tab_ref[4, q1], CL_DEV - 1))
            def _():
                s = nt_dot(load(q1), load(q2))
                t = jnp.where(cid_col[q1] == cid_row[q2], s, -1.0)
                row_acc[q1] = jnp.maximum(row_acc[q1], lane_fold(t))
                col_acc[q2] = jnp.maximum(col_acc[q2], sub_fold(t))

            return inner

        return lax.fori_loop(q1 + 1, chunks, other, carry)

    lax.fori_loop(0, chunks, own, 0)

    eye = iota((chunk, chunk), 0) == iota((chunk, chunk), 1)
    lanes = iota((chunk, half), 1)
    best_z = jnp.zeros((chunk, half), f32)
    gap_z = jnp.zeros((chunk, half), f32)
    for q in range(chunks):
        col = jnp.max(col_acc[q], axis=0, keepdims=True)
        both = jnp.maximum(row_acc[q], lane_fold(jnp.where(eye, col, -1.0)))
        best = jnp.max(both, axis=1, keepdims=True)
        dots = nt_dot(load(q), centroid)
        hit = cid_col[q] == iota((chunk, 8), 1).astype(f32)
        gap = 1.0 - jnp.sum(jnp.where(hit, dots, 0.0), axis=1, keepdims=True)
        here = (lanes // STEP) == q
        best_z = jnp.where(here, best, best_z)
        gap_z = jnp.where(here, gap, gap_z)
    keep = (lanes % STEP) == (iota((chunk, half), 0) % STEP)
    for i, z in enumerate((best_z, gap_z)):
        z = jnp.where(keep, z, 0.0).reshape(owners, STEP, half)
        out_ref[:, i * half : (i + 1) * half] = jnp.sum(z, axis=1)


def score(incoming, tab, bound, bound_t):
    owners, slots, width = incoming.shape
    chunk, chunks = owners * STEP, slots // STEP
    vmem = pl.BlockSpec(memory_space=pltpu.VMEM)
    return pl.pallas_call(
        score_kernel,
        out_shape=jax.ShapeDtypeStruct((owners, 2 * round_up(slots, 128)), f32),
        in_specs=[pl.BlockSpec(memory_space=pltpu.SMEM), vmem, vmem, vmem],
        out_specs=vmem,
        scratch_shapes=[
            pltpu.VMEM((chunks, chunk, 1), f32),
            pltpu.VMEM((chunks, 1, chunk), f32),
            pltpu.VMEM((chunks, chunk, 128), f32),
            pltpu.VMEM((chunks, 8, chunk), f32),
        ],
        compiler_params=pltpu.CompilerParams(vmem_limit_bytes=48 * MIB),
        name="score_rows",
    )(tab, bound, bound_t, incoming)


def restore_kernel(slots, ids_ref, rank_ref, place_ref, back_ref, best_ref, gap_ref):
    rows = ids_ref.shape[1]
    clusters = place_ref.shape[0]
    owners = back_ref.shape[0]
    half = back_ref.shape[1] // 2
    hot = ids_ref[...] == iota((clusters, rows), 0)
    owner = jnp.sum(jnp.where(hot, place_ref[:, 0:1], 0.0), axis=0, keepdims=True)
    offset = jnp.sum(jnp.where(hot, place_ref[:, 1:2], 0.0), axis=0, keepdims=True)
    slot = (offset + rank_ref[...]).astype(i32)
    from_owner = (owner.astype(i32) == iota((owners, rows), 0)).astype(f32).astype(bf16)
    from_owner = jnp.concatenate([from_owner] * 3, axis=0)
    at_slot = slot == iota((slots, rows), 0)
    back = back_ref[...]
    part0 = back.astype(bf16)
    rest = back - part0.astype(f32)
    part1 = rest.astype(bf16)
    part2 = (rest - part1.astype(f32)).astype(bf16)
    parts = jnp.concatenate([part0, part1, part2], axis=0)
    for i, ref in enumerate((best_ref, gap_ref)):
        table = lax.dot_general(
            parts[:, i * half : i * half + slots],
            from_owner,
            (((0,), (0,)), ((), ())),
            preferred_element_type=f32,
        )
        ref[...] = jnp.sum(jnp.where(at_slot, table, 0.0), axis=0, keepdims=True)


def restore(ids_row, rank, place, back, slots):
    rows = ids_row.shape[1]
    vmem = pl.BlockSpec(memory_space=pltpu.VMEM)
    return pl.pallas_call(
        functools.partial(restore_kernel, slots),
        out_shape=(jax.ShapeDtypeStruct((1, rows), f32),) * 2,
        in_specs=[vmem] * 4,
        out_specs=(vmem, vmem),
        compiler_params=pltpu.CompilerParams(vmem_limit_bytes=40 * MIB),
        name="restore_rows",
    )(ids_row, rank, place, back)


def exchange(x):
    return lax.all_to_all(x, "owner", split_axis=0, concat_axis=0, tiled=True)


def local(embeddings, cluster_ids):
    rows = embeddings.shape[0]
    owners = lax.axis_size("owner")
    clusters = CL_DEV * owners
    row_limit = 2 * rows // clusters
    window = round_up(row_limit, STEP) + STEP
    most = round_up(CL_DEV * row_limit, STEP)
    usual = min(most, round_up(9 * rows // (8 * owners), STEP))
    me = lax.axis_index("owner").astype(i32).reshape(1)
    labels = jnp.arange(clusters, dtype=i32)
    local_counts = jnp.sum((cluster_ids[:, None] == labels[None, :]).astype(i32), axis=0)
    counts = exchange(jnp.broadcast_to(local_counts[None, :], (owners, clusters)))
    ids_row = cluster_ids.reshape(1, rows)
    sorted_rows, rank = sort_rows(embeddings, ids_row, clusters, window)
    tab, bound, bound_t, place = assign(counts, me)

    def compare(slots):
        incoming = exchange(pack(sorted_rows, tab, owners, slots, window))
        back = exchange(score(incoming, tab, bound, bound_t))
        return restore(ids_row, rank, place, back, slots)

    best, gap = compare(usual)
    if usual < most:
        best, gap = lax.cond(tab[5, 0] <= usual, lambda: (best, gap), lambda: compare(most))
    return best.reshape(rows), gap.reshape(rows)


def solution(mesh):
    return jax.shard_map(
        local,
        mesh=mesh,
        in_specs=(P(("groups", "owner"), None), P(("groups", "owner"))),
        out_specs=(P(("groups", "owner")), P(("groups", "owner"))),
        check_vma=False,
    )
```

time: 356 us -> 137 us (0.38)
  blocking collectives: 158 us -> 84.5 us
  local copies, waits for them, and re-layouts: 76.9 us -> 3.66 us
  waiting for transfers between devices: 46.9 us -> 5.47 us
  other arithmetic: 29.3 us -> 0.85 us
  Pallas kernels: 0 us -> 27.2 us
  between operations: 15 us -> 1.35 us
  matrix products: 12.2 us -> 0 us
    psum x1 -> x0, blocking collectives: 138 us -> none  [local(): counts = lax.psum(local_counts, 'owner')]
    all_to_all x0 -> x1, blocking collectives: none -> 84.5 us  [exchange(): return lax.all_to_all(x, 'owner', split_axis=0, concat_axis=0, tiled=True)]
    gather x2 -> x0, local copies, waits for them, and re-layouts: 43.6 us -> none  [the longest x1 23 us: local(): flat_best[jnp.minimum(bucket_index, CL_DEV * cluster_cap - 1)]]
    unnamed x2 -> x0, waiting for transfers between devices: 41.1 us -> none
    scatter x2 -> x0, local copies, waits for them, and re-layouts: 31.4 us -> none  [the longest x1 22.8 us: local(): gathered = jnp.zeros((CL_DEV * cluster_cap, feature_width), jnp.bfloat16)...]
    pallas_call x0 -> x5, Pallas kernels: none -> 27.2 us  [the longest x1 10.9 us: score(): pl.pallas_call(score_kernel, out_shape=jax.ShapeDtypeStruct((owners, 2 *...]
    all_gather x1 -> x0, blocking collectives: 19.8 us -> none  [local(): lax.all_gather(centroids, 'owner', axis=0, tiled=True)]
    scatter x1 -> x0, other arithmetic: 14.2 us -> none  [local(): jnp.zeros((owners * slot_rows, feature_width), jnp.bfloat16).at[flat_index]]
  transfers between devices with their start and end apart: 4 -> 2, of which waited for: 2 -> 1; matrix products, arithmetic and copies ran while one was open for 8% -> 0% of each run, Pallas kernels for 0% -> 8%
where the time goes in v1:
time: 137 us
  blocking collectives  84.5 us (62%)
  Pallas kernels  27.2 us (20%)
  starting transfers between devices  13.6 us (10%)
  waiting for transfers between devices  5.47 us (4%)
  local copies, waits for them, and re-layouts  3.66 us (3%)
    all_to_all x1, blocking collectives, exchange(): return lax.all_to_all(x, 'owner', split_axis=0, concat_axis=0, tiled=True)  84.5 us
    all_to_all x2, starting transfers between devices, exchange(): return lax.all_to_all(x, 'owner', split_axis=0, concat_axis=0, tiled=True)  13.6 us
    pallas_call x1, Pallas kernels, score(): pl.pallas_call(score_kernel, out_shape=jax.ShapeDtypeStruct((owners, 2 *...  10.9 us
    pallas_call x1, Pallas kernels, sort_rows(): pl.pallas_call(functools.partial(sort_kernel, clusters), out_shape=(jax.S...  10.5 us
    all_to_all x2, waiting for transfers between devices, exchange(): return lax.all_to_all(x, 'owner', split_axis=0, concat_axis=0, tiled=True)  5.47 us
    pallas_call x1, Pallas kernels, pack(): pl.pallas_call(functools.partial(pack_kernel, owners, window, group), out...  3.79 us
  transfers between devices with their start and end apart: 2, of which 1 were waited for; matrix products, arithmetic and copies ran while one was open for 0% of the time, Pallas kernels for 8%

profile of v1, /device:TPU:0, one launch (start us, length us, event | category | flops | bytes accessed | tf_op | source)
XLA Modules:
  0.0 136.7 jit_solution(13901241594820979861)
XLA Ops:
  0.6 0.9 convert_reduce_fusion
  1.5 0.6 broadcast_in_dim.2
  2.1 7.4 %all-to-all-start.2 = ((s32[16,1,64]{2,1,0:T(1,128)}), s32[16,1,64]{2,1,0:T(1,128)S(1)}, u32[]{:S(2)}, u32[]{:S(2)}) async-start(s32[16,1,64]{2,1,0:T(1,128)} %broadcast_in_dim.2), calls=%async_computation.2 | async-start | bytes 16384 | tf_op jit(solution)/shard_map/all_to_all | solution.py:393
  9.5 0.0 copy-start
  9.5 1.9 %copy-done = bf16[2048,768]{1,0:T(8,128)(2,1)S(1)} copy-done((bf16[2048,768]{1,0:T(8,128)(2,1)S(1)}, bf16[2048,768]{1,0:T(8,128)(2,1)}, u32[]{:S(2)}) %copy-start) | copy-done | bytes 3145752
  11.4 10.5 %sort_rows.1 = (bf16[2128,768]{1,0:T(8,128)(2,1)S(1)}, f32[1,2048]{1,0:T(1,128)S(1)}) custom-call(s32[1,2048]{1,0:T(1,128)} %bitcast.19, bf16[2048,768]{1,0:T(8,128)(2,1)S(1)} %copy-done), custom_call_target="tpu_custom_call" | custom-call | flops 6442450944 | bytes 6291456 | tf_op jit(solution)/shard_map/sort_rows/pallas_call | solution.py:89
  21.9 0.0 all-to-all-done.2
  21.9 0.7 assign.1
  22.6 3.8 %pack_rows.3 = bf16[16,144,768]{2,1,0:T(8,128)(2,1)S(1)} custom-call(s32[8,128]{1,0:T(8,128)S(1)} %get-tuple-element.43.tab_ref, bf16[2128,768]{1,0:T(8,128)(2,1)S(1)} %get-tuple-element.44.sorted_ref), custom_call_target="tpu_custom_call" | custom-call | tf_op jit(solution)/shard_map/pack_rows/pallas_call | solution.py:231
  26.4 84.5 %all_to_all.38.x_ref = bf16[16,144,768]{2,1,0:T(8,128)(2,1)S(1)} all-to-all(bf16[16,144,768]{2,1,0:T(8,128)(2,1)S(1)} %pack_rows.3), channel_id=1, replica_groups=mesh['groups'=2,'owner'=16] {'owner'}, dimensions={0} | all-to-all | bytes 7077888 | tf_op jit(solution)/shard_map/all_to_all | solution.py:393
  110.9 0.0 copy-start.1
  110.9 10.9 %score_rows.3 = f32[16,512]{1,0:T(8,128)S(1)} custom-call(s32[8,128]{1,0:T(8,128)S(1)} %get-tuple-element.43.tab_ref, f32[16,128]{1,0:T(8,128)S(1)} %get-tuple-element.45.bound_ref, f32[8,16]{1,0:T(8,128)S(1)} %get-tuple-element.46.bound_t_ref, bf16[16,144,768]{2,1,0:T(8,128)(2,1)S(1)} %all_to_all.38.x_ref), custom_call_target="tpu_custom_call" | custom-call | tf_op jit(solution)/shard_map/score_rows/pallas_call | solution.py:335
  121.8 0.6 copy.7
  122.5 6.2 %all-to-all-start.4 = ((f32[16,1,512]{2,1,0:T(1,128)}), f32[16,1,512]{2,1,0:T(1,128)S(1)}, u32[]{:S(2)}, u32[]{:S(2)}) async-start(f32[16,1,512]{2,1,0:T(1,128)} %copy.7), calls=%async_computation.4 | async-start | bytes 65536 | tf_op jit(solution)/shard_map/all_to_all | solution.py:393
  128.7 0.5 slice.3
  129.9 5.5 %all-to-all-done.4 = f32[16,1,512]{2,1,0:T(1,128)S(1)} async-done(((f32[16,1,512]{2,1,0:T(1,128)}), f32[16,1,512]{2,1,0:T(1,128)S(1)}, u32[]{:S(2)}, u32[]{:S(2)}) %all-to-all-start.4) | async-done | bytes 32800 | tf_op jit(solution)/shard_map/all_to_all | solution.py:393
  135.3 0.0 copy-done.1
  135.4 1.3 restore_rows.3
  (2 shorter events, 0.0 us)
Async XLA Ops:
  2.1 19.8 %all-to-all-start.2 = ((s32[16,1,64]{2,1,0:T(1,128)}), s32[16,1,64]{2,1,0:T(1,128)S(1)}, u32[]{:S(2)}, u32[]{:S(2)}) async-start(s32[16,1,64]{2,1,0:T(1,128)} %broadcast_in_dim.2), calls=%async_computation.2 | async-start | bytes 16384 | tf_op jit(solution)/shard_map/all_to_all | solution.py:393
  9.5 1.9 %copy-start = (bf16[2048,768]{1,0:T(8,128)(2,1)S(1)}, bf16[2048,768]{1,0:T(8,128)(2,1)}, u32[]{:S(2)}) copy-start(bf16[2048,768]{1,0:T(8,128)(2,1)} %rows_ref.1) | copy-start | bytes 9437188
  110.9 24.5 %copy-start.1 = (s32[2048]{0:T(1024)S(1)}, s32[2048]{0:T(1024)}, u32[]{:S(2)}) copy-start(s32[2048]{0:T(1024)} %param.5) | copy-start | bytes 24580
  122.5 12.9 %all-to-all-start.4 = ((f32[16,1,512]{2,1,0:T(1,128)}), f32[16,1,512]{2,1,0:T(1,128)S(1)}, u32[]{:S(2)}, u32[]{:S(2)}) async-start(f32[16,1,512]{2,1,0:T(1,128)} %copy.7), calls=%async_computation.4 | async-start | bytes 65536 | tf_op jit(solution)/shard_map/all_to_all | solution.py:393

commit v2 on v1

--- a/solution.py
+++ b/solution.py
@@ -11,6 +11,8 @@
 VARIANTS = 8
 STEP = 16
 TILE = 256
+GROUP = 4
+MAX_PERMUTES = 16
 MIB = 1 << 20
 
 epsilon = 1e-06
@@ -103,11 +105,12 @@
     )(ids_row, embeddings)
 
 
-def assign_kernel(owners, me_ref, counts_ref, tab_ref, bound_ref, bound_t_ref, place_ref):
-    clusters = counts_ref.shape[1]
+def assign_kernel(owners, me_ref, *refs):
+    counts_refs, (tab_ref, bound_ref, bound_t_ref, place_ref) = refs[:owners], refs[owners:]
+    clusters = counts_refs[0].shape[1]
     shift = owners.bit_length() - 1
     me = me_ref[0]
-    count = counts_ref[...].astype(f32)
+    count = jnp.concatenate([ref[...] for ref in counts_refs], axis=0).astype(f32)
     count16 = count.astype(bf16)
     square = (clusters, clusters)
     sub, lane = iota(square, 0), iota(square, 1)
@@ -151,14 +154,12 @@
     owner_row = owner_of(rank_row, chosen + jnp.zeros_like(rank_row))
     layer_col, layer_row = rank_col >> shift, rank_row >> shift
 
-    mine_row = jnp.sum(
-        jnp.where(iota(count.shape, 0) == me, count, 0.0), axis=0, keepdims=True
-    )
+    mine_row = count[0:1, :]
     mine_col = to_col(mine_row)
     start_col = jnp.sum(jnp.where(lane < sub, mine_row, 0.0), axis=1, keepdims=True)
     earlier = (owner_row == owner_col) & (layer_row < layer_col)
     offset_col = jnp.sum(jnp.where(earlier, mine_row, 0.0), axis=1, keepdims=True)
-    perm = lane == layer_col * owners + owner_col
+    perm = lane == layer_col * owners + (owner_col ^ me)
 
     def by_slot(col):
         return jnp.sum(jnp.where(perm, col, 0.0), axis=0, keepdims=True).astype(i32)
@@ -184,12 +185,12 @@
     tab_ref[3:4, 0:128] = jnp.min(low, axis=0, keepdims=True).astype(i32)
     tab_ref[4:5, 0:128] = jnp.max(high, axis=0, keepdims=True).astype(i32)
     place_ref[...] = jnp.where(
-        iota((clusters, 128), 1) == 0, owner_col.astype(f32), offset_col
+        iota((clusters, 128), 1) == 0, (owner_col ^ me).astype(f32), offset_col
     )
 
 
 def assign(counts, me):
-    owners, clusters = counts.shape
+    owners, clusters = len(counts), counts[0].shape[1]
     vmem = pl.BlockSpec(memory_space=pltpu.VMEM)
     return pl.pallas_call(
         functools.partial(assign_kernel, owners),
@@ -199,59 +200,57 @@
             jax.ShapeDtypeStruct((8, owners), f32),
             jax.ShapeDtypeStruct((clusters, 128), f32),
         ),
-        in_specs=[pl.BlockSpec(memory_space=pltpu.SMEM), vmem],
+        in_specs=[pl.BlockSpec(memory_space=pltpu.SMEM)] + [vmem] * owners,
         out_specs=(vmem,) * 4,
         compiler_params=pltpu.CompilerParams(vmem_limit_bytes=24 * MIB),
         name="assign",
-    )(me, counts)
-
-
-def pack_kernel(owners, window, group, tab_ref, sorted_ref, out_ref):
-    slots = out_ref.shape[1]
+    )(me, *counts)
+
+
+def pack_kernel(owners, window, partners, tab_ref, sorted_ref, *out_refs):
+    slots = out_refs[0].shape[0]
     slot = iota((slots, 1), 0)
-    for g in range(group):
-        owner = pl.program_id(0) * group + g
+    for partner, out_ref in zip(partners, out_refs):
         runs = []
         source = jnp.full((slots, 1), -1, i32)
         for k in range(CL_DEV):
-            start = tab_ref[0, k * owners + owner]
-            size = tab_ref[1, k * owners + owner]
-            offset = tab_ref[2, k * owners + owner]
+            start = tab_ref[0, k * owners + partner]
+            size = tab_ref[1, k * owners + partner]
+            offset = tab_ref[2, k * owners + partner]
             first = pl.multiple_of((start // STEP) * STEP, STEP)
             runs.append(sorted_ref[pl.ds(first, window), :])
             inside = (slot >= offset) & (slot < offset + size)
             source = jnp.where(inside, slot + (k * window + start - first - offset), source)
         take = iota((slots, CL_DEV * window), 1) == source
-        out_ref[g] = mm(take.astype(f32).astype(bf16), jnp.concatenate(runs, axis=0)).astype(bf16)
-
-
-def pack(sorted_rows, tab, owners, slots, window):
-    total, width = sorted_rows.shape
-    group = 4
+        out_ref[...] = mm(take.astype(f32).astype(bf16), jnp.concatenate(runs, axis=0)).astype(bf16)
+
+
+def pack(sorted_rows, tab, owners, partners, slots, window):
+    width = sorted_rows.shape[1]
+    vmem = pl.BlockSpec(memory_space=pltpu.VMEM)
     return pl.pallas_call(
-        functools.partial(pack_kernel, owners, window, group),
-        out_shape=jax.ShapeDtypeStruct((owners, slots, width), bf16),
-        grid=(owners // group,),
-        in_specs=[
-            pl.BlockSpec(memory_space=pltpu.SMEM),
-            pl.BlockSpec((total, width), lambda i: (0, 0)),
-        ],
-        out_specs=pl.BlockSpec((group, slots, width), lambda i: (i, 0, 0)),
-        compiler_params=pltpu.CompilerParams(vmem_limit_bytes=40 * MIB),
+        functools.partial(pack_kernel, owners, window, partners),
+        out_shape=(jax.ShapeDtypeStruct((slots, width), bf16),) * len(partners),
+        in_specs=[pl.BlockSpec(memory_space=pltpu.SMEM), vmem],
+        out_specs=(vmem,) * len(partners),
+        compiler_params=pltpu.CompilerParams(vmem_limit_bytes=24 * MIB),
         name="pack_rows",
     )(tab, sorted_rows)
 
 
 def score_kernel(
-    tab_ref, bound_ref, bound_t_ref, x_ref, out_ref, cid_col, cid_row, row_acc, col_acc
+    owners, tab_ref, bound_ref, bound_t_ref, *refs
 ):
-    owners, slots, width = x_ref.shape
+    x_refs, out_refs = refs[:owners], refs[owners : 2 * owners]
+    cid_col, cid_row, row_acc, col_acc = refs[2 * owners :]
+    slots, width = x_refs[0].shape
     chunk = owners * STEP
     chunks = slots // STEP
-    half = out_ref.shape[1] // 2
+    half = out_refs[0].shape[1] // 2
 
     def load(q):
-        return x_ref[:, pl.ds(pl.multiple_of(q * STEP, STEP), STEP), :].reshape(chunk, width)
+        at = pl.ds(pl.multiple_of(q * STEP, STEP), STEP)
+        return jnp.concatenate([ref[at, :] for ref in x_refs], axis=0)
 
     spread = (iota((chunk, owners), 0) // STEP) == iota((chunk, owners), 1)
     edges = mm(spread.astype(f32).astype(bf16), bound_ref[...].astype(bf16))
@@ -325,18 +324,21 @@
     keep = (lanes % STEP) == (iota((chunk, half), 0) % STEP)
     for i, z in enumerate((best_z, gap_z)):
         z = jnp.where(keep, z, 0.0).reshape(owners, STEP, half)
-        out_ref[:, i * half : (i + 1) * half] = jnp.sum(z, axis=1)
+        z = jnp.sum(z, axis=1)
+        for r, ref in enumerate(out_refs):
+            ref[:, i * half : (i + 1) * half] = z[r : r + 1, :]
 
 
 def score(incoming, tab, bound, bound_t):
-    owners, slots, width = incoming.shape
+    owners = len(incoming)
+    slots, width = incoming[0].shape
     chunk, chunks = owners * STEP, slots // STEP
     vmem = pl.BlockSpec(memory_space=pltpu.VMEM)
     return pl.pallas_call(
-        score_kernel,
-        out_shape=jax.ShapeDtypeStruct((owners, 2 * round_up(slots, 128)), f32),
-        in_specs=[pl.BlockSpec(memory_space=pltpu.SMEM), vmem, vmem, vmem],
-        out_specs=vmem,
+        functools.partial(score_kernel, owners),
+        out_shape=(jax.ShapeDtypeStruct((1, 2 * round_up(slots, 128)), f32),) * owners,
+        in_specs=[pl.BlockSpec(memory_space=pltpu.SMEM)] + [vmem] * (2 + owners),
+        out_specs=(vmem,) * owners,
         scratch_shapes=[
             pltpu.VMEM((chunks, chunk, 1), f32),
             pltpu.VMEM((chunks, 1, chunk), f32),
@@ -345,14 +347,15 @@
         ],
         compiler_params=pltpu.CompilerParams(vmem_limit_bytes=48 * MIB),
         name="score_rows",
-    )(tab, bound, bound_t, incoming)
-
-
-def restore_kernel(slots, ids_ref, rank_ref, place_ref, back_ref, best_ref, gap_ref):
+    )(tab, bound, bound_t, *incoming)
+
+
+def restore_kernel(slots, ids_ref, rank_ref, place_ref, *refs):
+    back_refs, (best_ref, gap_ref) = refs[:-2], refs[-2:]
     rows = ids_ref.shape[1]
     clusters = place_ref.shape[0]
-    owners = back_ref.shape[0]
-    half = back_ref.shape[1] // 2
+    owners = len(back_refs)
+    half = back_refs[0].shape[1] // 2
     hot = ids_ref[...] == iota((clusters, rows), 0)
     owner = jnp.sum(jnp.where(hot, place_ref[:, 0:1], 0.0), axis=0, keepdims=True)
     offset = jnp.sum(jnp.where(hot, place_ref[:, 1:2], 0.0), axis=0, keepdims=True)
@@ -360,7 +363,7 @@
     from_owner = (owner.astype(i32) == iota((owners, rows), 0)).astype(f32).astype(bf16)
     from_owner = jnp.concatenate([from_owner] * 3, axis=0)
     at_slot = slot == iota((slots, rows), 0)
-    back = back_ref[...]
+    back = jnp.concatenate([ref[...] for ref in back_refs], axis=0)
     part0 = back.astype(bf16)
     rest = back - part0.astype(f32)
     part1 = rest.astype(bf16)
@@ -382,15 +385,32 @@
     return pl.pallas_call(
         functools.partial(restore_kernel, slots),
         out_shape=(jax.ShapeDtypeStruct((1, rows), f32),) * 2,
-        in_specs=[vmem] * 4,
+        in_specs=[vmem] * (3 + len(back)),
         out_specs=(vmem, vmem),
         compiler_params=pltpu.CompilerParams(vmem_limit_bytes=40 * MIB),
         name="restore_rows",
-    )(ids_row, rank, place, back)
-
-
-def exchange(x):
-    return lax.all_to_all(x, "owner", split_axis=0, concat_axis=0, tiled=True)
+    )(ids_row, rank, place, *back)
+
+
+def swap(x, partner):
+    if partner == 0:
+        return x
+    owners = lax.axis_size("owner")
+    return lax.ppermute(x, "owner", [(i, i ^ partner) for i in range(owners)])
+
+
+def swap_together(blocks):
+    owners = len(blocks)
+    order = jnp.arange(owners, dtype=i32) ^ lax.axis_index("owner").astype(i32)
+    stacked = jnp.stack(blocks)[order]
+    arrived = lax.all_to_all(stacked, "owner", split_axis=0, concat_axis=0, tiled=True)[order]
+    return [arrived[r] for r in range(owners)]
+
+
+def swap_all(blocks, apart):
+    if not apart:
+        return swap_together(blocks)
+    return [swap(block, r) for r, block in enumerate(blocks)]
 
 
 def local(embeddings, cluster_ids):
@@ -404,19 +424,32 @@
     me = lax.axis_index("owner").astype(i32).reshape(1)
     labels = jnp.arange(clusters, dtype=i32)
     local_counts = jnp.sum((cluster_ids[:, None] == labels[None, :]).astype(i32), axis=0)
-    counts = exchange(jnp.broadcast_to(local_counts[None, :], (owners, clusters)))
+    local_counts = local_counts.reshape(1, clusters)
+    few = owners <= MAX_PERMUTES
+    counts = swap_all([local_counts] * owners, few)
     ids_row = cluster_ids.reshape(1, rows)
     sorted_rows, rank = sort_rows(embeddings, ids_row, clusters, window)
     tab, bound, bound_t, place = assign(counts, me)
 
-    def compare(slots):
-        incoming = exchange(pack(sorted_rows, tab, owners, slots, window))
-        back = exchange(score(incoming, tab, bound, bound_t))
+    half = owners // 2
+    order = [r for i in reversed(range(half)) for r in (half + i, i)]
+
+    def compare(slots, apart):
+        blocks = [None] * owners
+        for first in range(0, owners, GROUP):
+            partners = tuple(order[first : first + GROUP])
+            packed = pack(sorted_rows, tab, owners, partners, slots, window)
+            for r, block in zip(partners, packed):
+                blocks[r] = swap(block, r) if apart else block
+        incoming = blocks if apart else swap_together(blocks)
+        back = swap_all(score(incoming, tab, bound, bound_t), apart)
         return restore(ids_row, rank, place, back, slots)
 
-    best, gap = compare(usual)
+    best, gap = compare(usual, few)
     if usual < most:
-        best, gap = lax.cond(tab[5, 0] <= usual, lambda: (best, gap), lambda: compare(most))
+        best, gap = lax.cond(
+            tab[5, 0] <= usual, lambda: (best, gap), lambda: compare(most, False)
+        )
     return best.reshape(rows), gap.reshape(rows)
 
 

time: 137 us -> 173 us (1.26)
  blocking collectives: 84.5 us -> 0 us
  starting transfers between devices: 13.6 us -> 79.4 us
  waiting for transfers between devices: 5.47 us -> 59.4 us
  Pallas kernels: 27.2 us -> 29.1 us
    all_to_all x1 -> x0, blocking collectives: 84.5 us -> none  [exchange(): return lax.all_to_all(x, 'owner', split_axis=0, concat_axis=0, tiled=True)]
    ppermute x0 -> x45, starting transfers between devices: none -> 79.4 us  [swap(): return lax.ppermute(x, 'owner', [(i, i ^ partner) for i in range(owners)])]
    ppermute x0 -> x45, waiting for transfers between devices: none -> 59.4 us  [swap(): return lax.ppermute(x, 'owner', [(i, i ^ partner) for i in range(owners)])]
    all_to_all x2 -> x0, starting transfers between devices: 13.6 us -> none  [exchange(): return lax.all_to_all(x, 'owner', split_axis=0, concat_axis=0, tiled=True)]
    all_to_all x2 -> x0, waiting for transfers between devices: 5.47 us -> none  [exchange(): return lax.all_to_all(x, 'owner', split_axis=0, concat_axis=0, tiled=True)]
    pallas_call x2 -> x5, Pallas kernels: 14.7 us -> 16.7 us  [the longest x1 11.1 us: score(): pl.pallas_call(functools.partial(score_kernel, owners), out_shape=(jax.Sh...]
  transfers between devices with their start and end apart: 2 -> 45, of which waited for: 1 -> 13; matrix products, arithmetic and copies ran while one was open for 0% -> 0% of each run, Pallas kernels for 8% -> 8%
where the time goes in v2:
time: 173 us
  starting transfers between devices  79.4 us (46%)
  waiting for transfers between devices  59.4 us (34%)
  Pallas kernels  29.1 us (17%)
  local copies, waits for them, and re-layouts  2.41 us (1%)
    ppermute x45, starting transfers between devices, swap(): return lax.ppermute(x, 'owner', [(i, i ^ partner) for i in range(owners)])  79.4 us
    ppermute x45, waiting for transfers between devices, swap(): return lax.ppermute(x, 'owner', [(i, i ^ partner) for i in range(owners)])  59.4 us
    pallas_call x1, Pallas kernels, score(): pl.pallas_call(functools.partial(score_kernel, owners), out_shape=(jax.Sh...  11.1 us
    pallas_call x1, Pallas kernels, sort_rows(): pl.pallas_call(functools.partial(sort_kernel, clusters), out_shape=(jax.S...  10.5 us
    pallas_call x4, Pallas kernels, pack(): pl.pallas_call(functools.partial(pack_kernel, owners, window, partners),...  5.57 us
  transfers between devices with their start and end apart: 45, of which 13 were waited for; matrix products, arithmetic and copies ran while one was open for 0% of the time, Pallas kernels for 8%

profile of v2, /device:TPU:0, one launch (start us, length us, event | category | flops | bytes accessed | tf_op | source)
XLA Modules:
  0.0 172.6 jit_solution(13141952314718016018)
XLA Ops:
  2.0 2.6 %collective-permute-start.1 = (s32[1,64]{1,0:T(1,128)S(1)}, s32[1,64]{1,0:T(1,128)S(1)}, u32[]{:S(2)}, u32[]{:S(2)}) collective-permute-start(s32[1,64]{1,0:T(1,128)S(1)} %bitcast.110), channel_id=1, source_target_pairs={{0,2},{1,3},{2,0},{3,1},{4,6},{5,7},{6,4},{7,5},{8,10},{9,11},{10,... | collective-permute-start | bytes 776 | tf_op jit(solution)/shard_map/ppermute | solution.py:399
  4.6 2.3 %collective-permute-start.10 = (s32[1,64]{1,0:T(1,128)S(1)}, s32[1,64]{1,0:T(1,128)S(1)}, u32[]{:S(2)}, u32[]{:S(2)}) collective-permute-start(s32[1,64]{1,0:T(1,128)S(1)} %bitcast.111), channel_id=1, source_target_pairs={{0,11},{1,10},{2,9},{3,8},{4,15},{5,14},{6,13},{7,12},{8,3},{9,2},... | collective-permute-start | bytes 776 | tf_op jit(solution)/shard_map/ppermute | solution.py:399
  8.2 2.1 %collective-permute-start.12 = (s32[1,64]{1,0:T(1,128)S(1)}, s32[1,64]{1,0:T(1,128)S(1)}, u32[]{:S(2)}, u32[]{:S(2)}) collective-permute-start(s32[1,64]{1,0:T(1,128)S(1)} %bitcast.113), channel_id=1, source_target_pairs={{0,13},{1,12},{2,15},{3,14},{4,9},{5,8},{6,11},{7,10},{8,5},{9,4},... | collective-permute-start | bytes 776 | tf_op jit(solution)/shard_map/ppermute | solution.py:399
  10.4 1.9 %copy-done = bf16[2048,768]{1,0:T(8,128)(2,1)S(1)} copy-done((bf16[2048,768]{1,0:T(8,128)(2,1)S(1)}, bf16[2048,768]{1,0:T(8,128)(2,1)}, u32[]{:S(2)}) %copy-start) | copy-done | bytes 3145752
  12.3 10.5 %sort_rows.1 = (bf16[2128,768]{1,0:T(8,128)(2,1)S(1)}, f32[1,2048]{1,0:T(1,128)S(1)}) custom-call(s32[1,2048]{1,0:T(1,128)} %bitcast.128, bf16[2048,768]{1,0:T(8,128)(2,1)S(1)} %copy-done), custom_call_target="tpu_custom_call" | custom-call | flops 6442450944 | bytes 6291456 | tf_op jit(solution)/shard_map/sort_rows/pallas_call | solution.py:91
  22.8 2.4 %collective-permute-start.13 = (s32[1,64]{1,0:T(1,128)S(1)}, s32[1,64]{1,0:T(1,128)S(1)}, u32[]{:S(2)}, u32[]{:S(2)}) collective-permute-start(s32[1,64]{1,0:T(1,128)S(1)} %bitcast.114), channel_id=1, source_target_pairs={{0,14},{1,15},{2,12},{3,13},{4,10},{5,11},{6,8},{7,9},{8,6},{9,7},... | collective-permute-start | bytes 776 | tf_op jit(solution)/shard_map/ppermute | solution.py:399
  25.2 2.2 %collective-permute-start.14 = (s32[1,64]{1,0:T(1,128)S(1)}, s32[1,64]{1,0:T(1,128)S(1)}, u32[]{:S(2)}, u32[]{:S(2)}) collective-permute-start(s32[1,64]{1,0:T(1,128)S(1)} %bitcast.115), channel_id=1, source_target_pairs={{0,15},{1,14},{2,13},{3,12},{4,11},{5,10},{6,9},{7,8},{8,7},{9,6},... | collective-permute-start | bytes 776 | tf_op jit(solution)/shard_map/ppermute | solution.py:399
  28.8 1.5 collective-permute-start.4
  30.9 2.4 %collective-permute-start.6 = (s32[1,64]{1,0:T(1,128)S(1)}, s32[1,64]{1,0:T(1,128)S(1)}, u32[]{:S(2)}, u32[]{:S(2)}) collective-permute-start(s32[1,64]{1,0:T(1,128)S(1)} %bitcast.120), channel_id=1, source_target_pairs={{0,7},{1,6},{2,5},{3,4},{4,3},{5,2},{6,1},{7,0},{8,15},{9,14},{10,... | collective-permute-start | bytes 776 | tf_op jit(solution)/shard_map/ppermute | solution.py:399
  33.6 2.1 %collective-permute-start.8 = (s32[1,64]{1,0:T(1,128)S(1)}, s32[1,64]{1,0:T(1,128)S(1)}, u32[]{:S(2)}, u32[]{:S(2)}) collective-permute-start(s32[1,64]{1,0:T(1,128)S(1)} %bitcast.122), channel_id=1, source_target_pairs={{0,9},{1,8},{2,11},{3,10},{4,13},{5,12},{6,15},{7,14},{8,1},{9,0},... | collective-permute-start | bytes 776 | tf_op jit(solution)/shard_map/ppermute | solution.py:399
  35.7 1.5 collective-permute-start.9
  37.7 3.3 %collective-permute-done.9.refs_10_ = s32[1,64]{1,0:T(1,128)S(1)} collective-permute-done((s32[1,64]{1,0:T(1,128)S(1)}, s32[1,64]{1,0:T(1,128)S(1)}, u32[]{:S(2)}, u32[]{:S(2)}) %collective-permute-start.9) | collective-permute-done | bytes 288 | tf_op jit(solution)/shard_map/ppermute | solution.py:399
  53.8 3.0 %collective-permute-done.17.refs_3_ = bf16[144,768]{1,0:T(8,128)(2,1)S(1)} collective-permute-done((bf16[144,768]{1,0:T(8,128)(2,1)S(1)}, bf16[144,768]{1,0:T(8,128)(2,1)S(1)}, u32[]{:S(2)}, u32[]{:S(2)}) %collective-permute-start.17) | collective-permute-done | bytes 221216 | tf_op jit(solution)/shard_map/ppermute | solution.py:399
  57.4 2.2 %collective-permute-start.23 = (bf16[144,768]{1,0:T(8,128)(2,1)S(1)}, bf16[144,768]{1,0:T(8,128)(2,1)S(1)}, u32[]{:S(2)}, u32[]{:S(2)}) collective-permute-start(bf16[144,768]{1,0:T(8,128)(2,1)S(1)} %get-tuple-element.122), channel_id=1, source_target_pairs={{0,9},{1,8},{2,11},{3,10},{4,13},{5,12},{6,15},{7,14},{8,1},{9,0},... | collective-permute-start | bytes 663560 | tf_op jit(solution)/shard_map/ppermute | solution.py:399
  61.1 14.5 %collective-permute-done.20.refs_6_ = bf16[144,768]{1,0:T(8,128)(2,1)S(1)} collective-permute-done((bf16[144,768]{1,0:T(8,128)(2,1)S(1)}, bf16[144,768]{1,0:T(8,128)(2,1)S(1)}, u32[]{:S(2)}, u32[]{:S(2)}) %collective-permute-start.20) | collective-permute-done | bytes 221216 | tf_op jit(solution)/shard_map/ppermute | solution.py:399
  75.6 3.5 %collective-permute-done.21.refs_7_ = bf16[144,768]{1,0:T(8,128)(2,1)S(1)} collective-permute-done((bf16[144,768]{1,0:T(8,128)(2,1)S(1)}, bf16[144,768]{1,0:T(8,128)(2,1)S(1)}, u32[]{:S(2)}, u32[]{:S(2)}) %collective-permute-start.21) | collective-permute-done | bytes 221216 | tf_op jit(solution)/shard_map/ppermute | solution.py:399
  80.5 2.5 %collective-permute-start.27 = (bf16[144,768]{1,0:T(8,128)(2,1)S(1)}, bf16[144,768]{1,0:T(8,128)(2,1)S(1)}, u32[]{:S(2)}, u32[]{:S(2)}) collective-permute-start(bf16[144,768]{1,0:T(8,128)(2,1)S(1)} %get-tuple-element.126), channel_id=1, source_target_pairs={{0,13},{1,12},{2,15},{3,14},{4,9},{5,8},{6,11},{7,10},{8,5},{9,4},... | collective-permute-start | bytes 663560 | tf_op jit(solution)/shard_map/ppermute | solution.py:399
  83.0 20.1 %collective-permute-done.23.refs_9_ = bf16[144,768]{1,0:T(8,128)(2,1)S(1)} collective-permute-done((bf16[144,768]{1,0:T(8,128)(2,1)S(1)}, bf16[144,768]{1,0:T(8,128)(2,1)S(1)}, u32[]{:S(2)}, u32[]{:S(2)}) %collective-permute-start.23) | collective-permute-done | bytes 221216 | tf_op jit(solution)/shard_map/ppermute | solution.py:399
  103.1 4.6 %collective-permute-start.29 = (bf16[144,768]{1,0:T(8,128)(2,1)S(1)}, bf16[144,768]{1,0:T(8,128)(2,1)S(1)}, u32[]{:S(2)}, u32[]{:S(2)}) collective-permute-start(bf16[144,768]{1,0:T(8,128)(2,1)S(1)} %get-tuple-element.128), channel_id=1, source_target_pairs={{0,15},{1,14},{2,13},{3,12},{4,11},{5,10},{6,9},{7,8},{8,7},{9,6},... | collective-permute-start | bytes 663560 | tf_op jit(solution)/shard_map/ppermute | solution.py:399
  108.8 5.4 %collective-permute-done.28.refs_14_ = bf16[144,768]{1,0:T(8,128)(2,1)S(1)} collective-permute-done((bf16[144,768]{1,0:T(8,128)(2,1)S(1)}, bf16[144,768]{1,0:T(8,128)(2,1)S(1)}, u32[]{:S(2)}, u32[]{:S(2)}) %collective-permute-start.28) | collective-permute-done | bytes 221216 | tf_op jit(solution)/shard_map/ppermute | solution.py:399
  114.1 4.1 %collective-permute-done.29.refs_15_ = bf16[144,768]{1,0:T(8,128)(2,1)S(1)} collective-permute-done((bf16[144,768]{1,0:T(8,128)(2,1)S(1)}, bf16[144,768]{1,0:T(8,128)(2,1)S(1)}, u32[]{:S(2)}, u32[]{:S(2)}) %collective-permute-start.29) | collective-permute-done | bytes 221216 | tf_op jit(solution)/shard_map/ppermute | solution.py:399
  118.2 11.1 %score_rows.3 = (f32[1,512]{1,0:T(1,128)S(1)}, f32[1,512]{1,0:T(1,128)S(1)}, f32[1,512]{1,0:T(1,128)S(1)}, f32[1,512]{1,0:T(1,128)S(1)}, f32[1,512]{1,0:T(1,128)...) custom-call(s32[8,128]{1,0:T(8,128)S(1)} %get-tuple-element.107.tab_, ...), custom_call_target="tpu_custom_call" | custom-call | tf_op jit(solution)/shard_map/score_rows/pallas_call | solution.py:337
  129.5 1.9 %collective-permute-start.31 = (f32[1,512]{1,0:T(1,128)S(1)}, f32[1,512]{1,0:T(1,128)S(1)}, u32[]{:S(2)}, u32[]{:S(2)}) collective-permute-start(f32[1,512]{1,0:T(1,128)S(1)} %get-tuple-element.131), channel_id=1, source_target_pairs={{0,2},{1,3},{2,0},{3,1},{4,6},{5,7},{6,4},{7,5},{8,10},{9,11},{10,... | collective-permute-start | bytes 6152 | tf_op jit(solution)/shard_map/ppermute | solution.py:399
  131.5 19.1 %collective-permute-start.33 = (f32[1,512]{1,0:T(1,128)S(1)}, f32[1,512]{1,0:T(1,128)S(1)}, u32[]{:S(2)}, u32[]{:S(2)}) collective-permute-start(f32[1,512]{1,0:T(1,128)S(1)} %get-tuple-element.133), channel_id=1, source_target_pairs={{0,4},{1,5},{2,6},{3,7},{4,0},{5,1},{6,2},{7,3},{8,12},{9,13},{10,... | collective-permute-start | bytes 6152 | tf_op jit(solution)/shard_map/ppermute | solution.py:399
  150.6 2.7 %collective-permute-start.35 = (f32[1,512]{1,0:T(1,128)S(1)}, f32[1,512]{1,0:T(1,128)S(1)}, u32[]{:S(2)}, u32[]{:S(2)}) collective-permute-start(f32[1,512]{1,0:T(1,128)S(1)} %get-tuple-element.135), channel_id=1, source_target_pairs={{0,6},{1,7},{2,4},{3,5},{4,2},{5,3},{6,0},{7,1},{8,14},{9,15},{10,... | collective-permute-start | bytes 6152 | tf_op jit(solution)/shard_map/ppermute | solution.py:399
  153.3 1.7 collective-permute-start.37
  155.9 2.8 %collective-permute-start.39 = (f32[1,512]{1,0:T(1,128)S(1)}, f32[1,512]{1,0:T(1,128)S(1)}, u32[]{:S(2)}, u32[]{:S(2)}) collective-permute-start(f32[1,512]{1,0:T(1,128)S(1)} %get-tuple-element.139), channel_id=1, source_target_pairs={{0,10},{1,11},{2,8},{3,9},{4,14},{5,15},{6,12},{7,13},{8,2},{9,3},... | collective-permute-start | bytes 6152 | tf_op jit(solution)/shard_map/ppermute | solution.py:399
  159.5 1.7 collective-permute-start.41
  161.2 1.8 %collective-permute-start.42 = (f32[1,512]{1,0:T(1,128)S(1)}, f32[1,512]{1,0:T(1,128)S(1)}, u32[]{:S(2)}, u32[]{:S(2)}) collective-permute-start(f32[1,512]{1,0:T(1,128)S(1)} %get-tuple-element.142), channel_id=1, source_target_pairs={{0,13},{1,12},{2,15},{3,14},{4,9},{5,8},{6,11},{7,10},{8,5},{9,4},... | collective-permute-start | bytes 6152 | tf_op jit(solution)/shard_map/ppermute | solution.py:399
  163.0 2.6 %collective-permute-start.43 = (f32[1,512]{1,0:T(1,128)S(1)}, f32[1,512]{1,0:T(1,128)S(1)}, u32[]{:S(2)}, u32[]{:S(2)}) collective-permute-start(f32[1,512]{1,0:T(1,128)S(1)} %get-tuple-element.143), channel_id=1, source_target_pairs={{0,14},{1,15},{2,12},{3,13},{4,10},{5,11},{6,8},{7,9},{8,6},{9,7},... | collective-permute-start | bytes 6152 | tf_op jit(solution)/shard_map/ppermute | solution.py:399
  165.6 1.9 %collective-permute-start.44 = (f32[1,512]{1,0:T(1,128)S(1)}, f32[1,512]{1,0:T(1,128)S(1)}, u32[]{:S(2)}, u32[]{:S(2)}) collective-permute-start(f32[1,512]{1,0:T(1,128)S(1)} %get-tuple-element.144), channel_id=1, source_target_pairs={{0,15},{1,14},{2,13},{3,12},{4,11},{5,10},{6,9},{7,8},{8,7},{9,6},... | collective-permute-start | bytes 6152 | tf_op jit(solution)/shard_map/ppermute | solution.py:399
  169.3 2.0 %collective-permute-done.44.refs_15_ = f32[1,512]{1,0:T(1,128)S(1)} collective-permute-done((f32[1,512]{1,0:T(1,128)S(1)}, f32[1,512]{1,0:T(1,128)S(1)}, u32[]{:S(2)}, u32[]{:S(2)}) %collective-permute-start.44) | collective-permute-done | bytes 2080 | tf_op jit(solution)/shard_map/ppermute | solution.py:399
  (73 shorter events, 27.5 us)
Async XLA Ops:
  1.5 21.3 %collective-permute-start = (s32[1,64]{1,0:T(1,128)S(1)}, s32[1,64]{1,0:T(1,128)S(1)}, u32[]{:S(2)}, u32[]{:S(2)}) collective-permute-start(s32[1,64]{1,0:T(1,128)S(1)} %bitcast.109), channel_id=1, source_target_pairs={{0,1},{1,0},{2,3},{3,2},{4,5},{5,4},{6,7},{7,6},{8,9},{9,8},{10,11... | collective-permute-start | bytes 776 | tf_op jit(solution)/shard_map/ppermute | solution.py:399
  2.0 23.2 %collective-permute-start.1 = (s32[1,64]{1,0:T(1,128)S(1)}, s32[1,64]{1,0:T(1,128)S(1)}, u32[]{:S(2)}, u32[]{:S(2)}) collective-permute-start(s32[1,64]{1,0:T(1,128)S(1)} %bitcast.110), channel_id=1, source_target_pairs={{0,2},{1,3},{2,0},{3,1},{4,6},{5,7},{6,4},{7,5},{8,10},{9,11},{10,... | collective-permute-start | bytes 776 | tf_op jit(solution)/shard_map/ppermute | solution.py:399
  4.6 22.8 %collective-permute-start.10 = (s32[1,64]{1,0:T(1,128)S(1)}, s32[1,64]{1,0:T(1,128)S(1)}, u32[]{:S(2)}, u32[]{:S(2)}) collective-permute-start(s32[1,64]{1,0:T(1,128)S(1)} %bitcast.111), channel_id=1, source_target_pairs={{0,11},{1,10},{2,9},{3,8},{4,15},{5,14},{6,13},{7,12},{8,3},{9,2},... | collective-permute-start | bytes 776 | tf_op jit(solution)/shard_map/ppermute | solution.py:399
  6.9 21.9 %collective-permute-start.11 = (s32[1,64]{1,0:T(1,128)S(1)}, s32[1,64]{1,0:T(1,128)S(1)}, u32[]{:S(2)}, u32[]{:S(2)}) collective-permute-start(s32[1,64]{1,0:T(1,128)S(1)} %bitcast.112), channel_id=1, source_target_pairs={{0,12},{1,13},{2,14},{3,15},{4,8},{5,9},{6,10},{7,11},{8,4},{9,5},... | collective-permute-start | bytes 776 | tf_op jit(solution)/shard_map/ppermute | solution.py:399
  8.2 20.6 %collective-permute-start.12 = (s32[1,64]{1,0:T(1,128)S(1)}, s32[1,64]{1,0:T(1,128)S(1)}, u32[]{:S(2)}, u32[]{:S(2)}) collective-permute-start(s32[1,64]{1,0:T(1,128)S(1)} %bitcast.113), channel_id=1, source_target_pairs={{0,13},{1,12},{2,15},{3,14},{4,9},{5,8},{6,11},{7,10},{8,5},{9,4},... | collective-permute-start | bytes 776 | tf_op jit(solution)/shard_map/ppermute | solution.py:399
  22.8 7.6 %collective-permute-start.13 = (s32[1,64]{1,0:T(1,128)S(1)}, s32[1,64]{1,0:T(1,128)S(1)}, u32[]{:S(2)}, u32[]{:S(2)}) collective-permute-start(s32[1,64]{1,0:T(1,128)S(1)} %bitcast.114), channel_id=1, source_target_pairs={{0,14},{1,15},{2,12},{3,13},{4,10},{5,11},{6,8},{7,9},{8,6},{9,7},... | collective-permute-start | bytes 776 | tf_op jit(solution)/shard_map/ppermute | solution.py:399
  43.1 7.9 %collective-permute-start.15 = (bf16[144,768]{1,0:T(8,128)(2,1)S(1)}, bf16[144,768]{1,0:T(8,128)(2,1)S(1)}, u32[]{:S(2)}, u32[]{:S(2)}) collective-permute-start(bf16[144,768]{1,0:T(8,128)(2,1)S(1)} %get-tuple-element.114), channel_id=1, source_target_pairs={{0,1},{1,0},{2,3},{3,2},{4,5},{5,4},{6,7},{7,6},{8,9},{9,8},{10,11... | collective-permute-start | bytes 663560 | tf_op jit(solution)/shard_map/ppermute | solution.py:399
  44.5 8.3 %collective-permute-start.16 = (bf16[144,768]{1,0:T(8,128)(2,1)S(1)}, bf16[144,768]{1,0:T(8,128)(2,1)S(1)}, u32[]{:S(2)}, u32[]{:S(2)}) collective-permute-start(bf16[144,768]{1,0:T(8,128)(2,1)S(1)} %get-tuple-element.115), channel_id=1, source_target_pairs={{0,2},{1,3},{2,0},{3,1},{4,6},{5,7},{6,4},{7,5},{8,10},{9,11},{10,... | collective-permute-start | bytes 663560 | tf_op jit(solution)/shard_map/ppermute | solution.py:399
  45.1 11.7 %collective-permute-start.17 = (bf16[144,768]{1,0:T(8,128)(2,1)S(1)}, bf16[144,768]{1,0:T(8,128)(2,1)S(1)}, u32[]{:S(2)}, u32[]{:S(2)}) collective-permute-start(bf16[144,768]{1,0:T(8,128)(2,1)S(1)} %get-tuple-element.116), channel_id=1, source_target_pairs={{0,3},{1,2},{2,1},{3,0},{4,7},{5,6},{6,5},{7,4},{8,11},{9,10},{10,... | collective-permute-start | bytes 663560 | tf_op jit(solution)/shard_map/ppermute | solution.py:399
  47.9 9.5 %collective-permute-start.18 = (bf16[144,768]{1,0:T(8,128)(2,1)S(1)}, bf16[144,768]{1,0:T(8,128)(2,1)S(1)}, u32[]{:S(2)}, u32[]{:S(2)}) collective-permute-start(bf16[144,768]{1,0:T(8,128)(2,1)S(1)} %get-tuple-element.117), channel_id=1, source_target_pairs={{0,4},{1,5},{2,6},{3,7},{4,0},{5,1},{6,2},{7,3},{8,12},{9,13},{10,... | collective-permute-start | bytes 663560 | tf_op jit(solution)/shard_map/ppermute | solution.py:399
  48.5 11.1 %collective-permute-start.19 = (bf16[144,768]{1,0:T(8,128)(2,1)S(1)}, bf16[144,768]{1,0:T(8,128)(2,1)S(1)}, u32[]{:S(2)}, u32[]{:S(2)}) collective-permute-start(bf16[144,768]{1,0:T(8,128)(2,1)S(1)} %get-tuple-element.118), channel_id=1, source_target_pairs={{0,5},{1,4},{2,7},{3,6},{4,1},{5,0},{6,3},{7,2},{8,13},{9,12},{10,... | collective-permute-start | bytes 663560 | tf_op jit(solution)/shard_map/ppermute | solution.py:399
  51.0 24.6 %collective-permute-start.20 = (bf16[144,768]{1,0:T(8,128)(2,1)S(1)}, bf16[144,768]{1,0:T(8,128)(2,1)S(1)}, u32[]{:S(2)}, u32[]{:S(2)}) collective-permute-start(bf16[144,768]{1,0:T(8,128)(2,1)S(1)} %get-tuple-element.119), channel_id=1, source_target_pairs={{0,6},{1,7},{2,4},{3,5},{4,2},{5,3},{6,0},{7,1},{8,14},{9,15},{10,... | collective-permute-start | bytes 663560 | tf_op jit(solution)/shard_map/ppermute | solution.py:399
  52.8 26.2 %collective-permute-start.21 = (bf16[144,768]{1,0:T(8,128)(2,1)S(1)}, bf16[144,768]{1,0:T(8,128)(2,1)S(1)}, u32[]{:S(2)}, u32[]{:S(2)}) collective-permute-start(bf16[144,768]{1,0:T(8,128)(2,1)S(1)} %get-tuple-element.120), channel_id=1, source_target_pairs={{0,7},{1,6},{2,5},{3,4},{4,3},{5,2},{6,1},{7,0},{8,15},{9,14},{10,... | collective-permute-start | bytes 663560 | tf_op jit(solution)/shard_map/ppermute | solution.py:399
  56.8 23.8 %collective-permute-start.22 = (bf16[144,768]{1,0:T(8,128)(2,1)S(1)}, bf16[144,768]{1,0:T(8,128)(2,1)S(1)}, u32[]{:S(2)}, u32[]{:S(2)}) collective-permute-start(bf16[144,768]{1,0:T(8,128)(2,1)S(1)} %get-tuple-element.121), channel_id=1, source_target_pairs={{0,8},{1,9},{2,10},{3,11},{4,12},{5,13},{6,14},{7,15},{8,0},{9,1},... | collective-permute-start | bytes 663560 | tf_op jit(solution)/shard_map/ppermute | solution.py:399
  57.4 45.8 %collective-permute-start.23 = (bf16[144,768]{1,0:T(8,128)(2,1)S(1)}, bf16[144,768]{1,0:T(8,128)(2,1)S(1)}, u32[]{:S(2)}, u32[]{:S(2)}) collective-permute-start(bf16[144,768]{1,0:T(8,128)(2,1)S(1)} %get-tuple-element.122), channel_id=1, source_target_pairs={{0,9},{1,8},{2,11},{3,10},{4,13},{5,12},{6,15},{7,14},{8,1},{9,0},... | collective-permute-start | bytes 663560 | tf_op jit(solution)/shard_map/ppermute | solution.py:399
  59.7 43.5 %collective-permute-start.24 = (bf16[144,768]{1,0:T(8,128)(2,1)S(1)}, bf16[144,768]{1,0:T(8,128)(2,1)S(1)}, u32[]{:S(2)}, u32[]{:S(2)}) collective-permute-start(bf16[144,768]{1,0:T(8,128)(2,1)S(1)} %get-tuple-element.123), channel_id=1, source_target_pairs={{0,10},{1,11},{2,8},{3,9},{4,14},{5,15},{6,12},{7,13},{8,2},{9,3},... | collective-permute-start | bytes 663560 | tf_op jit(solution)/shard_map/ppermute | solution.py:399
  75.6 33.2 %collective-permute-start.25 = (bf16[144,768]{1,0:T(8,128)(2,1)S(1)}, bf16[144,768]{1,0:T(8,128)(2,1)S(1)}, u32[]{:S(2)}, u32[]{:S(2)}) collective-permute-start(bf16[144,768]{1,0:T(8,128)(2,1)S(1)} %get-tuple-element.124), channel_id=1, source_target_pairs={{0,11},{1,10},{2,9},{3,8},{4,15},{5,14},{6,13},{7,12},{8,3},{9,2},... | collective-permute-start | bytes 663560 | tf_op jit(solution)/shard_map/ppermute | solution.py:399
  79.1 29.7 %collective-permute-start.26 = (bf16[144,768]{1,0:T(8,128)(2,1)S(1)}, bf16[144,768]{1,0:T(8,128)(2,1)S(1)}, u32[]{:S(2)}, u32[]{:S(2)}) collective-permute-start(bf16[144,768]{1,0:T(8,128)(2,1)S(1)} %get-tuple-element.125), channel_id=1, source_target_pairs={{0,12},{1,13},{2,14},{3,15},{4,8},{5,9},{6,10},{7,11},{8,4},{9,5},... | collective-permute-start | bytes 663560 | tf_op jit(solution)/shard_map/ppermute | solution.py:399
  80.5 28.2 %collective-permute-start.27 = (bf16[144,768]{1,0:T(8,128)(2,1)S(1)}, bf16[144,768]{1,0:T(8,128)(2,1)S(1)}, u32[]{:S(2)}, u32[]{:S(2)}) collective-permute-start(bf16[144,768]{1,0:T(8,128)(2,1)S(1)} %get-tuple-element.126), channel_id=1, source_target_pairs={{0,13},{1,12},{2,15},{3,14},{4,9},{5,8},{6,11},{7,10},{8,5},{9,4},... | collective-permute-start | bytes 663560 | tf_op jit(solution)/shard_map/ppermute | solution.py:399
  103.1 11.0 %collective-permute-start.28 = (bf16[144,768]{1,0:T(8,128)(2,1)S(1)}, bf16[144,768]{1,0:T(8,128)(2,1)S(1)}, u32[]{:S(2)}, u32[]{:S(2)}) collective-permute-start(bf16[144,768]{1,0:T(8,128)(2,1)S(1)} %get-tuple-element.127), channel_id=1, source_target_pairs={{0,14},{1,15},{2,12},{3,13},{4,10},{5,11},{6,8},{7,9},{8,6},{9,7},... | collective-permute-start | bytes 663560 | tf_op jit(solution)/shard_map/ppermute | solution.py:399
  103.1 15.1 %collective-permute-start.29 = (bf16[144,768]{1,0:T(8,128)(2,1)S(1)}, bf16[144,768]{1,0:T(8,128)(2,1)S(1)}, u32[]{:S(2)}, u32[]{:S(2)}) collective-permute-start(bf16[144,768]{1,0:T(8,128)(2,1)S(1)} %get-tuple-element.128), channel_id=1, source_target_pairs={{0,15},{1,14},{2,13},{3,12},{4,11},{5,10},{6,9},{7,8},{8,7},{9,6},... | collective-permute-start | bytes 663560 | tf_op jit(solution)/shard_map/ppermute | solution.py:399
  129.3 21.3 %collective-permute-start.30 = (f32[1,512]{1,0:T(1,128)S(1)}, f32[1,512]{1,0:T(1,128)S(1)}, u32[]{:S(2)}, u32[]{:S(2)}) collective-permute-start(f32[1,512]{1,0:T(1,128)S(1)} %get-tuple-element.130), channel_id=1, source_target_pairs={{0,1},{1,0},{2,3},{3,2},{4,5},{5,4},{6,7},{7,6},{8,9},{9,8},{10,11... | collective-permute-start | bytes 6152 | tf_op jit(solution)/shard_map/ppermute | solution.py:399
  129.5 23.7 %collective-permute-start.31 = (f32[1,512]{1,0:T(1,128)S(1)}, f32[1,512]{1,0:T(1,128)S(1)}, u32[]{:S(2)}, u32[]{:S(2)}) collective-permute-start(f32[1,512]{1,0:T(1,128)S(1)} %get-tuple-element.131), channel_id=1, source_target_pairs={{0,2},{1,3},{2,0},{3,1},{4,6},{5,7},{6,4},{7,5},{8,10},{9,11},{10,... | collective-permute-start | bytes 6152 | tf_op jit(solution)/shard_map/ppermute | solution.py:399
  131.4 21.9 %collective-permute-start.32 = (f32[1,512]{1,0:T(1,128)S(1)}, f32[1,512]{1,0:T(1,128)S(1)}, u32[]{:S(2)}, u32[]{:S(2)}) collective-permute-start(f32[1,512]{1,0:T(1,128)S(1)} %get-tuple-element.132), channel_id=1, source_target_pairs={{0,3},{1,2},{2,1},{3,0},{4,7},{5,6},{6,5},{7,4},{8,11},{9,10},{10,... | collective-permute-start | bytes 6152 | tf_op jit(solution)/shard_map/ppermute | solution.py:399
  131.5 23.5 %collective-permute-start.33 = (f32[1,512]{1,0:T(1,128)S(1)}, f32[1,512]{1,0:T(1,128)S(1)}, u32[]{:S(2)}, u32[]{:S(2)}) collective-permute-start(f32[1,512]{1,0:T(1,128)S(1)} %get-tuple-element.133), channel_id=1, source_target_pairs={{0,4},{1,5},{2,6},{3,7},{4,0},{5,1},{6,2},{7,3},{8,12},{9,13},{10,... | collective-permute-start | bytes 6152 | tf_op jit(solution)/shard_map/ppermute | solution.py:399
  150.6 8.1 %collective-permute-start.35 = (f32[1,512]{1,0:T(1,128)S(1)}, f32[1,512]{1,0:T(1,128)S(1)}, u32[]{:S(2)}, u32[]{:S(2)}) collective-permute-start(f32[1,512]{1,0:T(1,128)S(1)} %get-tuple-element.135), channel_id=1, source_target_pairs={{0,6},{1,7},{2,4},{3,5},{4,2},{5,3},{6,0},{7,1},{8,14},{9,15},{10,... | collective-permute-start | bytes 6152 | tf_op jit(solution)/shard_map/ppermute | solution.py:399
  153.3 7.9 %collective-permute-start.37 = (f32[1,512]{1,0:T(1,128)S(1)}, f32[1,512]{1,0:T(1,128)S(1)}, u32[]{:S(2)}, u32[]{:S(2)}) collective-permute-start(f32[1,512]{1,0:T(1,128)S(1)} %get-tuple-element.137), channel_id=1, source_target_pairs={{0,8},{1,9},{2,10},{3,11},{4,12},{5,13},{6,14},{7,15},{8,0},{9,1},... | collective-permute-start | bytes 6152 | tf_op jit(solution)/shard_map/ppermute | solution.py:399
  155.0 8.1 %collective-permute-start.38 = (f32[1,512]{1,0:T(1,128)S(1)}, f32[1,512]{1,0:T(1,128)S(1)}, u32[]{:S(2)}, u32[]{:S(2)}) collective-permute-start(f32[1,512]{1,0:T(1,128)S(1)} %get-tuple-element.138), channel_id=1, source_target_pairs={{0,9},{1,8},{2,11},{3,10},{4,13},{5,12},{6,15},{7,14},{8,1},{9,0},... | collective-permute-start | bytes 6152 | tf_op jit(solution)/shard_map/ppermute | solution.py:399
  155.9 9.7 %collective-permute-start.39 = (f32[1,512]{1,0:T(1,128)S(1)}, f32[1,512]{1,0:T(1,128)S(1)}, u32[]{:S(2)}, u32[]{:S(2)}) collective-permute-start(f32[1,512]{1,0:T(1,128)S(1)} %get-tuple-element.139), channel_id=1, source_target_pairs={{0,10},{1,11},{2,8},{3,9},{4,14},{5,15},{6,12},{7,13},{8,2},{9,3},... | collective-permute-start | bytes 6152 | tf_op jit(solution)/shard_map/ppermute | solution.py:399
  158.7 10.0 %collective-permute-start.40 = (f32[1,512]{1,0:T(1,128)S(1)}, f32[1,512]{1,0:T(1,128)S(1)}, u32[]{:S(2)}, u32[]{:S(2)}) collective-permute-start(f32[1,512]{1,0:T(1,128)S(1)} %get-tuple-element.140), channel_id=1, source_target_pairs={{0,11},{1,10},{2,9},{3,8},{4,15},{5,14},{6,13},{7,12},{8,3},{9,2},... | collective-permute-start | bytes 6152 | tf_op jit(solution)/shard_map/ppermute | solution.py:399
  159.5 9.2 %collective-permute-start.41 = (f32[1,512]{1,0:T(1,128)S(1)}, f32[1,512]{1,0:T(1,128)S(1)}, u32[]{:S(2)}, u32[]{:S(2)}) collective-permute-start(f32[1,512]{1,0:T(1,128)S(1)} %get-tuple-element.141), channel_id=1, source_target_pairs={{0,12},{1,13},{2,14},{3,15},{4,8},{5,9},{6,10},{7,11},{8,4},{9,5},... | collective-permute-start | bytes 6152 | tf_op jit(solution)/shard_map/ppermute | solution.py:399
  161.2 7.5 %collective-permute-start.42 = (f32[1,512]{1,0:T(1,128)S(1)}, f32[1,512]{1,0:T(1,128)S(1)}, u32[]{:S(2)}, u32[]{:S(2)}) collective-permute-start(f32[1,512]{1,0:T(1,128)S(1)} %get-tuple-element.142), channel_id=1, source_target_pairs={{0,13},{1,12},{2,15},{3,14},{4,9},{5,8},{6,11},{7,10},{8,5},{9,4},... | collective-permute-start | bytes 6152 | tf_op jit(solution)/shard_map/ppermute | solution.py:399
  (15 other events, 203.9 us)

commit v3 on v0

v3 whole, which is shorter than its diff:
```python
import functools

import jax
import jax.numpy as jnp
from jax import lax
from jax.experimental import pallas as pl
from jax.experimental.pallas import tpu as pltpu
from jax.sharding import PartitionSpec as P

CL_DEV = 4
VARIANTS = 8
STEP = 16
TILE = 256
LANES = 128
GROUP = 4
FLIGHT = 5
MAX_PERMUTES = 16
MIB = 1 << 20

epsilon = 1e-06
f32 = jnp.float32
bf16 = jnp.bfloat16
i32 = jnp.int32
VMEM = pl.BlockSpec(memory_space=pltpu.VMEM)
SMEM = pl.BlockSpec(memory_space=pltpu.SMEM)


def iota(shape, axis):
    return lax.broadcasted_iota(i32, shape, axis)


def round_up(value, unit):
    return -(-value // unit) * unit


def nt_dot(a, b):
    return lax.dot_general(a, b, (((1,), (1,)), ((), ())), preferred_element_type=f32)


def mm(a, b):
    return jnp.dot(a, b, preferred_element_type=f32)


def to_bf16(mask):
    return mask.astype(f32).astype(bf16)


def count_kernel(ids_ref, counts_ref, rank_ref):
    rows = ids_ref.shape[1]
    owners, _, clusters = counts_ref.shape
    label = iota((clusters, TILE), 0)
    upto = to_bf16(iota((TILE, TILE), 0) <= iota((TILE, TILE), 1))
    total = jnp.zeros((clusters, 1), f32)
    for b in range(rows // TILE):
        at = slice(b * TILE, (b + 1) * TILE)
        hot = ids_ref[:, at] == label
        prefix = mm(to_bf16(hot), upto)
        rank_ref[:, at] = jnp.sum(jnp.where(hot, prefix + total - 1.0, 0.0), axis=0, keepdims=True)
        total = total + prefix[:, TILE - 1 :]
    square = (clusters, clusters)
    eye = iota(square, 0) == iota(square, 1)
    total_row = jnp.sum(jnp.where(eye, total, 0.0), axis=0, keepdims=True).astype(i32)
    for owner in range(owners):
        counts_ref[owner] = total_row


def count_rows(ids_row, owners, clusters):
    return pl.pallas_call(
        count_kernel,
        out_shape=(
            jax.ShapeDtypeStruct((owners, 1, clusters), i32),
            jax.ShapeDtypeStruct(ids_row.shape, f32),
        ),
        in_specs=[VMEM],
        out_specs=(VMEM, VMEM),
        compiler_params=pltpu.CompilerParams(vmem_limit_bytes=16 * MIB),
        name="count_rows",
    )(ids_row)


def assign_kernel(
    me_ref, counts_ref, ids_ref, rank_ref, owner_ref, slot_ref, bound_ref, total_ref, load_ref
):
    owners, _, clusters = counts_ref.shape
    rows = ids_ref.shape[1]
    shift = owners.bit_length() - 1
    me = me_ref[0]
    count = jnp.concatenate([counts_ref[s] for s in range(owners)], axis=0).astype(f32)
    count16 = count.astype(bf16)
    square = (clusters, clusters)
    sub, lane = iota(square, 0), iota(square, 1)
    total_row = jnp.sum(count, axis=0, keepdims=True)
    total_col = jnp.sum(jnp.where(sub == lane, total_row, 0.0), axis=1, keepdims=True)
    tie = total_row == total_col
    outranks_col = (total_row > total_col) | (tie & (lane < sub))
    outranks_row = (total_col > total_row) | (tie & (sub < lane))
    rank_col = jnp.sum(outranks_col.astype(f32), axis=1, keepdims=True).astype(i32)
    rank_row = jnp.sum(outranks_row.astype(f32), axis=0, keepdims=True).astype(i32)

    def owner_of(rank, variant):
        layer = rank >> shift
        within = rank & (owners - 1)
        flip = jnp.zeros_like(variant)
        for p in range(1, CL_DEV):
            flip = flip + jnp.where(layer == p, (variant >> (p - 1)) & 1, 0)
        within = within ^ flip
        return jnp.where((layer & 1) == 1, owners - 1 - within, within)

    wide = (clusters, VARIANTS * owners)
    variant = iota(wide, 1) >> shift
    tried = owner_of(rank_col, variant) == (iota(wide, 1) & (owners - 1))
    load = jnp.max(mm(count16, to_bf16(tried)), axis=0, keepdims=True)
    by_variant = (VARIANTS, VARIANTS * owners)
    worst = jnp.max(
        jnp.where((iota(by_variant, 1) >> shift) == iota(by_variant, 0), load, 0.0),
        axis=1,
        keepdims=True,
    )
    best = jnp.min(worst, axis=0, keepdims=True)
    chosen = jnp.min(
        jnp.where(worst == best, iota((VARIANTS, 1), 0), VARIANTS), axis=0, keepdims=True
    )
    owner_col = owner_of(rank_col, chosen + jnp.zeros_like(rank_col))
    owner_row = owner_of(rank_row, chosen + jnp.zeros_like(rank_row))
    layer_col, layer_row = rank_col >> shift, rank_row >> shift
    load_ref[...] = jnp.broadcast_to(best, load_ref.shape).astype(i32)

    mine = jnp.sum(jnp.where(iota(count.shape, 0) == me, count, 0.0), axis=0, keepdims=True)
    earlier = (owner_row == owner_col) & (layer_row < layer_col)
    offset_col = jnp.sum(jnp.where(earlier, mine, 0.0), axis=1, keepdims=True)
    hot = ids_ref[...] == iota((clusters, rows), 0)
    owner_ref[...] = jnp.sum(
        jnp.where(hot, owner_col.astype(f32), 0.0), axis=0, keepdims=True
    ).astype(i32)
    slot_ref[...] = (
        jnp.sum(jnp.where(hot, offset_col, 0.0), axis=0, keepdims=True) + rank_ref[...]
    ).astype(i32)

    select = (owner_col == me) & (layer_col <= iota((clusters, LANES), 1))
    turn = iota((owners, owners), 1) == (iota((owners, owners), 0) ^ me)
    turned = mm(to_bf16(turn), count16).astype(bf16)
    bound_ref[...] = mm(turned, to_bf16(select))
    own = (owner_row == me) & (layer_row == iota((8, clusters), 0))
    total_ref[...] = jnp.broadcast_to(
        jnp.sum(jnp.where(own, total_row, 0.0), axis=1, keepdims=True), total_ref.shape
    )


def assign(me, counts, ids_row, rank):
    owners, _, clusters = counts.shape
    rows = ids_row.shape[1]
    return pl.pallas_call(
        assign_kernel,
        out_shape=(
            jax.ShapeDtypeStruct((1, rows), i32),
            jax.ShapeDtypeStruct((1, rows), i32),
            jax.ShapeDtypeStruct((owners, LANES), f32),
            jax.ShapeDtypeStruct((8, LANES), f32),
            jax.ShapeDtypeStruct((1, LANES), i32),
        ),
        in_specs=[SMEM, VMEM, VMEM, VMEM],
        out_specs=(VMEM,) * 5,
        compiler_params=pltpu.CompilerParams(vmem_limit_bytes=16 * MIB),
        name="assign",
    )(me, counts, ids_row, rank)


def pack_kernel(slots, partners, me_ref, owner_ref, slot_ref, rows_ref, *out_refs):
    rows = rows_ref.shape[0]
    me = me_ref[0]
    slot = iota((slots, rows), 0)
    takes = []
    for partner in partners:
        key = jnp.where(owner_ref[...] == (me ^ partner), slot_ref[...], -1)
        takes.append(to_bf16(slot == key))
    picked = mm(jnp.concatenate(takes, axis=0), rows_ref[...]).astype(bf16)
    for i, ref in enumerate(out_refs):
        ref[...] = picked[i * slots : (i + 1) * slots]


def pack(me, owner_row, slot_row, embeddings, partners, slots):
    rows, width = embeddings.shape
    flops = 2 * len(partners) * slots * rows * width
    return pl.pallas_call(
        functools.partial(pack_kernel, slots, partners),
        out_shape=(jax.ShapeDtypeStruct((slots, width), bf16),) * len(partners),
        in_specs=[SMEM, VMEM, VMEM, VMEM],
        out_specs=(VMEM,) * len(partners),
        compiler_params=pltpu.CompilerParams(vmem_limit_bytes=28 * MIB),
        cost_estimate=pl.CostEstimate(
            flops=flops, bytes_accessed=2 * rows * width, transcendentals=0
        ),
        name="pack_rows",
    )(me, owner_row, slot_row, embeddings)


def unit_rows(ref):
    x = ref[...].astype(f32)
    scale = lax.rsqrt(jnp.sum(x * x, axis=1, keepdims=True) + epsilon)
    return (x * scale).astype(bf16)


def cluster_lanes(bound_ref, partners, slots, width):
    lane = iota((1, width), 1).astype(f32)
    result = jnp.where(lane < len(partners) * slots, 0.0, -1.0)
    for i, r in enumerate(partners):
        for k in range(CL_DEV):
            first = bound_ref[r : r + 1, k : k + 1] + float(i * slots)
            result = result + ((lane >= first) & (lane < float((i + 1) * slots))).astype(f32)
    return result


def cluster_rows(bound_ref, r, slots):
    slot = iota((slots, LANES), 0).astype(f32)
    result = jnp.zeros((slots, LANES), f32)
    for k in range(CL_DEV):
        result = result + (slot >= bound_ref[r : r + 1, k : k + 1]).astype(f32)
    return result


def score_group(new_ref, new_cids, olds, cid_row, slots_new):
    padded = new_ref.shape[0]
    groups = padded // LANES
    new = new_ref[...]

    def folded(scores, cids, skip_same):
        rows = scores.shape[0]
        row = iota((rows, LANES), 0)
        lane = iota((rows, LANES), 1)
        best, cols = None, []
        for g in range(groups):
            at = slice(g * LANES, (g + 1) * LANES)
            allowed = cids == cid_row[:, at]
            if skip_same:
                allowed = allowed & (row != lane + g * LANES)
            part = jnp.where(allowed, scores[:, at], -1.0)
            best = part if best is None else jnp.maximum(best, part)
            cols.append(jnp.max(part, axis=0, keepdims=True))
        return best, cols

    columns = None
    results = []
    for unit_ref, acc_ref, cid_ref in olds:
        scores = nt_dot(unit_ref[...], new)
        best, cols = folded(scores, cid_ref[...], False)
        columns = cols if columns is None else [jnp.maximum(a, b) for a, b in zip(columns, cols)]
        results.append((scores, jnp.maximum(acc_ref[...], best)))
    scores = nt_dot(new[0:slots_new], new)
    best, _ = folded(scores, new_cids, True)
    if columns is not None:
        row = iota((slots_new, LANES), 0)
        lane = iota((slots_new, LANES), 1)
        for g, col in enumerate(columns):
            best = jnp.maximum(best, jnp.where(row == lane + g * LANES, col, -1.0))
    results.append((scores, best))
    return results


def member_sums(cid_row, new):
    hot = to_bf16(cid_row == iota((8, cid_row.shape[1]), 0).astype(f32))
    return mm(hot, new)


def score_kernel(slots, partners, olds, bound_ref, *refs):
    fresh = len(partners)
    raw_refs, refs = refs[:fresh], refs[fresh:]
    old_refs = [refs[3 * i : 3 * i + 3] for i in range(olds)]
    refs = refs[3 * olds :]
    if olds:
        sums_ref, refs = refs[0], refs[1:]
    unit_ref, acc_ref, cid_ref, sums_out = refs[:4]
    old_accs = refs[4 : 4 + olds]
    new_ref = refs[4 + olds]
    rows = fresh * slots
    for i, r in enumerate(partners):
        at = slice(i * slots, (i + 1) * slots)
        new_ref[at, :] = unit_rows(raw_refs[i])
        cid_ref[at, :] = cluster_rows(bound_ref, r, slots)
    padded = new_ref.shape[0]
    if padded > rows:
        new_ref[rows:, :] = jnp.zeros((padded - rows, new_ref.shape[1]), bf16)
    unit_ref[...] = new_ref[0:rows, :]
    cid_row = cluster_lanes(bound_ref, partners, slots, padded)
    results = score_group(new_ref, cid_ref[...], old_refs, cid_row, rows)
    for (_, best), ref in zip(results, list(old_accs) + [acc_ref]):
        ref[...] = best
    sums = member_sums(cid_row, new_ref[...])
    sums_out[...] = sums + sums_ref[...] if olds else sums


def score(bound, blocks, partners, state):
    slots, width = blocks[0].shape
    units, accs, cids, sums = state
    rows = len(blocks) * slots
    padded = round_up(rows, LANES)
    old = [x for group in zip(units, accs, cids) for x in group]
    old_rows = sum(u.shape[0] for u in units)
    acc_shapes = [jax.ShapeDtypeStruct(a.shape, f32) for a in accs]
    out_shape = (
        jax.ShapeDtypeStruct((rows, width), bf16),
        jax.ShapeDtypeStruct((rows, LANES), f32),
        jax.ShapeDtypeStruct((rows, LANES), f32),
        jax.ShapeDtypeStruct((8, width), f32),
        *acc_shapes,
    )
    args = [bound, *blocks, *old] + ([sums] if units else [])
    out = pl.pallas_call(
        functools.partial(score_kernel, slots, partners, len(units)),
        out_shape=out_shape,
        in_specs=[VMEM] * len(args),
        out_specs=(VMEM,) * len(out_shape),
        scratch_shapes=[pltpu.VMEM((padded, width), bf16)],
        compiler_params=pltpu.CompilerParams(vmem_limit_bytes=36 * MIB),
        cost_estimate=pl.CostEstimate(
            flops=2 * (old_rows + rows) * padded * width,
            bytes_accessed=2 * (old_rows + rows) * width,
            transcendentals=rows,
        ),
        name="score_rows",
    )(*args)
    return units + [out[0]], list(out[4:]) + [out[1]], cids + [out[2]], out[3]


def finish_kernel(slots, partners, earlier, olds, me_ref, bound_ref, total_ref, *refs):
    fresh = len(partners)
    raw_refs, refs = refs[:fresh], refs[fresh:]
    old_refs = [refs[3 * i : 3 * i + 3] for i in range(olds)]
    sums_ref, out_ref, new_ref = refs[3 * olds :]
    me = me_ref[0]
    rows = fresh * slots
    padded, width = new_ref.shape
    new_ref[rows:, :] = jnp.zeros((padded - rows, width), bf16)
    pieces = []
    for i, r in enumerate(partners):
        new_ref[i * slots : (i + 1) * slots, :] = unit_rows(raw_refs[i])
        pieces.append(cluster_rows(bound_ref, r, slots))
    new_cids = jnp.concatenate(pieces, axis=0)
    cid_row = cluster_lanes(bound_ref, partners, slots, padded)
    sums = sums_ref[...] + member_sums(cid_row, new_ref[...])
    centroid = (sums / jnp.maximum(total_ref[:, 0:1], 1.0)).astype(bf16)
    centroid = jnp.concatenate([centroid, jnp.zeros_like(centroid)], axis=0)
    new_ref[rows : rows + STEP, :] = centroid
    results = score_group(new_ref, new_cids, old_refs, cid_row, rows)
    half = out_ref.shape[2] // 2
    group, within = rows // LANES, rows % LANES
    eye = iota((slots, half), 0) == iota((slots, half), 1)
    all_cids = [old[2][...] for old in old_refs] + [new_cids]
    for (scores, acc), cids, names in zip(results, all_cids, earlier + [partners]):
        best = jnp.max(acc, axis=1, keepdims=True)
        lane = iota(cids.shape, 1).astype(f32)
        dots = scores[:, group * LANES : (group + 1) * LANES]
        gap = 1.0 - jnp.sum(
            jnp.where(lane == cids + float(within), dots, 0.0), axis=1, keepdims=True
        )
        for i, r in enumerate(names):
            at = slice(i * slots, (i + 1) * slots)
            for j, col in enumerate((best, gap)):
                line = jnp.sum(jnp.where(eye, col[at], 0.0), axis=0, keepdims=True)
                out_ref[r ^ me, :, j * half : (j + 1) * half] = line


def finish(me, bound, total, blocks, partners, earlier, state):
    slots, width = blocks[0].shape
    owners = bound.shape[0]
    units, accs, cids, sums = state
    rows = len(blocks) * slots
    padded = round_up(rows + STEP, LANES)
    old = [x for group in zip(units, accs, cids) for x in group]
    args = [me, bound, total, *blocks, *old, sums]
    return pl.pallas_call(
        functools.partial(finish_kernel, slots, partners, earlier, len(units)),
        out_shape=jax.ShapeDtypeStruct((owners, 1, 2 * round_up(slots, LANES)), f32),
        in_specs=[SMEM] + [VMEM] * (len(args) - 1),
        out_specs=VMEM,
        scratch_shapes=[pltpu.VMEM((padded, width), bf16)],
        compiler_params=pltpu.CompilerParams(vmem_limit_bytes=36 * MIB),
        cost_estimate=pl.CostEstimate(
            flops=2 * owners * slots * padded * width,
            bytes_accessed=2 * owners * slots * width,
            transcendentals=rows,
        ),
        name="finish_rows",
    )(*args)


def restore_kernel(slots, owner_ref, slot_ref, back_ref, best_ref, gap_ref):
    rows = owner_ref.shape[1]
    owners, _, width = back_ref.shape
    half = width // 2
    from_owner = to_bf16(owner_ref[...] == iota((owners, rows), 0))
    from_owner = jnp.concatenate([from_owner] * 3, axis=0)
    at_slot = slot_ref[...] == iota((slots, rows), 0)
    back = jnp.concatenate([back_ref[s] for s in range(owners)], axis=0)
    part0 = back.astype(bf16)
    rest = back - part0.astype(f32)
    part1 = rest.astype(bf16)
    part2 = (rest - part1.astype(f32)).astype(bf16)
    parts = jnp.concatenate([part0, part1, part2], axis=0)
    for i, ref in enumerate((best_ref, gap_ref)):
        table = lax.dot_general(
            parts[:, i * half : i * half + slots],
            from_owner,
            (((0,), (0,)), ((), ())),
            preferred_element_type=f32,
        )
        ref[...] = jnp.sum(jnp.where(at_slot, table, 0.0), axis=0, keepdims=True)


def restore(owner_row, slot_row, back, slots):
    return pl.pallas_call(
        functools.partial(restore_kernel, slots),
        out_shape=(jax.ShapeDtypeStruct(owner_row.shape, f32),) * 2,
        in_specs=[VMEM] * 3,
        out_specs=(VMEM, VMEM),
        compiler_params=pltpu.CompilerParams(vmem_limit_bytes=28 * MIB),
        name="restore_rows",
    )(owner_row, slot_row, back)


def exchange(x):
    return lax.all_to_all(x, "owner", split_axis=0, concat_axis=0, tiled=True)


def swap_together(blocks):
    owners = len(blocks)
    order = jnp.arange(owners, dtype=i32) ^ lax.axis_index("owner").astype(i32)
    arrived = exchange(jnp.stack(blocks)[order])[order]
    return [arrived[r] for r in range(owners)]


def swap_apart(blocks, order):
    owners = len(blocks)
    arrived = list(blocks)
    for i, r in enumerate(order):
        block = blocks[r]
        if i >= FLIGHT:
            before = order[i - FLIGHT]
            block, arrived[before] = lax.optimization_barrier((block, arrived[before]))
        arrived[r] = lax.ppermute(block, "owner", [(s, s ^ r) for s in range(owners)])
    return arrived


def local(embeddings, cluster_ids):
    rows = embeddings.shape[0]
    owners = lax.axis_size("owner")
    clusters = CL_DEV * owners
    row_limit = 2 * rows // clusters
    most = round_up(CL_DEV * row_limit, STEP)
    usual = min(most, round_up(9 * rows // (8 * owners), STEP))
    few = owners <= MAX_PERMUTES
    me = lax.axis_index("owner").astype(i32).reshape(1)
    ids_row = cluster_ids.reshape(1, rows)
    counts, rank = count_rows(ids_row, owners, clusters)
    owner_row, slot_row, bound, total, load = assign(me, exchange(counts), ids_row, rank)

    half = owners // 2
    order = [r for i in reversed(range(half)) for r in (half + i, i)][:-1]
    sent = order + [0]
    seen = [0] + order
    share = owners // 16 if owners >= 16 else 1
    groups, at = [], 0
    for size in (5, 4, 4, 2):
        groups.append(seen[at : at + size * share])
        at += size * share
    groups.append(seen[at:])

    def compare(slots, apart):
        blocks = [None] * owners
        for first in range(0, owners, GROUP):
            partners = tuple(sent[first : first + GROUP])
            packed = pack(me, owner_row, slot_row, embeddings, partners, slots)
            for r, block in zip(partners, packed):
                blocks[r] = block
        arrived = swap_apart(blocks, order) if apart else swap_together(blocks)
        state = ([], [], [], None)
        for group in groups[:-1]:
            state = score(bound, [arrived[r] for r in group], group, state)
        last = groups[-1]
        answers = finish(
            me, bound, total, [arrived[r] for r in last], last, groups[:-1], state
        )
        return restore(owner_row, slot_row, exchange(answers), slots)

    best, gap = compare(usual, few)
    if usual < most:
        best, gap = lax.cond(
            load[0, 0] <= usual, lambda: (best, gap), lambda: compare(most, False)
        )
    return best.reshape(rows), gap.reshape(rows)


def solution(mesh):
    return jax.shard_map(
        local,
        mesh=mesh,
        in_specs=(P(("groups", "owner"), None), P(("groups", "owner"))),
        out_specs=(P(("groups", "owner")), P(("groups", "owner"))),
        check_vma=False,
    )
```

time: 356 us -> 119 us (0.33)
  blocking collectives: 158 us -> 0 us
  local copies, waits for them, and re-layouts: 76.9 us -> 1.4 us
  other arithmetic: 29.3 us -> 0 us
  Pallas kernels: 0 us -> 24.2 us
  starting transfers between devices: 17.1 us -> 37 us
  between operations: 15 us -> 0.8 us
  matrix products: 12.2 us -> 0 us
  waiting for transfers between devices: 46.9 us -> 54.8 us
    psum x1 -> x0, blocking collectives: 138 us -> none  [local(): counts = lax.psum(local_counts, 'owner')]
    gather x2 -> x0, local copies, waits for them, and re-layouts: 43.6 us -> none  [the longest x1 23 us: local(): flat_best[jnp.minimum(bucket_index, CL_DEV * cluster_cap - 1)]]
    ppermute x0 -> x15, waiting for transfers between devices: none -> 41.9 us  [swap_apart(): lax.ppermute(block, 'owner', [(s, s ^ r) for s in range(owners)])]
    unnamed x2 -> x0, waiting for transfers between devices: 41.1 us -> none
    scatter x2 -> x0, local copies, waits for them, and re-layouts: 31.4 us -> none  [the longest x1 22.8 us: local(): gathered = jnp.zeros((CL_DEV * cluster_cap, feature_width), jnp.bfloat16)...]
    ppermute x0 -> x15, starting transfers between devices: none -> 26.1 us  [swap_apart(): lax.ppermute(block, 'owner', [(s, s ^ r) for s in range(owners)])]
    pallas_call x0 -> x12, Pallas kernels: none -> 24.2 us  [the longest x4 10.2 us: pack(): pl.pallas_call(functools.partial(pack_kernel, slots, partners), out_shape...]
    all_gather x1 -> x0, blocking collectives: 19.8 us -> none  [local(): lax.all_gather(centroids, 'owner', axis=0, tiled=True)]
  transfers between devices with their start and end apart: 4 -> 17, of which waited for: 2 -> 11; matrix products, arithmetic and copies ran while one was open for 8% -> 0% of each run, Pallas kernels for 0% -> 13%
where the time goes in v3:
time: 119 us; the launch traced here: 118 us
  waiting for transfers between devices  54.8 us (46%)
  starting transfers between devices  37 us (31%)
  Pallas kernels  24.2 us (20%)
  local copies, waits for them, and re-layouts  1.4 us (1%)
    ppermute x15, waiting for transfers between devices, swap_apart(): lax.ppermute(block, 'owner', [(s, s ^ r) for s in range(owners)])  41.9 us
    ppermute x15, starting transfers between devices, swap_apart(): lax.ppermute(block, 'owner', [(s, s ^ r) for s in range(owners)])  26.1 us
    all_to_all x2, waiting for transfers between devices, exchange(): return lax.all_to_all(x, 'owner', split_axis=0, concat_axis=0, tiled=True)  12.9 us
    all_to_all x2, starting transfers between devices, exchange(): return lax.all_to_all(x, 'owner', split_axis=0, concat_axis=0, tiled=True)  10.9 us
    pallas_call x4, Pallas kernels, pack(): pl.pallas_call(functools.partial(pack_kernel, slots, partners), out_shape...  10.2 us
    pallas_call x4, Pallas kernels, score(): pl.pallas_call(functools.partial(score_kernel, slots, partners, len(units...  8.82 us
  transfers between devices with their start and end apart: 17, of which 11 were waited for; matrix products, arithmetic and copies ran while one was open for 0% of the time, Pallas kernels for 13%

profile of v3, /device:TPU:0, one launch (start us, length us, event | category | flops | bytes accessed | tf_op | source)
XLA Modules:
  0.0 118.2 jit_solution(6731756438296901028)
XLA Ops:
  1.3 1.0 count_rows.1
  2.3 7.4 %all-to-all-start.2 = ((s32[16,1,64]{2,1,0:T(1,128)}), s32[16,1,64]{2,1,0:T(1,128)S(1)}, u32[]{:S(2)}, u32[]{:S(2)}) async-start(s32[16,1,64]{2,1,0:T(1,128)} %get-tuple-element.137), calls=%async_computation.2 | async-start | bytes 16384 | tf_op jit(solution)/shard_map/all_to_all | solution.py:421
  9.7 6.3 %all-to-all-done.2.counts_ref = s32[16,1,64]{2,1,0:T(1,128)S(1)} async-done(((s32[16,1,64]{2,1,0:T(1,128)}), s32[16,1,64]{2,1,0:T(1,128)S(1)}, u32[]{:S(2)}, u32[]{:S(2)}) %all-to-all-start.2) | async-done | bytes 4128 | tf_op jit(solution)/shard_map/all_to_all | solution.py:421
  17.4 4.2 %pack_rows.15 = (bf16[144,768]{1,0:T(8,128)(2,1)S(1)}, bf16[144,768]{1,0:T(8,128)(2,1)S(1)}, bf16[144,768]{1,0:T(8,128)(2,1)S(1)}, bf16[144,768]{1,0:T(8,128)(2,1)S(1)}) custom-call(s32[1]{0:T(128)} %bitcast.33.me_ref, s32[1,2048]{1,0:T(1,128)S(1)} %get-tuple-element.140.owner_ref, s32[1,2048]{1,0:T(1,128)S(1)} %get-tuple-element.141.slot_ref, ...), custom_call_target="tpu_custom_call" | custom-call | flops 1811939328 | bytes 3145728 | tf_op jit(solution)/shard_map/pack_rows/pallas_call | solution.py:184
  21.7 1.7 %collective-permute-start.4 = (bf16[144,768]{1,0:T(8,128)(2,1)S(1)}, bf16[144,768]{1,0:T(8,128)(2,1)S(1)}, u32[]{:S(2)}, u32[]{:S(2)}) collective-permute-start(bf16[144,768]{1,0:T(8,128)(2,1)S(1)} %get-tuple-element.154), channel_id=1, source_target_pairs={{0,7},{1,6},{2,5},{3,4},{4,3},{5,2},{6,1},{7,0},{8,15},{9,14},{10,... | collective-permute-start | bytes 663560 | tf_op jit(solution)/shard_map/ppermute | solution.py:439
  23.4 2.4 %collective-permute-start.5 = (bf16[144,768]{1,0:T(8,128)(2,1)S(1)}, bf16[144,768]{1,0:T(8,128)(2,1)S(1)}, u32[]{:S(2)}, u32[]{:S(2)}) collective-permute-start(bf16[144,768]{1,0:T(8,128)(2,1)S(1)} %get-tuple-element.157), channel_id=1, source_target_pairs={{0,14},{1,15},{2,12},{3,13},{4,10},{5,11},{6,8},{7,9},{8,6},{9,7},... | collective-permute-start | bytes 663560 | tf_op jit(solution)/shard_map/ppermute | solution.py:439
  25.8 2.4 %collective-permute-start.6 = (bf16[144,768]{1,0:T(8,128)(2,1)S(1)}, bf16[144,768]{1,0:T(8,128)(2,1)S(1)}, u32[]{:S(2)}, u32[]{:S(2)}) collective-permute-start(bf16[144,768]{1,0:T(8,128)(2,1)S(1)} %get-tuple-element.160), channel_id=1, source_target_pairs={{0,6},{1,7},{2,4},{3,5},{4,2},{5,3},{6,0},{7,1},{8,14},{9,15},{10,... | collective-permute-start | bytes 663560 | tf_op jit(solution)/shard_map/ppermute | solution.py:439
  28.1 2.0 %pack_rows.14 = (bf16[144,768]{1,0:T(8,128)(2,1)S(1)}, bf16[144,768]{1,0:T(8,128)(2,1)S(1)}, bf16[144,768]{1,0:T(8,128)(2,1)S(1)}, bf16[144,768]{1,0:T(8,128)(2,1)S(1)}) custom-call(s32[1]{0:T(128)} %bitcast.33.me_ref, s32[1,2048]{1,0:T(1,128)S(1)} %get-tuple-element.140.owner_ref, s32[1,2048]{1,0:T(1,128)S(1)} %get-tuple-element.141.slot_ref, ...), custom_call_target="tpu_custom_call" | custom-call | flops 1811939328 | bytes 3145728 | tf_op jit(solution)/shard_map/pack_rows/pallas_call | solution.py:184
  30.2 1.9 %collective-permute-done.3.refs_1_ = bf16[144,768]{1,0:T(8,128)(2,1)S(1)} collective-permute-done((bf16[144,768]{1,0:T(8,128)(2,1)S(1)}, bf16[144,768]{1,0:T(8,128)(2,1)S(1)}, u32[]{:S(2)}, u32[]{:S(2)}) %collective-permute-start.3) | collective-permute-done | bytes 221216 | tf_op jit(solution)/shard_map/ppermute | solution.py:439
  32.1 5.7 %collective-permute-start.11 = (bf16[144,768]{1,0:T(8,128)(2,1)S(1)}, bf16[144,768]{1,0:T(8,128)(2,1)S(1)}, u32[]{:S(2)}, u32[]{:S(2)}) collective-permute-start(bf16[144,768]{1,0:T(8,128)(2,1)S(1)} %get-tuple-element.172), channel_id=1, source_target_pairs={{0,5},{1,4},{2,7},{3,6},{4,1},{5,0},{6,3},{7,2},{8,13},{9,12},{10,... | collective-permute-start | bytes 663560 | tf_op jit(solution)/shard_map/ppermute | solution.py:439
  37.8 1.5 %collective-permute-start.13 = (bf16[144,768]{1,0:T(8,128)(2,1)S(1)}, bf16[144,768]{1,0:T(8,128)(2,1)S(1)}, u32[]{:S(2)}, u32[]{:S(2)}) collective-permute-start(bf16[144,768]{1,0:T(8,128)(2,1)S(1)} %get-tuple-element.175), channel_id=1, source_target_pairs={{0,12},{1,13},{2,14},{3,15},{4,8},{5,9},{6,10},{7,11},{8,4},{9,5},... | collective-permute-start | bytes 663560 | tf_op jit(solution)/shard_map/ppermute | solution.py:439
  39.4 2.0 %pack_rows.13 = (bf16[144,768]{1,0:T(8,128)(2,1)S(1)}, bf16[144,768]{1,0:T(8,128)(2,1)S(1)}, bf16[144,768]{1,0:T(8,128)(2,1)S(1)}, bf16[144,768]{1,0:T(8,128)(2,1)S(1)}) custom-call(s32[1]{0:T(128)} %bitcast.33.me_ref, s32[1,2048]{1,0:T(1,128)S(1)} %get-tuple-element.140.owner_ref, s32[1,2048]{1,0:T(1,128)S(1)} %get-tuple-element.141.slot_ref, ...), custom_call_target="tpu_custom_call" | custom-call | flops 1811939328 | bytes 3145728 | tf_op jit(solution)/shard_map/pack_rows/pallas_call | solution.py:184
  41.4 3.7 %collective-permute-done.5.refs_3_ = bf16[144,768]{1,0:T(8,128)(2,1)S(1)} collective-permute-done((bf16[144,768]{1,0:T(8,128)(2,1)S(1)}, bf16[144,768]{1,0:T(8,128)(2,1)S(1)}, u32[]{:S(2)}, u32[]{:S(2)}) %collective-permute-start.5) | collective-permute-done | bytes 221216 | tf_op jit(solution)/shard_map/ppermute | solution.py:439
  45.2 4.1 %collective-permute-start.7 = (bf16[144,768]{1,0:T(8,128)(2,1)S(1)}, bf16[144,768]{1,0:T(8,128)(2,1)S(1)}, u32[]{:S(2)}, u32[]{:S(2)}) collective-permute-start(bf16[144,768]{1,0:T(8,128)(2,1)S(1)} %get-tuple-element.164), channel_id=1, source_target_pairs={{0,4},{1,5},{2,6},{3,7},{4,0},{5,1},{6,2},{7,3},{8,12},{9,13},{10,... | collective-permute-start | bytes 663560 | tf_op jit(solution)/shard_map/ppermute | solution.py:439
  49.3 6.2 %collective-permute-done.refs_0_ = bf16[144,768]{1,0:T(8,128)(2,1)S(1)} collective-permute-done((bf16[144,768]{1,0:T(8,128)(2,1)S(1)}, bf16[144,768]{1,0:T(8,128)(2,1)S(1)}, u32[]{:S(2)}, u32[]{:S(2)}) %collective-permute-start) | collective-permute-done | bytes 221216 | tf_op jit(solution)/shard_map/ppermute | solution.py:439
  55.5 1.8 %collective-permute-start.9 = (bf16[144,768]{1,0:T(8,128)(2,1)S(1)}, bf16[144,768]{1,0:T(8,128)(2,1)S(1)}, u32[]{:S(2)}, u32[]{:S(2)}) collective-permute-start(bf16[144,768]{1,0:T(8,128)(2,1)S(1)} %get-tuple-element.167), channel_id=1, source_target_pairs={{0,11},{1,10},{2,9},{3,8},{4,15},{5,14},{6,13},{7,12},{8,3},{9,2},... | collective-permute-start | bytes 663560 | tf_op jit(solution)/shard_map/ppermute | solution.py:439
  58.0 7.1 %collective-permute-done.13.refs_2_ = bf16[144,768]{1,0:T(8,128)(2,1)S(1)} collective-permute-done((bf16[144,768]{1,0:T(8,128)(2,1)S(1)}, bf16[144,768]{1,0:T(8,128)(2,1)S(1)}, u32[]{:S(2)}, u32[]{:S(2)}) %collective-permute-start.13) | collective-permute-done | bytes 221216 | tf_op jit(solution)/shard_map/ppermute | solution.py:439
  65.0 2.1 %collective-permute-start.12 = (bf16[144,768]{1,0:T(8,128)(2,1)S(1)}, bf16[144,768]{1,0:T(8,128)(2,1)S(1)}, u32[]{:S(2)}, u32[]{:S(2)}) collective-permute-start(bf16[144,768]{1,0:T(8,128)(2,1)S(1)} %get-tuple-element.173), channel_id=1, source_target_pairs={{0,10},{1,11},{2,8},{3,9},{4,14},{5,15},{6,12},{7,13},{8,2},{9,3},... | collective-permute-start | bytes 663560 | tf_op jit(solution)/shard_map/ppermute | solution.py:439
  67.8 2.0 %pack_rows.12 = (bf16[144,768]{1,0:T(8,128)(2,1)S(1)}, bf16[144,768]{1,0:T(8,128)(2,1)S(1)}, bf16[144,768]{1,0:T(8,128)(2,1)S(1)}, bf16[144,768]{1,0:T(8,128)(2,1)S(1)}) custom-call(s32[1]{0:T(128)} %bitcast.33.me_ref, s32[1,2048]{1,0:T(1,128)S(1)} %get-tuple-element.140.owner_ref, s32[1,2048]{1,0:T(1,128)S(1)} %get-tuple-element.141.slot_ref, ...), custom_call_target="tpu_custom_call" | custom-call | flops 1811939328 | bytes 3145728 | tf_op jit(solution)/shard_map/pack_rows/pallas_call | solution.py:184
  69.8 1.5 %score_rows.12 = (bf16[720,768]{1,0:T(8,128)(2,1)S(1)}, f32[720,128]{1,0:T(8,128)S(1)}, f32[720,128]{1,0:T(8,128)S(1)}, f32[8,768]{1,0:T(8,128)S(1)}) custom-call(f32[16,128]{1,0:T(8,128)S(1)} %get-tuple-element.142.bound_ref, bf16[144,768]{1,0:T(8,128)(2,1)S(1)} %get-tuple-element.149.refs_0_, bf16[144,768]{1,0:T(8,128)(2,1)S(1)} %collective-permute-done.3.refs_1_, ...), custom_call_target="tpu_custom_call" | custom-call | flops 849346560 | bytes 1105920 | tf_op jit(solution)/shard_map/score_rows/pallas_call | solution.py:307
  71.3 10.4 %collective-permute-done.9.refs_0_ = bf16[144,768]{1,0:T(8,128)(2,1)S(1)} collective-permute-done((bf16[144,768]{1,0:T(8,128)(2,1)S(1)}, bf16[144,768]{1,0:T(8,128)(2,1)S(1)}, u32[]{:S(2)}, u32[]{:S(2)}) %collective-permute-start.9) | collective-permute-done | bytes 221216 | tf_op jit(solution)/shard_map/ppermute | solution.py:439
  81.8 2.9 %collective-permute-start.2 = (bf16[144,768]{1,0:T(8,128)(2,1)S(1)}, bf16[144,768]{1,0:T(8,128)(2,1)S(1)}, u32[]{:S(2)}, u32[]{:S(2)}) collective-permute-start(bf16[144,768]{1,0:T(8,128)(2,1)S(1)} %get-tuple-element.148), channel_id=1, source_target_pairs={{0,8},{1,9},{2,10},{3,11},{4,12},{5,13},{6,14},{7,15},{8,0},{9,1},... | collective-permute-start | bytes 663560 | tf_op jit(solution)/shard_map/ppermute | solution.py:439
  84.7 2.1 %score_rows.13 = (bf16[576,768]{1,0:T(8,128)(2,1)S(1)}, f32[576,128]{1,0:T(8,128)S(1)}, f32[576,128]{1,0:T(8,128)S(1)}, f32[8,768]{1,0:T(8,128)S(1)}, f32[720,128]{1,0:T(8,128)S(1)}) custom-call(f32[16,128]{1,0:T(8,128)S(1)} %get-tuple-element.142.bound_ref, bf16[144,768]{1,0:T(8,128)(2,1)S(1)} %collective-permute-done.refs_0_, ...), custom_call_target="tpu_custom_call" | custom-call | flops 1274019840 | bytes 1990656 | tf_op jit(solution)/shard_map/score_rows/pallas_call | solution.py:307
  86.8 9.1 %collective-permute-done.12.refs_2_ = bf16[144,768]{1,0:T(8,128)(2,1)S(1)} collective-permute-done((bf16[144,768]{1,0:T(8,128)(2,1)S(1)}, bf16[144,768]{1,0:T(8,128)(2,1)S(1)}, u32[]{:S(2)}, u32[]{:S(2)}) %collective-permute-start.12) | collective-permute-done | bytes 221216 | tf_op jit(solution)/shard_map/ppermute | solution.py:439
  95.9 3.1 %score_rows.14 = (bf16[576,768]{1,0:T(8,128)(2,1)S(1)}, f32[576,128]{1,0:T(8,128)S(1)}, f32[576,128]{1,0:T(8,128)S(1)}, f32[8,768]{1,0:T(8,128)S(1)}, f32[720,128]{1,0:T(8,128)S(1)}, /*index=5*/f32[576,128]{1,0:T(8,128)S(1)}) custom-call(f32[16,128]{1,0:T(8,128)S(1)} %get-tuple-element.142.bound_ref, bf16[144,768]{1,0:T(8,128)(2,1)S(1)} %collective-permute-done.9.refs_0_, ...), custom_call_target="tpu_custom_call" | custom-call | flops 1840250880 | bytes 2875392 | tf_op jit(solution)/shard_map/score_rows/pallas_call | solution.py:307
  99.0 0.7 collective-permute-done.8.refs_0_
  99.8 2.1 %score_rows.15 = (bf16[288,768]{1,0:T(8,128)(2,1)S(1)}, f32[288,128]{1,0:T(8,128)S(1)}, f32[288,128]{1,0:T(8,128)S(1)}, f32[8,768]{1,0:T(8,128)S(1)}, f32[720,12...) custom-call(f32[16,128]{1,0:T(8,128)S(1)} %get-tuple-element.142.bound_ref, ...), custom_call_target="tpu_custom_call" | custom-call | flops 1274019840 | bytes 3317760 | tf_op jit(solution)/shard_map/score_rows/pallas_call | solution.py:307
  101.9 2.6 %collective-permute-done.2.refs_0_ = bf16[144,768]{1,0:T(8,128)(2,1)S(1)} collective-permute-done((bf16[144,768]{1,0:T(8,128)(2,1)S(1)}, bf16[144,768]{1,0:T(8,128)(2,1)S(1)}, u32[]{:S(2)}, u32[]{:S(2)}) %collective-permute-start.2) | collective-permute-done | bytes 221216 | tf_op jit(solution)/shard_map/ppermute | solution.py:439
  104.6 2.3 %finish_rows.3 = f32[16,1,512]{2,1,0:T(1,128)} custom-call(s32[1]{0:T(128)} %bitcast.33.me_ref, f32[16,128]{1,0:T(8,128)S(1)} %get-tuple-element.142.bound_ref, f32[8,128]{1,0:T(8,128)S(1)} %get-tuple-element.143.total_ref, bf16[144,768]{1,0:T(8,128)(2,1)S(1)} %collective-permute-done.2.refs_0_, ...), custom_call_target="tpu_custom_call" | custom-call | flops 905969664 | bytes 3538944 | tf_op jit(solution)/shard_map/finish_rows/pallas_call | solution.py:370
  106.9 3.5 %all-to-all-start.3 = ((f32[16,1,512]{2,1,0:T(1,128)}), f32[16,1,512]{2,1,0:T(1,128)S(1)}, u32[]{:S(2)}, u32[]{:S(2)}) async-start(f32[16,1,512]{2,1,0:T(1,128)} %finish_rows.3), calls=%async_computation.3 | async-start | bytes 65536 | tf_op jit(solution)/shard_map/all_to_all | solution.py:421
  110.4 6.6 %all-to-all-done.3.back_ref = f32[16,1,512]{2,1,0:T(1,128)S(1)} async-done(((f32[16,1,512]{2,1,0:T(1,128)}), f32[16,1,512]{2,1,0:T(1,128)S(1)}, u32[]{:S(2)}, u32[]{:S(2)}) %all-to-all-start.3) | async-done | bytes 32800 | tf_op jit(solution)/shard_map/all_to_all | solution.py:421
  117.0 1.2 %restore_rows.3 = (f32[1,2048]{1,0:T(1,128)}, f32[1,2048]{1,0:T(1,128)}) custom-call(s32[1,2048]{1,0:T(1,128)S(1)} %get-tuple-element.140.owner_ref, s32[1,2048]{1,0:T(1,128)S(1)} %get-tuple-element.141.slot_ref, f32[16,1,512]{2,1,0:T(1,128)S(1)} %all-to-all-done.3.back_ref), custom_call_target="tpu_custom_call" | custom-call | tf_op jit(solution)/shard_map/restore_rows/pallas_call | solution.py:410
  (23 shorter events, 3.7 us)
Async XLA Ops:
  0.6 0.7 copy-start
  2.3 13.7 %all-to-all-start.2 = ((s32[16,1,64]{2,1,0:T(1,128)}), s32[16,1,64]{2,1,0:T(1,128)S(1)}, u32[]{:S(2)}, u32[]{:S(2)}) async-start(s32[16,1,64]{2,1,0:T(1,128)} %get-tuple-element.137), calls=%async_computation.2 | async-start | bytes 16384 | tf_op jit(solution)/shard_map/all_to_all | solution.py:421
  16.1 0.7 copy-start.1
  16.7 11.4 %copy-start.6 = (bf16[2048,768]{1,0:T(8,128)(2,1)S(1)}, bf16[2048,768]{1,0:T(8,128)(2,1)}, u32[]{:S(2)}) copy-start(bf16[2048,768]{1,0:T(8,128)(2,1)} %rows_ref.10) | copy-start | bytes 9437188
  17.4 87.2 %copy-start.4 = (f32[8,128]{1,0:T(8,128)}, f32[8,128]{1,0:T(8,128)S(1)}, u32[]{:S(2)}) copy-start(f32[8,128]{1,0:T(8,128)S(1)} %get-tuple-element.143.total_ref) | copy-start | bytes 12292
  21.6 10.6 %collective-permute-start.3 = (bf16[144,768]{1,0:T(8,128)(2,1)S(1)}, bf16[144,768]{1,0:T(8,128)(2,1)S(1)}, u32[]{:S(2)}, u32[]{:S(2)}) collective-permute-start(bf16[144,768]{1,0:T(8,128)(2,1)S(1)} %get-tuple-element.151), channel_id=1, source_target_pairs={{0,15},{1,14},{2,13},{3,12},{4,11},{5,10},{6,9},{7,8},{8,7},{9,6},... | collective-permute-start | bytes 663560 | tf_op jit(solution)/shard_map/ppermute | solution.py:439
  21.7 16.2 %collective-permute-start.4 = (bf16[144,768]{1,0:T(8,128)(2,1)S(1)}, bf16[144,768]{1,0:T(8,128)(2,1)S(1)}, u32[]{:S(2)}, u32[]{:S(2)}) collective-permute-start(bf16[144,768]{1,0:T(8,128)(2,1)S(1)} %get-tuple-element.154), channel_id=1, source_target_pairs={{0,7},{1,6},{2,5},{3,4},{4,3},{5,2},{6,1},{7,0},{8,15},{9,14},{10,... | collective-permute-start | bytes 663560 | tf_op jit(solution)/shard_map/ppermute | solution.py:439
  23.4 21.8 %collective-permute-start.5 = (bf16[144,768]{1,0:T(8,128)(2,1)S(1)}, bf16[144,768]{1,0:T(8,128)(2,1)S(1)}, u32[]{:S(2)}, u32[]{:S(2)}) collective-permute-start(bf16[144,768]{1,0:T(8,128)(2,1)S(1)} %get-tuple-element.157), channel_id=1, source_target_pairs={{0,14},{1,15},{2,12},{3,13},{4,10},{5,11},{6,8},{7,9},{8,6},{9,7},... | collective-permute-start | bytes 663560 | tf_op jit(solution)/shard_map/ppermute | solution.py:439
  25.8 19.5 %collective-permute-start.6 = (bf16[144,768]{1,0:T(8,128)(2,1)S(1)}, bf16[144,768]{1,0:T(8,128)(2,1)S(1)}, u32[]{:S(2)}, u32[]{:S(2)}) collective-permute-start(bf16[144,768]{1,0:T(8,128)(2,1)S(1)} %get-tuple-element.160), channel_id=1, source_target_pairs={{0,6},{1,7},{2,4},{3,5},{4,2},{5,3},{6,0},{7,1},{8,14},{9,15},{10,... | collective-permute-start | bytes 663560 | tf_op jit(solution)/shard_map/ppermute | solution.py:439
  30.1 25.4 %collective-permute-start = (bf16[144,768]{1,0:T(8,128)(2,1)S(1)}, bf16[144,768]{1,0:T(8,128)(2,1)S(1)}, u32[]{:S(2)}, u32[]{:S(2)}) collective-permute-start(bf16[144,768]{1,0:T(8,128)(2,1)S(1)} %get-tuple-element.146), channel_id=1, source_target_pairs={{0,13},{1,12},{2,15},{3,14},{4,9},{5,8},{6,11},{7,10},{8,5},{9,4},... | collective-permute-start | bytes 663560 | tf_op jit(solution)/shard_map/ppermute | solution.py:439
  32.1 25.8 %collective-permute-start.11 = (bf16[144,768]{1,0:T(8,128)(2,1)S(1)}, bf16[144,768]{1,0:T(8,128)(2,1)S(1)}, u32[]{:S(2)}, u32[]{:S(2)}) collective-permute-start(bf16[144,768]{1,0:T(8,128)(2,1)S(1)} %get-tuple-element.172), channel_id=1, source_target_pairs={{0,5},{1,4},{2,7},{3,6},{4,1},{5,0},{6,3},{7,2},{8,13},{9,12},{10,... | collective-permute-start | bytes 663560 | tf_op jit(solution)/shard_map/ppermute | solution.py:439
  37.8 27.2 %collective-permute-start.13 = (bf16[144,768]{1,0:T(8,128)(2,1)S(1)}, bf16[144,768]{1,0:T(8,128)(2,1)S(1)}, u32[]{:S(2)}, u32[]{:S(2)}) collective-permute-start(bf16[144,768]{1,0:T(8,128)(2,1)S(1)} %get-tuple-element.175), channel_id=1, source_target_pairs={{0,12},{1,13},{2,14},{3,15},{4,8},{5,9},{6,10},{7,11},{8,4},{9,5},... | collective-permute-start | bytes 663560 | tf_op jit(solution)/shard_map/ppermute | solution.py:439
  45.2 26.0 %collective-permute-start.7 = (bf16[144,768]{1,0:T(8,128)(2,1)S(1)}, bf16[144,768]{1,0:T(8,128)(2,1)S(1)}, u32[]{:S(2)}, u32[]{:S(2)}) collective-permute-start(bf16[144,768]{1,0:T(8,128)(2,1)S(1)} %get-tuple-element.164), channel_id=1, source_target_pairs={{0,4},{1,5},{2,6},{3,7},{4,0},{5,1},{6,2},{7,3},{8,12},{9,13},{10,... | collective-permute-start | bytes 663560 | tf_op jit(solution)/shard_map/ppermute | solution.py:439
  55.5 26.1 %collective-permute-start.9 = (bf16[144,768]{1,0:T(8,128)(2,1)S(1)}, bf16[144,768]{1,0:T(8,128)(2,1)S(1)}, u32[]{:S(2)}, u32[]{:S(2)}) collective-permute-start(bf16[144,768]{1,0:T(8,128)(2,1)S(1)} %get-tuple-element.167), channel_id=1, source_target_pairs={{0,11},{1,10},{2,9},{3,8},{4,15},{5,14},{6,13},{7,12},{8,3},{9,2},... | collective-permute-start | bytes 663560 | tf_op jit(solution)/shard_map/ppermute | solution.py:439
  57.4 24.3 %collective-permute-start.1 = (bf16[144,768]{1,0:T(8,128)(2,1)S(1)}, bf16[144,768]{1,0:T(8,128)(2,1)S(1)}, u32[]{:S(2)}, u32[]{:S(2)}) collective-permute-start(bf16[144,768]{1,0:T(8,128)(2,1)S(1)} %get-tuple-element.147), channel_id=1, source_target_pairs={{0,3},{1,2},{2,1},{3,0},{4,7},{5,6},{6,5},{7,4},{8,11},{9,10},{10,... | collective-permute-start | bytes 663560 | tf_op jit(solution)/shard_map/ppermute | solution.py:439
  65.0 30.9 %collective-permute-start.12 = (bf16[144,768]{1,0:T(8,128)(2,1)S(1)}, bf16[144,768]{1,0:T(8,128)(2,1)S(1)}, u32[]{:S(2)}, u32[]{:S(2)}) collective-permute-start(bf16[144,768]{1,0:T(8,128)(2,1)S(1)} %get-tuple-element.173), channel_id=1, source_target_pairs={{0,10},{1,11},{2,8},{3,9},{4,14},{5,15},{6,12},{7,13},{8,2},{9,3},... | collective-permute-start | bytes 663560 | tf_op jit(solution)/shard_map/ppermute | solution.py:439
  67.1 28.8 %collective-permute-start.14 = (bf16[144,768]{1,0:T(8,128)(2,1)S(1)}, bf16[144,768]{1,0:T(8,128)(2,1)S(1)}, u32[]{:S(2)}, u32[]{:S(2)}) collective-permute-start(bf16[144,768]{1,0:T(8,128)(2,1)S(1)} %get-tuple-element.176), channel_id=1, source_target_pairs={{0,2},{1,3},{2,0},{3,1},{4,6},{5,7},{6,4},{7,5},{8,10},{9,11},{10,... | collective-permute-start | bytes 663560 | tf_op jit(solution)/shard_map/ppermute | solution.py:439
  81.6 17.4 %collective-permute-start.10 = (bf16[144,768]{1,0:T(8,128)(2,1)S(1)}, bf16[144,768]{1,0:T(8,128)(2,1)S(1)}, u32[]{:S(2)}, u32[]{:S(2)}) collective-permute-start(bf16[144,768]{1,0:T(8,128)(2,1)S(1)} %get-tuple-element.168), channel_id=1, source_target_pairs={{0,1},{1,0},{2,3},{3,2},{4,5},{5,4},{6,7},{7,6},{8,9},{9,8},{10,11... | collective-permute-start | bytes 663560 | tf_op jit(solution)/shard_map/ppermute | solution.py:439
  81.8 18.0 %collective-permute-start.8 = (bf16[144,768]{1,0:T(8,128)(2,1)S(1)}, bf16[144,768]{1,0:T(8,128)(2,1)S(1)}, u32[]{:S(2)}, u32[]{:S(2)}) collective-permute-start(bf16[144,768]{1,0:T(8,128)(2,1)S(1)} %get-tuple-element.165), channel_id=1, source_target_pairs={{0,9},{1,8},{2,11},{3,10},{4,13},{5,12},{6,15},{7,14},{8,1},{9,0},... | collective-permute-start | bytes 663560 | tf_op jit(solution)/shard_map/ppermute | solution.py:439
  81.8 22.8 %collective-permute-start.2 = (bf16[144,768]{1,0:T(8,128)(2,1)S(1)}, bf16[144,768]{1,0:T(8,128)(2,1)S(1)}, u32[]{:S(2)}, u32[]{:S(2)}) collective-permute-start(bf16[144,768]{1,0:T(8,128)(2,1)S(1)} %get-tuple-element.148), channel_id=1, source_target_pairs={{0,8},{1,9},{2,10},{3,11},{4,12},{5,13},{6,14},{7,15},{8,0},{9,1},... | collective-permute-start | bytes 663560 | tf_op jit(solution)/shard_map/ppermute | solution.py:439
  106.9 10.1 %all-to-all-start.3 = ((f32[16,1,512]{2,1,0:T(1,128)}), f32[16,1,512]{2,1,0:T(1,128)S(1)}, u32[]{:S(2)}, u32[]{:S(2)}) async-start(f32[16,1,512]{2,1,0:T(1,128)} %finish_rows.3), calls=%async_computation.3 | async-start | bytes 65536 | tf_op jit(solution)/shard_map/all_to_all | solution.py:421

commit v4 on v3

--- a/solution.py
+++ b/solution.py
@@ -13,8 +13,8 @@
 TILE = 256
 LANES = 128
 GROUP = 4
-FLIGHT = 5
 MAX_PERMUTES = 16
+RANKS = 4096
 MIB = 1 << 20
 
 epsilon = 1e-06
@@ -47,7 +47,7 @@
 
 def count_kernel(ids_ref, counts_ref, rank_ref):
     rows = ids_ref.shape[1]
-    owners, _, clusters = counts_ref.shape
+    peers, _, clusters = counts_ref.shape
     label = iota((clusters, TILE), 0)
     upto = to_bf16(iota((TILE, TILE), 0) <= iota((TILE, TILE), 1))
     total = jnp.zeros((clusters, 1), f32)
@@ -55,21 +55,22 @@
         at = slice(b * TILE, (b + 1) * TILE)
         hot = ids_ref[:, at] == label
         prefix = mm(to_bf16(hot), upto)
-        rank_ref[:, at] = jnp.sum(jnp.where(hot, prefix + total - 1.0, 0.0), axis=0, keepdims=True)
+        rank = jnp.sum(jnp.where(hot, prefix + total - 1.0, 0.0), axis=0, keepdims=True)
+        rank_ref[:, at] = ids_ref[:, at] * RANKS + rank.astype(i32)
         total = total + prefix[:, TILE - 1 :]
     square = (clusters, clusters)
     eye = iota(square, 0) == iota(square, 1)
     total_row = jnp.sum(jnp.where(eye, total, 0.0), axis=0, keepdims=True).astype(i32)
-    for owner in range(owners):
-        counts_ref[owner] = total_row
-
-
-def count_rows(ids_row, owners, clusters):
+    for peer in range(peers):
+        counts_ref[peer] = total_row
+
+
+def count_rows(ids_row, peers, clusters):
     return pl.pallas_call(
         count_kernel,
         out_shape=(
-            jax.ShapeDtypeStruct((owners, 1, clusters), i32),
-            jax.ShapeDtypeStruct(ids_row.shape, f32),
+            jax.ShapeDtypeStruct((peers, 1, clusters), i32),
+            jax.ShapeDtypeStruct(ids_row.shape, i32),
         ),
         in_specs=[VMEM],
         out_specs=(VMEM, VMEM),
@@ -79,13 +80,14 @@
 
 
 def assign_kernel(
-    me_ref, counts_ref, ids_ref, rank_ref, owner_ref, slot_ref, bound_ref, total_ref, load_ref
+    me_ref, counts_ref, rank_ref, owner_ref, slot_ref, bound_ref, total_ref, load_ref
 ):
-    owners, _, clusters = counts_ref.shape
-    rows = ids_ref.shape[1]
+    far, near, clusters = counts_ref.shape
+    owners = far * near
+    rows = rank_ref.shape[1]
     shift = owners.bit_length() - 1
     me = me_ref[0]
-    count = jnp.concatenate([counts_ref[s] for s in range(owners)], axis=0).astype(f32)
+    count = jnp.concatenate([counts_ref[s].astype(f32) for s in range(far)], axis=0)
     count16 = count.astype(bf16)
     square = (clusters, clusters)
     sub, lane = iota(square, 0), iota(square, 1)
@@ -128,13 +130,14 @@
     mine = jnp.sum(jnp.where(iota(count.shape, 0) == me, count, 0.0), axis=0, keepdims=True)
     earlier = (owner_row == owner_col) & (layer_row < layer_col)
     offset_col = jnp.sum(jnp.where(earlier, mine, 0.0), axis=1, keepdims=True)
-    hot = ids_ref[...] == iota((clusters, rows), 0)
+    ids = rank_ref[...] // RANKS
+    hot = ids == iota((clusters, rows), 0)
     owner_ref[...] = jnp.sum(
         jnp.where(hot, owner_col.astype(f32), 0.0), axis=0, keepdims=True
     ).astype(i32)
     slot_ref[...] = (
-        jnp.sum(jnp.where(hot, offset_col, 0.0), axis=0, keepdims=True) + rank_ref[...]
-    ).astype(i32)
+        jnp.sum(jnp.where(hot, offset_col, 0.0), axis=0, keepdims=True)
+    ).astype(i32) + (rank_ref[...] & (RANKS - 1))
 
     select = (owner_col == me) & (layer_col <= iota((clusters, LANES), 1))
     turn = iota((owners, owners), 1) == (iota((owners, owners), 0) ^ me)
@@ -146,9 +149,9 @@
     )
 
 
-def assign(me, counts, ids_row, rank):
-    owners, _, clusters = counts.shape
-    rows = ids_row.shape[1]
+def assign(me, counts, rank):
+    far, near, clusters = counts.shape
+    owners, rows = far * near, rank.shape[1]
     return pl.pallas_call(
         assign_kernel,
         out_shape=(
@@ -158,11 +161,11 @@
             jax.ShapeDtypeStruct((8, LANES), f32),
             jax.ShapeDtypeStruct((1, LANES), i32),
         ),
-        in_specs=[SMEM, VMEM, VMEM, VMEM],
+        in_specs=[SMEM, VMEM, VMEM],
         out_specs=(VMEM,) * 5,
         compiler_params=pltpu.CompilerParams(vmem_limit_bytes=16 * MIB),
         name="assign",
-    )(me, counts, ids_row, rank)
+    )(me, counts, rank)
 
 
 def pack_kernel(slots, partners, me_ref, owner_ref, slot_ref, rows_ref, *out_refs):
@@ -178,8 +181,8 @@
         ref[...] = picked[i * slots : (i + 1) * slots]
 
 
-def pack(me, owner_row, slot_row, embeddings, partners, slots):
-    rows, width = embeddings.shape
+def pack(me, owner_row, slot_row, unit, partners, slots):
+    rows, width = unit.shape
     flops = 2 * len(partners) * slots * rows * width
     return pl.pallas_call(
         functools.partial(pack_kernel, slots, partners),
@@ -191,13 +194,33 @@
             flops=flops, bytes_accessed=2 * rows * width, transcendentals=0
         ),
         name="pack_rows",
-    )(me, owner_row, slot_row, embeddings)
-
-
-def unit_rows(ref):
-    x = ref[...].astype(f32)
-    scale = lax.rsqrt(jnp.sum(x * x, axis=1, keepdims=True) + epsilon)
-    return (x * scale).astype(bf16)
+    )(me, owner_row, slot_row, unit)
+
+
+def unit_kernel(rows_ref, unit_ref):
+    def body(b, carry):
+        at = pl.ds(pl.multiple_of(b * TILE, TILE), TILE)
+        x = rows_ref[at, :].astype(f32)
+        scale = lax.rsqrt(jnp.sum(x * x, axis=1, keepdims=True) + epsilon)
+        unit_ref[at, :] = (x * scale).astype(bf16)
+        return carry
+
+    lax.fori_loop(0, rows_ref.shape[0] // TILE, body, 0)
+
+
+def unit_rows(embeddings):
+    rows, width = embeddings.shape
+    return pl.pallas_call(
+        unit_kernel,
+        out_shape=jax.ShapeDtypeStruct((rows, width), bf16),
+        in_specs=[VMEM],
+        out_specs=VMEM,
+        compiler_params=pltpu.CompilerParams(vmem_limit_bytes=16 * MIB),
+        cost_estimate=pl.CostEstimate(
+            flops=8 * rows * width, bytes_accessed=4 * rows * width, transcendentals=rows
+        ),
+        name="unit_rows",
+    )(embeddings)
 
 
 def cluster_lanes(bound_ref, partners, slots, width):
@@ -274,7 +297,7 @@
     rows = fresh * slots
     for i, r in enumerate(partners):
         at = slice(i * slots, (i + 1) * slots)
-        new_ref[at, :] = unit_rows(raw_refs[i])
+        new_ref[at, :] = raw_refs[i][...]
         cid_ref[at, :] = cluster_rows(bound_ref, r, slots)
     padded = new_ref.shape[0]
     if padded > rows:
@@ -332,7 +355,7 @@
     new_ref[rows:, :] = jnp.zeros((padded - rows, width), bf16)
     pieces = []
     for i, r in enumerate(partners):
-        new_ref[i * slots : (i + 1) * slots, :] = unit_rows(raw_refs[i])
+        new_ref[i * slots : (i + 1) * slots, :] = raw_refs[i][...]
         pieces.append(cluster_rows(bound_ref, r, slots))
     new_cids = jnp.concatenate(pieces, axis=0)
     cid_row = cluster_lanes(bound_ref, partners, slots, padded)
@@ -428,16 +451,21 @@
     return [arrived[r] for r in range(owners)]
 
 
-def swap_apart(blocks, order):
-    owners = len(blocks)
-    arrived = list(blocks)
-    for i, r in enumerate(order):
-        block = blocks[r]
-        if i >= FLIGHT:
-            before = order[i - FLIGHT]
-            block, arrived[before] = lax.optimization_barrier((block, arrived[before]))
-        arrived[r] = lax.ppermute(block, "owner", [(s, s ^ r) for s in range(owners)])
-    return arrived
+def swap_apart(blocks):
+    pairs = [[(s, s ^ r) for s in range(len(blocks))] for r in range(len(blocks))]
+    return blocks[:1] + [
+        lax.ppermute(block, "owner", pair) for block, pair in zip(blocks[1:], pairs[1:])
+    ]
+
+
+def gather_counts(counts, owners):
+    near, _, clusters = counts.shape
+    far = owners // near
+    close = [[f * near + n for n in range(near)] for f in range(far)]
+    apart = [[f * near + n for f in range(far)] for n in range(near)]
+    seen = lax.all_to_all(counts, "owner", 0, 0, axis_index_groups=close, tiled=True)
+    seen = jnp.broadcast_to(seen.reshape(1, near, clusters), (far, near, clusters))
+    return lax.all_to_all(seen, "owner", 0, 0, axis_index_groups=apart, tiled=True)
 
 
 def local(embeddings, cluster_ids):
@@ -450,13 +478,21 @@
     few = owners <= MAX_PERMUTES
     me = lax.axis_index("owner").astype(i32).reshape(1)
     ids_row = cluster_ids.reshape(1, rows)
-    counts, rank = count_rows(ids_row, owners, clusters)
-    owner_row, slot_row, bound, total, load = assign(me, exchange(counts), ids_row, rank)
+    peers = 1 << ((owners.bit_length() - 1) // 2)
+    counts, rank = count_rows(ids_row, peers, clusters)
+    unit = unit_rows(embeddings)
+    counts = gather_counts(counts, owners)
+    owner_row, slot_row, bound, total, load = assign(me, counts, rank)
 
     half = owners // 2
-    order = [r for i in reversed(range(half)) for r in (half + i, i)][:-1]
-    sent = order + [0]
-    seen = [0] + order
+    far = list(range(owners - 1, half - 1, -1))
+    near = list(range(half - 1, 0, -1))
+    sent = far[:2] + [r for pair in zip(far[2:-1], near) for r in pair]
+    sent = sent + near[len(far) - 3 :] + far[-1:]
+    seen = [0] + sent
+    sent = sent + [0]
+    packs = [tuple(sent[:2]), tuple(sent[2:4])]
+    packs += [tuple(sent[i : i + GROUP]) for i in range(4, owners, GROUP)]
     share = owners // 16 if owners >= 16 else 1
     groups, at = [], 0
     for size in (5, 4, 4, 2):
@@ -466,12 +502,13 @@
 
     def compare(slots, apart):
         blocks = [None] * owners
-        for first in range(0, owners, GROUP):
-            partners = tuple(sent[first : first + GROUP])
-            packed = pack(me, owner_row, slot_row, embeddings, partners, slots)
+        slot_in = slot_row
+        for partners in packs:
+            packed = pack(me, owner_row, slot_in, unit, partners, slots)
+            slot_in, *packed = lax.optimization_barrier((slot_in, *packed))
             for r, block in zip(partners, packed):
                 blocks[r] = block
-        arrived = swap_apart(blocks, order) if apart else swap_together(blocks)
+        arrived = swap_apart(blocks) if apart else swap_together(blocks)
         state = ([], [], [], None)
         for group in groups[:-1]:
             state = score(bound, [arrived[r] for r in group], group, state)

time: 119 us -> 121 us (1.017)
  waiting for transfers between devices: 54.8 us -> 30.7 us
  starting transfers between devices: 37 us -> 55.3 us
  blocking collectives: 0 us -> 7.79 us
  local copies, waits for them, and re-layouts: 1.4 us -> 3.86 us
  Pallas kernels: 24.2 us -> 21.9 us
    ppermute x15, starting transfers between devices: 26.1 us -> 47 us  [swap_apart(): lax.ppermute(block, 'owner', pair)]
    ppermute x15, waiting for transfers between devices: 41.9 us -> 21.8 us  [swap_apart(): lax.ppermute(block, 'owner', pair)]
    all_to_all x0 -> x1, blocking collectives: none -> 7.79 us  [gather_counts(): lax.all_to_all(counts, 'owner', 0, 0, axis_index_groups=close, tiled=True)]
    all_to_all x2 -> x1, starting transfers between devices: 10.9 us -> 3.48 us  [exchange(): return lax.all_to_all(x, 'owner', split_axis=0, concat_axis=0, tiled=True)]
    all_to_all x2 -> x1, waiting for transfers between devices: 12.9 us -> 6.56 us  [exchange(): return lax.all_to_all(x, 'owner', split_axis=0, concat_axis=0, tiled=True)]
    all_to_all x0 -> x1, starting transfers between devices: none -> 4.87 us  [gather_counts(): lax.all_to_all(seen, 'owner', 0, 0, axis_index_groups=apart, tiled=True)]
    all_to_all x0 -> x1, waiting for transfers between devices: none -> 2.39 us  [gather_counts(): lax.all_to_all(seen, 'owner', 0, 0, axis_index_groups=apart, tiled=True)]
    pallas_call x4 -> x5, Pallas kernels: 10.2 us -> 8.19 us  [pack(): pl.pallas_call(functools.partial(pack_kernel, slots, partners), out_shape...]
  transfers between devices with their start and end apart: 17 -> 17, of which waited for: 11 -> 6; matrix products, arithmetic and copies ran while one was open for 0% -> 0% of each run, Pallas kernels for 13% -> 13%
where the time goes in v4:
time: 121 us
  starting transfers between devices  55.3 us (46%)
  waiting for transfers between devices  30.7 us (25%)
  Pallas kernels  21.9 us (18%)
  blocking collectives  7.79 us (6%)
  local copies, waits for them, and re-layouts  3.86 us (3%)
    ppermute x15, starting transfers between devices, swap_apart(): lax.ppermute(block, 'owner', pair)  47 us
    ppermute x15, waiting for transfers between devices, swap_apart(): lax.ppermute(block, 'owner', pair)  21.8 us
    pallas_call x5, Pallas kernels, pack(): pl.pallas_call(functools.partial(pack_kernel, slots, partners), out_shape...  8.19 us
    pallas_call x4, Pallas kernels, score(): pl.pallas_call(functools.partial(score_kernel, slots, partners, len(units...  8.03 us
    all_to_all x1, blocking collectives, gather_counts(): lax.all_to_all(counts, 'owner', 0, 0, axis_index_groups=close, tiled=True)  7.79 us
    all_to_all x1, waiting for transfers between devices, exchange(): return lax.all_to_all(x, 'owner', split_axis=0, concat_axis=0, tiled=True)  6.56 us
    all_to_all x1, starting transfers between devices, gather_counts(): lax.all_to_all(seen, 'owner', 0, 0, axis_index_groups=apart, tiled=True)  4.87 us
    all_to_all x1, starting transfers between devices, exchange(): return lax.all_to_all(x, 'owner', split_axis=0, concat_axis=0, tiled=True)  3.48 us
  transfers between devices with their start and end apart: 17, of which 6 were waited for; matrix products, arithmetic and copies ran while one was open for 0% of the time, Pallas kernels for 13%

profile of v4, /device:TPU:0, one launch (start us, length us, event | category | flops | bytes accessed | tf_op | source)
XLA Modules:
  0.0 121.1 jit_solution(17720317047469558958)
XLA Ops:
  0.6 0.7 copy-done.7
  1.7 7.8 %all_to_all.25 = s32[4,1,64]{2,1,0:T(1,128)S(1)} all-to-all(s32[4,1,64]{2,1,0:T(1,128)S(1)} %get-tuple-element.157), channel_id=1, replica_groups={{0,1,2,3},{4,5,6,7},{8,9,10,11},{12,13,14,15},{16,17,18,19},{20,21,22,2..., dimensions={0} | all-to-all | bytes 2048 | tf_op jit(solution)/shard_map/all_to_all | solution.py:466
  9.5 0.7 reshape.67
  10.2 4.9 %all-to-all-start.3 = ((s32[4,1,256]{2,1,0:T(1,128)}), s32[4,1,256]{2,1,0:T(1,128)S(1)}, u32[]{:S(2)}, u32[]{:S(2)}) async-start(s32[4,1,256]{2,1,0:T(1,128)} %reshape.67), calls=%async_computation.3 | async-start | bytes 8192 | tf_op jit(solution)/shard_map/all_to_all | solution.py:468
  15.1 1.9 %copy-done = bf16[2048,768]{1,0:T(8,128)(2,1)S(1)} copy-done((bf16[2048,768]{1,0:T(8,128)(2,1)S(1)}, bf16[2048,768]{1,0:T(8,128)(2,1)}, u32[]{:S(2)}) %copy-start) | copy-done | bytes 3145752
  17.0 1.3 %unit_rows.1.rows_ref = bf16[2048,768]{1,0:T(8,128)(2,1)S(1)} custom-call(bf16[2048,768]{1,0:T(8,128)(2,1)S(1)} %copy-done), custom_call_target="tpu_custom_call" | custom-call | flops 12582912 | bytes 6291456 | tf_op jit(solution)/shard_map/unit_rows/pallas_call | solution.py:213
  18.3 2.4 %all-to-all-done.3 = s32[4,1,256]{2,1,0:T(1,128)S(1)} async-done(((s32[4,1,256]{2,1,0:T(1,128)}), s32[4,1,256]{2,1,0:T(1,128)S(1)}, u32[]{:S(2)}, u32[]{:S(2)}) %all-to-all-start.3) | async-done | bytes 4128 | tf_op jit(solution)/shard_map/all_to_all | solution.py:468
  22.6 1.1 pack_rows.15
  23.7 1.1 pack_rows.16
  25.1 2.7 %collective-permute-start.1 = (bf16[144,768]{1,0:T(8,128)(2,1)S(1)}, bf16[144,768]{1,0:T(8,128)(2,1)S(1)}, u32[]{:S(2)}, u32[]{:S(2)}) collective-permute-start(bf16[144,768]{1,0:T(8,128)(2,1)S(1)} %get-tuple-element.186), channel_id=1, source_target_pairs={{0,15},{1,14},{2,13},{3,12},{4,11},{5,10},{6,9},{7,8},{8,7},{9,6},... | collective-permute-start | bytes 663560 | tf_op jit(solution)/shard_map/ppermute | solution.py:457
  27.8 2.9 %collective-permute-start.2 = (bf16[144,768]{1,0:T(8,128)(2,1)S(1)}, bf16[144,768]{1,0:T(8,128)(2,1)S(1)}, u32[]{:S(2)}, u32[]{:S(2)}) collective-permute-start(bf16[144,768]{1,0:T(8,128)(2,1)S(1)} %get-tuple-element.187), channel_id=1, source_target_pairs={{0,14},{1,15},{2,12},{3,13},{4,10},{5,11},{6,8},{7,9},{8,6},{9,7},... | collective-permute-start | bytes 663560 | tf_op jit(solution)/shard_map/ppermute | solution.py:457
  30.7 2.0 %pack_rows.17 = (bf16[144,768]{1,0:T(8,128)(2,1)S(1)}, bf16[144,768]{1,0:T(8,128)(2,1)S(1)}, bf16[144,768]{1,0:T(8,128)(2,1)S(1)}, bf16[144,768]{1,0:T(8,128)(2,1)S(1)}) custom-call(s32[1]{0:T(128)} %bitcast.33.me_ref, s32[1,2048]{1,0:T(1,128)S(1)} %get-tuple-element.160.owner_ref, s32[1,2048]{1,0:T(1,128)S(1)} %get-tuple-element.179.slot_ref, ...), custom_call_target="tpu_custom_call" | custom-call | flops 1811939328 | bytes 3145728 | tf_op jit(solution)/shard_map/pack_rows/pallas_call | solution.py:187
  32.7 2.4 %collective-permute-start.11 = (bf16[144,768]{1,0:T(8,128)(2,1)S(1)}, bf16[144,768]{1,0:T(8,128)(2,1)S(1)}, u32[]{:S(2)}, u32[]{:S(2)}) collective-permute-start(bf16[144,768]{1,0:T(8,128)(2,1)S(1)} %get-tuple-element.197), channel_id=1, source_target_pairs={{0,12},{1,13},{2,14},{3,15},{4,8},{5,9},{6,10},{7,11},{8,4},{9,5},... | collective-permute-start | bytes 663560 | tf_op jit(solution)/shard_map/ppermute | solution.py:457
  35.2 3.2 %collective-permute-start.12 = (bf16[144,768]{1,0:T(8,128)(2,1)S(1)}, bf16[144,768]{1,0:T(8,128)(2,1)S(1)}, u32[]{:S(2)}, u32[]{:S(2)}) collective-permute-start(bf16[144,768]{1,0:T(8,128)(2,1)S(1)} %get-tuple-element.198), channel_id=1, source_target_pairs={{0,6},{1,7},{2,4},{3,5},{4,2},{5,3},{6,0},{7,1},{8,14},{9,15},{10,... | collective-permute-start | bytes 663560 | tf_op jit(solution)/shard_map/ppermute | solution.py:457
  38.5 2.0 %pack_rows.18 = (bf16[144,768]{1,0:T(8,128)(2,1)S(1)}, bf16[144,768]{1,0:T(8,128)(2,1)S(1)}, bf16[144,768]{1,0:T(8,128)(2,1)S(1)}, bf16[144,768]{1,0:T(8,128)(2,1)S(1)}) custom-call(s32[1]{0:T(128)} %bitcast.33.me_ref, s32[1,2048]{1,0:T(1,128)S(1)} %get-tuple-element.160.owner_ref, s32[1,2048]{1,0:T(1,128)S(1)} %get-tuple-element.179.slot_ref, ...), custom_call_target="tpu_custom_call" | custom-call | flops 1811939328 | bytes 3145728 | tf_op jit(solution)/shard_map/pack_rows/pallas_call | solution.py:187
  40.5 2.9 %collective-permute-done.1.refs_1_ = bf16[144,768]{1,0:T(8,128)(2,1)S(1)} collective-permute-done((bf16[144,768]{1,0:T(8,128)(2,1)S(1)}, bf16[144,768]{1,0:T(8,128)(2,1)S(1)}, u32[]{:S(2)}, u32[]{:S(2)}) %collective-permute-start.1) | collective-permute-done | bytes 221216 | tf_op jit(solution)/shard_map/ppermute | solution.py:457
  43.4 12.9 %collective-permute-start.14 = (bf16[144,768]{1,0:T(8,128)(2,1)S(1)}, bf16[144,768]{1,0:T(8,128)(2,1)S(1)}, u32[]{:S(2)}, u32[]{:S(2)}) collective-permute-start(bf16[144,768]{1,0:T(8,128)(2,1)S(1)} %get-tuple-element.200), channel_id=1, source_target_pairs={{0,5},{1,4},{2,7},{3,6},{4,1},{5,0},{6,3},{7,2},{8,13},{9,12},{10,... | collective-permute-start | bytes 663560 | tf_op jit(solution)/shard_map/ppermute | solution.py:457
  56.3 10.3 %collective-permute-start.10 = (bf16[144,768]{1,0:T(8,128)(2,1)S(1)}, bf16[144,768]{1,0:T(8,128)(2,1)S(1)}, u32[]{:S(2)}, u32[]{:S(2)}) collective-permute-start(bf16[144,768]{1,0:T(8,128)(2,1)S(1)} %get-tuple-element.196), channel_id=1, source_target_pairs={{0,3},{1,2},{2,1},{3,0},{4,7},{5,6},{6,5},{7,4},{8,11},{9,10},{10,... | collective-permute-start | bytes 663560 | tf_op jit(solution)/shard_map/ppermute | solution.py:457
  66.6 7.0 %collective-permute-start.7 = (bf16[144,768]{1,0:T(8,128)(2,1)S(1)}, bf16[144,768]{1,0:T(8,128)(2,1)S(1)}, u32[]{:S(2)}, u32[]{:S(2)}) collective-permute-start(bf16[144,768]{1,0:T(8,128)(2,1)S(1)} %get-tuple-element.193), channel_id=1, source_target_pairs={{0,10},{1,11},{2,8},{3,9},{4,14},{5,15},{6,12},{7,13},{8,2},{9,3},... | collective-permute-start | bytes 663560 | tf_op jit(solution)/shard_map/ppermute | solution.py:457
  73.6 9.3 %collective-permute-done.13.refs_2_ = bf16[144,768]{1,0:T(8,128)(2,1)S(1)} collective-permute-done((bf16[144,768]{1,0:T(8,128)(2,1)S(1)}, bf16[144,768]{1,0:T(8,128)(2,1)S(1)}, u32[]{:S(2)}, u32[]{:S(2)}) %collective-permute-start.13) | collective-permute-done | bytes 221216 | tf_op jit(solution)/shard_map/ppermute | solution.py:457
  83.1 2.0 %pack_rows.19 = (bf16[144,768]{1,0:T(8,128)(2,1)S(1)}, bf16[144,768]{1,0:T(8,128)(2,1)S(1)}, bf16[144,768]{1,0:T(8,128)(2,1)S(1)}, bf16[144,768]{1,0:T(8,128)(2,1)S(1)}) custom-call(s32[1]{0:T(128)} %bitcast.33.me_ref, s32[1,2048]{1,0:T(1,128)S(1)} %get-tuple-element.160.owner_ref, s32[1,2048]{1,0:T(1,128)S(1)} %get-tuple-element.179.slot_ref, ...), custom_call_target="tpu_custom_call" | custom-call | flops 1811939328 | bytes 3145728 | tf_op jit(solution)/shard_map/pack_rows/pallas_call | solution.py:187
  85.1 1.3 %score_rows.12 = (bf16[720,768]{1,0:T(8,128)(2,1)S(1)}, f32[720,128]{1,0:T(8,128)S(1)}, f32[720,128]{1,0:T(8,128)S(1)}, f32[8,768]{1,0:T(8,128)S(1)}) custom-call(f32[16,128]{1,0:T(8,128)S(1)} %get-tuple-element.162.bound_ref, bf16[144,768]{1,0:T(8,128)(2,1)S(1)} %get-tuple-element.185.refs_0_, bf16[144,768]{1,0:T(8,128)(2,1)S(1)} %collective-permute-done.1.refs_1_, ...), custom_call_target="tpu_custom_call" | custom-call | flops 849346560 | bytes 1105920 | tf_op jit(solution)/shard_map/score_rows/pallas_call | solution.py:330
  86.4 2.3 %collective-permute-start.5 = (bf16[144,768]{1,0:T(8,128)(2,1)S(1)}, bf16[144,768]{1,0:T(8,128)(2,1)S(1)}, u32[]{:S(2)}, u32[]{:S(2)}) collective-permute-start(bf16[144,768]{1,0:T(8,128)(2,1)S(1)} %get-tuple-element.191), channel_id=1, source_target_pairs={{0,2},{1,3},{2,0},{3,1},{4,6},{5,7},{6,4},{7,5},{8,10},{9,11},{10,... | collective-permute-start | bytes 663560 | tf_op jit(solution)/shard_map/ppermute | solution.py:457
  88.6 1.9 %score_rows.13 = (bf16[576,768]{1,0:T(8,128)(2,1)S(1)}, f32[576,128]{1,0:T(8,128)S(1)}, f32[576,128]{1,0:T(8,128)S(1)}, f32[8,768]{1,0:T(8,128)S(1)}, f32[720,128]{1,0:T(8,128)S(1)}) custom-call(f32[16,128]{1,0:T(8,128)S(1)} %get-tuple-element.162.bound_ref, bf16[144,768]{1,0:T(8,128)(2,1)S(1)} %collective-permute-done.11.refs_0_, ...), custom_call_target="tpu_custom_call" | custom-call | flops 1274019840 | bytes 1990656 | tf_op jit(solution)/shard_map/score_rows/pallas_call | solution.py:330
  90.6 2.8 %collective-permute-start = (bf16[144,768]{1,0:T(8,128)(2,1)S(1)}, bf16[144,768]{1,0:T(8,128)(2,1)S(1)}, u32[]{:S(2)}, u32[]{:S(2)}) collective-permute-start(bf16[144,768]{1,0:T(8,128)(2,1)S(1)} %get-tuple-element.184), channel_id=1, source_target_pairs={{0,8},{1,9},{2,10},{3,11},{4,12},{5,13},{6,14},{7,15},{8,0},{9,1},... | collective-permute-start | bytes 663560 | tf_op jit(solution)/shard_map/ppermute | solution.py:457
  93.4 9.4 %collective-permute-done.9.refs_2_ = bf16[144,768]{1,0:T(8,128)(2,1)S(1)} collective-permute-done((bf16[144,768]{1,0:T(8,128)(2,1)S(1)}, bf16[144,768]{1,0:T(8,128)(2,1)S(1)}, u32[]{:S(2)}, u32[]{:S(2)}) %collective-permute-start.9) | collective-permute-done | bytes 221216 | tf_op jit(solution)/shard_map/ppermute | solution.py:457
  102.7 2.9 %score_rows.14 = (bf16[576,768]{1,0:T(8,128)(2,1)S(1)}, f32[576,128]{1,0:T(8,128)S(1)}, f32[576,128]{1,0:T(8,128)S(1)}, f32[8,768]{1,0:T(8,128)S(1)}, f32[720,128]{1,0:T(8,128)S(1)}, /*index=5*/f32[576,128]{1,0:T(8,128)S(1)}) custom-call(f32[16,128]{1,0:T(8,128)S(1)} %get-tuple-element.162.bound_ref, bf16[144,768]{1,0:T(8,128)(2,1)S(1)} %collective-permute-done.7.refs_0_, ...), custom_call_target="tpu_custom_call" | custom-call | flops 1840250880 | bytes 2875392 | tf_op jit(solution)/shard_map/score_rows/pallas_call | solution.py:330
  105.6 2.0 %score_rows.15 = (bf16[288,768]{1,0:T(8,128)(2,1)S(1)}, f32[288,128]{1,0:T(8,128)S(1)}, f32[288,128]{1,0:T(8,128)S(1)}, f32[8,768]{1,0:T(8,128)S(1)}, f32[720,12...) custom-call(f32[16,128]{1,0:T(8,128)S(1)} %get-tuple-element.162.bound_ref, ...), custom_call_target="tpu_custom_call" | custom-call | flops 1274019840 | bytes 3317760 | tf_op jit(solution)/shard_map/score_rows/pallas_call | solution.py:330
  107.6 2.2 %finish_rows.3 = f32[16,1,512]{2,1,0:T(1,128)} custom-call(s32[1]{0:T(128)} %bitcast.33.me_ref, f32[16,128]{1,0:T(8,128)S(1)} %get-tuple-element.162.bound_ref, f32[8,128]{1,0:T(8,128)S(1)} %get-tuple-element.163.total_ref, bf16[144,768]{1,0:T(8,128)(2,1)S(1)} %collective-permute-done.refs_0_, ...), custom_call_target="tpu_custom_call" | custom-call | flops 905969664 | bytes 3538944 | tf_op jit(solution)/shard_map/finish_rows/pallas_call | solution.py:393
  109.8 3.5 %all-to-all-start.4 = ((f32[16,1,512]{2,1,0:T(1,128)}), f32[16,1,512]{2,1,0:T(1,128)S(1)}, u32[]{:S(2)}, u32[]{:S(2)}) async-start(f32[16,1,512]{2,1,0:T(1,128)} %finish_rows.3), calls=%async_computation.4 | async-start | bytes 65536 | tf_op jit(solution)/shard_map/all_to_all | solution.py:444
  113.3 6.6 %all-to-all-done.4.back_ref = f32[16,1,512]{2,1,0:T(1,128)S(1)} async-done(((f32[16,1,512]{2,1,0:T(1,128)}), f32[16,1,512]{2,1,0:T(1,128)S(1)}, u32[]{:S(2)}, u32[]{:S(2)}) %all-to-all-start.4) | async-done | bytes 32800 | tf_op jit(solution)/shard_map/all_to_all | solution.py:444
  119.9 1.2 restore_rows.3
  (29 shorter events, 3.0 us)
Async XLA Ops:
  0.6 0.7 copy-start.7
  10.2 10.4 %all-to-all-start.3 = ((s32[4,1,256]{2,1,0:T(1,128)}), s32[4,1,256]{2,1,0:T(1,128)S(1)}, u32[]{:S(2)}, u32[]{:S(2)}) async-start(s32[4,1,256]{2,1,0:T(1,128)} %reshape.67), calls=%async_computation.3 | async-start | bytes 8192 | tf_op jit(solution)/shard_map/all_to_all | solution.py:468
  15.1 1.9 %copy-start = (bf16[2048,768]{1,0:T(8,128)(2,1)S(1)}, bf16[2048,768]{1,0:T(8,128)(2,1)}, u32[]{:S(2)}) copy-start(bf16[2048,768]{1,0:T(8,128)(2,1)} %rows_ref.1) | copy-start | bytes 9437188
  22.6 85.1 %copy-start.13 = (f32[8,128]{1,0:T(8,128)}, f32[8,128]{1,0:T(8,128)S(1)}, u32[]{:S(2)}) copy-start(f32[8,128]{1,0:T(8,128)S(1)} %get-tuple-element.163.total_ref) | copy-start | bytes 12292
  24.8 10.4 %collective-permute-start.3 = (bf16[144,768]{1,0:T(8,128)(2,1)S(1)}, bf16[144,768]{1,0:T(8,128)(2,1)S(1)}, u32[]{:S(2)}, u32[]{:S(2)}) collective-permute-start(bf16[144,768]{1,0:T(8,128)(2,1)S(1)} %get-tuple-element.188), channel_id=1, source_target_pairs={{0,13},{1,12},{2,15},{3,14},{4,9},{5,8},{6,11},{7,10},{8,5},{9,4},... | collective-permute-start | bytes 663560 | tf_op jit(solution)/shard_map/ppermute | solution.py:457
  25.1 13.4 %collective-permute-start.4 = (bf16[144,768]{1,0:T(8,128)(2,1)S(1)}, bf16[144,768]{1,0:T(8,128)(2,1)S(1)}, u32[]{:S(2)}, u32[]{:S(2)}) collective-permute-start(bf16[144,768]{1,0:T(8,128)(2,1)S(1)} %get-tuple-element.189), channel_id=1, source_target_pairs={{0,7},{1,6},{2,5},{3,4},{4,3},{5,2},{6,1},{7,0},{8,15},{9,14},{10,... | collective-permute-start | bytes 663560 | tf_op jit(solution)/shard_map/ppermute | solution.py:457
  25.1 18.3 %collective-permute-start.1 = (bf16[144,768]{1,0:T(8,128)(2,1)S(1)}, bf16[144,768]{1,0:T(8,128)(2,1)S(1)}, u32[]{:S(2)}, u32[]{:S(2)}) collective-permute-start(bf16[144,768]{1,0:T(8,128)(2,1)S(1)} %get-tuple-element.186), channel_id=1, source_target_pairs={{0,15},{1,14},{2,13},{3,12},{4,11},{5,10},{6,9},{7,8},{8,7},{9,6},... | collective-permute-start | bytes 663560 | tf_op jit(solution)/shard_map/ppermute | solution.py:457
  27.8 28.5 %collective-permute-start.2 = (bf16[144,768]{1,0:T(8,128)(2,1)S(1)}, bf16[144,768]{1,0:T(8,128)(2,1)S(1)}, u32[]{:S(2)}, u32[]{:S(2)}) collective-permute-start(bf16[144,768]{1,0:T(8,128)(2,1)S(1)} %get-tuple-element.187), channel_id=1, source_target_pairs={{0,14},{1,15},{2,12},{3,13},{4,10},{5,11},{6,8},{7,9},{8,6},{9,7},... | collective-permute-start | bytes 663560 | tf_op jit(solution)/shard_map/ppermute | solution.py:457
  32.7 33.9 %collective-permute-start.11 = (bf16[144,768]{1,0:T(8,128)(2,1)S(1)}, bf16[144,768]{1,0:T(8,128)(2,1)S(1)}, u32[]{:S(2)}, u32[]{:S(2)}) collective-permute-start(bf16[144,768]{1,0:T(8,128)(2,1)S(1)} %get-tuple-element.197), channel_id=1, source_target_pairs={{0,12},{1,13},{2,14},{3,15},{4,8},{5,9},{6,10},{7,11},{8,4},{9,5},... | collective-permute-start | bytes 663560 | tf_op jit(solution)/shard_map/ppermute | solution.py:457
  35.2 38.5 %collective-permute-start.12 = (bf16[144,768]{1,0:T(8,128)(2,1)S(1)}, bf16[144,768]{1,0:T(8,128)(2,1)S(1)}, u32[]{:S(2)}, u32[]{:S(2)}) collective-permute-start(bf16[144,768]{1,0:T(8,128)(2,1)S(1)} %get-tuple-element.198), channel_id=1, source_target_pairs={{0,6},{1,7},{2,4},{3,5},{4,2},{5,3},{6,0},{7,1},{8,14},{9,15},{10,... | collective-permute-start | bytes 663560 | tf_op jit(solution)/shard_map/ppermute | solution.py:457
  38.5 44.4 %collective-permute-start.13 = (bf16[144,768]{1,0:T(8,128)(2,1)S(1)}, bf16[144,768]{1,0:T(8,128)(2,1)S(1)}, u32[]{:S(2)}, u32[]{:S(2)}) collective-permute-start(bf16[144,768]{1,0:T(8,128)(2,1)S(1)} %get-tuple-element.199), channel_id=1, source_target_pairs={{0,11},{1,10},{2,9},{3,8},{4,15},{5,14},{6,13},{7,12},{8,3},{9,2},... | collective-permute-start | bytes 663560 | tf_op jit(solution)/shard_map/ppermute | solution.py:457
  43.4 42.9 %collective-permute-start.14 = (bf16[144,768]{1,0:T(8,128)(2,1)S(1)}, bf16[144,768]{1,0:T(8,128)(2,1)S(1)}, u32[]{:S(2)}, u32[]{:S(2)}) collective-permute-start(bf16[144,768]{1,0:T(8,128)(2,1)S(1)} %get-tuple-element.200), channel_id=1, source_target_pairs={{0,5},{1,4},{2,7},{3,6},{4,1},{5,0},{6,3},{7,2},{8,13},{9,12},{10,... | collective-permute-start | bytes 663560 | tf_op jit(solution)/shard_map/ppermute | solution.py:457
  56.3 32.3 %collective-permute-start.10 = (bf16[144,768]{1,0:T(8,128)(2,1)S(1)}, bf16[144,768]{1,0:T(8,128)(2,1)S(1)}, u32[]{:S(2)}, u32[]{:S(2)}) collective-permute-start(bf16[144,768]{1,0:T(8,128)(2,1)S(1)} %get-tuple-element.196), channel_id=1, source_target_pairs={{0,3},{1,2},{2,1},{3,0},{4,7},{5,6},{6,5},{7,4},{8,11},{9,10},{10,... | collective-permute-start | bytes 663560 | tf_op jit(solution)/shard_map/ppermute | solution.py:457
  66.6 23.9 %collective-permute-start.7 = (bf16[144,768]{1,0:T(8,128)(2,1)S(1)}, bf16[144,768]{1,0:T(8,128)(2,1)S(1)}, u32[]{:S(2)}, u32[]{:S(2)}) collective-permute-start(bf16[144,768]{1,0:T(8,128)(2,1)S(1)} %get-tuple-element.193), channel_id=1, source_target_pairs={{0,10},{1,11},{2,8},{3,9},{4,14},{5,15},{6,12},{7,13},{8,2},{9,3},... | collective-permute-start | bytes 663560 | tf_op jit(solution)/shard_map/ppermute | solution.py:457
  73.6 19.7 %collective-permute-start.8 = (bf16[144,768]{1,0:T(8,128)(2,1)S(1)}, bf16[144,768]{1,0:T(8,128)(2,1)S(1)}, u32[]{:S(2)}, u32[]{:S(2)}) collective-permute-start(bf16[144,768]{1,0:T(8,128)(2,1)S(1)} %get-tuple-element.194), channel_id=1, source_target_pairs={{0,4},{1,5},{2,6},{3,7},{4,0},{5,1},{6,2},{7,3},{8,12},{9,13},{10,... | collective-permute-start | bytes 663560 | tf_op jit(solution)/shard_map/ppermute | solution.py:457
  82.9 19.8 %collective-permute-start.9 = (bf16[144,768]{1,0:T(8,128)(2,1)S(1)}, bf16[144,768]{1,0:T(8,128)(2,1)S(1)}, u32[]{:S(2)}, u32[]{:S(2)}) collective-permute-start(bf16[144,768]{1,0:T(8,128)(2,1)S(1)} %get-tuple-element.195), channel_id=1, source_target_pairs={{0,9},{1,8},{2,11},{3,10},{4,13},{5,12},{6,15},{7,14},{8,1},{9,0},... | collective-permute-start | bytes 663560 | tf_op jit(solution)/shard_map/ppermute | solution.py:457
  86.4 19.3 %collective-permute-start.5 = (bf16[144,768]{1,0:T(8,128)(2,1)S(1)}, bf16[144,768]{1,0:T(8,128)(2,1)S(1)}, u32[]{:S(2)}, u32[]{:S(2)}) collective-permute-start(bf16[144,768]{1,0:T(8,128)(2,1)S(1)} %get-tuple-element.191), channel_id=1, source_target_pairs={{0,2},{1,3},{2,0},{3,1},{4,6},{5,7},{6,4},{7,5},{8,10},{9,11},{10,... | collective-permute-start | bytes 663560 | tf_op jit(solution)/shard_map/ppermute | solution.py:457
  88.6 17.0 %collective-permute-start.6 = (bf16[144,768]{1,0:T(8,128)(2,1)S(1)}, bf16[144,768]{1,0:T(8,128)(2,1)S(1)}, u32[]{:S(2)}, u32[]{:S(2)}) collective-permute-start(bf16[144,768]{1,0:T(8,128)(2,1)S(1)} %get-tuple-element.192), channel_id=1, source_target_pairs={{0,1},{1,0},{2,3},{3,2},{4,5},{5,4},{6,7},{7,6},{8,9},{9,8},{10,11... | collective-permute-start | bytes 663560 | tf_op jit(solution)/shard_map/ppermute | solution.py:457
  90.6 17.0 %collective-permute-start = (bf16[144,768]{1,0:T(8,128)(2,1)S(1)}, bf16[144,768]{1,0:T(8,128)(2,1)S(1)}, u32[]{:S(2)}, u32[]{:S(2)}) collective-permute-start(bf16[144,768]{1,0:T(8,128)(2,1)S(1)} %get-tuple-element.184), channel_id=1, source_target_pairs={{0,8},{1,9},{2,10},{3,11},{4,12},{5,13},{6,14},{7,15},{8,0},{9,1},... | collective-permute-start | bytes 663560 | tf_op jit(solution)/shard_map/ppermute | solution.py:457
  109.8 10.1 %all-to-all-start.4 = ((f32[16,1,512]{2,1,0:T(1,128)}), f32[16,1,512]{2,1,0:T(1,128)S(1)}, u32[]{:S(2)}, u32[]{:S(2)}) async-start(f32[16,1,512]{2,1,0:T(1,128)} %finish_rows.3), calls=%async_computation.4 | async-start | bytes 65536 | tf_op jit(solution)/shard_map/all_to_all | solution.py:444

commit v5 on v4

--- a/solution.py
+++ b/solution.py
@@ -12,7 +12,6 @@
 STEP = 16
 TILE = 256
 LANES = 128
-GROUP = 4
 MAX_PERMUTES = 16
 RANKS = 4096
 MIB = 1 << 20
@@ -82,12 +81,11 @@
 def assign_kernel(
     me_ref, counts_ref, rank_ref, owner_ref, slot_ref, bound_ref, total_ref, load_ref
 ):
-    far, near, clusters = counts_ref.shape
-    owners = far * near
+    owners, _, clusters = counts_ref.shape
     rows = rank_ref.shape[1]
     shift = owners.bit_length() - 1
     me = me_ref[0]
-    count = jnp.concatenate([counts_ref[s].astype(f32) for s in range(far)], axis=0)
+    count = jnp.concatenate([counts_ref[s].astype(f32) for s in range(owners)], axis=0)
     count16 = count.astype(bf16)
     square = (clusters, clusters)
     sub, lane = iota(square, 0), iota(square, 1)
@@ -150,8 +148,8 @@
 
 
 def assign(me, counts, rank):
-    far, near, clusters = counts.shape
-    owners, rows = far * near, rank.shape[1]
+    owners, _, clusters = counts.shape
+    rows = rank.shape[1]
     return pl.pallas_call(
         assign_kernel,
         out_shape=(
@@ -177,19 +175,27 @@
         key = jnp.where(owner_ref[...] == (me ^ partner), slot_ref[...], -1)
         takes.append(to_bf16(slot == key))
     picked = mm(jnp.concatenate(takes, axis=0), rows_ref[...]).astype(bf16)
-    for i, ref in enumerate(out_refs):
-        ref[...] = picked[i * slots : (i + 1) * slots]
-
-
-def pack(me, owner_row, slot_row, unit, partners, slots):
+    for i, r in enumerate(partners):
+        block = picked[i * slots : (i + 1) * slots]
+        if len(out_refs) == 1:
+            out_refs[0][(r ^ me) & (len(partners) - 1)] = block
+        else:
+            out_refs[i][...] = block
+
+
+def pack(me, owner_row, slot_row, unit, partners, slots, stacked):
     rows, width = unit.shape
     flops = 2 * len(partners) * slots * rows * width
+    if stacked:
+        out_shape = (jax.ShapeDtypeStruct((len(partners), slots, width), bf16),)
+    else:
+        out_shape = (jax.ShapeDtypeStruct((slots, width), bf16),) * len(partners)
     return pl.pallas_call(
         functools.partial(pack_kernel, slots, partners),
-        out_shape=(jax.ShapeDtypeStruct((slots, width), bf16),) * len(partners),
+        out_shape=out_shape,
         in_specs=[SMEM, VMEM, VMEM, VMEM],
-        out_specs=(VMEM,) * len(partners),
-        compiler_params=pltpu.CompilerParams(vmem_limit_bytes=28 * MIB),
+        out_specs=(VMEM,) * len(out_shape),
+        compiler_params=pltpu.CompilerParams(vmem_limit_bytes=40 * MIB),
         cost_estimate=pl.CostEstimate(
             flops=flops, bytes_accessed=2 * rows * width, transcendentals=0
         ),
@@ -284,9 +290,13 @@
     return mm(hot, new)
 
 
-def score_kernel(slots, partners, olds, bound_ref, *refs):
+def score_kernel(slots, partners, olds, me_ref, bound_ref, *refs):
     fresh = len(partners)
-    raw_refs, refs = refs[:fresh], refs[fresh:]
+    if olds:
+        raw_refs, refs = refs[:fresh], refs[fresh:]
+    else:
+        stack_ref, refs = refs[0], refs[1:]
+        raw_refs = [stack_ref.at[(r ^ me_ref[0]) & (fresh - 1)] for r in partners]
     old_refs = [refs[3 * i : 3 * i + 3] for i in range(olds)]
     refs = refs[3 * olds :]
     if olds:
@@ -311,10 +321,10 @@
     sums_out[...] = sums + sums_ref[...] if olds else sums
 
 
-def score(bound, blocks, partners, state):
-    slots, width = blocks[0].shape
+def score(me, bound, blocks, partners, state):
+    slots, width = blocks[0].shape[-2:]
     units, accs, cids, sums = state
-    rows = len(blocks) * slots
+    rows = len(partners) * slots
     padded = round_up(rows, LANES)
     old = [x for group in zip(units, accs, cids) for x in group]
     old_rows = sum(u.shape[0] for u in units)
@@ -326,11 +336,11 @@
         jax.ShapeDtypeStruct((8, width), f32),
         *acc_shapes,
     )
-    args = [bound, *blocks, *old] + ([sums] if units else [])
+    args = [me, bound, *blocks, *old] + ([sums] if units else [])
     out = pl.pallas_call(
         functools.partial(score_kernel, slots, partners, len(units)),
         out_shape=out_shape,
-        in_specs=[VMEM] * len(args),
+        in_specs=[SMEM] + [VMEM] * (len(args) - 1),
         out_specs=(VMEM,) * len(out_shape),
         scratch_shapes=[pltpu.VMEM((padded, width), bf16)],
         compiler_params=pltpu.CompilerParams(vmem_limit_bytes=36 * MIB),
@@ -444,28 +454,31 @@
     return lax.all_to_all(x, "owner", split_axis=0, concat_axis=0, tiled=True)
 
 
-def swap_together(blocks):
-    owners = len(blocks)
-    order = jnp.arange(owners, dtype=i32) ^ lax.axis_index("owner").astype(i32)
-    arrived = exchange(jnp.stack(blocks)[order])[order]
-    return [arrived[r] for r in range(owners)]
-
-
-def swap_apart(blocks):
-    pairs = [[(s, s ^ r) for s in range(len(blocks))] for r in range(len(blocks))]
-    return blocks[:1] + [
-        lax.ppermute(block, "owner", pair) for block, pair in zip(blocks[1:], pairs[1:])
+def exchange_near(x):
+    owners = lax.axis_size("owner")
+    half = owners // 2
+    halves = [list(range(half)), list(range(half, owners))]
+    return lax.all_to_all(
+        x, "owner", split_axis=0, concat_axis=0, axis_index_groups=halves, tiled=True
+    )
+
+
+def swap_far(blocks, partners):
+    owners = lax.axis_size("owner")
+    return [
+        lax.ppermute(block, "owner", [(s, s ^ r) for s in range(owners)])
+        for block, r in zip(blocks, partners)
     ]
 
 
-def gather_counts(counts, owners):
-    near, _, clusters = counts.shape
-    far = owners // near
-    close = [[f * near + n for n in range(near)] for f in range(far)]
-    apart = [[f * near + n for f in range(far)] for n in range(near)]
-    seen = lax.all_to_all(counts, "owner", 0, 0, axis_index_groups=close, tiled=True)
-    seen = jnp.broadcast_to(seen.reshape(1, near, clusters), (far, near, clusters))
-    return lax.all_to_all(seen, "owner", 0, 0, axis_index_groups=apart, tiled=True)
+def swap_far_together(blocks, partners):
+    owners = lax.axis_size("owner")
+    half = owners // 2
+    turn = (lax.axis_index("owner").astype(i32) ^ jnp.array(partners, i32)) & (half - 1)
+    by_owner = jnp.stack(blocks)[jnp.argsort(turn)]
+    across = lax.ppermute(by_owner, "owner", [(s, s ^ half) for s in range(owners)])
+    arrived = exchange_near(across)[turn]
+    return [arrived[i] for i in range(half)]
 
 
 def local(embeddings, cluster_ids):
@@ -478,43 +491,38 @@
     few = owners <= MAX_PERMUTES
     me = lax.axis_index("owner").astype(i32).reshape(1)
     ids_row = cluster_ids.reshape(1, rows)
-    peers = 1 << ((owners.bit_length() - 1) // 2)
-    counts, rank = count_rows(ids_row, peers, clusters)
+    counts, rank = count_rows(ids_row, owners, clusters)
     unit = unit_rows(embeddings)
-    counts = gather_counts(counts, owners)
-    owner_row, slot_row, bound, total, load = assign(me, counts, rank)
+    owner_row, slot_row, bound, total, load = assign(me, exchange(counts), rank)
 
     half = owners // 2
-    far = list(range(owners - 1, half - 1, -1))
-    near = list(range(half - 1, 0, -1))
-    sent = far[:2] + [r for pair in zip(far[2:-1], near) for r in pair]
-    sent = sent + near[len(far) - 3 :] + far[-1:]
-    seen = [0] + sent
-    sent = sent + [0]
-    packs = [tuple(sent[:2]), tuple(sent[2:4])]
-    packs += [tuple(sent[i : i + GROUP]) for i in range(4, owners, GROUP)]
-    share = owners // 16 if owners >= 16 else 1
-    groups, at = [], 0
-    for size in (5, 4, 4, 2):
-        groups.append(seen[at : at + size * share])
-        at += size * share
-    groups.append(seen[at:])
+    near = tuple(range(half))
+    far = tuple(range(owners - 1, half - 1, -1))
+    share = half // 8
+    cuts = [0, 3 * share, 6 * share, 7 * share, 8 * share]
+    groups = [far[a:b] for a, b in zip(cuts, cuts[1:])]
 
     def compare(slots, apart):
-        blocks = [None] * owners
-        slot_in = slot_row
-        for partners in packs:
-            packed = pack(me, owner_row, slot_in, unit, partners, slots)
-            slot_in, *packed = lax.optimization_barrier((slot_in, *packed))
-            for r, block in zip(partners, packed):
-                blocks[r] = block
-        arrived = swap_apart(blocks) if apart else swap_together(blocks)
-        state = ([], [], [], None)
+        def packed(slot_in, partners, stacked):
+            out = pack(me, owner_row, slot_in, unit, partners, slots, stacked)
+            slot_in, *out = lax.optimization_barrier((slot_in, *out))
+            return slot_in, out
+
+        slot_in, blocks = slot_row, []
+        for first in range(0, half, 2):
+            slot_in, pair = packed(slot_in, far[first : first + 2], False)
+            blocks += pair
+            if first == 2:
+                slot_in, stack = packed(slot_in, near, True)
+        close = exchange_near(stack[0])
+        swap = swap_far if apart else swap_far_together
+        arrived = dict(zip(far, swap(blocks, far)))
+        state = score(me, bound, [close], near, ([], [], [], None))
         for group in groups[:-1]:
-            state = score(bound, [arrived[r] for r in group], group, state)
+            state = score(me, bound, [arrived[r] for r in group], group, state)
         last = groups[-1]
         answers = finish(
-            me, bound, total, [arrived[r] for r in last], last, groups[:-1], state
+            me, bound, total, [arrived[r] for r in last], last, [near] + groups[:-1], state
         )
         return restore(owner_row, slot_row, exchange(answers), slots)
 

time: 121 us -> 134 us (1.11)
  waiting for transfers between devices: 30.7 us -> 58.6 us
  starting transfers between devices: 55.3 us -> 41 us
  Pallas kernels: 21.9 us -> 30.9 us
  blocking collectives: 7.79 us -> 0 us
    ppermute x15 -> x8, waiting for transfers between devices: 21.8 us -> 48.9 us  [swap_far(): lax.ppermute(block, 'owner', [(s, s ^ r) for s in range(owners)])]
    ppermute x15 -> x8, starting transfers between devices: 47 us -> 26.2 us  [swap_far(): lax.ppermute(block, 'owner', [(s, s ^ r) for s in range(owners)])]
    all_to_all x1 -> x0, blocking collectives: 7.79 us -> none  [gather_counts(): lax.all_to_all(counts, 'owner', 0, 0, axis_index_groups=close, tiled=True)]
    all_to_all x1 -> x2, starting transfers between devices: 3.48 us -> 10.9 us  [exchange(): return lax.all_to_all(x, 'owner', split_axis=0, concat_axis=0, tiled=True)]
    pallas_call x5, Pallas kernels: 8.19 us -> 14.8 us  [pack(): pl.pallas_call(functools.partial(pack_kernel, slots, partners), out_shape...]
    all_to_all x1 -> x2, waiting for transfers between devices: 6.56 us -> 9.69 us  [exchange(): return lax.all_to_all(x, 'owner', split_axis=0, concat_axis=0, tiled=True)]
    all_to_all x1, waiting for transfers between devices: 2.39 us -> 0.01 us  [exchange_near(): lax.all_to_all(x, 'owner', split_axis=0, concat_axis=0, axis_index_groups...]
    pallas_call x4, Pallas kernels: 8.03 us -> 9.66 us  [score(): pl.pallas_call(functools.partial(score_kernel, slots, partners, len(units...]
  transfers between devices with their start and end apart: 17 -> 11, of which waited for: 6 -> 8; matrix products, arithmetic and copies ran while one was open for 0% -> 0% of each run, Pallas kernels for 13% -> 12%
where the time goes in v5:
time: 134 us
  waiting for transfers between devices  58.6 us (44%)
  starting transfers between devices  41 us (31%)
  Pallas kernels  30.9 us (23%)
  local copies, waits for them, and re-layouts  2.64 us (2%)
    ppermute x8, waiting for transfers between devices, swap_far(): lax.ppermute(block, 'owner', [(s, s ^ r) for s in range(owners)])  48.9 us
    ppermute x8, starting transfers between devices, swap_far(): lax.ppermute(block, 'owner', [(s, s ^ r) for s in range(owners)])  26.2 us
    pallas_call x5, Pallas kernels, pack(): pl.pallas_call(functools.partial(pack_kernel, slots, partners), out_shape...  14.8 us
    all_to_all x2, starting transfers between devices, exchange(): return lax.all_to_all(x, 'owner', split_axis=0, concat_axis=0, tiled=True)  10.9 us
    all_to_all x2, waiting for transfers between devices, exchange(): return lax.all_to_all(x, 'owner', split_axis=0, concat_axis=0, tiled=True)  9.69 us
    pallas_call x4, Pallas kernels, score(): pl.pallas_call(functools.partial(score_kernel, slots, partners, len(units...  9.66 us
    all_to_all x1, starting transfers between devices, exchange_near(): lax.all_to_all(x, 'owner', split_axis=0, concat_axis=0, axis_index_groups...  3.9 us
  transfers between devices with their start and end apart: 11, of which 8 were waited for; matrix products, arithmetic and copies ran while one was open for 0% of the time, Pallas kernels for 12%

profile of v5, /device:TPU:0, one launch (start us, length us, event | category | flops | bytes accessed | tf_op | source)
XLA Modules:
  0.0 134.0 jit_solution(13143790223784377998)
XLA Ops:
  0.6 0.7 copy-done.17
  1.3 1.0 count_rows.1
  2.3 7.4 %all-to-all-start.3 = ((s32[16,1,64]{2,1,0:T(1,128)}), s32[16,1,64]{2,1,0:T(1,128)S(1)}, u32[]{:S(2)}, u32[]{:S(2)}) async-start(s32[16,1,64]{2,1,0:T(1,128)} %get-tuple-element.131), calls=%async_computation.3 | async-start | bytes 16384 | tf_op jit(solution)/shard_map/all_to_all | solution.py:454
  9.7 1.9 %copy-done.2 = bf16[2048,768]{1,0:T(8,128)(2,1)S(1)} copy-done((bf16[2048,768]{1,0:T(8,128)(2,1)S(1)}, bf16[2048,768]{1,0:T(8,128)(2,1)}, u32[]{:S(2)}) %copy-start.2) | copy-done | bytes 3145752
  11.6 1.3 unit_rows.1.rows_ref
  12.9 3.1 %all-to-all-done.3.counts_ref = s32[16,1,64]{2,1,0:T(1,128)S(1)} async-done(((s32[16,1,64]{2,1,0:T(1,128)}), s32[16,1,64]{2,1,0:T(1,128)S(1)}, u32[]{:S(2)}, u32[]{:S(2)}) %all-to-all-start.3) | async-done | bytes 4128 | tf_op jit(solution)/shard_map/all_to_all | solution.py:454
  16.1 0.6 assign.1
  16.7 1.8 %pack_rows.15 = (bf16[144,768]{1,0:T(8,128)(2,1)}, bf16[144,768]{1,0:T(8,128)(2,1)}) custom-call(s32[1]{0:T(128)} %bitcast.16.me_ref, s32[1,2048]{1,0:T(1,128)S(1)} %get-tuple-element.134.owner_ref, s32[1,2048]{1,0:T(1,128)S(1)} %get-tuple-element.147.slot_ref, bf16[2048,768]{1,0:T(8,128)(2,1)S(1)} %unit_rows.1.rows_ref), custom_call_target="tpu_custom_call" | custom-call | flops 905969664 | bytes 3145728 | tf_op jit(solution)/shard_map/pack_rows/pallas_call | solution.py:193
  18.5 3.1 %pack_rows.16 = (bf16[144,768]{1,0:T(8,128)(2,1)S(1)}, bf16[144,768]{1,0:T(8,128)(2,1)S(1)}) custom-call(s32[1]{0:T(128)} %bitcast.16.me_ref, s32[1,2048]{1,0:T(1,128)S(1)} %get-tuple-element.134.owner_ref, s32[1,2048]{1,0:T(1,128)S(1)} %get-tuple-element.147.slot_ref, bf16[2048,768]{1,0:T(8,128)(2,1)} %copy-done.20), custom_call_target="tpu_custom_call" | custom-call | flops 905969664 | bytes 3145728 | tf_op jit(solution)/shard_map/pack_rows/pallas_call | solution.py:193
  21.7 5.1 %pack_rows.17 = bf16[8,144,768]{2,1,0:T(8,128)(2,1)} custom-call(s32[1]{0:T(128)} %bitcast.16.me_ref, s32[1,2048]{1,0:T(1,128)S(1)} %get-tuple-element.134.owner_ref, s32[1,2048]{1,0:T(1,128)S(1)} %get-tuple-element.147.slot_ref, bf16[2048,768]{1,0:T(8,128)(2,1)S(1)} %copy-done.21), custom_call_target="tpu_custom_call" | custom-call | flops 3623878656 | bytes 3145728 | tf_op jit(solution)/shard_map/pack_rows/pallas_call | solution.py:193
  26.8 3.9 %all-to-all-start.4 = ((bf16[8,144,768]{2,1,0:T(8,128)(2,1)}), bf16[8,144,768]{2,1,0:T(8,128)(2,1)S(1)}, u32[]{:S(2)}, u32[]{:S(2)}) async-start(bf16[8,144,768]{2,1,0:T(8,128)(2,1)} %pack_rows.17), calls=%async_computation.4 | async-start | bytes 3538944 | tf_op jit(solution)/shard_map/all_to_all | solution.py:461
  30.8 2.4 %collective-permute-start.6 = (bf16[144,768]{1,0:T(8,128)(2,1)}, bf16[144,768]{1,0:T(8,128)(2,1)S(1)}, u32[]{:S(2)}, u32[]{:S(2)}) collective-permute-start(bf16[144,768]{1,0:T(8,128)(2,1)} %get-tuple-element.157), channel_id=1, source_target_pairs={{0,15},{1,14},{2,13},{3,12},{4,11},{5,10},{6,9},{7,8},{8,7},{9,6},... | collective-permute-start | bytes 663560 | tf_op jit(solution)/shard_map/ppermute | solution.py:469
  33.2 2.2 %collective-permute-start.7 = (bf16[144,768]{1,0:T(8,128)(2,1)}, bf16[144,768]{1,0:T(8,128)(2,1)}, u32[]{:S(2)}, u32[]{:S(2)}) collective-permute-start(bf16[144,768]{1,0:T(8,128)(2,1)} %get-tuple-element.158), channel_id=1, source_target_pairs={{0,14},{1,15},{2,12},{3,13},{4,10},{5,11},{6,8},{7,9},{8,6},{9,7},... | collective-permute-start | bytes 663560 | tf_op jit(solution)/shard_map/ppermute | solution.py:469
  35.4 1.7 %collective-permute-start.3 = (bf16[144,768]{1,0:T(8,128)(2,1)S(1)}, bf16[144,768]{1,0:T(8,128)(2,1)S(1)}, u32[]{:S(2)}, u32[]{:S(2)}) collective-permute-start(bf16[144,768]{1,0:T(8,128)(2,1)S(1)} %get-tuple-element.154), channel_id=1, source_target_pairs={{0,12},{1,13},{2,14},{3,15},{4,8},{5,9},{6,10},{7,11},{8,4},{9,5},... | collective-permute-start | bytes 663560 | tf_op jit(solution)/shard_map/ppermute | solution.py:469
  37.0 1.5 %collective-permute-start.8 = (bf16[144,768]{1,0:T(8,128)(2,1)S(1)}, bf16[144,768]{1,0:T(8,128)(2,1)}, u32[]{:S(2)}, u32[]{:S(2)}) collective-permute-start(bf16[144,768]{1,0:T(8,128)(2,1)S(1)} %get-tuple-element.159), channel_id=1, source_target_pairs={{0,13},{1,12},{2,15},{3,14},{4,9},{5,8},{6,11},{7,10},{8,5},{9,4},... | collective-permute-start | bytes 663560 | tf_op jit(solution)/shard_map/ppermute | solution.py:469
  38.5 3.6 %pack_rows.18 = (bf16[144,768]{1,0:T(8,128)(2,1)}, bf16[144,768]{1,0:T(8,128)(2,1)S(1)}) custom-call(s32[1]{0:T(128)} %bitcast.16.me_ref, s32[1,2048]{1,0:T(1,128)S(1)} %copy-done.28, s32[1,2048]{1,0:T(1,128)S(1)} %copy-done.35, bf16[2048,768]{1,0:T(8,128)(2,1)} %copy-done.20), custom_call_target="tpu_custom_call" | custom-call | flops 905969664 | bytes 3145728 | tf_op jit(solution)/shard_map/pack_rows/pallas_call | solution.py:193
  42.2 1.1 pack_rows.19
  43.3 20.1 %collective-permute-done.6.refs_0_ = bf16[144,768]{1,0:T(8,128)(2,1)S(1)} collective-permute-done((bf16[144,768]{1,0:T(8,128)(2,1)}, bf16[144,768]{1,0:T(8,128)(2,1)S(1)}, u32[]{:S(2)}, u32[]{:S(2)}) %collective-permute-start.6) | collective-permute-done | bytes 221216 | tf_op jit(solution)/shard_map/ppermute | solution.py:469
  63.4 2.9 %score_rows.12 = (bf16[1152,768]{1,0:T(8,128)(2,1)S(1)}, f32[1152,128]{1,0:T(8,128)S(1)}, f32[1152,128]{1,0:T(8,128)S(1)}, f32[8,768]{1,0:T(8,128)S(1)}) custom-call(s32[1]{0:T(128)} %bitcast.16.me_ref, f32[16,128]{1,0:T(8,128)S(1)} %get-tuple-element.136.bound_ref, bf16[8,144,768]{2,1,0:T(8,128)(2,1)S(1)} %all-to-all-done.4.refs_0_), custom_call_target="tpu_custom_call" | custom-call | flops 2038431744 | bytes 1769472 | tf_op jit(solution)/shard_map/score_rows/pallas_call | solution.py:340
  66.3 2.8 %collective-permute-done.7.refs_1_ = bf16[144,768]{1,0:T(8,128)(2,1)} collective-permute-done((bf16[144,768]{1,0:T(8,128)(2,1)}, bf16[144,768]{1,0:T(8,128)(2,1)}, u32[]{:S(2)}, u32[]{:S(2)}) %collective-permute-start.7) | collective-permute-done | bytes 221216 | tf_op jit(solution)/shard_map/ppermute | solution.py:469
  69.3 7.5 %collective-permute-done.8.refs_2_ = bf16[144,768]{1,0:T(8,128)(2,1)} collective-permute-done((bf16[144,768]{1,0:T(8,128)(2,1)S(1)}, bf16[144,768]{1,0:T(8,128)(2,1)}, u32[]{:S(2)}, u32[]{:S(2)}) %collective-permute-start.8) | collective-permute-done | bytes 221216 | tf_op jit(solution)/shard_map/ppermute | solution.py:469
  76.8 18.4 %collective-permute-start.2 = (bf16[144,768]{1,0:T(8,128)(2,1)S(1)}, bf16[144,768]{1,0:T(8,128)(2,1)S(1)}, u32[]{:S(2)}, u32[]{:S(2)}) collective-permute-start(bf16[144,768]{1,0:T(8,128)(2,1)S(1)} %get-tuple-element.153), channel_id=1, source_target_pairs={{0,9},{1,8},{2,11},{3,10},{4,13},{5,12},{6,15},{7,14},{8,1},{9,0},... | collective-permute-start | bytes 663560 | tf_op jit(solution)/shard_map/ppermute | solution.py:469
  95.1 2.7 %score_rows.13 = (bf16[432,768]{1,0:T(8,128)(2,1)S(1)}, f32[432,128]{1,0:T(8,128)S(1)}, f32[432,128]{1,0:T(8,128)S(1)}, f32[8,768]{1,0:T(8,128)S(1)}, f32[1152,128]{1,0:T(8,128)S(1)}) custom-call(s32[1]{0:T(128)} %bitcast.16.me_ref, f32[16,128]{1,0:T(8,128)S(1)} %get-tuple-element.136.bound_ref, bf16[144,768]{1,0:T(8,128)(2,1)S(1)} %collective-permute-done.6.refs_0_, ...), custom_call_target="tpu_custom_call" | custom-call | flops 1245708288 | bytes 2433024 | tf_op jit(solution)/shard_map/score_rows/pallas_call | solution.py:340
  97.8 7.0 %collective-permute-done.4.refs_1_ = bf16[144,768]{1,0:T(8,128)(2,1)S(1)} collective-permute-done((bf16[144,768]{1,0:T(8,128)(2,1)}, bf16[144,768]{1,0:T(8,128)(2,1)S(1)}, u32[]{:S(2)}, u32[]{:S(2)}) %collective-permute-start.4) | collective-permute-done | bytes 221216 | tf_op jit(solution)/shard_map/ppermute | solution.py:469
  104.8 5.5 %collective-permute-done.5.refs_2_ = bf16[144,768]{1,0:T(8,128)(2,1)} collective-permute-done((bf16[144,768]{1,0:T(8,128)(2,1)S(1)}, bf16[144,768]{1,0:T(8,128)(2,1)}, u32[]{:S(2)}, u32[]{:S(2)}) %collective-permute-start.5) | collective-permute-done | bytes 221216 | tf_op jit(solution)/shard_map/ppermute | solution.py:469
  110.3 2.9 %score_rows.14 = (bf16[432,768]{1,0:T(8,128)(2,1)S(1)}, f32[432,128]{1,0:T(8,128)S(1)}, f32[432,128]{1,0:T(8,128)S(1)}, f32[8,768]{1,0:T(8,128)S(1)}, f32[1152,128]{1,0:T(8,128)S(1)}, /*index=5*/f32[432,128]{1,0:T(8,128)S(1)}) custom-call(s32[1]{0:T(128)} %bitcast.16.me_ref, f32[16,128]{1,0:T(8,128)S(1)} %get-tuple-element.136.bound_ref, ...), custom_call_target="tpu_custom_call" | custom-call | flops 1585446912 | bytes 3096576 | tf_op jit(solution)/shard_map/score_rows/pallas_call | solution.py:340
  113.2 6.0 %collective-permute-done.2.refs_0_ = bf16[144,768]{1,0:T(8,128)(2,1)S(1)} collective-permute-done((bf16[144,768]{1,0:T(8,128)(2,1)S(1)}, bf16[144,768]{1,0:T(8,128)(2,1)S(1)}, u32[]{:S(2)}, u32[]{:S(2)}) %collective-permute-start.2) | collective-permute-done | bytes 221216 | tf_op jit(solution)/shard_map/ppermute | solution.py:469
  119.2 1.2 score_rows.15
  120.4 2.3 %finish_rows.3 = f32[16,1,512]{2,1,0:T(1,128)} custom-call(s32[1]{0:T(128)} %bitcast.16.me_ref, f32[16,128]{1,0:T(8,128)S(1)} %get-tuple-element.136.bound_ref, f32[8,128]{1,0:T(8,128)S(1)} %get-tuple-element.137.total_ref, bf16[144,768]{1,0:T(8,128)(2,1)S(1)} %collective-permute-done.1.refs_0_, bf16[1152,768]{1,0:T(8,128)(2,1)S(1)} %get-tuple-element.152.refs_3_.refs_1_, ...), custom_call_target="tpu_custom_call" | custom-call | flops 905969664 | bytes 3538944 | tf_op jit(solution)/shard_map/finish_rows/pallas_call | solution.py:403
  122.7 3.5 %all-to-all-start.5 = ((f32[16,1,512]{2,1,0:T(1,128)}), f32[16,1,512]{2,1,0:T(1,128)S(1)}, u32[]{:S(2)}, u32[]{:S(2)}) async-start(f32[16,1,512]{2,1,0:T(1,128)} %finish_rows.3), calls=%async_computation.5 | async-start | bytes 65536 | tf_op jit(solution)/shard_map/all_to_all | solution.py:454
  126.2 6.6 %all-to-all-done.5.back_ref = f32[16,1,512]{2,1,0:T(1,128)S(1)} async-done(((f32[16,1,512]{2,1,0:T(1,128)}), f32[16,1,512]{2,1,0:T(1,128)S(1)}, u32[]{:S(2)}, u32[]{:S(2)}) %all-to-all-start.5) | async-done | bytes 32800 | tf_op jit(solution)/shard_map/all_to_all | solution.py:454
  132.8 1.2 restore_rows.3
  (33 shorter events, 0.2 us)
Async XLA Ops:
  0.6 0.7 copy-start.17
  2.3 13.7 %all-to-all-start.3 = ((s32[16,1,64]{2,1,0:T(1,128)}), s32[16,1,64]{2,1,0:T(1,128)S(1)}, u32[]{:S(2)}, u32[]{:S(2)}) async-start(s32[16,1,64]{2,1,0:T(1,128)} %get-tuple-element.131), calls=%async_computation.3 | async-start | bytes 16384 | tf_op jit(solution)/shard_map/all_to_all | solution.py:454
  9.7 1.9 %copy-start.2 = (bf16[2048,768]{1,0:T(8,128)(2,1)S(1)}, bf16[2048,768]{1,0:T(8,128)(2,1)}, u32[]{:S(2)}) copy-start(bf16[2048,768]{1,0:T(8,128)(2,1)} %rows_ref.1) | copy-start | bytes 9437188
  12.9 5.6 %copy-start.20 = (bf16[2048,768]{1,0:T(8,128)(2,1)}, bf16[2048,768]{1,0:T(8,128)(2,1)S(1)}, u32[]{:S(2)}) copy-start(bf16[2048,768]{1,0:T(8,128)(2,1)S(1)} %unit_rows.1.rows_ref) | copy-start | bytes 9437188
  16.7 5.0 %copy-start.27 = (s32[1,2048]{1,0:T(1,128)}, s32[1,2048]{1,0:T(1,128)S(1)}, u32[]{:S(2)}) copy-start(s32[1,2048]{1,0:T(1,128)S(1)} %get-tuple-element.134.owner_ref) | copy-start | bytes 24580
  16.7 5.0 %copy-start.34 = (s32[1,2048]{1,0:T(1,128)}, s32[1,2048]{1,0:T(1,128)S(1)}, u32[]{:S(2)}) copy-start(s32[1,2048]{1,0:T(1,128)S(1)} %get-tuple-element.147.slot_ref) | copy-start | bytes 24580
  18.5 3.2 %copy-start.21 = (bf16[2048,768]{1,0:T(8,128)(2,1)S(1)}, bf16[2048,768]{1,0:T(8,128)(2,1)}, u32[]{:S(2)}) copy-start(bf16[2048,768]{1,0:T(8,128)(2,1)} %copy-done.20) | copy-start | bytes 9437188
  26.8 11.7 %copy-start.28 = (s32[1,2048]{1,0:T(1,128)S(1)}, s32[1,2048]{1,0:T(1,128)}, u32[]{:S(2)}) copy-start(s32[1,2048]{1,0:T(1,128)} %copy-done.27) | copy-start | bytes 24580
  26.8 11.7 %copy-start.35 = (s32[1,2048]{1,0:T(1,128)S(1)}, s32[1,2048]{1,0:T(1,128)}, u32[]{:S(2)}) copy-start(s32[1,2048]{1,0:T(1,128)} %copy-done.34) | copy-start | bytes 24580
  26.8 36.6 %all-to-all-start.4 = ((bf16[8,144,768]{2,1,0:T(8,128)(2,1)}), bf16[8,144,768]{2,1,0:T(8,128)(2,1)S(1)}, u32[]{:S(2)}, u32[]{:S(2)}) async-start(bf16[8,144,768]{2,1,0:T(8,128)(2,1)} %pack_rows.17), calls=%async_computation.4 | async-start | bytes 3538944 | tf_op jit(solution)/shard_map/all_to_all | solution.py:461
  30.7 11.4 %copy-start.22 = (bf16[2048,768]{1,0:T(8,128)(2,1)S(1)}, bf16[2048,768]{1,0:T(8,128)(2,1)}, u32[]{:S(2)}) copy-start(bf16[2048,768]{1,0:T(8,128)(2,1)} %copy-done.20) | copy-start | bytes 9437188
  30.7 11.4 %copy-start.29 = (s32[1,2048]{1,0:T(1,128)S(1)}, s32[1,2048]{1,0:T(1,128)}, u32[]{:S(2)}) copy-start(s32[1,2048]{1,0:T(1,128)} %copy-done.27) | copy-start | bytes 24580
  30.8 11.4 %copy-start.36 = (s32[1,2048]{1,0:T(1,128)S(1)}, s32[1,2048]{1,0:T(1,128)}, u32[]{:S(2)}) copy-start(s32[1,2048]{1,0:T(1,128)} %copy-done.34) | copy-start | bytes 24580
  30.8 32.6 %collective-permute-start.6 = (bf16[144,768]{1,0:T(8,128)(2,1)}, bf16[144,768]{1,0:T(8,128)(2,1)S(1)}, u32[]{:S(2)}, u32[]{:S(2)}) collective-permute-start(bf16[144,768]{1,0:T(8,128)(2,1)} %get-tuple-element.157), channel_id=1, source_target_pairs={{0,15},{1,14},{2,13},{3,12},{4,11},{5,10},{6,9},{7,8},{8,7},{9,6},... | collective-permute-start | bytes 663560 | tf_op jit(solution)/shard_map/ppermute | solution.py:469
  33.2 36.0 %collective-permute-start.7 = (bf16[144,768]{1,0:T(8,128)(2,1)}, bf16[144,768]{1,0:T(8,128)(2,1)}, u32[]{:S(2)}, u32[]{:S(2)}) collective-permute-start(bf16[144,768]{1,0:T(8,128)(2,1)} %get-tuple-element.158), channel_id=1, source_target_pairs={{0,14},{1,15},{2,12},{3,13},{4,10},{5,11},{6,8},{7,9},{8,6},{9,7},... | collective-permute-start | bytes 663560 | tf_op jit(solution)/shard_map/ppermute | solution.py:469
  35.4 62.4 %collective-permute-start.3 = (bf16[144,768]{1,0:T(8,128)(2,1)S(1)}, bf16[144,768]{1,0:T(8,128)(2,1)S(1)}, u32[]{:S(2)}, u32[]{:S(2)}) collective-permute-start(bf16[144,768]{1,0:T(8,128)(2,1)S(1)} %get-tuple-element.154), channel_id=1, source_target_pairs={{0,12},{1,13},{2,14},{3,15},{4,8},{5,9},{6,10},{7,11},{8,4},{9,5},... | collective-permute-start | bytes 663560 | tf_op jit(solution)/shard_map/ppermute | solution.py:469
  37.0 39.8 %collective-permute-start.8 = (bf16[144,768]{1,0:T(8,128)(2,1)S(1)}, bf16[144,768]{1,0:T(8,128)(2,1)}, u32[]{:S(2)}, u32[]{:S(2)}) collective-permute-start(bf16[144,768]{1,0:T(8,128)(2,1)S(1)} %get-tuple-element.159), channel_id=1, source_target_pairs={{0,13},{1,12},{2,15},{3,14},{4,9},{5,8},{6,11},{7,10},{8,5},{9,4},... | collective-permute-start | bytes 663560 | tf_op jit(solution)/shard_map/ppermute | solution.py:469
  42.2 62.7 %collective-permute-start.4 = (bf16[144,768]{1,0:T(8,128)(2,1)}, bf16[144,768]{1,0:T(8,128)(2,1)S(1)}, u32[]{:S(2)}, u32[]{:S(2)}) collective-permute-start(bf16[144,768]{1,0:T(8,128)(2,1)} %get-tuple-element.155), channel_id=1, source_target_pairs={{0,11},{1,10},{2,9},{3,8},{4,15},{5,14},{6,13},{7,12},{8,3},{9,2},... | collective-permute-start | bytes 663560 | tf_op jit(solution)/shard_map/ppermute | solution.py:469
  63.4 46.9 %collective-permute-start.5 = (bf16[144,768]{1,0:T(8,128)(2,1)S(1)}, bf16[144,768]{1,0:T(8,128)(2,1)}, u32[]{:S(2)}, u32[]{:S(2)}) collective-permute-start(bf16[144,768]{1,0:T(8,128)(2,1)S(1)} %get-tuple-element.156), channel_id=1, source_target_pairs={{0,10},{1,11},{2,8},{3,9},{4,14},{5,15},{6,12},{7,13},{8,2},{9,3},... | collective-permute-start | bytes 663560 | tf_op jit(solution)/shard_map/ppermute | solution.py:469
  69.2 51.2 %collective-permute-start.1 = (bf16[144,768]{1,0:T(8,128)(2,1)S(1)}, bf16[144,768]{1,0:T(8,128)(2,1)S(1)}, u32[]{:S(2)}, u32[]{:S(2)}) collective-permute-start(bf16[144,768]{1,0:T(8,128)(2,1)S(1)} %get-tuple-element.150), channel_id=1, source_target_pairs={{0,8},{1,9},{2,10},{3,11},{4,12},{5,13},{6,14},{7,15},{8,0},{9,1},... | collective-permute-start | bytes 663560 | tf_op jit(solution)/shard_map/ppermute | solution.py:469
  76.8 42.4 %collective-permute-start.2 = (bf16[144,768]{1,0:T(8,128)(2,1)S(1)}, bf16[144,768]{1,0:T(8,128)(2,1)S(1)}, u32[]{:S(2)}, u32[]{:S(2)}) collective-permute-start(bf16[144,768]{1,0:T(8,128)(2,1)S(1)} %get-tuple-element.153), channel_id=1, source_target_pairs={{0,9},{1,8},{2,11},{3,10},{4,13},{5,12},{6,15},{7,14},{8,1},{9,0},... | collective-permute-start | bytes 663560 | tf_op jit(solution)/shard_map/ppermute | solution.py:469
  120.4 12.4 %copy-start.30 = (s32[1,2048]{1,0:T(1,128)S(1)}, s32[1,2048]{1,0:T(1,128)}, u32[]{:S(2)}) copy-start(s32[1,2048]{1,0:T(1,128)} %copy-done.27) | copy-start | bytes 24580
  120.4 12.4 %copy-start.37 = (s32[1,2048]{1,0:T(1,128)S(1)}, s32[1,2048]{1,0:T(1,128)}, u32[]{:S(2)}) copy-start(s32[1,2048]{1,0:T(1,128)} %copy-done.34) | copy-start | bytes 24580
  120.4 13.6 %copy-start.23 = (bf16[2048,768]{1,0:T(8,128)(2,1)S(1)}, bf16[2048,768]{1,0:T(8,128)(2,1)}, u32[]{:S(2)}) copy-start(bf16[2048,768]{1,0:T(8,128)(2,1)} %copy-done.20) | copy-start | bytes 9437188
  122.7 10.1 %all-to-all-start.5 = ((f32[16,1,512]{2,1,0:T(1,128)}), f32[16,1,512]{2,1,0:T(1,128)S(1)}, u32[]{:S(2)}, u32[]{:S(2)}) async-start(f32[16,1,512]{2,1,0:T(1,128)} %finish_rows.3), calls=%async_computation.5 | async-start | bytes 65536 | tf_op jit(solution)/shard_map/all_to_all | solution.py:454

commit v6 on v4

--- a/solution.py
+++ b/solution.py
@@ -82,12 +82,11 @@
 def assign_kernel(
     me_ref, counts_ref, rank_ref, owner_ref, slot_ref, bound_ref, total_ref, load_ref
 ):
-    far, near, clusters = counts_ref.shape
-    owners = far * near
+    owners, _, clusters = counts_ref.shape
     rows = rank_ref.shape[1]
     shift = owners.bit_length() - 1
     me = me_ref[0]
-    count = jnp.concatenate([counts_ref[s].astype(f32) for s in range(far)], axis=0)
+    count = jnp.concatenate([counts_ref[s].astype(f32) for s in range(owners)], axis=0)
     count16 = count.astype(bf16)
     square = (clusters, clusters)
     sub, lane = iota(square, 0), iota(square, 1)
@@ -150,8 +149,8 @@
 
 
 def assign(me, counts, rank):
-    far, near, clusters = counts.shape
-    owners, rows = far * near, rank.shape[1]
+    owners, _, clusters = counts.shape
+    rows = rank.shape[1]
     return pl.pallas_call(
         assign_kernel,
         out_shape=(
@@ -458,16 +457,6 @@
     ]
 
 
-def gather_counts(counts, owners):
-    near, _, clusters = counts.shape
-    far = owners // near
-    close = [[f * near + n for n in range(near)] for f in range(far)]
-    apart = [[f * near + n for f in range(far)] for n in range(near)]
-    seen = lax.all_to_all(counts, "owner", 0, 0, axis_index_groups=close, tiled=True)
-    seen = jnp.broadcast_to(seen.reshape(1, near, clusters), (far, near, clusters))
-    return lax.all_to_all(seen, "owner", 0, 0, axis_index_groups=apart, tiled=True)
-
-
 def local(embeddings, cluster_ids):
     rows = embeddings.shape[0]
     owners = lax.axis_size("owner")
@@ -478,24 +467,18 @@
     few = owners <= MAX_PERMUTES
     me = lax.axis_index("owner").astype(i32).reshape(1)
     ids_row = cluster_ids.reshape(1, rows)
-    peers = 1 << ((owners.bit_length() - 1) // 2)
-    counts, rank = count_rows(ids_row, peers, clusters)
+    counts, rank = count_rows(ids_row, owners, clusters)
     unit = unit_rows(embeddings)
-    counts = gather_counts(counts, owners)
-    owner_row, slot_row, bound, total, load = assign(me, counts, rank)
-
-    half = owners // 2
-    far = list(range(owners - 1, half - 1, -1))
-    near = list(range(half - 1, 0, -1))
-    sent = far[:2] + [r for pair in zip(far[2:-1], near) for r in pair]
-    sent = sent + near[len(far) - 3 :] + far[-1:]
+    owner_row, slot_row, bound, total, load = assign(me, exchange(counts), rank)
+
+    sent = list(range(owners - 1, 0, -1))
     seen = [0] + sent
     sent = sent + [0]
     packs = [tuple(sent[:2]), tuple(sent[2:4])]
     packs += [tuple(sent[i : i + GROUP]) for i in range(4, owners, GROUP)]
     share = owners // 16 if owners >= 16 else 1
     groups, at = [], 0
-    for size in (5, 4, 4, 2):
+    for size in (5, 4, 4):
         groups.append(seen[at : at + size * share])
         at += size * share
     groups.append(seen[at:])

time: 121 us -> 135 us (1.12)
  starting transfers between devices: 55.3 us -> 68.1 us
  waiting for transfers between devices: 30.7 us -> 41.2 us
  blocking collectives: 7.79 us -> 0 us
    ppermute x15, starting transfers between devices: 47 us -> 57.3 us  [swap_apart(): lax.ppermute(block, 'owner', pair)]
    ppermute x15, waiting for transfers between devices: 21.8 us -> 31.5 us  [swap_apart(): lax.ppermute(block, 'owner', pair)]
    all_to_all x1 -> x0, blocking collectives: 7.79 us -> none  [gather_counts(): lax.all_to_all(counts, 'owner', 0, 0, axis_index_groups=close, tiled=True)]
    all_to_all x1 -> x2, starting transfers between devices: 3.48 us -> 10.9 us  [exchange(): return lax.all_to_all(x, 'owner', split_axis=0, concat_axis=0, tiled=True)]
    all_to_all x1 -> x0, starting transfers between devices: 4.87 us -> none  [gather_counts(): lax.all_to_all(seen, 'owner', 0, 0, axis_index_groups=apart, tiled=True)]
    all_to_all x1 -> x2, waiting for transfers between devices: 6.56 us -> 9.7 us  [exchange(): return lax.all_to_all(x, 'owner', split_axis=0, concat_axis=0, tiled=True)]
    all_to_all x1 -> x0, waiting for transfers between devices: 2.39 us -> none  [gather_counts(): lax.all_to_all(seen, 'owner', 0, 0, axis_index_groups=apart, tiled=True)]
    pallas_call x4 -> x3, Pallas kernels: 8.03 us -> 6.04 us  [score(): pl.pallas_call(functools.partial(score_kernel, slots, partners, len(units...]
  transfers between devices with their start and end apart: 17 -> 17, of which waited for: 6 -> 11; matrix products, arithmetic and copies ran while one was open for 0% -> 0% of each run, Pallas kernels for 13% -> 10%
where the time goes in v6:
time: 135 us; the launch traced here: 134 us
  starting transfers between devices  68.1 us (50%)
  waiting for transfers between devices  41.2 us (31%)
  Pallas kernels  21.5 us (16%)
  local copies, waits for them, and re-layouts  2.58 us (2%)
    ppermute x15, starting transfers between devices, swap_apart(): lax.ppermute(block, 'owner', pair)  57.3 us
    ppermute x15, waiting for transfers between devices, swap_apart(): lax.ppermute(block, 'owner', pair)  31.5 us
    all_to_all x2, starting transfers between devices, exchange(): return lax.all_to_all(x, 'owner', split_axis=0, concat_axis=0, tiled=True)  10.9 us
    all_to_all x2, waiting for transfers between devices, exchange(): return lax.all_to_all(x, 'owner', split_axis=0, concat_axis=0, tiled=True)  9.7 us
    pallas_call x5, Pallas kernels, pack(): pl.pallas_call(functools.partial(pack_kernel, slots, partners), out_shape...  8.19 us
    pallas_call x3, Pallas kernels, score(): pl.pallas_call(functools.partial(score_kernel, slots, partners, len(units...  6.04 us
    pallas_call x1, Pallas kernels, finish(): pl.pallas_call(functools.partial(finish_kernel, slots, partners, earlier,...  3.18 us
  transfers between devices with their start and end apart: 17, of which 11 were waited for; matrix products, arithmetic and copies ran while one was open for 0% of the time, Pallas kernels for 10%

profile of v6, /device:TPU:0, one launch (start us, length us, event | category | flops | bytes accessed | tf_op | source)
XLA Modules:
  0.0 134.3 jit_solution(12354793650580563804)
XLA Ops:
  1.3 1.0 count_rows.1
  2.3 7.4 %all-to-all-start.2 = ((s32[16,1,64]{2,1,0:T(1,128)}), s32[16,1,64]{2,1,0:T(1,128)S(1)}, u32[]{:S(2)}, u32[]{:S(2)}) async-start(s32[16,1,64]{2,1,0:T(1,128)} %get-tuple-element.143), calls=%async_computation.2 | async-start | bytes 16384 | tf_op jit(solution)/shard_map/all_to_all | solution.py:443
  9.7 1.9 %copy-done = bf16[2048,768]{1,0:T(8,128)(2,1)S(1)} copy-done((bf16[2048,768]{1,0:T(8,128)(2,1)S(1)}, bf16[2048,768]{1,0:T(8,128)(2,1)}, u32[]{:S(2)}) %copy-start) | copy-done | bytes 3145752
  11.6 1.3 unit_rows.1.rows_ref
  12.9 3.1 %all-to-all-done.2.counts_ref = s32[16,1,64]{2,1,0:T(1,128)S(1)} async-done(((s32[16,1,64]{2,1,0:T(1,128)}), s32[16,1,64]{2,1,0:T(1,128)S(1)}, u32[]{:S(2)}, u32[]{:S(2)}) %all-to-all-start.2) | async-done | bytes 4128 | tf_op jit(solution)/shard_map/all_to_all | solution.py:443
  16.7 1.1 pack_rows.15
  17.8 1.1 pack_rows.16
  19.3 2.9 %collective-permute-start.6 = (bf16[144,768]{1,0:T(8,128)(2,1)S(1)}, bf16[144,768]{1,0:T(8,128)(2,1)S(1)}, u32[]{:S(2)}, u32[]{:S(2)}) collective-permute-start(bf16[144,768]{1,0:T(8,128)(2,1)S(1)} %get-tuple-element.177), channel_id=1, source_target_pairs={{0,12},{1,13},{2,14},{3,15},{4,8},{5,9},{6,10},{7,11},{8,4},{9,5},... | collective-permute-start | bytes 663560 | tf_op jit(solution)/shard_map/ppermute | solution.py:456
  22.2 1.5 %collective-permute-start.3 = (bf16[144,768]{1,0:T(8,128)(2,1)S(1)}, bf16[144,768]{1,0:T(8,128)(2,1)S(1)}, u32[]{:S(2)}, u32[]{:S(2)}) collective-permute-start(bf16[144,768]{1,0:T(8,128)(2,1)S(1)} %get-tuple-element.174), channel_id=1, source_target_pairs={{0,15},{1,14},{2,13},{3,12},{4,11},{5,10},{6,9},{7,8},{8,7},{9,6},... | collective-permute-start | bytes 663560 | tf_op jit(solution)/shard_map/ppermute | solution.py:456
  23.7 3.2 %collective-permute-start.4 = (bf16[144,768]{1,0:T(8,128)(2,1)S(1)}, bf16[144,768]{1,0:T(8,128)(2,1)S(1)}, u32[]{:S(2)}, u32[]{:S(2)}) collective-permute-start(bf16[144,768]{1,0:T(8,128)(2,1)S(1)} %get-tuple-element.175), channel_id=1, source_target_pairs={{0,14},{1,15},{2,12},{3,13},{4,10},{5,11},{6,8},{7,9},{8,6},{9,7},... | collective-permute-start | bytes 663560 | tf_op jit(solution)/shard_map/ppermute | solution.py:456
  27.0 2.0 %pack_rows.17 = (bf16[144,768]{1,0:T(8,128)(2,1)S(1)}, bf16[144,768]{1,0:T(8,128)(2,1)S(1)}, bf16[144,768]{1,0:T(8,128)(2,1)S(1)}, bf16[144,768]{1,0:T(8,128)(2,1)S(1)}) custom-call(s32[1]{0:T(128)} %bitcast.33.me_ref, s32[1,2048]{1,0:T(1,128)S(1)} %get-tuple-element.146.owner_ref, s32[1,2048]{1,0:T(1,128)S(1)} %get-tuple-element.165.slot_ref, ...), custom_call_target="tpu_custom_call" | custom-call | flops 1811939328 | bytes 3145728 | tf_op jit(solution)/shard_map/pack_rows/pallas_call | solution.py:186
  29.1 21.6 %collective-permute-start.12 = (bf16[144,768]{1,0:T(8,128)(2,1)S(1)}, bf16[144,768]{1,0:T(8,128)(2,1)S(1)}, u32[]{:S(2)}, u32[]{:S(2)}) collective-permute-start(bf16[144,768]{1,0:T(8,128)(2,1)S(1)} %get-tuple-element.184), channel_id=1, source_target_pairs={{0,10},{1,11},{2,8},{3,9},{4,14},{5,15},{6,12},{7,13},{8,2},{9,3},... | collective-permute-start | bytes 663560 | tf_op jit(solution)/shard_map/ppermute | solution.py:456
  50.7 9.4 %collective-permute-start.13 = (bf16[144,768]{1,0:T(8,128)(2,1)S(1)}, bf16[144,768]{1,0:T(8,128)(2,1)S(1)}, u32[]{:S(2)}, u32[]{:S(2)}) collective-permute-start(bf16[144,768]{1,0:T(8,128)(2,1)S(1)} %get-tuple-element.185), channel_id=1, source_target_pairs={{0,9},{1,8},{2,11},{3,10},{4,13},{5,12},{6,15},{7,14},{8,1},{9,0},... | collective-permute-start | bytes 663560 | tf_op jit(solution)/shard_map/ppermute | solution.py:456
  60.1 2.0 %pack_rows.18 = (bf16[144,768]{1,0:T(8,128)(2,1)S(1)}, bf16[144,768]{1,0:T(8,128)(2,1)S(1)}, bf16[144,768]{1,0:T(8,128)(2,1)S(1)}, bf16[144,768]{1,0:T(8,128)(2,1)S(1)}) custom-call(s32[1]{0:T(128)} %bitcast.33.me_ref, s32[1,2048]{1,0:T(1,128)S(1)} %get-tuple-element.146.owner_ref, s32[1,2048]{1,0:T(1,128)S(1)} %get-tuple-element.165.slot_ref, ...), custom_call_target="tpu_custom_call" | custom-call | flops 1811939328 | bytes 3145728 | tf_op jit(solution)/shard_map/pack_rows/pallas_call | solution.py:186
  62.1 7.5 %collective-permute-start.14 = (bf16[144,768]{1,0:T(8,128)(2,1)S(1)}, bf16[144,768]{1,0:T(8,128)(2,1)S(1)}, u32[]{:S(2)}, u32[]{:S(2)}) collective-permute-start(bf16[144,768]{1,0:T(8,128)(2,1)S(1)} %get-tuple-element.186), channel_id=1, source_target_pairs={{0,8},{1,9},{2,10},{3,11},{4,12},{5,13},{6,14},{7,15},{8,0},{9,1},... | collective-permute-start | bytes 663560 | tf_op jit(solution)/shard_map/ppermute | solution.py:456
  69.6 9.8 %collective-permute-start.10 = (bf16[144,768]{1,0:T(8,128)(2,1)S(1)}, bf16[144,768]{1,0:T(8,128)(2,1)S(1)}, u32[]{:S(2)}, u32[]{:S(2)}) collective-permute-start(bf16[144,768]{1,0:T(8,128)(2,1)S(1)} %get-tuple-element.182), channel_id=1, source_target_pairs={{0,4},{1,5},{2,6},{3,7},{4,0},{5,1},{6,2},{7,3},{8,12},{9,13},{10,... | collective-permute-start | bytes 663560 | tf_op jit(solution)/shard_map/ppermute | solution.py:456
  79.4 4.2 %collective-permute-done.11.refs_0_ = bf16[144,768]{1,0:T(8,128)(2,1)S(1)} collective-permute-done((bf16[144,768]{1,0:T(8,128)(2,1)S(1)}, bf16[144,768]{1,0:T(8,128)(2,1)S(1)}, u32[]{:S(2)}, u32[]{:S(2)}) %collective-permute-start.11) | collective-permute-done | bytes 221216 | tf_op jit(solution)/shard_map/ppermute | solution.py:456
  83.6 4.8 %collective-permute-done.12.refs_1_ = bf16[144,768]{1,0:T(8,128)(2,1)S(1)} collective-permute-done((bf16[144,768]{1,0:T(8,128)(2,1)S(1)}, bf16[144,768]{1,0:T(8,128)(2,1)S(1)}, u32[]{:S(2)}, u32[]{:S(2)}) %collective-permute-start.12) | collective-permute-done | bytes 221216 | tf_op jit(solution)/shard_map/ppermute | solution.py:456
  88.4 4.7 %collective-permute-done.13.refs_2_ = bf16[144,768]{1,0:T(8,128)(2,1)S(1)} collective-permute-done((bf16[144,768]{1,0:T(8,128)(2,1)S(1)}, bf16[144,768]{1,0:T(8,128)(2,1)S(1)}, u32[]{:S(2)}, u32[]{:S(2)}) %collective-permute-start.13) | collective-permute-done | bytes 221216 | tf_op jit(solution)/shard_map/ppermute | solution.py:456
  93.1 2.0 %pack_rows.19 = (bf16[144,768]{1,0:T(8,128)(2,1)S(1)}, bf16[144,768]{1,0:T(8,128)(2,1)S(1)}, bf16[144,768]{1,0:T(8,128)(2,1)S(1)}, bf16[144,768]{1,0:T(8,128)(2,1)S(1)}) custom-call(s32[1]{0:T(128)} %bitcast.33.me_ref, s32[1,2048]{1,0:T(1,128)S(1)} %get-tuple-element.146.owner_ref, s32[1,2048]{1,0:T(1,128)S(1)} %get-tuple-element.165.slot_ref, ...), custom_call_target="tpu_custom_call" | custom-call | flops 1811939328 | bytes 3145728 | tf_op jit(solution)/shard_map/pack_rows/pallas_call | solution.py:186
  95.1 1.3 score_rows.9
  96.4 1.5 %collective-permute-done.14.refs_3_ = bf16[144,768]{1,0:T(8,128)(2,1)S(1)} collective-permute-done((bf16[144,768]{1,0:T(8,128)(2,1)S(1)}, bf16[144,768]{1,0:T(8,128)(2,1)S(1)}, u32[]{:S(2)}, u32[]{:S(2)}) %collective-permute-start.14) | collective-permute-done | bytes 221216 | tf_op jit(solution)/shard_map/ppermute | solution.py:456
  98.1 4.5 %collective-permute-done.10.refs_3_ = bf16[144,768]{1,0:T(8,128)(2,1)S(1)} collective-permute-done((bf16[144,768]{1,0:T(8,128)(2,1)S(1)}, bf16[144,768]{1,0:T(8,128)(2,1)S(1)}, u32[]{:S(2)}, u32[]{:S(2)}) %collective-permute-start.10) | collective-permute-done | bytes 221216 | tf_op jit(solution)/shard_map/ppermute | solution.py:456
  103.1 4.2 %collective-permute-done.7.refs_0_ = bf16[144,768]{1,0:T(8,128)(2,1)S(1)} collective-permute-done((bf16[144,768]{1,0:T(8,128)(2,1)S(1)}, bf16[144,768]{1,0:T(8,128)(2,1)S(1)}, u32[]{:S(2)}, u32[]{:S(2)}) %collective-permute-start.7) | collective-permute-done | bytes 221216 | tf_op jit(solution)/shard_map/ppermute | solution.py:456
  107.3 1.9 %score_rows.10 = (bf16[576,768]{1,0:T(8,128)(2,1)S(1)}, f32[576,128]{1,0:T(8,128)S(1)}, f32[576,128]{1,0:T(8,128)S(1)}, f32[8,768]{1,0:T(8,128)S(1)}, f32[720,128]{1,0:T(8,128)S(1)}) custom-call(f32[16,128]{1,0:T(8,128)S(1)} %get-tuple-element.148.bound_ref, bf16[144,768]{1,0:T(8,128)(2,1)S(1)} %collective-permute-done.11.refs_0_, ...), custom_call_target="tpu_custom_call" | custom-call | flops 1274019840 | bytes 1990656 | tf_op jit(solution)/shard_map/score_rows/pallas_call | solution.py:329
  109.3 2.8 %collective-permute-done.8.refs_1_ = bf16[144,768]{1,0:T(8,128)(2,1)S(1)} collective-permute-done((bf16[144,768]{1,0:T(8,128)(2,1)S(1)}, bf16[144,768]{1,0:T(8,128)(2,1)S(1)}, u32[]{:S(2)}, u32[]{:S(2)}) %collective-permute-start.8) | collective-permute-done | bytes 221216 | tf_op jit(solution)/shard_map/ppermute | solution.py:456
  112.1 4.6 %collective-permute-done.9.refs_2_ = bf16[144,768]{1,0:T(8,128)(2,1)S(1)} collective-permute-done((bf16[144,768]{1,0:T(8,128)(2,1)S(1)}, bf16[144,768]{1,0:T(8,128)(2,1)S(1)}, u32[]{:S(2)}, u32[]{:S(2)}) %collective-permute-start.9) | collective-permute-done | bytes 221216 | tf_op jit(solution)/shard_map/ppermute | solution.py:456
  116.7 2.9 %score_rows.11 = (bf16[576,768]{1,0:T(8,128)(2,1)S(1)}, f32[576,128]{1,0:T(8,128)S(1)}, f32[576,128]{1,0:T(8,128)S(1)}, f32[8,768]{1,0:T(8,128)S(1)}, f32[720,128]{1,0:T(8,128)S(1)}, /*index=5*/f32[576,128]{1,0:T(8,128)S(1)}) custom-call(f32[16,128]{1,0:T(8,128)S(1)} %get-tuple-element.148.bound_ref, bf16[144,768]{1,0:T(8,128)(2,1)S(1)} %collective-permute-done.7.refs_0_, ...), custom_call_target="tpu_custom_call" | custom-call | flops 1840250880 | bytes 2875392 | tf_op jit(solution)/shard_map/score_rows/pallas_call | solution.py:329
  119.8 3.2 %finish_rows.3 = f32[16,1,512]{2,1,0:T(1,128)} custom-call(s32[1]{0:T(128)} %bitcast.33.me_ref, f32[16,128]{1,0:T(8,128)S(1)} %get-tuple-element.148.bound_ref, f32[8,128]{1,0:T(8,128)S(1)} %get-tuple-element.149.total_ref, bf16[144,768]{1,0:T(8,128)(2,1)S(1)} %collective-permute-done.refs_0_, bf16[144,768]{1,0:T(8,128)(2,1)S(1)} %collective-permute-done.1.refs_1_, ...), custom_call_target="tpu_custom_call" | custom-call | flops 1811939328 | bytes 3538944 | tf_op jit(solution)/shard_map/finish_rows/pallas_call | solution.py:392
  123.0 3.5 %all-to-all-start.3 = ((f32[16,1,512]{2,1,0:T(1,128)}), f32[16,1,512]{2,1,0:T(1,128)S(1)}, u32[]{:S(2)}, u32[]{:S(2)}) async-start(f32[16,1,512]{2,1,0:T(1,128)} %finish_rows.3), calls=%async_computation.3 | async-start | bytes 65536 | tf_op jit(solution)/shard_map/all_to_all | solution.py:443
  126.5 6.6 %all-to-all-done.3.back_ref = f32[16,1,512]{2,1,0:T(1,128)S(1)} async-done(((f32[16,1,512]{2,1,0:T(1,128)}), f32[16,1,512]{2,1,0:T(1,128)S(1)}, u32[]{:S(2)}, u32[]{:S(2)}) %all-to-all-start.3) | async-done | bytes 32800 | tf_op jit(solution)/shard_map/all_to_all | solution.py:443
  133.1 1.2 restore_rows.3
  (24 shorter events, 2.9 us)
Async XLA Ops:
  0.6 0.7 copy-start.7
  2.3 13.7 %all-to-all-start.2 = ((s32[16,1,64]{2,1,0:T(1,128)}), s32[16,1,64]{2,1,0:T(1,128)S(1)}, u32[]{:S(2)}, u32[]{:S(2)}) async-start(s32[16,1,64]{2,1,0:T(1,128)} %get-tuple-element.143), calls=%async_computation.2 | async-start | bytes 16384 | tf_op jit(solution)/shard_map/all_to_all | solution.py:443
  9.7 1.9 %copy-start = (bf16[2048,768]{1,0:T(8,128)(2,1)S(1)}, bf16[2048,768]{1,0:T(8,128)(2,1)}, u32[]{:S(2)}) copy-start(bf16[2048,768]{1,0:T(8,128)(2,1)} %rows_ref.1) | copy-start | bytes 9437188
  16.7 103.1 %copy-start.10 = (f32[16,128]{1,0:T(8,128)}, f32[16,128]{1,0:T(8,128)S(1)}, u32[]{:S(2)}) copy-start(f32[16,128]{1,0:T(8,128)S(1)} %get-tuple-element.148.bound_ref) | copy-start | bytes 24580
  16.7 103.1 %copy-start.12 = (f32[8,128]{1,0:T(8,128)}, f32[8,128]{1,0:T(8,128)S(1)}, u32[]{:S(2)}) copy-start(f32[8,128]{1,0:T(8,128)S(1)} %get-tuple-element.149.total_ref) | copy-start | bytes 12292
  18.9 10.1 %collective-permute-start.5 = (bf16[144,768]{1,0:T(8,128)(2,1)S(1)}, bf16[144,768]{1,0:T(8,128)(2,1)S(1)}, u32[]{:S(2)}, u32[]{:S(2)}) collective-permute-start(bf16[144,768]{1,0:T(8,128)(2,1)S(1)} %get-tuple-element.176), channel_id=1, source_target_pairs={{0,13},{1,12},{2,15},{3,14},{4,9},{5,8},{6,11},{7,10},{8,5},{9,4},... | collective-permute-start | bytes 663560 | tf_op jit(solution)/shard_map/ppermute | solution.py:456
  19.3 31.3 %collective-permute-start.6 = (bf16[144,768]{1,0:T(8,128)(2,1)S(1)}, bf16[144,768]{1,0:T(8,128)(2,1)S(1)}, u32[]{:S(2)}, u32[]{:S(2)}) collective-permute-start(bf16[144,768]{1,0:T(8,128)(2,1)S(1)} %get-tuple-element.177), channel_id=1, source_target_pairs={{0,12},{1,13},{2,14},{3,15},{4,8},{5,9},{6,10},{7,11},{8,4},{9,5},... | collective-permute-start | bytes 663560 | tf_op jit(solution)/shard_map/ppermute | solution.py:456
  22.2 39.9 %collective-permute-start.3 = (bf16[144,768]{1,0:T(8,128)(2,1)S(1)}, bf16[144,768]{1,0:T(8,128)(2,1)S(1)}, u32[]{:S(2)}, u32[]{:S(2)}) collective-permute-start(bf16[144,768]{1,0:T(8,128)(2,1)S(1)} %get-tuple-element.174), channel_id=1, source_target_pairs={{0,15},{1,14},{2,13},{3,12},{4,11},{5,10},{6,9},{7,8},{8,7},{9,6},... | collective-permute-start | bytes 663560 | tf_op jit(solution)/shard_map/ppermute | solution.py:456
  23.7 45.9 %collective-permute-start.4 = (bf16[144,768]{1,0:T(8,128)(2,1)S(1)}, bf16[144,768]{1,0:T(8,128)(2,1)S(1)}, u32[]{:S(2)}, u32[]{:S(2)}) collective-permute-start(bf16[144,768]{1,0:T(8,128)(2,1)S(1)} %get-tuple-element.175), channel_id=1, source_target_pairs={{0,14},{1,15},{2,12},{3,13},{4,10},{5,11},{6,8},{7,9},{8,6},{9,7},... | collective-permute-start | bytes 663560 | tf_op jit(solution)/shard_map/ppermute | solution.py:456
  29.0 54.6 %collective-permute-start.11 = (bf16[144,768]{1,0:T(8,128)(2,1)S(1)}, bf16[144,768]{1,0:T(8,128)(2,1)S(1)}, u32[]{:S(2)}, u32[]{:S(2)}) collective-permute-start(bf16[144,768]{1,0:T(8,128)(2,1)S(1)} %get-tuple-element.183), channel_id=1, source_target_pairs={{0,11},{1,10},{2,9},{3,8},{4,15},{5,14},{6,13},{7,12},{8,3},{9,2},... | collective-permute-start | bytes 663560 | tf_op jit(solution)/shard_map/ppermute | solution.py:456
  29.1 59.4 %collective-permute-start.12 = (bf16[144,768]{1,0:T(8,128)(2,1)S(1)}, bf16[144,768]{1,0:T(8,128)(2,1)S(1)}, u32[]{:S(2)}, u32[]{:S(2)}) collective-permute-start(bf16[144,768]{1,0:T(8,128)(2,1)S(1)} %get-tuple-element.184), channel_id=1, source_target_pairs={{0,10},{1,11},{2,8},{3,9},{4,14},{5,15},{6,12},{7,13},{8,2},{9,3},... | collective-permute-start | bytes 663560 | tf_op jit(solution)/shard_map/ppermute | solution.py:456
  50.7 42.4 %collective-permute-start.13 = (bf16[144,768]{1,0:T(8,128)(2,1)S(1)}, bf16[144,768]{1,0:T(8,128)(2,1)S(1)}, u32[]{:S(2)}, u32[]{:S(2)}) collective-permute-start(bf16[144,768]{1,0:T(8,128)(2,1)S(1)} %get-tuple-element.185), channel_id=1, source_target_pairs={{0,9},{1,8},{2,11},{3,10},{4,13},{5,12},{6,15},{7,14},{8,1},{9,0},... | collective-permute-start | bytes 663560 | tf_op jit(solution)/shard_map/ppermute | solution.py:456
  62.1 35.7 %collective-permute-start.14 = (bf16[144,768]{1,0:T(8,128)(2,1)S(1)}, bf16[144,768]{1,0:T(8,128)(2,1)S(1)}, u32[]{:S(2)}, u32[]{:S(2)}) collective-permute-start(bf16[144,768]{1,0:T(8,128)(2,1)S(1)} %get-tuple-element.186), channel_id=1, source_target_pairs={{0,8},{1,9},{2,10},{3,11},{4,12},{5,13},{6,14},{7,15},{8,0},{9,1},... | collective-permute-start | bytes 663560 | tf_op jit(solution)/shard_map/ppermute | solution.py:456
  69.6 32.9 %collective-permute-start.10 = (bf16[144,768]{1,0:T(8,128)(2,1)S(1)}, bf16[144,768]{1,0:T(8,128)(2,1)S(1)}, u32[]{:S(2)}, u32[]{:S(2)}) collective-permute-start(bf16[144,768]{1,0:T(8,128)(2,1)S(1)} %get-tuple-element.182), channel_id=1, source_target_pairs={{0,4},{1,5},{2,6},{3,7},{4,0},{5,1},{6,2},{7,3},{8,12},{9,13},{10,... | collective-permute-start | bytes 663560 | tf_op jit(solution)/shard_map/ppermute | solution.py:456
  83.6 23.7 %collective-permute-start.7 = (bf16[144,768]{1,0:T(8,128)(2,1)S(1)}, bf16[144,768]{1,0:T(8,128)(2,1)S(1)}, u32[]{:S(2)}, u32[]{:S(2)}) collective-permute-start(bf16[144,768]{1,0:T(8,128)(2,1)S(1)} %get-tuple-element.179), channel_id=1, source_target_pairs={{0,7},{1,6},{2,5},{3,4},{4,3},{5,2},{6,1},{7,0},{8,15},{9,14},{10,... | collective-permute-start | bytes 663560 | tf_op jit(solution)/shard_map/ppermute | solution.py:456
  88.4 23.7 %collective-permute-start.8 = (bf16[144,768]{1,0:T(8,128)(2,1)S(1)}, bf16[144,768]{1,0:T(8,128)(2,1)S(1)}, u32[]{:S(2)}, u32[]{:S(2)}) collective-permute-start(bf16[144,768]{1,0:T(8,128)(2,1)S(1)} %get-tuple-element.180), channel_id=1, source_target_pairs={{0,6},{1,7},{2,4},{3,5},{4,2},{5,3},{6,0},{7,1},{8,14},{9,15},{10,... | collective-permute-start | bytes 663560 | tf_op jit(solution)/shard_map/ppermute | solution.py:456
  93.1 23.6 %collective-permute-start.9 = (bf16[144,768]{1,0:T(8,128)(2,1)S(1)}, bf16[144,768]{1,0:T(8,128)(2,1)S(1)}, u32[]{:S(2)}, u32[]{:S(2)}) collective-permute-start(bf16[144,768]{1,0:T(8,128)(2,1)S(1)} %get-tuple-element.181), channel_id=1, source_target_pairs={{0,5},{1,4},{2,7},{3,6},{4,1},{5,0},{6,3},{7,2},{8,13},{9,12},{10,... | collective-permute-start | bytes 663560 | tf_op jit(solution)/shard_map/ppermute | solution.py:456
  97.9 21.7 %collective-permute-start = (bf16[144,768]{1,0:T(8,128)(2,1)S(1)}, bf16[144,768]{1,0:T(8,128)(2,1)S(1)}, u32[]{:S(2)}, u32[]{:S(2)}) collective-permute-start(bf16[144,768]{1,0:T(8,128)(2,1)S(1)} %get-tuple-element.170), channel_id=1, source_target_pairs={{0,3},{1,2},{2,1},{3,0},{4,7},{5,6},{6,5},{7,4},{8,11},{9,10},{10,... | collective-permute-start | bytes 663560 | tf_op jit(solution)/shard_map/ppermute | solution.py:456
  102.6 17.3 %collective-permute-start.1 = (bf16[144,768]{1,0:T(8,128)(2,1)S(1)}, bf16[144,768]{1,0:T(8,128)(2,1)S(1)}, u32[]{:S(2)}, u32[]{:S(2)}) collective-permute-start(bf16[144,768]{1,0:T(8,128)(2,1)S(1)} %get-tuple-element.171), channel_id=1, source_target_pairs={{0,2},{1,3},{2,0},{3,1},{4,6},{5,7},{6,4},{7,5},{8,10},{9,11},{10,... | collective-permute-start | bytes 663560 | tf_op jit(solution)/shard_map/ppermute | solution.py:456
  107.3 12.5 %collective-permute-start.2 = (bf16[144,768]{1,0:T(8,128)(2,1)S(1)}, bf16[144,768]{1,0:T(8,128)(2,1)S(1)}, u32[]{:S(2)}, u32[]{:S(2)}) collective-permute-start(bf16[144,768]{1,0:T(8,128)(2,1)S(1)} %get-tuple-element.172), channel_id=1, source_target_pairs={{0,1},{1,0},{2,3},{3,2},{4,5},{5,4},{6,7},{7,6},{8,9},{9,8},{10,11... | collective-permute-start | bytes 663560 | tf_op jit(solution)/shard_map/ppermute | solution.py:456
  123.0 10.1 %all-to-all-start.3 = ((f32[16,1,512]{2,1,0:T(1,128)}), f32[16,1,512]{2,1,0:T(1,128)S(1)}, u32[]{:S(2)}, u32[]{:S(2)}) async-start(f32[16,1,512]{2,1,0:T(1,128)} %finish_rows.3), calls=%async_computation.3 | async-start | bytes 65536 | tf_op jit(solution)/shard_map/all_to_all | solution.py:443

commit v7 on v6

--- a/solution.py
+++ b/solution.py
@@ -471,14 +471,14 @@
     unit = unit_rows(embeddings)
     owner_row, slot_row, bound, total, load = assign(me, exchange(counts), rank)
 
-    sent = list(range(owners - 1, 0, -1))
+    sent = list(range(1, owners))
     seen = [0] + sent
     sent = sent + [0]
     packs = [tuple(sent[:2]), tuple(sent[2:4])]
     packs += [tuple(sent[i : i + GROUP]) for i in range(4, owners, GROUP)]
     share = owners // 16 if owners >= 16 else 1
     groups, at = [], 0
-    for size in (5, 4, 4):
+    for size in (5, 4, 4, 2):
         groups.append(seen[at : at + size * share])
         at += size * share
     groups.append(seen[at:])

time: 135 us -> 124 us (0.919)
  starting transfers between devices: 68.1 us -> 35.1 us
  waiting for transfers between devices: 41.2 us -> 62.9 us
    ppermute x15, starting transfers between devices: 57.3 us -> 15.2 us  [swap_apart(): lax.ppermute(block, 'owner', pair)]
    ppermute x15, waiting for transfers between devices: 31.5 us -> 53.2 us  [swap_apart(): lax.ppermute(block, 'owner', pair)]
    all_to_all x2, starting transfers between devices: 10.9 us -> 19.9 us  [exchange(): return lax.all_to_all(x, 'owner', split_axis=0, concat_axis=0, tiled=True)]
    pallas_call x3 -> x4, Pallas kernels: 6.04 us -> 8.03 us  [score(): pl.pallas_call(functools.partial(score_kernel, slots, partners, len(units...]
  transfers between devices with their start and end apart: 17 -> 17, of which waited for: 11 -> 9; matrix products, arithmetic and copies ran while one was open for 0% -> 0% of each run, Pallas kernels for 10% -> 12%
where the time goes in v7:
time: 124 us
  waiting for transfers between devices  62.9 us (51%)
  starting transfers between devices  35.1 us (28%)
  Pallas kernels  22.6 us (18%)
  local copies, waits for them, and re-layouts  2.58 us (2%)
    ppermute x15, waiting for transfers between devices, swap_apart(): lax.ppermute(block, 'owner', pair)  53.2 us
    all_to_all x2, starting transfers between devices, exchange(): return lax.all_to_all(x, 'owner', split_axis=0, concat_axis=0, tiled=True)  19.9 us
    ppermute x15, starting transfers between devices, swap_apart(): lax.ppermute(block, 'owner', pair)  15.2 us
    all_to_all x2, waiting for transfers between devices, exchange(): return lax.all_to_all(x, 'owner', split_axis=0, concat_axis=0, tiled=True)  9.74 us
    pallas_call x5, Pallas kernels, pack(): pl.pallas_call(functools.partial(pack_kernel, slots, partners), out_shape...  8.19 us
    pallas_call x4, Pallas kernels, score(): pl.pallas_call(functools.partial(score_kernel, slots, partners, len(units...  8.03 us
    unnamed x6, local copies, waits for them, and re-layouts  2.58 us
  transfers between devices with their start and end apart: 17, of which 9 were waited for; matrix products, arithmetic and copies ran while one was open for 0% of the time, Pallas kernels for 12%

profile of v7, /device:TPU:0, one launch (start us, length us, event | category | flops | bytes accessed | tf_op | source)
XLA Modules:
  0.0 123.9 jit_solution(3558082089829972930)
XLA Ops:
  0.6 0.7 copy-done.7
  1.3 1.0 count_rows.1
  2.3 7.4 %all-to-all-start.2 = ((s32[16,1,64]{2,1,0:T(1,128)}), s32[16,1,64]{2,1,0:T(1,128)S(1)}, u32[]{:S(2)}, u32[]{:S(2)}) async-start(s32[16,1,64]{2,1,0:T(1,128)} %get-tuple-element.157), calls=%async_computation.2 | async-start | bytes 16384 | tf_op jit(solution)/shard_map/all_to_all | solution.py:443
  9.7 1.9 %copy-done = bf16[2048,768]{1,0:T(8,128)(2,1)S(1)} copy-done((bf16[2048,768]{1,0:T(8,128)(2,1)S(1)}, bf16[2048,768]{1,0:T(8,128)(2,1)}, u32[]{:S(2)}) %copy-start) | copy-done | bytes 3145752
  11.6 1.3 %unit_rows.1.rows_ref = bf16[2048,768]{1,0:T(8,128)(2,1)S(1)} custom-call(bf16[2048,768]{1,0:T(8,128)(2,1)S(1)} %copy-done), custom_call_target="tpu_custom_call" | custom-call | flops 12582912 | bytes 6291456 | tf_op jit(solution)/shard_map/unit_rows/pallas_call | solution.py:212
  12.9 3.1 %all-to-all-done.2.counts_ref = s32[16,1,64]{2,1,0:T(1,128)S(1)} async-done(((s32[16,1,64]{2,1,0:T(1,128)}), s32[16,1,64]{2,1,0:T(1,128)S(1)}, u32[]{:S(2)}, u32[]{:S(2)}) %all-to-all-start.2) | async-done | bytes 4128 | tf_op jit(solution)/shard_map/all_to_all | solution.py:443
  16.7 1.1 pack_rows.15
  17.8 1.1 pack_rows.16
  19.9 1.4 %collective-permute-start.2 = (bf16[144,768]{1,0:T(8,128)(2,1)S(1)}, bf16[144,768]{1,0:T(8,128)(2,1)S(1)}, u32[]{:S(2)}, u32[]{:S(2)}) collective-permute-start(bf16[144,768]{1,0:T(8,128)(2,1)S(1)} %get-tuple-element.187), channel_id=1, source_target_pairs={{0,2},{1,3},{2,0},{3,1},{4,6},{5,7},{6,4},{7,5},{8,10},{9,11},{10,... | collective-permute-start | bytes 663560 | tf_op jit(solution)/shard_map/ppermute | solution.py:456
  21.3 2.0 %pack_rows.17 = (bf16[144,768]{1,0:T(8,128)(2,1)S(1)}, bf16[144,768]{1,0:T(8,128)(2,1)S(1)}, bf16[144,768]{1,0:T(8,128)(2,1)S(1)}, bf16[144,768]{1,0:T(8,128)(2,1)S(1)}) custom-call(s32[1]{0:T(128)} %bitcast.33.me_ref, s32[1,2048]{1,0:T(1,128)S(1)} %get-tuple-element.160.owner_ref, s32[1,2048]{1,0:T(1,128)S(1)} %get-tuple-element.179.slot_ref, ...), custom_call_target="tpu_custom_call" | custom-call | flops 1811939328 | bytes 3145728 | tf_op jit(solution)/shard_map/pack_rows/pallas_call | solution.py:186
  23.4 1.0 collective-permute-start.11
  24.3 2.4 %collective-permute-done.3.refs_3_ = bf16[144,768]{1,0:T(8,128)(2,1)S(1)} collective-permute-done((bf16[144,768]{1,0:T(8,128)(2,1)S(1)}, bf16[144,768]{1,0:T(8,128)(2,1)S(1)}, u32[]{:S(2)}, u32[]{:S(2)}) %collective-permute-start.3) | collective-permute-done | bytes 221216 | tf_op jit(solution)/shard_map/ppermute | solution.py:456
  27.3 1.7 %collective-permute-start.13 = (bf16[144,768]{1,0:T(8,128)(2,1)S(1)}, bf16[144,768]{1,0:T(8,128)(2,1)S(1)}, u32[]{:S(2)}, u32[]{:S(2)}) collective-permute-start(bf16[144,768]{1,0:T(8,128)(2,1)S(1)} %get-tuple-element.199), channel_id=1, source_target_pairs={{0,7},{1,6},{2,5},{3,4},{4,3},{5,2},{6,1},{7,0},{8,15},{9,14},{10,... | collective-permute-start | bytes 663560 | tf_op jit(solution)/shard_map/ppermute | solution.py:456
  29.0 2.0 %pack_rows.18 = (bf16[144,768]{1,0:T(8,128)(2,1)S(1)}, bf16[144,768]{1,0:T(8,128)(2,1)S(1)}, bf16[144,768]{1,0:T(8,128)(2,1)S(1)}, bf16[144,768]{1,0:T(8,128)(2,1)S(1)}) custom-call(s32[1]{0:T(128)} %bitcast.33.me_ref, s32[1,2048]{1,0:T(1,128)S(1)} %get-tuple-element.160.owner_ref, s32[1,2048]{1,0:T(1,128)S(1)} %get-tuple-element.179.slot_ref, ...), custom_call_target="tpu_custom_call" | custom-call | flops 1811939328 | bytes 3145728 | tf_op jit(solution)/shard_map/pack_rows/pallas_call | solution.py:186
  31.7 2.4 %collective-permute-start.10 = (bf16[144,768]{1,0:T(8,128)(2,1)S(1)}, bf16[144,768]{1,0:T(8,128)(2,1)S(1)}, u32[]{:S(2)}, u32[]{:S(2)}) collective-permute-start(bf16[144,768]{1,0:T(8,128)(2,1)S(1)} %get-tuple-element.196), channel_id=1, source_target_pairs={{0,12},{1,13},{2,14},{3,15},{4,8},{5,9},{6,10},{7,11},{8,4},{9,5},... | collective-permute-start | bytes 663560 | tf_op jit(solution)/shard_map/ppermute | solution.py:456
  34.2 8.2 %collective-permute-done.12.refs_1_ = bf16[144,768]{1,0:T(8,128)(2,1)S(1)} collective-permute-done((bf16[144,768]{1,0:T(8,128)(2,1)S(1)}, bf16[144,768]{1,0:T(8,128)(2,1)S(1)}, u32[]{:S(2)}, u32[]{:S(2)}) %collective-permute-start.12) | collective-permute-done | bytes 221216 | tf_op jit(solution)/shard_map/ppermute | solution.py:456
  42.4 4.2 %collective-permute-done.13.refs_2_ = bf16[144,768]{1,0:T(8,128)(2,1)S(1)} collective-permute-done((bf16[144,768]{1,0:T(8,128)(2,1)S(1)}, bf16[144,768]{1,0:T(8,128)(2,1)S(1)}, u32[]{:S(2)}, u32[]{:S(2)}) %collective-permute-start.13) | collective-permute-done | bytes 221216 | tf_op jit(solution)/shard_map/ppermute | solution.py:456
  46.6 2.0 %pack_rows.19 = (bf16[144,768]{1,0:T(8,128)(2,1)S(1)}, bf16[144,768]{1,0:T(8,128)(2,1)S(1)}, bf16[144,768]{1,0:T(8,128)(2,1)S(1)}, bf16[144,768]{1,0:T(8,128)(2,1)S(1)}) custom-call(s32[1]{0:T(128)} %bitcast.33.me_ref, s32[1,2048]{1,0:T(1,128)S(1)} %get-tuple-element.160.owner_ref, s32[1,2048]{1,0:T(1,128)S(1)} %get-tuple-element.179.slot_ref, ...), custom_call_target="tpu_custom_call" | custom-call | flops 1811939328 | bytes 3145728 | tf_op jit(solution)/shard_map/pack_rows/pallas_call | solution.py:186
  48.6 1.3 %score_rows.12 = (bf16[720,768]{1,0:T(8,128)(2,1)S(1)}, f32[720,128]{1,0:T(8,128)S(1)}, f32[720,128]{1,0:T(8,128)S(1)}, f32[8,768]{1,0:T(8,128)S(1)}) custom-call(f32[16,128]{1,0:T(8,128)S(1)} %get-tuple-element.162.bound_ref, bf16[144,768]{1,0:T(8,128)(2,1)S(1)} %get-tuple-element.185.refs_0_, bf16[144,768]{1,0:T(8,128)(2,1)S(1)} %collective-permute-done.1.refs_1_, ...), custom_call_target="tpu_custom_call" | custom-call | flops 849346560 | bytes 1105920 | tf_op jit(solution)/shard_map/score_rows/pallas_call | solution.py:329
  49.9 2.0 %collective-permute-start.5 = (bf16[144,768]{1,0:T(8,128)(2,1)S(1)}, bf16[144,768]{1,0:T(8,128)(2,1)S(1)}, u32[]{:S(2)}, u32[]{:S(2)}) collective-permute-start(bf16[144,768]{1,0:T(8,128)(2,1)S(1)} %get-tuple-element.191), channel_id=1, source_target_pairs={{0,13},{1,12},{2,15},{3,14},{4,9},{5,8},{6,11},{7,10},{8,5},{9,4},... | collective-permute-start | bytes 663560 | tf_op jit(solution)/shard_map/ppermute | solution.py:456
  51.9 2.4 %collective-permute-start.6 = (bf16[144,768]{1,0:T(8,128)(2,1)S(1)}, bf16[144,768]{1,0:T(8,128)(2,1)S(1)}, u32[]{:S(2)}, u32[]{:S(2)}) collective-permute-start(bf16[144,768]{1,0:T(8,128)(2,1)S(1)} %get-tuple-element.192), channel_id=1, source_target_pairs={{0,14},{1,15},{2,12},{3,13},{4,10},{5,11},{6,8},{7,9},{8,6},{9,7},... | collective-permute-start | bytes 663560 | tf_op jit(solution)/shard_map/ppermute | solution.py:456
  54.3 1.9 %score_rows.13 = (bf16[576,768]{1,0:T(8,128)(2,1)S(1)}, f32[576,128]{1,0:T(8,128)S(1)}, f32[576,128]{1,0:T(8,128)S(1)}, f32[8,768]{1,0:T(8,128)S(1)}, f32[720,128]{1,0:T(8,128)S(1)}) custom-call(f32[16,128]{1,0:T(8,128)S(1)} %get-tuple-element.162.bound_ref, bf16[144,768]{1,0:T(8,128)(2,1)S(1)} %collective-permute-done.11.refs_0_, ...), custom_call_target="tpu_custom_call" | custom-call | flops 1274019840 | bytes 1990656 | tf_op jit(solution)/shard_map/score_rows/pallas_call | solution.py:329
  56.2 26.4 %collective-permute-done.7.refs_0_ = bf16[144,768]{1,0:T(8,128)(2,1)S(1)} collective-permute-done((bf16[144,768]{1,0:T(8,128)(2,1)S(1)}, bf16[144,768]{1,0:T(8,128)(2,1)S(1)}, u32[]{:S(2)}, u32[]{:S(2)}) %collective-permute-start.7) | collective-permute-done | bytes 221216 | tf_op jit(solution)/shard_map/ppermute | solution.py:456
  82.6 2.0 %collective-permute-start = (bf16[144,768]{1,0:T(8,128)(2,1)S(1)}, bf16[144,768]{1,0:T(8,128)(2,1)S(1)}, u32[]{:S(2)}, u32[]{:S(2)}) collective-permute-start(bf16[144,768]{1,0:T(8,128)(2,1)S(1)} %get-tuple-element.184), channel_id=1, source_target_pairs={{0,15},{1,14},{2,13},{3,12},{4,11},{5,10},{6,9},{7,8},{8,7},{9,6},... | collective-permute-start | bytes 663560 | tf_op jit(solution)/shard_map/ppermute | solution.py:456
  84.6 3.1 %collective-permute-done.8.refs_1_ = bf16[144,768]{1,0:T(8,128)(2,1)S(1)} collective-permute-done((bf16[144,768]{1,0:T(8,128)(2,1)S(1)}, bf16[144,768]{1,0:T(8,128)(2,1)S(1)}, u32[]{:S(2)}, u32[]{:S(2)}) %collective-permute-start.8) | collective-permute-done | bytes 221216 | tf_op jit(solution)/shard_map/ppermute | solution.py:456
  87.7 8.8 %collective-permute-done.9.refs_2_ = bf16[144,768]{1,0:T(8,128)(2,1)S(1)} collective-permute-done((bf16[144,768]{1,0:T(8,128)(2,1)S(1)}, bf16[144,768]{1,0:T(8,128)(2,1)S(1)}, u32[]{:S(2)}, u32[]{:S(2)}) %collective-permute-start.9) | collective-permute-done | bytes 221216 | tf_op jit(solution)/shard_map/ppermute | solution.py:456
  96.5 2.9 %score_rows.14 = (bf16[576,768]{1,0:T(8,128)(2,1)S(1)}, f32[576,128]{1,0:T(8,128)S(1)}, f32[576,128]{1,0:T(8,128)S(1)}, f32[8,768]{1,0:T(8,128)S(1)}, f32[720,128]{1,0:T(8,128)S(1)}, /*index=5*/f32[576,128]{1,0:T(8,128)S(1)}) custom-call(f32[16,128]{1,0:T(8,128)S(1)} %get-tuple-element.162.bound_ref, bf16[144,768]{1,0:T(8,128)(2,1)S(1)} %collective-permute-done.7.refs_0_, ...), custom_call_target="tpu_custom_call" | custom-call | flops 1840250880 | bytes 2875392 | tf_op jit(solution)/shard_map/score_rows/pallas_call | solution.py:329
  99.4 2.0 %score_rows.15 = (bf16[288,768]{1,0:T(8,128)(2,1)S(1)}, f32[288,128]{1,0:T(8,128)S(1)}, f32[288,128]{1,0:T(8,128)S(1)}, f32[8,768]{1,0:T(8,128)S(1)}, f32[720,12...) custom-call(f32[16,128]{1,0:T(8,128)S(1)} %get-tuple-element.162.bound_ref, ...), custom_call_target="tpu_custom_call" | custom-call | flops 1274019840 | bytes 3317760 | tf_op jit(solution)/shard_map/score_rows/pallas_call | solution.py:329
  101.4 2.2 %finish_rows.3 = f32[16,1,512]{2,1,0:T(1,128)} custom-call(s32[1]{0:T(128)} %bitcast.33.me_ref, f32[16,128]{1,0:T(8,128)S(1)} %get-tuple-element.162.bound_ref, f32[8,128]{1,0:T(8,128)S(1)} %get-tuple-element.163.total_ref, bf16[144,768]{1,0:T(8,128)(2,1)S(1)} %collective-permute-done.refs_0_, ...), custom_call_target="tpu_custom_call" | custom-call | flops 905969664 | bytes 3538944 | tf_op jit(solution)/shard_map/finish_rows/pallas_call | solution.py:392
  103.6 12.5 %all-to-all-start.3 = ((f32[16,1,512]{2,1,0:T(1,128)}), f32[16,1,512]{2,1,0:T(1,128)S(1)}, u32[]{:S(2)}, u32[]{:S(2)}) async-start(f32[16,1,512]{2,1,0:T(1,128)} %finish_rows.3), calls=%async_computation.3 | async-start | bytes 65536 | tf_op jit(solution)/shard_map/all_to_all | solution.py:443
  116.1 6.6 %all-to-all-done.3.back_ref = f32[16,1,512]{2,1,0:T(1,128)S(1)} async-done(((f32[16,1,512]{2,1,0:T(1,128)}), f32[16,1,512]{2,1,0:T(1,128)S(1)}, u32[]{:S(2)}, u32[]{:S(2)}) %all-to-all-start.3) | async-done | bytes 32800 | tf_op jit(solution)/shard_map/all_to_all | solution.py:443
  122.7 1.2 restore_rows.3
  (23 shorter events, 3.0 us)
Async XLA Ops:
  0.6 0.7 copy-start.7
  2.3 13.7 %all-to-all-start.2 = ((s32[16,1,64]{2,1,0:T(1,128)}), s32[16,1,64]{2,1,0:T(1,128)S(1)}, u32[]{:S(2)}, u32[]{:S(2)}) async-start(s32[16,1,64]{2,1,0:T(1,128)} %get-tuple-element.157), calls=%async_computation.2 | async-start | bytes 16384 | tf_op jit(solution)/shard_map/all_to_all | solution.py:443
  9.7 1.9 %copy-start = (bf16[2048,768]{1,0:T(8,128)(2,1)S(1)}, bf16[2048,768]{1,0:T(8,128)(2,1)}, u32[]{:S(2)}) copy-start(bf16[2048,768]{1,0:T(8,128)(2,1)} %rows_ref.1) | copy-start | bytes 9437188
  16.7 84.7 %copy-start.12 = (f32[8,128]{1,0:T(8,128)}, f32[8,128]{1,0:T(8,128)S(1)}, u32[]{:S(2)}) copy-start(f32[8,128]{1,0:T(8,128)S(1)} %get-tuple-element.163.total_ref) | copy-start | bytes 12292
  18.9 7.8 %collective-permute-start.3 = (bf16[144,768]{1,0:T(8,128)(2,1)S(1)}, bf16[144,768]{1,0:T(8,128)(2,1)S(1)}, u32[]{:S(2)}, u32[]{:S(2)}) collective-permute-start(bf16[144,768]{1,0:T(8,128)(2,1)S(1)} %get-tuple-element.188), channel_id=1, source_target_pairs={{0,3},{1,2},{2,1},{3,0},{4,7},{5,6},{6,5},{7,4},{8,11},{9,10},{10,... | collective-permute-start | bytes 663560 | tf_op jit(solution)/shard_map/ppermute | solution.py:456
  19.0 8.3 %collective-permute-start.4 = (bf16[144,768]{1,0:T(8,128)(2,1)S(1)}, bf16[144,768]{1,0:T(8,128)(2,1)S(1)}, u32[]{:S(2)}, u32[]{:S(2)}) collective-permute-start(bf16[144,768]{1,0:T(8,128)(2,1)S(1)} %get-tuple-element.189), channel_id=1, source_target_pairs={{0,4},{1,5},{2,6},{3,7},{4,0},{5,1},{6,2},{7,3},{8,12},{9,13},{10,... | collective-permute-start | bytes 663560 | tf_op jit(solution)/shard_map/ppermute | solution.py:456
  19.6 11.4 %collective-permute-start.1 = (bf16[144,768]{1,0:T(8,128)(2,1)S(1)}, bf16[144,768]{1,0:T(8,128)(2,1)S(1)}, u32[]{:S(2)}, u32[]{:S(2)}) collective-permute-start(bf16[144,768]{1,0:T(8,128)(2,1)S(1)} %get-tuple-element.186), channel_id=1, source_target_pairs={{0,1},{1,0},{2,3},{3,2},{4,5},{5,4},{6,7},{7,6},{8,9},{9,8},{10,11... | collective-permute-start | bytes 663560 | tf_op jit(solution)/shard_map/ppermute | solution.py:456
  19.9 11.8 %collective-permute-start.2 = (bf16[144,768]{1,0:T(8,128)(2,1)S(1)}, bf16[144,768]{1,0:T(8,128)(2,1)S(1)}, u32[]{:S(2)}, u32[]{:S(2)}) collective-permute-start(bf16[144,768]{1,0:T(8,128)(2,1)S(1)} %get-tuple-element.187), channel_id=1, source_target_pairs={{0,2},{1,3},{2,0},{3,1},{4,6},{5,7},{6,4},{7,5},{8,10},{9,11},{10,... | collective-permute-start | bytes 663560 | tf_op jit(solution)/shard_map/ppermute | solution.py:456
  23.4 10.7 %collective-permute-start.11 = (bf16[144,768]{1,0:T(8,128)(2,1)S(1)}, bf16[144,768]{1,0:T(8,128)(2,1)S(1)}, u32[]{:S(2)}, u32[]{:S(2)}) collective-permute-start(bf16[144,768]{1,0:T(8,128)(2,1)S(1)} %get-tuple-element.197), channel_id=1, source_target_pairs={{0,5},{1,4},{2,7},{3,6},{4,1},{5,0},{6,3},{7,2},{8,13},{9,12},{10,... | collective-permute-start | bytes 663560 | tf_op jit(solution)/shard_map/ppermute | solution.py:456
  26.7 15.6 %collective-permute-start.12 = (bf16[144,768]{1,0:T(8,128)(2,1)S(1)}, bf16[144,768]{1,0:T(8,128)(2,1)S(1)}, u32[]{:S(2)}, u32[]{:S(2)}) collective-permute-start(bf16[144,768]{1,0:T(8,128)(2,1)S(1)} %get-tuple-element.198), channel_id=1, source_target_pairs={{0,6},{1,7},{2,4},{3,5},{4,2},{5,3},{6,0},{7,1},{8,14},{9,15},{10,... | collective-permute-start | bytes 663560 | tf_op jit(solution)/shard_map/ppermute | solution.py:456
  27.3 19.3 %collective-permute-start.13 = (bf16[144,768]{1,0:T(8,128)(2,1)S(1)}, bf16[144,768]{1,0:T(8,128)(2,1)S(1)}, u32[]{:S(2)}, u32[]{:S(2)}) collective-permute-start(bf16[144,768]{1,0:T(8,128)(2,1)S(1)} %get-tuple-element.199), channel_id=1, source_target_pairs={{0,7},{1,6},{2,5},{3,4},{4,3},{5,2},{6,1},{7,0},{8,15},{9,14},{10,... | collective-permute-start | bytes 663560 | tf_op jit(solution)/shard_map/ppermute | solution.py:456
  31.0 18.9 %collective-permute-start.14 = (bf16[144,768]{1,0:T(8,128)(2,1)S(1)}, bf16[144,768]{1,0:T(8,128)(2,1)S(1)}, u32[]{:S(2)}, u32[]{:S(2)}) collective-permute-start(bf16[144,768]{1,0:T(8,128)(2,1)S(1)} %get-tuple-element.200), channel_id=1, source_target_pairs={{0,8},{1,9},{2,10},{3,11},{4,12},{5,13},{6,14},{7,15},{8,0},{9,1},... | collective-permute-start | bytes 663560 | tf_op jit(solution)/shard_map/ppermute | solution.py:456
  31.7 20.2 %collective-permute-start.10 = (bf16[144,768]{1,0:T(8,128)(2,1)S(1)}, bf16[144,768]{1,0:T(8,128)(2,1)S(1)}, u32[]{:S(2)}, u32[]{:S(2)}) collective-permute-start(bf16[144,768]{1,0:T(8,128)(2,1)S(1)} %get-tuple-element.196), channel_id=1, source_target_pairs={{0,12},{1,13},{2,14},{3,15},{4,8},{5,9},{6,10},{7,11},{8,4},{9,5},... | collective-permute-start | bytes 663560 | tf_op jit(solution)/shard_map/ppermute | solution.py:456
  34.1 48.5 %collective-permute-start.7 = (bf16[144,768]{1,0:T(8,128)(2,1)S(1)}, bf16[144,768]{1,0:T(8,128)(2,1)S(1)}, u32[]{:S(2)}, u32[]{:S(2)}) collective-permute-start(bf16[144,768]{1,0:T(8,128)(2,1)S(1)} %get-tuple-element.193), channel_id=1, source_target_pairs={{0,9},{1,8},{2,11},{3,10},{4,13},{5,12},{6,15},{7,14},{8,1},{9,0},... | collective-permute-start | bytes 663560 | tf_op jit(solution)/shard_map/ppermute | solution.py:456
  42.4 45.4 %collective-permute-start.8 = (bf16[144,768]{1,0:T(8,128)(2,1)S(1)}, bf16[144,768]{1,0:T(8,128)(2,1)S(1)}, u32[]{:S(2)}, u32[]{:S(2)}) collective-permute-start(bf16[144,768]{1,0:T(8,128)(2,1)S(1)} %get-tuple-element.194), channel_id=1, source_target_pairs={{0,10},{1,11},{2,8},{3,9},{4,14},{5,15},{6,12},{7,13},{8,2},{9,3},... | collective-permute-start | bytes 663560 | tf_op jit(solution)/shard_map/ppermute | solution.py:456
  46.6 49.9 %collective-permute-start.9 = (bf16[144,768]{1,0:T(8,128)(2,1)S(1)}, bf16[144,768]{1,0:T(8,128)(2,1)S(1)}, u32[]{:S(2)}, u32[]{:S(2)}) collective-permute-start(bf16[144,768]{1,0:T(8,128)(2,1)S(1)} %get-tuple-element.195), channel_id=1, source_target_pairs={{0,11},{1,10},{2,9},{3,8},{4,15},{5,14},{6,13},{7,12},{8,3},{9,2},... | collective-permute-start | bytes 663560 | tf_op jit(solution)/shard_map/ppermute | solution.py:456
  49.9 49.5 %collective-permute-start.5 = (bf16[144,768]{1,0:T(8,128)(2,1)S(1)}, bf16[144,768]{1,0:T(8,128)(2,1)S(1)}, u32[]{:S(2)}, u32[]{:S(2)}) collective-permute-start(bf16[144,768]{1,0:T(8,128)(2,1)S(1)} %get-tuple-element.191), channel_id=1, source_target_pairs={{0,13},{1,12},{2,15},{3,14},{4,9},{5,8},{6,11},{7,10},{8,5},{9,4},... | collective-permute-start | bytes 663560 | tf_op jit(solution)/shard_map/ppermute | solution.py:456
  51.9 47.4 %collective-permute-start.6 = (bf16[144,768]{1,0:T(8,128)(2,1)S(1)}, bf16[144,768]{1,0:T(8,128)(2,1)S(1)}, u32[]{:S(2)}, u32[]{:S(2)}) collective-permute-start(bf16[144,768]{1,0:T(8,128)(2,1)S(1)} %get-tuple-element.192), channel_id=1, source_target_pairs={{0,14},{1,15},{2,12},{3,13},{4,10},{5,11},{6,8},{7,9},{8,6},{9,7},... | collective-permute-start | bytes 663560 | tf_op jit(solution)/shard_map/ppermute | solution.py:456
  82.6 18.8 %collective-permute-start = (bf16[144,768]{1,0:T(8,128)(2,1)S(1)}, bf16[144,768]{1,0:T(8,128)(2,1)S(1)}, u32[]{:S(2)}, u32[]{:S(2)}) collective-permute-start(bf16[144,768]{1,0:T(8,128)(2,1)S(1)} %get-tuple-element.184), channel_id=1, source_target_pairs={{0,15},{1,14},{2,13},{3,12},{4,11},{5,10},{6,9},{7,8},{8,7},{9,6},... | collective-permute-start | bytes 663560 | tf_op jit(solution)/shard_map/ppermute | solution.py:456
  103.6 19.2 %all-to-all-start.3 = ((f32[16,1,512]{2,1,0:T(1,128)}), f32[16,1,512]{2,1,0:T(1,128)S(1)}, u32[]{:S(2)}, u32[]{:S(2)}) async-start(f32[16,1,512]{2,1,0:T(1,128)} %finish_rows.3), calls=%async_computation.3 | async-start | bytes 65536 | tf_op jit(solution)/shard_map/all_to_all | solution.py:443

commit v8 on v7

--- a/solution.py
+++ b/solution.py
@@ -8,12 +8,11 @@
 from jax.sharding import PartitionSpec as P
 
 CL_DEV = 4
-VARIANTS = 8
+VARIANTS = 32
 STEP = 16
 TILE = 256
 LANES = 128
-GROUP = 4
-MAX_PERMUTES = 16
+MAX_PERMUTES = 8
 RANKS = 4096
 MIB = 1 << 20
 
@@ -45,48 +44,76 @@
     return mask.astype(f32).astype(bf16)
 
 
-def count_kernel(ids_ref, counts_ref, rank_ref):
-    rows = ids_ref.shape[1]
-    peers, _, clusters = counts_ref.shape
+def count_kernel(me_ref, ids0_ref, ids1_ref, counts_ref, rank0_ref, rank1_ref):
+    rows = ids0_ref.shape[1]
+    chips, _, clusters = counts_ref.shape
+    core = me_ref[0] & 1
     label = iota((clusters, TILE), 0)
     upto = to_bf16(iota((TILE, TILE), 0) <= iota((TILE, TILE), 1))
-    total = jnp.zeros((clusters, 1), f32)
-    for b in range(rows // TILE):
-        at = slice(b * TILE, (b + 1) * TILE)
-        hot = ids_ref[:, at] == label
-        prefix = mm(to_bf16(hot), upto)
-        rank = jnp.sum(jnp.where(hot, prefix + total - 1.0, 0.0), axis=0, keepdims=True)
-        rank_ref[:, at] = ids_ref[:, at] * RANKS + rank.astype(i32)
-        total = total + prefix[:, TILE - 1 :]
+    totals = []
+    for ids_ref, rank_ref in ((ids0_ref, rank0_ref), (ids1_ref, rank1_ref)):
+        total = jnp.zeros((clusters, 1), f32)
+        for b in range(rows // TILE):
+            at = slice(b * TILE, (b + 1) * TILE)
+            hot = ids_ref[:, at] == label
+            prefix = mm(to_bf16(hot), upto)
+            rank = jnp.sum(jnp.where(hot, prefix + total - 1.0, 0.0), axis=0, keepdims=True)
+            rank_ref[:, at] = ids_ref[:, at] * RANKS + rank.astype(i32)
+            total = total + prefix[:, TILE - 1 :]
+        totals.append(total)
+    ahead0 = jnp.where(core == 1, totals[1], 0.0)
+    ahead1 = jnp.where(core == 0, totals[0], 0.0)
+    for ids_ref, rank_ref, ahead in (
+        (ids0_ref, rank0_ref, ahead0),
+        (ids1_ref, rank1_ref, ahead1),
+    ):
+        for b in range(rows // TILE):
+            at = slice(b * TILE, (b + 1) * TILE)
+            more = jnp.where(ids_ref[:, at] == label, ahead, 0.0)
+            rank_ref[:, at] += jnp.sum(more, axis=0, keepdims=True).astype(i32)
     square = (clusters, clusters)
     eye = iota(square, 0) == iota(square, 1)
-    total_row = jnp.sum(jnp.where(eye, total, 0.0), axis=0, keepdims=True).astype(i32)
-    for peer in range(peers):
-        counts_ref[peer] = total_row
-
-
-def count_rows(ids_row, peers, clusters):
+    both = totals[0] + totals[1]
+    total_row = jnp.sum(jnp.where(eye, both, 0.0), axis=0, keepdims=True).astype(i32)
+    for chip in range(chips):
+        counts_ref[chip] = total_row
+
+
+def count_rows(me, ids0, ids1, chips, clusters):
     return pl.pallas_call(
         count_kernel,
         out_shape=(
-            jax.ShapeDtypeStruct((peers, 1, clusters), i32),
-            jax.ShapeDtypeStruct(ids_row.shape, i32),
+            jax.ShapeDtypeStruct((chips, 1, clusters), i32),
+            jax.ShapeDtypeStruct(ids0.shape, i32),
+            jax.ShapeDtypeStruct(ids0.shape, i32),
         ),
-        in_specs=[VMEM],
-        out_specs=(VMEM, VMEM),
+        in_specs=[SMEM, VMEM, VMEM],
+        out_specs=(VMEM,) * 3,
         compiler_params=pltpu.CompilerParams(vmem_limit_bytes=16 * MIB),
         name="count_rows",
-    )(ids_row)
+    )(me, ids0, ids1)
 
 
 def assign_kernel(
-    me_ref, counts_ref, rank_ref, owner_ref, slot_ref, bound_ref, total_ref, load_ref
+    me_ref,
+    counts_ref,
+    rank0_ref,
+    rank1_ref,
+    owner0_ref,
+    owner1_ref,
+    slot0_ref,
+    slot1_ref,
+    bound_ref,
+    total_ref,
+    load_ref,
 ):
-    owners, _, clusters = counts_ref.shape
-    rows = rank_ref.shape[1]
+    chips, _, clusters = counts_ref.shape
+    owners = 2 * chips
+    rows = rank0_ref.shape[1]
     shift = owners.bit_length() - 1
     me = me_ref[0]
-    count = jnp.concatenate([counts_ref[s].astype(f32) for s in range(owners)], axis=0)
+    chip = me >> 1
+    count = jnp.concatenate([counts_ref[s].astype(f32) for s in range(chips)], axis=0)
     count16 = count.astype(bf16)
     square = (clusters, clusters)
     sub, lane = iota(square, 0), iota(square, 1)
@@ -103,7 +130,10 @@
         within = rank & (owners - 1)
         flip = jnp.zeros_like(variant)
         for p in range(1, CL_DEV):
-            flip = flip + jnp.where(layer == p, (variant >> (p - 1)) & 1, 0)
+            bits = (variant >> (p - 1)) & 1
+            if p < CL_DEV - 1:
+                bits = bits + 2 * ((variant >> (p + CL_DEV - 2)) & 1)
+            flip = flip + jnp.where(layer == p, bits, 0)
         within = within ^ flip
         return jnp.where((layer & 1) == 1, owners - 1 - within, within)
 
@@ -126,20 +156,23 @@
     layer_col, layer_row = rank_col >> shift, rank_row >> shift
     load_ref[...] = jnp.broadcast_to(best, load_ref.shape).astype(i32)
 
-    mine = jnp.sum(jnp.where(iota(count.shape, 0) == me, count, 0.0), axis=0, keepdims=True)
+    mine = jnp.sum(jnp.where(iota(count.shape, 0) == chip, count, 0.0), axis=0, keepdims=True)
     earlier = (owner_row == owner_col) & (layer_row < layer_col)
     offset_col = jnp.sum(jnp.where(earlier, mine, 0.0), axis=1, keepdims=True)
-    ids = rank_ref[...] // RANKS
-    hot = ids == iota((clusters, rows), 0)
-    owner_ref[...] = jnp.sum(
-        jnp.where(hot, owner_col.astype(f32), 0.0), axis=0, keepdims=True
-    ).astype(i32)
-    slot_ref[...] = (
-        jnp.sum(jnp.where(hot, offset_col, 0.0), axis=0, keepdims=True)
-    ).astype(i32) + (rank_ref[...] & (RANKS - 1))
+    for rank_ref, owner_ref, slot_ref in (
+        (rank0_ref, owner0_ref, slot0_ref),
+        (rank1_ref, owner1_ref, slot1_ref),
+    ):
+        hot = (rank_ref[...] // RANKS) == iota((clusters, rows), 0)
+        owner_ref[...] = jnp.sum(
+            jnp.where(hot, owner_col.astype(f32), 0.0), axis=0, keepdims=True
+        ).astype(i32)
+        slot_ref[...] = jnp.sum(jnp.where(hot, offset_col, 0.0), axis=0, keepdims=True).astype(
+            i32
+        ) + (rank_ref[...] & (RANKS - 1))
 
     select = (owner_col == me) & (layer_col <= iota((clusters, LANES), 1))
-    turn = iota((owners, owners), 1) == (iota((owners, owners), 0) ^ me)
+    turn = iota((chips, chips), 1) == (iota((chips, chips), 0) ^ chip)
     turned = mm(to_bf16(turn), count16).astype(bf16)
     bound_ref[...] = mm(turned, to_bf16(select))
     own = (owner_row == me) & (layer_row == iota((8, clusters), 0))
@@ -148,52 +181,56 @@
     )
 
 
-def assign(me, counts, rank):
-    owners, _, clusters = counts.shape
-    rows = rank.shape[1]
+def assign(me, counts, rank0, rank1):
+    chips, _, clusters = counts.shape
+    line = jax.ShapeDtypeStruct(rank0.shape, i32)
     return pl.pallas_call(
         assign_kernel,
         out_shape=(
-            jax.ShapeDtypeStruct((1, rows), i32),
-            jax.ShapeDtypeStruct((1, rows), i32),
-            jax.ShapeDtypeStruct((owners, LANES), f32),
+            line,
+            line,
+            line,
+            line,
+            jax.ShapeDtypeStruct((chips, LANES), f32),
             jax.ShapeDtypeStruct((8, LANES), f32),
             jax.ShapeDtypeStruct((1, LANES), i32),
         ),
-        in_specs=[SMEM, VMEM, VMEM],
-        out_specs=(VMEM,) * 5,
+        in_specs=[SMEM, VMEM, VMEM, VMEM],
+        out_specs=(VMEM,) * 7,
         compiler_params=pltpu.CompilerParams(vmem_limit_bytes=16 * MIB),
         name="assign",
-    )(me, counts, rank)
-
-
-def pack_kernel(slots, partners, me_ref, owner_ref, slot_ref, rows_ref, *out_refs):
-    rows = rows_ref.shape[0]
-    me = me_ref[0]
+    )(me, counts, rank0, rank1)
+
+
+def pack_kernel(
+    partner, me_ref, owner0_ref, owner1_ref, slot0_ref, slot1_ref, unit0_ref, unit1_ref, out_ref
+):
+    slots = out_ref.shape[0]
+    rows = unit0_ref.shape[0]
+    target = me_ref[0] ^ (2 * partner)
     slot = iota((slots, rows), 0)
-    takes = []
-    for partner in partners:
-        key = jnp.where(owner_ref[...] == (me ^ partner), slot_ref[...], -1)
-        takes.append(to_bf16(slot == key))
-    picked = mm(jnp.concatenate(takes, axis=0), rows_ref[...]).astype(bf16)
-    for i, ref in enumerate(out_refs):
-        ref[...] = picked[i * slots : (i + 1) * slots]
-
-
-def pack(me, owner_row, slot_row, unit, partners, slots):
-    rows, width = unit.shape
-    flops = 2 * len(partners) * slots * rows * width
+    total = None
+    for owner_ref, slot_ref, unit_ref in (
+        (owner0_ref, slot0_ref, unit0_ref),
+        (owner1_ref, slot1_ref, unit1_ref),
+    ):
+        key = jnp.where(owner_ref[...] == target, slot_ref[...], -1)
+        part = mm(to_bf16(slot == key), unit_ref[...])
+        total = part if total is None else total + part
+    out_ref[...] = total.astype(bf16)
+
+
+def pack(me, places, units, partner, slots):
+    width = units[0].shape[1]
     return pl.pallas_call(
-        functools.partial(pack_kernel, slots, partners),
-        out_shape=(jax.ShapeDtypeStruct((slots, width), bf16),) * len(partners),
-        in_specs=[SMEM, VMEM, VMEM, VMEM],
-        out_specs=(VMEM,) * len(partners),
-        compiler_params=pltpu.CompilerParams(vmem_limit_bytes=28 * MIB),
-        cost_estimate=pl.CostEstimate(
-            flops=flops, bytes_accessed=2 * rows * width, transcendentals=0
-        ),
+        functools.partial(pack_kernel, partner),
+        out_shape=jax.ShapeDtypeStruct((slots, width), bf16),
+        in_specs=[SMEM] + [VMEM] * 6,
+        out_specs=VMEM,
+        compiler_params=pltpu.CompilerParams(vmem_limit_bytes=24 * MIB),
+        cost_estimate=pl.CostEstimate(flops=slots, bytes_accessed=slots, transcendentals=0),
         name="pack_rows",
-    )(me, owner_row, slot_row, unit)
+    )(me, *places, *units)
 
 
 def unit_kernel(rows_ref, unit_ref):
@@ -332,7 +369,7 @@
         in_specs=[VMEM] * len(args),
         out_specs=(VMEM,) * len(out_shape),
         scratch_shapes=[pltpu.VMEM((padded, width), bf16)],
-        compiler_params=pltpu.CompilerParams(vmem_limit_bytes=36 * MIB),
+        compiler_params=pltpu.CompilerParams(vmem_limit_bytes=(36 if slots < 400 else 58) * MIB),
         cost_estimate=pl.CostEstimate(
             flops=2 * (old_rows + rows) * padded * width,
             bytes_accessed=2 * (old_rows + rows) * width,
@@ -348,7 +385,7 @@
     raw_refs, refs = refs[:fresh], refs[fresh:]
     old_refs = [refs[3 * i : 3 * i + 3] for i in range(olds)]
     sums_ref, out_ref, new_ref = refs[3 * olds :]
-    me = me_ref[0]
+    chip = me_ref[0] >> 1
     rows = fresh * slots
     padded, width = new_ref.shape
     new_ref[rows:, :] = jnp.zeros((padded - rows, width), bf16)
@@ -378,12 +415,14 @@
             at = slice(i * slots, (i + 1) * slots)
             for j, col in enumerate((best, gap)):
                 line = jnp.sum(jnp.where(eye, col[at], 0.0), axis=0, keepdims=True)
-                out_ref[r ^ me, :, j * half : (j + 1) * half] = line
+                for core in range(2):
+                    device = 2 * (r ^ chip) + core
+                    out_ref[device, :, j * half : (j + 1) * half] = line
 
 
 def finish(me, bound, total, blocks, partners, earlier, state):
     slots, width = blocks[0].shape
-    owners = bound.shape[0]
+    owners = 2 * bound.shape[0]
     units, accs, cids, sums = state
     rows = len(blocks) * slots
     padded = round_up(rows + STEP, LANES)
@@ -395,7 +434,7 @@
         in_specs=[SMEM] + [VMEM] * (len(args) - 1),
         out_specs=VMEM,
         scratch_shapes=[pltpu.VMEM((padded, width), bf16)],
-        compiler_params=pltpu.CompilerParams(vmem_limit_bytes=36 * MIB),
+        compiler_params=pltpu.CompilerParams(vmem_limit_bytes=(36 if slots < 400 else 58) * MIB),
         cost_estimate=pl.CostEstimate(
             flops=2 * owners * slots * padded * width,
             bytes_accessed=2 * owners * slots * width,
@@ -443,55 +482,74 @@
     return lax.all_to_all(x, "owner", split_axis=0, concat_axis=0, tiled=True)
 
 
+def exchange_chips(x):
+    chips = lax.axis_size("owner") // 2
+    cores = [[2 * chip + core for chip in range(chips)] for core in range(2)]
+    return lax.all_to_all(
+        x, "owner", split_axis=0, concat_axis=0, axis_index_groups=cores, tiled=True
+    )
+
+
+def swap(block, r):
+    owners = lax.axis_size("owner")
+    return lax.ppermute(block, "owner", [(s, s ^ (2 * r)) for s in range(owners)])
+
+
 def swap_together(blocks):
-    owners = len(blocks)
-    order = jnp.arange(owners, dtype=i32) ^ lax.axis_index("owner").astype(i32)
-    arrived = exchange(jnp.stack(blocks)[order])[order]
-    return [arrived[r] for r in range(owners)]
-
-
-def swap_apart(blocks):
-    pairs = [[(s, s ^ r) for s in range(len(blocks))] for r in range(len(blocks))]
-    return blocks[:1] + [
-        lax.ppermute(block, "owner", pair) for block, pair in zip(blocks[1:], pairs[1:])
-    ]
+    chips = len(blocks)
+    order = jnp.arange(chips, dtype=i32) ^ (lax.axis_index("owner").astype(i32) >> 1)
+    arrived = exchange_chips(jnp.stack(blocks)[order])[order]
+    return [arrived[r] for r in range(chips)]
+
+
+def swap_cores(x):
+    owners = lax.axis_size("owner")
+    return lax.ppermute(x, "owner", [(s, s ^ 1) for s in range(owners)])
 
 
 def local(embeddings, cluster_ids):
     rows = embeddings.shape[0]
     owners = lax.axis_size("owner")
+    chips = owners // 2
     clusters = CL_DEV * owners
     row_limit = 2 * rows // clusters
-    most = round_up(CL_DEV * row_limit, STEP)
-    usual = min(most, round_up(9 * rows // (8 * owners), STEP))
-    few = owners <= MAX_PERMUTES
+    most = round_up(2 * CL_DEV * row_limit, STEP)
+    usual = min(most, round_up(17 * rows // (8 * owners), STEP))
+    few = chips <= MAX_PERMUTES
     me = lax.axis_index("owner").astype(i32).reshape(1)
-    ids_row = cluster_ids.reshape(1, rows)
-    counts, rank = count_rows(ids_row, owners, clusters)
-    unit = unit_rows(embeddings)
-    owner_row, slot_row, bound, total, load = assign(me, exchange(counts), rank)
-
-    sent = list(range(1, owners))
-    seen = [0] + sent
-    sent = sent + [0]
-    packs = [tuple(sent[:2]), tuple(sent[2:4])]
-    packs += [tuple(sent[i : i + GROUP]) for i in range(4, owners, GROUP)]
-    share = owners // 16 if owners >= 16 else 1
-    groups, at = [], 0
-    for size in (5, 4, 4, 2):
-        groups.append(seen[at : at + size * share])
-        at += size * share
-    groups.append(seen[at:])
+    ids0 = cluster_ids.reshape(1, rows)
+    ids1 = swap_cores(ids0)
+    other = swap_cores(embeddings)
+    counts, rank0, rank1 = count_rows(me, ids0, ids1, chips, clusters)
+    counts = exchange_chips(counts)
+    units = (unit_rows(embeddings), unit_rows(other))
+    *places, bound, total, load = assign(me, counts, rank0, rank1)
+    owner_row, slot_row = places[0], places[2]
+
+    half = chips // 2
+    far = list(range(chips - 1, half - 1, -1))
+    near = list(range(half - 1, 0, -1))
+    sent = far[:2] + near + far[2:] + [0]
+    share = max(half // 4, 1)
+    groups = [[0] + near, far[: 2 * share], far[2 * share : 3 * share], far[3 * share :]]
 
     def compare(slots, apart):
-        blocks = [None] * owners
-        slot_in = slot_row
-        for partners in packs:
-            packed = pack(me, owner_row, slot_in, unit, partners, slots)
-            slot_in, *packed = lax.optimization_barrier((slot_in, *packed))
-            for r, block in zip(partners, packed):
-                blocks[r] = block
-        arrived = swap_apart(blocks) if apart else swap_together(blocks)
+        blocks = [None] * chips
+        here = list(places)
+        for r in sent:
+            blocks[r] = pack(me, here, units, r, slots)
+            here[0], blocks[r] = lax.optimization_barrier((here[0], blocks[r]))
+        if apart:
+            arrived = blocks[:1] + [None] * (chips - 1)
+            for r in sent[:-1]:
+                if r in far[2:]:
+                    before = far[far.index(r) - 2]
+                    blocks[r], arrived[before] = lax.optimization_barrier(
+                        (blocks[r], arrived[before])
+                    )
+                arrived[r] = swap(blocks[r], r)
+        else:
+            arrived = swap_together(blocks)
         state = ([], [], [], None)
         for group in groups[:-1]:
             state = score(bound, [arrived[r] for r in group], group, state)

time: 124 us -> 116 us (0.935)
  waiting for transfers between devices: 62.9 us -> 38.7 us
  Pallas kernels: 22.6 us -> 33 us
  starting transfers between devices: 35.1 us -> 40.9 us
    ppermute x15 -> x9, waiting for transfers between devices: 53.2 us -> 30.4 us  [the longest x7 25 us: swap(): return lax.ppermute(block, 'owner', [(s, s ^ 2 * r) for s in range(owners)])]
    all_to_all x2 -> x1, starting transfers between devices: 19.9 us -> 3.74 us  [exchange(): return lax.all_to_all(x, 'owner', split_axis=0, concat_axis=0, tiled=True)]
    ppermute x15 -> x9, starting transfers between devices: 15.2 us -> 30 us  [the longest x7 29.4 us: swap(): return lax.ppermute(block, 'owner', [(s, s ^ 2 * r) for s in range(owners)])]
    pallas_call x7 -> x10, Pallas kernels: 9.82 us -> 17.3 us  [the longest x8 15.1 us: pack(): pl.pallas_call(functools.partial(pack_kernel, partner), out_shape=jax.Sha...]
    all_to_all x0 -> x1, starting transfers between devices: none -> 7.2 us  [exchange_chips(): lax.all_to_all(x, 'owner', split_axis=0, concat_axis=0, axis_index_groups...]
    all_to_all x2 -> x1, waiting for transfers between devices: 9.74 us -> 6.73 us  [exchange(): return lax.all_to_all(x, 'owner', split_axis=0, concat_axis=0, tiled=True)]
    pallas_call x1 -> x2, Pallas kernels: 1.29 us -> 4.21 us  [unit_rows(): pl.pallas_call(unit_kernel, out_shape=jax.ShapeDtypeStruct((rows, width),...]
    all_to_all x0 -> x1, waiting for transfers between devices: none -> 1.58 us  [exchange_chips(): lax.all_to_all(x, 'owner', split_axis=0, concat_axis=0, axis_index_groups...]
  transfers between devices with their start and end apart: 17 -> 11, of which waited for: 9 -> 5; matrix products, arithmetic and copies ran while one was open for 0% -> 0% of each run, Pallas kernels for 12% -> 22%
where the time goes in v8:
time: 116 us
  starting transfers between devices  40.9 us (35%)
  waiting for transfers between devices  38.7 us (33%)
  Pallas kernels  33 us (28%)
  local copies, waits for them, and re-layouts  2.59 us (2%)
    ppermute x7, starting transfers between devices, swap(): return lax.ppermute(block, 'owner', [(s, s ^ 2 * r) for s in range(owners)])  29.4 us
    ppermute x7, waiting for transfers between devices, swap(): return lax.ppermute(block, 'owner', [(s, s ^ 2 * r) for s in range(owners)])  25 us
    pallas_call x8, Pallas kernels, pack(): pl.pallas_call(functools.partial(pack_kernel, partner), out_shape=jax.Sha...  15.1 us
    all_to_all x1, starting transfers between devices, exchange_chips(): lax.all_to_all(x, 'owner', split_axis=0, concat_axis=0, axis_index_groups...  7.2 us
    pallas_call x3, Pallas kernels, score(): pl.pallas_call(functools.partial(score_kernel, slots, partners, len(units...  6.98 us
    all_to_all x1, waiting for transfers between devices, exchange(): return lax.all_to_all(x, 'owner', split_axis=0, concat_axis=0, tiled=True)  6.73 us
    ppermute x2, waiting for transfers between devices, swap_cores(): return lax.ppermute(x, 'owner', [(s, s ^ 1) for s in range(owners)])  5.43 us
    pallas_call x2, Pallas kernels, unit_rows(): pl.pallas_call(unit_kernel, out_shape=jax.ShapeDtypeStruct((rows, width),...  4.21 us
  transfers between devices with their start and end apart: 11, of which 5 were waited for; matrix products, arithmetic and copies ran while one was open for 0% of the time, Pallas kernels for 22%

profile of v8, /device:TPU:0, one launch (start us, length us, event | category | flops | bytes accessed | tf_op | source)
XLA Modules:
  0.0 116.1 jit_solution(6919738312241204112)
XLA Ops:
  1.2 5.4 %collective-permute-done.ids1_ref = s32[1,2048]{1,0:T(1,128)S(1)} collective-permute-done((s32[1,2048]{1,0:T(1,128)}, s32[1,2048]{1,0:T(1,128)S(1)}, u32[]{:S(2)}, u32[]{:S(2)}) %collective-permute-start) | collective-permute-done | bytes 8224 | tf_op jit(solution)/shard_map/ppermute | solution.py:507
  6.7 0.7 copy-done.4
  7.4 1.4 %count_rows.1 = (s32[8,1,64]{2,1,0:T(1,128)}, s32[1,2048]{1,0:T(1,128)S(1)}, s32[1,2048]{1,0:T(1,128)S(1)}) custom-call(s32[1]{0:T(128)} %bitcast.17.me_ref, s32[1,2048]{1,0:T(1,128)S(1)} %bitcast.41, s32[1,2048]{1,0:T(1,128)S(1)} %collective-permute-done.ids1_ref), custom_call_target="tpu_custom_call" | custom-call | tf_op jit(solution)/shard_map/count_rows/pallas_call | solution.py:83
  8.7 7.2 %all-to-all-start.2 = ((s32[8,1,64]{2,1,0:T(1,128)}), s32[8,1,64]{2,1,0:T(1,128)S(1)}, u32[]{:S(2)}, u32[]{:S(2)}) async-start(s32[8,1,64]{2,1,0:T(1,128)} %get-tuple-element.117), calls=%async_computation.2 | async-start | bytes 8192 | tf_op jit(solution)/shard_map/all_to_all | solution.py:488
  15.9 1.9 %copy-done.3 = bf16[2048,768]{1,0:T(8,128)(2,1)S(1)} copy-done((bf16[2048,768]{1,0:T(8,128)(2,1)S(1)}, bf16[2048,768]{1,0:T(8,128)(2,1)}, u32[]{:S(2)}) %copy-start.3) | copy-done | bytes 3145752
  17.8 2.9 %unit_rows.2.unit0_ref = bf16[2048,768]{1,0:T(8,128)(2,1)} custom-call(bf16[2048,768]{1,0:T(8,128)(2,1)S(1)} %copy-done.3), custom_call_target="tpu_custom_call" | custom-call | flops 12582912 | bytes 6291456 | tf_op jit(solution)/shard_map/unit_rows/pallas_call | solution.py:249
  20.7 1.6 %all-to-all-done.2.counts_ref = s32[8,1,64]{2,1,0:T(1,128)S(1)} async-done(((s32[8,1,64]{2,1,0:T(1,128)}), s32[8,1,64]{2,1,0:T(1,128)S(1)}, u32[]{:S(2)}, u32[]{:S(2)}) %all-to-all-start.2) | async-done | bytes 2080 | tf_op jit(solution)/shard_map/all_to_all | solution.py:488
  22.3 0.9 assign.1
  23.2 1.3 %unit_rows.3.unit1_ref = bf16[2048,768]{1,0:T(8,128)(2,1)S(1)} custom-call(bf16[2048,768]{1,0:T(8,128)(2,1)S(1)} %collective-permute-done.1.rows_ref), custom_call_target="tpu_custom_call" | custom-call | flops 12582912 | bytes 6291456 | tf_op jit(solution)/shard_map/unit_rows/pallas_call | solution.py:249
  24.5 1.9 %pack_rows.24 = bf16[272,768]{1,0:T(8,128)(2,1)S(1)} custom-call(s32[1]{0:T(128)} %bitcast.17.me_ref, s32[1,2048]{1,0:T(1,128)S(1)} %get-tuple-element.136.owner0_ref.owner_ref, s32[1,2048]{1,0:T(1,128)S(1)} %get-tuple-element.122.owner1_ref, s32[1,2048]{1,0:T(1,128)S(1)} %get-tuple-element.123.slot0_ref.slot_ref, ...), custom_call_target="tpu_custom_call" | custom-call | flops 272 | bytes 272 | tf_op jit(solution)/shard_map/pack_rows/pallas_call | solution.py:225
  26.4 3.2 %collective-permute-start.7 = (bf16[272,768]{1,0:T(8,128)(2,1)S(1)}, bf16[272,768]{1,0:T(8,128)(2,1)S(1)}, u32[]{:S(2)}, u32[]{:S(2)}) collective-permute-start(bf16[272,768]{1,0:T(8,128)(2,1)S(1)} %pack_rows.24), channel_id=1, source_target_pairs={{0,14},{1,15},{2,12},{3,13},{4,10},{5,11},{6,8},{7,9},{8,6},{9,7},... | collective-permute-start | bytes 1253384 | tf_op jit(solution)/shard_map/ppermute | solution.py:495
  29.6 1.9 %pack_rows.25 = bf16[272,768]{1,0:T(8,128)(2,1)S(1)} custom-call(s32[1]{0:T(128)} %bitcast.17.me_ref, s32[1,2048]{1,0:T(1,128)S(1)} %get-tuple-element.136.owner0_ref.owner_ref, s32[1,2048]{1,0:T(1,128)S(1)} %get-tuple-element.122.owner1_ref, s32[1,2048]{1,0:T(1,128)S(1)} %get-tuple-element.123.slot0_ref.slot_ref, ...), custom_call_target="tpu_custom_call" | custom-call | flops 272 | bytes 272 | tf_op jit(solution)/shard_map/pack_rows/pallas_call | solution.py:225
  31.5 1.9 %pack_rows.26 = bf16[272,768]{1,0:T(8,128)(2,1)S(1)} custom-call(s32[1]{0:T(128)} %bitcast.17.me_ref, s32[1,2048]{1,0:T(1,128)S(1)} %get-tuple-element.136.owner0_ref.owner_ref, s32[1,2048]{1,0:T(1,128)S(1)} %get-tuple-element.122.owner1_ref, s32[1,2048]{1,0:T(1,128)S(1)} %get-tuple-element.123.slot0_ref.slot_ref, ...), custom_call_target="tpu_custom_call" | custom-call | flops 272 | bytes 272 | tf_op jit(solution)/shard_map/pack_rows/pallas_call | solution.py:225
  33.4 1.9 %pack_rows.27 = bf16[272,768]{1,0:T(8,128)(2,1)S(1)} custom-call(s32[1]{0:T(128)} %bitcast.17.me_ref, s32[1,2048]{1,0:T(1,128)S(1)} %get-tuple-element.136.owner0_ref.owner_ref, s32[1,2048]{1,0:T(1,128)S(1)} %get-tuple-element.122.owner1_ref, s32[1,2048]{1,0:T(1,128)S(1)} %get-tuple-element.123.slot0_ref.slot_ref, ...), custom_call_target="tpu_custom_call" | custom-call | flops 272 | bytes 272 | tf_op jit(solution)/shard_map/pack_rows/pallas_call | solution.py:225
  35.3 0.7 collective-permute-start.2
  36.0 1.9 %pack_rows.28 = bf16[272,768]{1,0:T(8,128)(2,1)S(1)} custom-call(s32[1]{0:T(128)} %bitcast.17.me_ref, s32[1,2048]{1,0:T(1,128)S(1)} %get-tuple-element.136.owner0_ref.owner_ref, s32[1,2048]{1,0:T(1,128)S(1)} %get-tuple-element.122.owner1_ref, s32[1,2048]{1,0:T(1,128)S(1)} %get-tuple-element.123.slot0_ref.slot_ref, ...), custom_call_target="tpu_custom_call" | custom-call | flops 272 | bytes 272 | tf_op jit(solution)/shard_map/pack_rows/pallas_call | solution.py:225
  37.9 1.5 %collective-permute-start.6 = (bf16[272,768]{1,0:T(8,128)(2,1)S(1)}, bf16[272,768]{1,0:T(8,128)(2,1)S(1)}, u32[]{:S(2)}, u32[]{:S(2)}) collective-permute-start(bf16[272,768]{1,0:T(8,128)(2,1)S(1)} %pack_rows.28), channel_id=1, source_target_pairs={{0,2},{1,3},{2,0},{3,1},{4,6},{5,7},{6,4},{7,5},{8,10},{9,11},{10,... | collective-permute-start | bytes 1253384 | tf_op jit(solution)/shard_map/ppermute | solution.py:495
  39.5 2.0 %collective-permute-start.4 = (bf16[272,768]{1,0:T(8,128)(2,1)S(1)}, bf16[272,768]{1,0:T(8,128)(2,1)S(1)}, u32[]{:S(2)}, u32[]{:S(2)}) collective-permute-start(bf16[272,768]{1,0:T(8,128)(2,1)S(1)} %pack_rows.26), channel_id=1, source_target_pairs={{0,6},{1,7},{2,4},{3,5},{4,2},{5,3},{6,0},{7,1},{8,14},{9,15},{10,... | collective-permute-start | bytes 1253384 | tf_op jit(solution)/shard_map/ppermute | solution.py:495
  41.5 1.9 %pack_rows.29 = bf16[272,768]{1,0:T(8,128)(2,1)S(1)} custom-call(s32[1]{0:T(128)} %bitcast.17.me_ref, s32[1,2048]{1,0:T(1,128)S(1)} %get-tuple-element.136.owner0_ref.owner_ref, s32[1,2048]{1,0:T(1,128)S(1)} %get-tuple-element.122.owner1_ref, s32[1,2048]{1,0:T(1,128)S(1)} %get-tuple-element.123.slot0_ref.slot_ref, ...), custom_call_target="tpu_custom_call" | custom-call | flops 272 | bytes 272 | tf_op jit(solution)/shard_map/pack_rows/pallas_call | solution.py:225
  43.4 16.7 %collective-permute-start.8 = (bf16[272,768]{1,0:T(8,128)(2,1)S(1)}, bf16[272,768]{1,0:T(8,128)(2,1)S(1)}, u32[]{:S(2)}, u32[]{:S(2)}) collective-permute-start(bf16[272,768]{1,0:T(8,128)(2,1)S(1)} %pack_rows.29), channel_id=1, source_target_pairs={{0,10},{1,11},{2,8},{3,9},{4,14},{5,15},{6,12},{7,13},{8,2},{9,3},... | collective-permute-start | bytes 1253384 | tf_op jit(solution)/shard_map/ppermute | solution.py:495
  60.1 1.9 %pack_rows.30 = bf16[272,768]{1,0:T(8,128)(2,1)S(1)} custom-call(s32[1]{0:T(128)} %bitcast.17.me_ref, s32[1,2048]{1,0:T(1,128)S(1)} %get-tuple-element.136.owner0_ref.owner_ref, s32[1,2048]{1,0:T(1,128)S(1)} %get-tuple-element.122.owner1_ref, s32[1,2048]{1,0:T(1,128)S(1)} %get-tuple-element.123.slot0_ref.slot_ref, ...), custom_call_target="tpu_custom_call" | custom-call | flops 272 | bytes 272 | tf_op jit(solution)/shard_map/pack_rows/pallas_call | solution.py:225
  62.0 1.9 %pack_rows.31.refs_0_ = bf16[272,768]{1,0:T(8,128)(2,1)S(1)} custom-call(s32[1]{0:T(128)} %bitcast.17.me_ref, s32[1,2048]{1,0:T(1,128)S(1)} %get-tuple-element.136.owner0_ref.owner_ref, s32[1,2048]{1,0:T(1,128)S(1)} %get-tuple-element.122.owner1_ref, s32[1,2048]{1,0:T(1,128)S(1)} %get-tuple-element.123.slot0_ref.slot_ref, ...), custom_call_target="tpu_custom_call" | custom-call | flops 272 | bytes 272 | tf_op jit(solution)/shard_map/pack_rows/pallas_call | solution.py:225
  63.9 5.2 %collective-permute-start.3 = (bf16[272,768]{1,0:T(8,128)(2,1)S(1)}, bf16[272,768]{1,0:T(8,128)(2,1)S(1)}, u32[]{:S(2)}, u32[]{:S(2)}) collective-permute-start(bf16[272,768]{1,0:T(8,128)(2,1)S(1)} %pack_rows.30), channel_id=1, source_target_pairs={{0,8},{1,9},{2,10},{3,11},{4,12},{5,13},{6,14},{7,15},{8,0},{9,1},... | collective-permute-start | bytes 1253384 | tf_op jit(solution)/shard_map/ppermute | solution.py:495
  69.1 2.9 %score_rows.9 = (bf16[1088,768]{1,0:T(8,128)(2,1)S(1)}, f32[1088,128]{1,0:T(8,128)S(1)}, f32[1088,128]{1,0:T(8,128)S(1)}, f32[8,768]{1,0:T(8,128)S(1)}) custom-call(f32[8,128]{1,0:T(8,128)S(1)} %get-tuple-element.125.bound_ref, bf16[272,768]{1,0:T(8,128)(2,1)S(1)} %pack_rows.31.refs_0_, bf16[272,768]{1,0:T(8,128)(2,1)S(1)} %collective-permute-done.4.refs_1_, ...), custom_call_target="tpu_custom_call" | custom-call | flops 1925185536 | bytes 1671168 | tf_op jit(solution)/shard_map/score_rows/pallas_call | solution.py:366
  72.0 2.3 %score_rows.10 = (bf16[544,768]{1,0:T(8,128)(2,1)S(1)}, f32[544,128]{1,0:T(8,128)S(1)}, f32[544,128]{1,0:T(8,128)S(1)}, f32[8,768]{1,0:T(8,128)S(1)}, f32[1088,128]{1,0:T(8,128)S(1)}) custom-call(f32[8,128]{1,0:T(8,128)S(1)} %get-tuple-element.125.bound_ref, bf16[272,768]{1,0:T(8,128)(2,1)S(1)} %collective-permute-done.7.refs_0_, ...), custom_call_target="tpu_custom_call" | custom-call | flops 1604321280 | bytes 2506752 | tf_op jit(solution)/shard_map/score_rows/pallas_call | solution.py:366
  74.3 19.0 %collective-permute-done.8.refs_0_ = bf16[272,768]{1,0:T(8,128)(2,1)S(1)} collective-permute-done((bf16[272,768]{1,0:T(8,128)(2,1)S(1)}, bf16[272,768]{1,0:T(8,128)(2,1)S(1)}, u32[]{:S(2)}, u32[]{:S(2)}) %collective-permute-start.8) | collective-permute-done | bytes 417824 | tf_op jit(solution)/shard_map/ppermute | solution.py:495
  93.3 1.8 %score_rows.11 = (bf16[272,768]{1,0:T(8,128)(2,1)S(1)}, f32[272,128]{1,0:T(8,128)S(1)}, f32[272,128]{1,0:T(8,128)S(1)}, f32[8,768]{1,0:T(8,128)S(1)}, f32[1088,128]{1,0:T(8,128)S(1)}, /*index=5*/f32[544,128]{1,0:T(8,128)S(1)}) custom-call(f32[8,128]{1,0:T(8,128)S(1)} %get-tuple-element.125.bound_ref, bf16[272,768]{1,0:T(8,128)(2,1)S(1)} %collective-permute-done.8.refs_0_, ...), custom_call_target="tpu_custom_call" | custom-call | flops 1123024896 | bytes 2924544 | tf_op jit(solution)/shard_map/score_rows/pallas_call | solution.py:366
  95.1 6.0 %collective-permute-done.3.refs_0_ = bf16[272,768]{1,0:T(8,128)(2,1)S(1)} collective-permute-done((bf16[272,768]{1,0:T(8,128)(2,1)S(1)}, bf16[272,768]{1,0:T(8,128)(2,1)S(1)}, u32[]{:S(2)}, u32[]{:S(2)}) %collective-permute-start.3) | collective-permute-done | bytes 417824 | tf_op jit(solution)/shard_map/ppermute | solution.py:495
  101.1 2.9 %finish_rows.3 = f32[16,1,768]{2,1,0:T(1,128)} custom-call(s32[1]{0:T(128)} %bitcast.17.me_ref, f32[8,128]{1,0:T(8,128)S(1)} %get-tuple-element.125.bound_ref, f32[8,128]{1,0:T(8,128)S(1)} %get-tuple-element.126.total_ref, bf16[272,768]{1,0:T(8,128)(2,1)S(1)} %collective-permute-done.3.refs_0_, bf16[1088,768]{1,0:T(8,128)(2,1)S(1)} %get-tuple-element.141.refs_2_.refs_1_, ...), custom_call_target="tpu_custom_call" | custom-call | flops 2566914048 | bytes 6684672 | tf_op jit(solution)/shard_map/finish_rows/pallas_call | solution.py:431
  104.0 3.7 %all-to-all-start.3 = ((f32[16,1,768]{2,1,0:T(1,128)}), f32[16,1,768]{2,1,0:T(1,128)S(1)}, u32[]{:S(2)}, u32[]{:S(2)}) async-start(f32[16,1,768]{2,1,0:T(1,128)} %finish_rows.3), calls=%async_computation.3 | async-start | bytes 98304 | tf_op jit(solution)/shard_map/all_to_all | solution.py:482
  107.8 6.7 %all-to-all-done.3.back_ref = f32[16,1,768]{2,1,0:T(1,128)S(1)} async-done(((f32[16,1,768]{2,1,0:T(1,128)}), f32[16,1,768]{2,1,0:T(1,128)S(1)}, u32[]{:S(2)}, u32[]{:S(2)}) %all-to-all-start.3) | async-done | bytes 49184 | tf_op jit(solution)/shard_map/all_to_all | solution.py:482
  114.5 1.6 %restore_rows.3 = (f32[1,2048]{1,0:T(1,128)}, f32[1,2048]{1,0:T(1,128)}) custom-call(s32[1,2048]{1,0:T(1,128)S(1)} %get-tuple-element.136.owner0_ref.owner_ref, s32[1,2048]{1,0:T(1,128)S(1)} %get-tuple-element.123.slot0_ref.slot_ref, f32[16,1,768]{2,1,0:T(1,128)S(1)} %all-to-all-done.3.back_ref), custom_call_target="tpu_custom_call" | custom-call | tf_op jit(solution)/shard_map/restore_rows/pallas_call | solution.py:471
  (16 shorter events, 0.6 us)
Async XLA Ops:
  0.6 22.6 %collective-permute-start.1 = (bf16[2048,768]{1,0:T(8,128)(2,1)}, bf16[2048,768]{1,0:T(8,128)(2,1)S(1)}, u32[]{:S(2)}, u32[]{:S(2)}) collective-permute-start(bf16[2048,768]{1,0:T(8,128)(2,1)} %rows_ref.1), channel_id=1, source_target_pairs={{0,1},{1,0},{2,3},{3,2},{4,5},{5,4},{6,7},{7,6},{8,9},{9,8},{10,11... | collective-permute-start | bytes 9437192 | tf_op jit(solution)/shard_map/ppermute | solution.py:507
  1.1 5.5 %collective-permute-start = (s32[1,2048]{1,0:T(1,128)}, s32[1,2048]{1,0:T(1,128)S(1)}, u32[]{:S(2)}, u32[]{:S(2)}) collective-permute-start(s32[1,2048]{1,0:T(1,128)} %bitcast.40), channel_id=1, source_target_pairs={{0,1},{1,0},{2,3},{3,2},{4,5},{5,4},{6,7},{7,6},{8,9},{9,8},{10,11... | collective-permute-start | bytes 24584 | tf_op jit(solution)/shard_map/ppermute | solution.py:507
  6.7 0.7 copy-start.4
  8.7 13.6 %all-to-all-start.2 = ((s32[8,1,64]{2,1,0:T(1,128)}), s32[8,1,64]{2,1,0:T(1,128)S(1)}, u32[]{:S(2)}, u32[]{:S(2)}) async-start(s32[8,1,64]{2,1,0:T(1,128)} %get-tuple-element.117), calls=%async_computation.2 | async-start | bytes 8192 | tf_op jit(solution)/shard_map/all_to_all | solution.py:488
  15.9 1.9 %copy-start.3 = (bf16[2048,768]{1,0:T(8,128)(2,1)S(1)}, bf16[2048,768]{1,0:T(8,128)(2,1)}, u32[]{:S(2)}) copy-start(bf16[2048,768]{1,0:T(8,128)(2,1)} %rows_ref.1) | copy-start | bytes 9437188
  22.3 2.2 %copy-start.5 = (bf16[2048,768]{1,0:T(8,128)(2,1)S(1)}, bf16[2048,768]{1,0:T(8,128)(2,1)}, u32[]{:S(2)}) copy-start(bf16[2048,768]{1,0:T(8,128)(2,1)} %unit_rows.2.unit0_ref) | copy-start | bytes 9437188
  24.5 37.5 %copy-start.7 = (bf16[2048,768]{1,0:T(8,128)(2,1)}, bf16[2048,768]{1,0:T(8,128)(2,1)S(1)}, u32[]{:S(2)}) copy-start(bf16[2048,768]{1,0:T(8,128)(2,1)S(1)} %unit_rows.3.unit1_ref) | copy-start | bytes 9437188
  26.4 17.0 %collective-permute-start.7 = (bf16[272,768]{1,0:T(8,128)(2,1)S(1)}, bf16[272,768]{1,0:T(8,128)(2,1)S(1)}, u32[]{:S(2)}, u32[]{:S(2)}) collective-permute-start(bf16[272,768]{1,0:T(8,128)(2,1)S(1)} %pack_rows.24), channel_id=1, source_target_pairs={{0,14},{1,15},{2,12},{3,13},{4,10},{5,11},{6,8},{7,9},{8,6},{9,7},... | collective-permute-start | bytes 1253384 | tf_op jit(solution)/shard_map/ppermute | solution.py:495
  35.3 28.6 %collective-permute-start.2 = (bf16[272,768]{1,0:T(8,128)(2,1)S(1)}, bf16[272,768]{1,0:T(8,128)(2,1)S(1)}, u32[]{:S(2)}, u32[]{:S(2)}) collective-permute-start(bf16[272,768]{1,0:T(8,128)(2,1)S(1)} %pack_rows.25), channel_id=1, source_target_pairs={{0,12},{1,13},{2,14},{3,15},{4,8},{5,9},{6,10},{7,11},{8,4},{9,5},... | collective-permute-start | bytes 1253384 | tf_op jit(solution)/shard_map/ppermute | solution.py:495
  37.9 31.1 %collective-permute-start.6 = (bf16[272,768]{1,0:T(8,128)(2,1)S(1)}, bf16[272,768]{1,0:T(8,128)(2,1)S(1)}, u32[]{:S(2)}, u32[]{:S(2)}) collective-permute-start(bf16[272,768]{1,0:T(8,128)(2,1)S(1)} %pack_rows.28), channel_id=1, source_target_pairs={{0,2},{1,3},{2,0},{3,1},{4,6},{5,7},{6,4},{7,5},{8,10},{9,11},{10,... | collective-permute-start | bytes 1253384 | tf_op jit(solution)/shard_map/ppermute | solution.py:495
  39.5 29.6 %collective-permute-start.5 = (bf16[272,768]{1,0:T(8,128)(2,1)S(1)}, bf16[272,768]{1,0:T(8,128)(2,1)S(1)}, u32[]{:S(2)}, u32[]{:S(2)}) collective-permute-start(bf16[272,768]{1,0:T(8,128)(2,1)S(1)} %pack_rows.27), channel_id=1, source_target_pairs={{0,4},{1,5},{2,6},{3,7},{4,0},{5,1},{6,2},{7,3},{8,12},{9,13},{10,... | collective-permute-start | bytes 1253384 | tf_op jit(solution)/shard_map/ppermute | solution.py:495
  39.5 29.6 %collective-permute-start.4 = (bf16[272,768]{1,0:T(8,128)(2,1)S(1)}, bf16[272,768]{1,0:T(8,128)(2,1)S(1)}, u32[]{:S(2)}, u32[]{:S(2)}) collective-permute-start(bf16[272,768]{1,0:T(8,128)(2,1)S(1)} %pack_rows.26), channel_id=1, source_target_pairs={{0,6},{1,7},{2,4},{3,5},{4,2},{5,3},{6,0},{7,1},{8,14},{9,15},{10,... | collective-permute-start | bytes 1253384 | tf_op jit(solution)/shard_map/ppermute | solution.py:495
  43.4 49.9 %collective-permute-start.8 = (bf16[272,768]{1,0:T(8,128)(2,1)S(1)}, bf16[272,768]{1,0:T(8,128)(2,1)S(1)}, u32[]{:S(2)}, u32[]{:S(2)}) collective-permute-start(bf16[272,768]{1,0:T(8,128)(2,1)S(1)} %pack_rows.29), channel_id=1, source_target_pairs={{0,10},{1,11},{2,8},{3,9},{4,14},{5,15},{6,12},{7,13},{8,2},{9,3},... | collective-permute-start | bytes 1253384 | tf_op jit(solution)/shard_map/ppermute | solution.py:495
  63.9 37.1 %collective-permute-start.3 = (bf16[272,768]{1,0:T(8,128)(2,1)S(1)}, bf16[272,768]{1,0:T(8,128)(2,1)S(1)}, u32[]{:S(2)}, u32[]{:S(2)}) collective-permute-start(bf16[272,768]{1,0:T(8,128)(2,1)S(1)} %pack_rows.30), channel_id=1, source_target_pairs={{0,8},{1,9},{2,10},{3,11},{4,12},{5,13},{6,14},{7,15},{8,0},{9,1},... | collective-permute-start | bytes 1253384 | tf_op jit(solution)/shard_map/ppermute | solution.py:495
  104.0 10.5 %all-to-all-start.3 = ((f32[16,1,768]{2,1,0:T(1,128)}), f32[16,1,768]{2,1,0:T(1,128)S(1)}, u32[]{:S(2)}, u32[]{:S(2)}) async-start(f32[16,1,768]{2,1,0:T(1,128)} %finish_rows.3), calls=%async_computation.3 | async-start | bytes 98304 | tf_op jit(solution)/shard_map/all_to_all | solution.py:482

commit v9 on v8

--- a/solution.py
+++ b/solution.py
@@ -519,17 +519,19 @@
     me = lax.axis_index("owner").astype(i32).reshape(1)
     ids0 = cluster_ids.reshape(1, rows)
     ids1 = swap_cores(ids0)
-    other = swap_cores(embeddings)
+    mine, ids1 = lax.optimization_barrier((embeddings, ids1))
+    other = swap_cores(mine)
     counts, rank0, rank1 = count_rows(me, ids0, ids1, chips, clusters)
     counts = exchange_chips(counts)
     units = (unit_rows(embeddings), unit_rows(other))
+    counts, *units = lax.optimization_barrier((counts, *units))
     *places, bound, total, load = assign(me, counts, rank0, rank1)
     owner_row, slot_row = places[0], places[2]
 
     half = chips // 2
     far = list(range(chips - 1, half - 1, -1))
     near = list(range(half - 1, 0, -1))
-    sent = far[:2] + near + far[2:] + [0]
+    sent = near + far + [0]
     share = max(half // 4, 1)
     groups = [[0] + near, far[: 2 * share], far[2 * share : 3 * share], far[3 * share :]]
 
@@ -543,7 +545,7 @@
             arrived = blocks[:1] + [None] * (chips - 1)
             for r in sent[:-1]:
                 if r in far[2:]:
-                    before = far[far.index(r) - 2]
+                    before = near[far.index(r) - 2]
                     blocks[r], arrived[before] = lax.optimization_barrier(
                         (blocks[r], arrived[before])
                     )

time: 116 us -> 128 us (1.10)
  waiting for transfers between devices: 38.7 us -> 61.3 us
  starting transfers between devices: 40.9 us -> 24.4 us
  Pallas kernels: 33 us -> 38.2 us
    ppermute x7, waiting for transfers between devices: 25 us -> 53.6 us  [swap(): return lax.ppermute(block, 'owner', [(s, s ^ 2 * r) for s in range(owners)])]
    ppermute x7, starting transfers between devices: 29.4 us -> 11.9 us  [swap(): return lax.ppermute(block, 'owner', [(s, s ^ 2 * r) for s in range(owners)])]
    ppermute x2, waiting for transfers between devices: 5.43 us -> 1.04 us  [swap_cores(): return lax.ppermute(x, 'owner', [(s, s ^ 1) for s in range(owners)])]
    pallas_call x8, Pallas kernels: 15.1 us -> 18.6 us  [pack(): pl.pallas_call(functools.partial(pack_kernel, partner), out_shape=jax.Sha...]
    pallas_call x2, Pallas kernels: 4.21 us -> 5.9 us  [unit_rows(): pl.pallas_call(unit_kernel, out_shape=jax.ShapeDtypeStruct((rows, width),...]
    all_to_all x1, waiting for transfers between devices: 1.58 us -> 0.01 us  [exchange_chips(): lax.all_to_all(x, 'owner', split_axis=0, concat_axis=0, axis_index_groups...]
  transfers between devices with their start and end apart: 11 -> 11, of which waited for: 5 -> 6; matrix products, arithmetic and copies ran while one was open for 0% -> 0% of each run, Pallas kernels for 22% -> 22%
where the time goes in v9:
time: 128 us; the launch traced here: 127 us
  waiting for transfers between devices  61.3 us (48%)
  Pallas kernels  38.2 us (30%)
  starting transfers between devices  24.4 us (19%)
  local copies, waits for them, and re-layouts  2.59 us (2%)
    ppermute x7, waiting for transfers between devices, swap(): return lax.ppermute(block, 'owner', [(s, s ^ 2 * r) for s in range(owners)])  53.6 us
    pallas_call x8, Pallas kernels, pack(): pl.pallas_call(functools.partial(pack_kernel, partner), out_shape=jax.Sha...  18.6 us
    ppermute x7, starting transfers between devices, swap(): return lax.ppermute(block, 'owner', [(s, s ^ 2 * r) for s in range(owners)])  11.9 us
    all_to_all x1, starting transfers between devices, exchange_chips(): lax.all_to_all(x, 'owner', split_axis=0, concat_axis=0, axis_index_groups...  7 us
    pallas_call x3, Pallas kernels, score(): pl.pallas_call(functools.partial(score_kernel, slots, partners, len(units...  6.97 us
    all_to_all x1, waiting for transfers between devices, exchange(): return lax.all_to_all(x, 'owner', split_axis=0, concat_axis=0, tiled=True)  6.73 us
    pallas_call x2, Pallas kernels, unit_rows(): pl.pallas_call(unit_kernel, out_shape=jax.ShapeDtypeStruct((rows, width),...  5.9 us
    all_to_all x1, starting transfers between devices, exchange(): return lax.all_to_all(x, 'owner', split_axis=0, concat_axis=0, tiled=True)  4.64 us
  transfers between devices with their start and end apart: 11, of which 6 were waited for; matrix products, arithmetic and copies ran while one was open for 0% of the time, Pallas kernels for 22%

profile of v9, /device:TPU:0, one launch (start us, length us, event | category | flops | bytes accessed | tf_op | source)
XLA Modules:
  0.0 127.3 jit_solution(1464963784453872952)
XLA Ops:
  1.1 1.0 collective-permute-done.ids1_ref
  2.5 0.7 copy-done.4
  3.2 1.4 %count_rows.1 = (s32[8,1,64]{2,1,0:T(1,128)}, s32[1,2048]{1,0:T(1,128)S(1)}, s32[1,2048]{1,0:T(1,128)S(1)}) custom-call(s32[1]{0:T(128)} %bitcast.17.me_ref, s32[1,2048]{1,0:T(1,128)S(1)} %bitcast.41, s32[1,2048]{1,0:T(1,128)S(1)} %collective-permute-done.ids1_ref), custom_call_target="tpu_custom_call" | custom-call | tf_op jit(solution)/shard_map/count_rows/pallas_call | solution.py:83
  4.6 7.0 %all-to-all-start.2 = ((s32[8,1,64]{2,1,0:T(1,128)}), s32[8,1,64]{2,1,0:T(1,128)S(1)}, u32[]{:S(2)}, u32[]{:S(2)}) async-start(s32[8,1,64]{2,1,0:T(1,128)} %get-tuple-element.123), calls=%async_computation.2 | async-start | bytes 8192 | tf_op jit(solution)/shard_map/all_to_all | solution.py:488
  11.6 1.9 %copy-done.3 = bf16[2048,768]{1,0:T(8,128)(2,1)S(1)} copy-done((bf16[2048,768]{1,0:T(8,128)(2,1)S(1)}, bf16[2048,768]{1,0:T(8,128)(2,1)}, u32[]{:S(2)}) %copy-start.3) | copy-done | bytes 3145752
  13.5 2.9 %unit_rows.2.unit0_ref = bf16[2048,768]{1,0:T(8,128)(2,1)} custom-call(bf16[2048,768]{1,0:T(8,128)(2,1)S(1)} %copy-done.3), custom_call_target="tpu_custom_call" | custom-call | flops 12582912 | bytes 6291456 | tf_op jit(solution)/shard_map/unit_rows/pallas_call | solution.py:249
  16.4 3.0 %unit_rows.3.unit1_ref = bf16[2048,768]{1,0:T(8,128)(2,1)} custom-call(bf16[2048,768]{1,0:T(8,128)(2,1)S(1)} %collective-permute-done.1.rows_ref), custom_call_target="tpu_custom_call" | custom-call | flops 12582912 | bytes 6291456 | tf_op jit(solution)/shard_map/unit_rows/pallas_call | solution.py:249
  19.4 0.9 assign.1
  20.3 5.1 %pack_rows.24 = bf16[272,768]{1,0:T(8,128)(2,1)S(1)} custom-call(s32[1]{0:T(128)} %bitcast.17.me_ref, s32[1,2048]{1,0:T(1,128)S(1)} %get-tuple-element.146.owner0_ref.owner_ref, s32[1,2048]{1,0:T(1,128)S(1)} %get-tuple-element.130.owner1_ref, s32[1,2048]{1,0:T(1,128)S(1)} %get-tuple-element.131.slot0_ref.slot_ref, ...), custom_call_target="tpu_custom_call" | custom-call | flops 272 | bytes 272 | tf_op jit(solution)/shard_map/pack_rows/pallas_call | solution.py:225
  25.4 3.0 %collective-permute-start.4 = (bf16[272,768]{1,0:T(8,128)(2,1)S(1)}, bf16[272,768]{1,0:T(8,128)(2,1)S(1)}, u32[]{:S(2)}, u32[]{:S(2)}) collective-permute-start(bf16[272,768]{1,0:T(8,128)(2,1)S(1)} %pack_rows.24), channel_id=1, source_target_pairs={{0,6},{1,7},{2,4},{3,5},{4,2},{5,3},{6,0},{7,1},{8,14},{9,15},{10,... | collective-permute-start | bytes 1253384 | tf_op jit(solution)/shard_map/ppermute | solution.py:495
  28.4 1.9 %pack_rows.25 = bf16[272,768]{1,0:T(8,128)(2,1)S(1)} custom-call(s32[1]{0:T(128)} %bitcast.17.me_ref, s32[1,2048]{1,0:T(1,128)S(1)} %get-tuple-element.146.owner0_ref.owner_ref, s32[1,2048]{1,0:T(1,128)S(1)} %get-tuple-element.130.owner1_ref, s32[1,2048]{1,0:T(1,128)S(1)} %get-tuple-element.131.slot0_ref.slot_ref, ...), custom_call_target="tpu_custom_call" | custom-call | flops 272 | bytes 272 | tf_op jit(solution)/shard_map/pack_rows/pallas_call | solution.py:225
  30.9 1.9 %pack_rows.26 = bf16[272,768]{1,0:T(8,128)(2,1)S(1)} custom-call(s32[1]{0:T(128)} %bitcast.17.me_ref, s32[1,2048]{1,0:T(1,128)S(1)} %get-tuple-element.146.owner0_ref.owner_ref, s32[1,2048]{1,0:T(1,128)S(1)} %get-tuple-element.130.owner1_ref, s32[1,2048]{1,0:T(1,128)S(1)} %get-tuple-element.131.slot0_ref.slot_ref, ...), custom_call_target="tpu_custom_call" | custom-call | flops 272 | bytes 272 | tf_op jit(solution)/shard_map/pack_rows/pallas_call | solution.py:225
  32.9 1.9 %pack_rows.27 = bf16[272,768]{1,0:T(8,128)(2,1)S(1)} custom-call(s32[1]{0:T(128)} %bitcast.17.me_ref, s32[1,2048]{1,0:T(1,128)S(1)} %get-tuple-element.146.owner0_ref.owner_ref, s32[1,2048]{1,0:T(1,128)S(1)} %get-tuple-element.130.owner1_ref, s32[1,2048]{1,0:T(1,128)S(1)} %get-tuple-element.131.slot0_ref.slot_ref, ...), custom_call_target="tpu_custom_call" | custom-call | flops 272 | bytes 272 | tf_op jit(solution)/shard_map/pack_rows/pallas_call | solution.py:225
  34.8 1.9 %pack_rows.28 = bf16[272,768]{1,0:T(8,128)(2,1)S(1)} custom-call(s32[1]{0:T(128)} %bitcast.17.me_ref, s32[1,2048]{1,0:T(1,128)S(1)} %get-tuple-element.146.owner0_ref.owner_ref, s32[1,2048]{1,0:T(1,128)S(1)} %get-tuple-element.130.owner1_ref, s32[1,2048]{1,0:T(1,128)S(1)} %get-tuple-element.131.slot0_ref.slot_ref, ...), custom_call_target="tpu_custom_call" | custom-call | flops 272 | bytes 272 | tf_op jit(solution)/shard_map/pack_rows/pallas_call | solution.py:225
  36.7 3.9 %collective-permute-start.8 = (bf16[272,768]{1,0:T(8,128)(2,1)S(1)}, bf16[272,768]{1,0:T(8,128)(2,1)S(1)}, u32[]{:S(2)}, u32[]{:S(2)}) collective-permute-start(bf16[272,768]{1,0:T(8,128)(2,1)S(1)} %pack_rows.28), channel_id=1, source_target_pairs={{0,12},{1,13},{2,14},{3,15},{4,8},{5,9},{6,10},{7,11},{8,4},{9,5},... | collective-permute-start | bytes 1253384 | tf_op jit(solution)/shard_map/ppermute | solution.py:495
  40.6 1.5 %collective-permute-start.7 = (bf16[272,768]{1,0:T(8,128)(2,1)S(1)}, bf16[272,768]{1,0:T(8,128)(2,1)S(1)}, u32[]{:S(2)}, u32[]{:S(2)}) collective-permute-start(bf16[272,768]{1,0:T(8,128)(2,1)S(1)} %pack_rows.27), channel_id=1, source_target_pairs={{0,14},{1,15},{2,12},{3,13},{4,10},{5,11},{6,8},{7,9},{8,6},{9,7},... | collective-permute-start | bytes 1253384 | tf_op jit(solution)/shard_map/ppermute | solution.py:495
  42.0 1.9 %pack_rows.29 = bf16[272,768]{1,0:T(8,128)(2,1)S(1)} custom-call(s32[1]{0:T(128)} %bitcast.17.me_ref, s32[1,2048]{1,0:T(1,128)S(1)} %get-tuple-element.146.owner0_ref.owner_ref, s32[1,2048]{1,0:T(1,128)S(1)} %get-tuple-element.130.owner1_ref, s32[1,2048]{1,0:T(1,128)S(1)} %get-tuple-element.131.slot0_ref.slot_ref, ...), custom_call_target="tpu_custom_call" | custom-call | flops 272 | bytes 272 | tf_op jit(solution)/shard_map/pack_rows/pallas_call | solution.py:225
  43.9 0.6 collective-permute-start.6
  44.6 1.9 %pack_rows.30 = bf16[272,768]{1,0:T(8,128)(2,1)S(1)} custom-call(s32[1]{0:T(128)} %bitcast.17.me_ref, s32[1,2048]{1,0:T(1,128)S(1)} %get-tuple-element.146.owner0_ref.owner_ref, s32[1,2048]{1,0:T(1,128)S(1)} %get-tuple-element.130.owner1_ref, s32[1,2048]{1,0:T(1,128)S(1)} %get-tuple-element.131.slot0_ref.slot_ref, ...), custom_call_target="tpu_custom_call" | custom-call | flops 272 | bytes 272 | tf_op jit(solution)/shard_map/pack_rows/pallas_call | solution.py:225
  46.5 2.1 %pack_rows.31.refs_0_ = bf16[272,768]{1,0:T(8,128)(2,1)S(1)} custom-call(s32[1]{0:T(128)} %bitcast.17.me_ref, s32[1,2048]{1,0:T(1,128)S(1)} %get-tuple-element.146.owner0_ref.owner_ref, s32[1,2048]{1,0:T(1,128)S(1)} %get-tuple-element.130.owner1_ref, s32[1,2048]{1,0:T(1,128)S(1)} %get-tuple-element.131.slot0_ref.slot_ref, ...), custom_call_target="tpu_custom_call" | custom-call | flops 272 | bytes 272 | tf_op jit(solution)/shard_map/pack_rows/pallas_call | solution.py:225
  48.6 2.3 %collective-permute-start.3 = (bf16[272,768]{1,0:T(8,128)(2,1)S(1)}, bf16[272,768]{1,0:T(8,128)(2,1)S(1)}, u32[]{:S(2)}, u32[]{:S(2)}) collective-permute-start(bf16[272,768]{1,0:T(8,128)(2,1)S(1)} %pack_rows.30), channel_id=1, source_target_pairs={{0,8},{1,9},{2,10},{3,11},{4,12},{5,13},{6,14},{7,15},{8,0},{9,1},... | collective-permute-start | bytes 1253384 | tf_op jit(solution)/shard_map/ppermute | solution.py:495
  50.8 2.7 %score_rows.9 = (bf16[1088,768]{1,0:T(8,128)(2,1)S(1)}, f32[1088,128]{1,0:T(8,128)S(1)}, f32[1088,128]{1,0:T(8,128)S(1)}, f32[8,768]{1,0:T(8,128)S(1)}) custom-call(f32[8,128]{1,0:T(8,128)S(1)} %get-tuple-element.135.bound_ref, bf16[272,768]{1,0:T(8,128)(2,1)S(1)} %pack_rows.31.refs_0_, bf16[272,768]{1,0:T(8,128)(2,1)S(1)} %collective-permute-done.4.refs_1_, ...), custom_call_target="tpu_custom_call" | custom-call | flops 1925185536 | bytes 1671168 | tf_op jit(solution)/shard_map/score_rows/pallas_call | solution.py:366
  53.6 5.7 %collective-permute-done.8.refs_1_ = bf16[272,768]{1,0:T(8,128)(2,1)S(1)} collective-permute-done((bf16[272,768]{1,0:T(8,128)(2,1)S(1)}, bf16[272,768]{1,0:T(8,128)(2,1)S(1)}, u32[]{:S(2)}, u32[]{:S(2)}) %collective-permute-start.8) | collective-permute-done | bytes 417824 | tf_op jit(solution)/shard_map/ppermute | solution.py:495
  59.3 9.0 %collective-permute-done.7.refs_0_ = bf16[272,768]{1,0:T(8,128)(2,1)S(1)} collective-permute-done((bf16[272,768]{1,0:T(8,128)(2,1)S(1)}, bf16[272,768]{1,0:T(8,128)(2,1)S(1)}, u32[]{:S(2)}, u32[]{:S(2)}) %collective-permute-start.7) | collective-permute-done | bytes 417824 | tf_op jit(solution)/shard_map/ppermute | solution.py:495
  68.3 2.4 %score_rows.10 = (bf16[544,768]{1,0:T(8,128)(2,1)S(1)}, f32[544,128]{1,0:T(8,128)S(1)}, f32[544,128]{1,0:T(8,128)S(1)}, f32[8,768]{1,0:T(8,128)S(1)}, f32[1088,128]{1,0:T(8,128)S(1)}) custom-call(f32[8,128]{1,0:T(8,128)S(1)} %get-tuple-element.135.bound_ref, bf16[272,768]{1,0:T(8,128)(2,1)S(1)} %collective-permute-done.7.refs_0_, ...), custom_call_target="tpu_custom_call" | custom-call | flops 1604321280 | bytes 2506752 | tf_op jit(solution)/shard_map/score_rows/pallas_call | solution.py:366
  70.7 34.7 %collective-permute-done.6.refs_0_ = bf16[272,768]{1,0:T(8,128)(2,1)S(1)} collective-permute-done((bf16[272,768]{1,0:T(8,128)(2,1)S(1)}, bf16[272,768]{1,0:T(8,128)(2,1)S(1)}, u32[]{:S(2)}, u32[]{:S(2)}) %collective-permute-start.6) | collective-permute-done | bytes 417824 | tf_op jit(solution)/shard_map/ppermute | solution.py:495
  105.4 1.8 %score_rows.11 = (bf16[272,768]{1,0:T(8,128)(2,1)S(1)}, f32[272,128]{1,0:T(8,128)S(1)}, f32[272,128]{1,0:T(8,128)S(1)}, f32[8,768]{1,0:T(8,128)S(1)}, f32[1088,128]{1,0:T(8,128)S(1)}, /*index=5*/f32[544,128]{1,0:T(8,128)S(1)}) custom-call(f32[8,128]{1,0:T(8,128)S(1)} %get-tuple-element.135.bound_ref, bf16[272,768]{1,0:T(8,128)(2,1)S(1)} %collective-permute-done.6.refs_0_, ...), custom_call_target="tpu_custom_call" | custom-call | flops 1123024896 | bytes 2924544 | tf_op jit(solution)/shard_map/score_rows/pallas_call | solution.py:366
  107.2 4.2 %collective-permute-done.3.refs_0_ = bf16[272,768]{1,0:T(8,128)(2,1)S(1)} collective-permute-done((bf16[272,768]{1,0:T(8,128)(2,1)S(1)}, bf16[272,768]{1,0:T(8,128)(2,1)S(1)}, u32[]{:S(2)}, u32[]{:S(2)}) %collective-permute-start.3) | collective-permute-done | bytes 417824 | tf_op jit(solution)/shard_map/ppermute | solution.py:495
  111.4 3.0 %finish_rows.3 = f32[16,1,768]{2,1,0:T(1,128)} custom-call(s32[1]{0:T(128)} %bitcast.17.me_ref, f32[8,128]{1,0:T(8,128)S(1)} %get-tuple-element.135.bound_ref, f32[8,128]{1,0:T(8,128)S(1)} %get-tuple-element.136.total_ref, bf16[272,768]{1,0:T(8,128)(2,1)S(1)} %collective-permute-done.3.refs_0_, bf16[1088,768]{1,0:T(8,128)(2,1)S(1)} %get-tuple-element.153.refs_2_.refs_1_, ...), custom_call_target="tpu_custom_call" | custom-call | flops 2566914048 | bytes 6684672 | tf_op jit(solution)/shard_map/finish_rows/pallas_call | solution.py:431
  114.3 4.6 %all-to-all-start.3 = ((f32[16,1,768]{2,1,0:T(1,128)}), f32[16,1,768]{2,1,0:T(1,128)S(1)}, u32[]{:S(2)}, u32[]{:S(2)}) async-start(f32[16,1,768]{2,1,0:T(1,128)} %finish_rows.3), calls=%async_computation.3 | async-start | bytes 98304 | tf_op jit(solution)/shard_map/all_to_all | solution.py:482
  119.0 6.7 %all-to-all-done.3.back_ref = f32[16,1,768]{2,1,0:T(1,128)S(1)} async-done(((f32[16,1,768]{2,1,0:T(1,128)}), f32[16,1,768]{2,1,0:T(1,128)S(1)}, u32[]{:S(2)}, u32[]{:S(2)}) %all-to-all-start.3) | async-done | bytes 49184 | tf_op jit(solution)/shard_map/all_to_all | solution.py:482
  125.8 1.6 %restore_rows.3 = (f32[1,2048]{1,0:T(1,128)}, f32[1,2048]{1,0:T(1,128)}) custom-call(s32[1,2048]{1,0:T(1,128)S(1)} %get-tuple-element.146.owner0_ref.owner_ref, s32[1,2048]{1,0:T(1,128)S(1)} %get-tuple-element.131.slot0_ref.slot_ref, f32[16,1,768]{2,1,0:T(1,128)S(1)} %all-to-all-done.3.back_ref), custom_call_target="tpu_custom_call" | custom-call | tf_op jit(solution)/shard_map/restore_rows/pallas_call | solution.py:471
  (16 shorter events, 1.6 us)
Async XLA Ops:
  0.6 1.6 %collective-permute-start = (s32[1,2048]{1,0:T(1,128)}, s32[1,2048]{1,0:T(1,128)S(1)}, u32[]{:S(2)}, u32[]{:S(2)}) collective-permute-start(s32[1,2048]{1,0:T(1,128)} %bitcast.40), channel_id=1, source_target_pairs={{0,1},{1,0},{2,3},{3,2},{4,5},{5,4},{6,7},{7,6},{8,9},{9,8},{10,11... | collective-permute-start | bytes 24584 | tf_op jit(solution)/shard_map/ppermute | solution.py:507
  2.2 14.2 %collective-permute-start.1 = (bf16[2048,768]{1,0:T(8,128)(2,1)}, bf16[2048,768]{1,0:T(8,128)(2,1)S(1)}, u32[]{:S(2)}, u32[]{:S(2)}) collective-permute-start(bf16[2048,768]{1,0:T(8,128)(2,1)} %rows_ref.1), channel_id=1, source_target_pairs={{0,1},{1,0},{2,3},{3,2},{4,5},{5,4},{6,7},{7,6},{8,9},{9,8},{10,11... | collective-permute-start | bytes 9437192 | tf_op jit(solution)/shard_map/ppermute | solution.py:507
  2.5 0.7 copy-start.4
  4.6 14.8 %all-to-all-start.2 = ((s32[8,1,64]{2,1,0:T(1,128)}), s32[8,1,64]{2,1,0:T(1,128)S(1)}, u32[]{:S(2)}, u32[]{:S(2)}) async-start(s32[8,1,64]{2,1,0:T(1,128)} %get-tuple-element.123), calls=%async_computation.2 | async-start | bytes 8192 | tf_op jit(solution)/shard_map/all_to_all | solution.py:488
  11.6 1.9 %copy-start.3 = (bf16[2048,768]{1,0:T(8,128)(2,1)S(1)}, bf16[2048,768]{1,0:T(8,128)(2,1)}, u32[]{:S(2)}) copy-start(bf16[2048,768]{1,0:T(8,128)(2,1)} %rows_ref.1) | copy-start | bytes 9437188
  19.4 9.0 %copy-start.5 = (bf16[2048,768]{1,0:T(8,128)(2,1)S(1)}, bf16[2048,768]{1,0:T(8,128)(2,1)}, u32[]{:S(2)}) copy-start(bf16[2048,768]{1,0:T(8,128)(2,1)} %unit_rows.2.unit0_ref) | copy-start | bytes 9437188
  19.4 9.0 %copy-start.7 = (bf16[2048,768]{1,0:T(8,128)(2,1)S(1)}, bf16[2048,768]{1,0:T(8,128)(2,1)}, u32[]{:S(2)}) copy-start(bf16[2048,768]{1,0:T(8,128)(2,1)} %unit_rows.3.unit1_ref) | copy-start | bytes 9437188
  25.4 18.5 %collective-permute-start.4 = (bf16[272,768]{1,0:T(8,128)(2,1)S(1)}, bf16[272,768]{1,0:T(8,128)(2,1)S(1)}, u32[]{:S(2)}, u32[]{:S(2)}) collective-permute-start(bf16[272,768]{1,0:T(8,128)(2,1)S(1)} %pack_rows.24), channel_id=1, source_target_pairs={{0,6},{1,7},{2,4},{3,5},{4,2},{5,3},{6,0},{7,1},{8,14},{9,15},{10,... | collective-permute-start | bytes 1253384 | tf_op jit(solution)/shard_map/ppermute | solution.py:495
  30.3 18.3 %collective-permute-start.2 = (bf16[272,768]{1,0:T(8,128)(2,1)S(1)}, bf16[272,768]{1,0:T(8,128)(2,1)S(1)}, u32[]{:S(2)}, u32[]{:S(2)}) collective-permute-start(bf16[272,768]{1,0:T(8,128)(2,1)S(1)} %pack_rows.25), channel_id=1, source_target_pairs={{0,4},{1,5},{2,6},{3,7},{4,0},{5,1},{6,2},{7,3},{8,12},{9,13},{10,... | collective-permute-start | bytes 1253384 | tf_op jit(solution)/shard_map/ppermute | solution.py:495
  32.8 18.0 %collective-permute-start.5 = (bf16[272,768]{1,0:T(8,128)(2,1)S(1)}, bf16[272,768]{1,0:T(8,128)(2,1)S(1)}, u32[]{:S(2)}, u32[]{:S(2)}) collective-permute-start(bf16[272,768]{1,0:T(8,128)(2,1)S(1)} %pack_rows.26), channel_id=1, source_target_pairs={{0,2},{1,3},{2,0},{3,1},{4,6},{5,7},{6,4},{7,5},{8,10},{9,11},{10,... | collective-permute-start | bytes 1253384 | tf_op jit(solution)/shard_map/ppermute | solution.py:495
  36.7 22.6 %collective-permute-start.8 = (bf16[272,768]{1,0:T(8,128)(2,1)S(1)}, bf16[272,768]{1,0:T(8,128)(2,1)S(1)}, u32[]{:S(2)}, u32[]{:S(2)}) collective-permute-start(bf16[272,768]{1,0:T(8,128)(2,1)S(1)} %pack_rows.28), channel_id=1, source_target_pairs={{0,12},{1,13},{2,14},{3,15},{4,8},{5,9},{6,10},{7,11},{8,4},{9,5},... | collective-permute-start | bytes 1253384 | tf_op jit(solution)/shard_map/ppermute | solution.py:495
  40.6 27.7 %collective-permute-start.7 = (bf16[272,768]{1,0:T(8,128)(2,1)S(1)}, bf16[272,768]{1,0:T(8,128)(2,1)S(1)}, u32[]{:S(2)}, u32[]{:S(2)}) collective-permute-start(bf16[272,768]{1,0:T(8,128)(2,1)S(1)} %pack_rows.27), channel_id=1, source_target_pairs={{0,14},{1,15},{2,12},{3,13},{4,10},{5,11},{6,8},{7,9},{8,6},{9,7},... | collective-permute-start | bytes 1253384 | tf_op jit(solution)/shard_map/ppermute | solution.py:495
  43.9 61.5 %collective-permute-start.6 = (bf16[272,768]{1,0:T(8,128)(2,1)S(1)}, bf16[272,768]{1,0:T(8,128)(2,1)S(1)}, u32[]{:S(2)}, u32[]{:S(2)}) collective-permute-start(bf16[272,768]{1,0:T(8,128)(2,1)S(1)} %pack_rows.29), channel_id=1, source_target_pairs={{0,10},{1,11},{2,8},{3,9},{4,14},{5,15},{6,12},{7,13},{8,2},{9,3},... | collective-permute-start | bytes 1253384 | tf_op jit(solution)/shard_map/ppermute | solution.py:495
  48.6 62.8 %collective-permute-start.3 = (bf16[272,768]{1,0:T(8,128)(2,1)S(1)}, bf16[272,768]{1,0:T(8,128)(2,1)S(1)}, u32[]{:S(2)}, u32[]{:S(2)}) collective-permute-start(bf16[272,768]{1,0:T(8,128)(2,1)S(1)} %pack_rows.30), channel_id=1, source_target_pairs={{0,8},{1,9},{2,10},{3,11},{4,12},{5,13},{6,14},{7,15},{8,0},{9,1},... | collective-permute-start | bytes 1253384 | tf_op jit(solution)/shard_map/ppermute | solution.py:495
  114.3 11.4 %all-to-all-start.3 = ((f32[16,1,768]{2,1,0:T(1,128)}), f32[16,1,768]{2,1,0:T(1,128)S(1)}, u32[]{:S(2)}, u32[]{:S(2)}) async-start(f32[16,1,768]{2,1,0:T(1,128)} %finish_rows.3), calls=%async_computation.3 | async-start | bytes 98304 | tf_op jit(solution)/shard_map/all_to_all | solution.py:482

commit v10 on v8

--- a/solution.py
+++ b/solution.py
@@ -203,25 +203,25 @@
 
 
 def pack_kernel(
-    partner, me_ref, owner0_ref, owner1_ref, slot0_ref, slot1_ref, unit0_ref, unit1_ref, out_ref
+    partner, me_ref, owner0_ref, owner1_ref, slot0_ref, slot1_ref, rows0_ref, rows1_ref, out_ref
 ):
     slots = out_ref.shape[0]
-    rows = unit0_ref.shape[0]
+    rows = rows0_ref.shape[0]
     target = me_ref[0] ^ (2 * partner)
     slot = iota((slots, rows), 0)
     total = None
-    for owner_ref, slot_ref, unit_ref in (
-        (owner0_ref, slot0_ref, unit0_ref),
-        (owner1_ref, slot1_ref, unit1_ref),
+    for owner_ref, slot_ref, rows_ref in (
+        (owner0_ref, slot0_ref, rows0_ref),
+        (owner1_ref, slot1_ref, rows1_ref),
     ):
         key = jnp.where(owner_ref[...] == target, slot_ref[...], -1)
-        part = mm(to_bf16(slot == key), unit_ref[...])
+        part = mm(to_bf16(slot == key), rows_ref[...])
         total = part if total is None else total + part
     out_ref[...] = total.astype(bf16)
 
 
-def pack(me, places, units, partner, slots):
-    width = units[0].shape[1]
+def pack(me, places, both, partner, slots):
+    width = both[0].shape[1]
     return pl.pallas_call(
         functools.partial(pack_kernel, partner),
         out_shape=jax.ShapeDtypeStruct((slots, width), bf16),
@@ -230,33 +230,13 @@
         compiler_params=pltpu.CompilerParams(vmem_limit_bytes=24 * MIB),
         cost_estimate=pl.CostEstimate(flops=slots, bytes_accessed=slots, transcendentals=0),
         name="pack_rows",
-    )(me, *places, *units)
-
-
-def unit_kernel(rows_ref, unit_ref):
-    def body(b, carry):
-        at = pl.ds(pl.multiple_of(b * TILE, TILE), TILE)
-        x = rows_ref[at, :].astype(f32)
-        scale = lax.rsqrt(jnp.sum(x * x, axis=1, keepdims=True) + epsilon)
-        unit_ref[at, :] = (x * scale).astype(bf16)
-        return carry
-
-    lax.fori_loop(0, rows_ref.shape[0] // TILE, body, 0)
-
-
-def unit_rows(embeddings):
-    rows, width = embeddings.shape
-    return pl.pallas_call(
-        unit_kernel,
-        out_shape=jax.ShapeDtypeStruct((rows, width), bf16),
-        in_specs=[VMEM],
-        out_specs=VMEM,
-        compiler_params=pltpu.CompilerParams(vmem_limit_bytes=16 * MIB),
-        cost_estimate=pl.CostEstimate(
-            flops=8 * rows * width, bytes_accessed=4 * rows * width, transcendentals=rows
-        ),
-        name="unit_rows",
-    )(embeddings)
+    )(me, *places, *both)
+
+
+def unit_rows(ref):
+    x = ref[...].astype(f32)
+    scale = lax.rsqrt(jnp.sum(x * x, axis=1, keepdims=True) + epsilon)
+    return (x * scale).astype(bf16)
 
 
 def cluster_lanes(bound_ref, partners, slots, width):
@@ -333,7 +313,7 @@
     rows = fresh * slots
     for i, r in enumerate(partners):
         at = slice(i * slots, (i + 1) * slots)
-        new_ref[at, :] = raw_refs[i][...]
+        new_ref[at, :] = unit_rows(raw_refs[i])
         cid_ref[at, :] = cluster_rows(bound_ref, r, slots)
     padded = new_ref.shape[0]
     if padded > rows:
@@ -391,7 +371,7 @@
     new_ref[rows:, :] = jnp.zeros((padded - rows, width), bf16)
     pieces = []
     for i, r in enumerate(partners):
-        new_ref[i * slots : (i + 1) * slots, :] = raw_refs[i][...]
+        new_ref[i * slots : (i + 1) * slots, :] = unit_rows(raw_refs[i])
         pieces.append(cluster_rows(bound_ref, r, slots))
     new_cids = jnp.concatenate(pieces, axis=0)
     cid_row = cluster_lanes(bound_ref, partners, slots, padded)
@@ -519,10 +499,11 @@
     me = lax.axis_index("owner").astype(i32).reshape(1)
     ids0 = cluster_ids.reshape(1, rows)
     ids1 = swap_cores(ids0)
-    other = swap_cores(embeddings)
+    mine, ids1 = lax.optimization_barrier((embeddings, ids1))
+    other = swap_cores(mine)
     counts, rank0, rank1 = count_rows(me, ids0, ids1, chips, clusters)
     counts = exchange_chips(counts)
-    units = (unit_rows(embeddings), unit_rows(other))
+    both = (embeddings, other)
     *places, bound, total, load = assign(me, counts, rank0, rank1)
     owner_row, slot_row = places[0], places[2]
 
@@ -537,7 +518,7 @@
         blocks = [None] * chips
         here = list(places)
         for r in sent:
-            blocks[r] = pack(me, here, units, r, slots)
+            blocks[r] = pack(me, here, both, r, slots)
             here[0], blocks[r] = lax.optimization_barrier((here[0], blocks[r]))
         if apart:
             arrived = blocks[:1] + [None] * (chips - 1)

time: 116 us -> 112 us (0.966)
  blocking collectives: 0 us -> 13.4 us
  starting transfers between devices: 40.9 us -> 32.2 us
  waiting for transfers between devices: 38.7 us -> 32.5 us
  local copies, waits for them, and re-layouts: 2.59 us -> 0.7 us
    all_to_all x0 -> x1, blocking collectives: none -> 13.4 us  [exchange_chips(): lax.all_to_all(x, 'owner', split_axis=0, concat_axis=0, axis_index_groups...]
    all_to_all x1 -> x0, starting transfers between devices: 7.2 us -> none  [exchange_chips(): lax.all_to_all(x, 'owner', split_axis=0, concat_axis=0, axis_index_groups...]
    ppermute x2, waiting for transfers between devices: 5.43 us -> 1.04 us  [swap_cores(): return lax.ppermute(x, 'owner', [(s, s ^ 1) for s in range(owners)])]
    pallas_call x2 -> x0, Pallas kernels: 4.21 us -> none  [unit_rows(): pl.pallas_call(unit_kernel, out_shape=jax.ShapeDtypeStruct((rows, width),...]
    pallas_call x8, Pallas kernels: 15.1 us -> 18.4 us  [pack(): pl.pallas_call(functools.partial(pack_kernel, partner), out_shape=jax.Sha...]
    unnamed x8 -> x6, local copies, waits for them, and re-layouts: 2.59 us -> 0.7 us
    ppermute x7, starting transfers between devices: 29.4 us -> 27.6 us  [swap(): return lax.ppermute(block, 'owner', [(s, s ^ 2 * r) for s in range(owners)])]
    all_to_all x1 -> x0, waiting for transfers between devices: 1.58 us -> none  [exchange_chips(): lax.all_to_all(x, 'owner', split_axis=0, concat_axis=0, axis_index_groups...]
  transfers between devices with their start and end apart: 11 -> 10, of which waited for: 5 -> 5; matrix products, arithmetic and copies ran while one was open for 0% -> 0% of each run, Pallas kernels for 22% -> 20%
where the time goes in v10:
time: 112 us
  waiting for transfers between devices  32.5 us (29%)
  starting transfers between devices  32.2 us (29%)
  Pallas kernels  32 us (29%)
  blocking collectives  13.4 us (12%)
    ppermute x7, starting transfers between devices, swap(): return lax.ppermute(block, 'owner', [(s, s ^ 2 * r) for s in range(owners)])  27.6 us
    ppermute x7, waiting for transfers between devices, swap(): return lax.ppermute(block, 'owner', [(s, s ^ 2 * r) for s in range(owners)])  24.7 us
    pallas_call x8, Pallas kernels, pack(): pl.pallas_call(functools.partial(pack_kernel, partner), out_shape=jax.Sha...  18.4 us
    all_to_all x1, blocking collectives, exchange_chips(): lax.all_to_all(x, 'owner', split_axis=0, concat_axis=0, axis_index_groups...  13.4 us
    pallas_call x3, Pallas kernels, score(): pl.pallas_call(functools.partial(score_kernel, slots, partners, len(units...  7.29 us
    all_to_all x1, waiting for transfers between devices, exchange(): return lax.all_to_all(x, 'owner', split_axis=0, concat_axis=0, tiled=True)  6.73 us
    all_to_all x1, starting transfers between devices, exchange(): return lax.all_to_all(x, 'owner', split_axis=0, concat_axis=0, tiled=True)  3.73 us
    pallas_call x1, Pallas kernels, finish(): pl.pallas_call(functools.partial(finish_kernel, slots, partners, earlier,...  3.06 us
  transfers between devices with their start and end apart: 10, of which 5 were waited for; matrix products, arithmetic and copies ran while one was open for 0% of the time, Pallas kernels for 20%

profile of v10, /device:TPU:0, one launch (start us, length us, event | category | flops | bytes accessed | tf_op | source)
XLA Modules:
  0.0 111.5 jit_solution(17077893352492251041)
XLA Ops:
  0.6 0.5 collective-permute-start
  1.1 1.0 collective-permute-done.ids1_ref
  2.2 0.3 collective-permute-start.1
  2.5 0.7 copy-done.3
  3.2 0.8 count_rows.1
  4.0 13.4 %all_to_all.20.counts_ref = s32[8,1,64]{2,1,0:T(1,128)S(1)} all-to-all(s32[8,1,64]{2,1,0:T(1,128)S(1)} %get-tuple-element.120), channel_id=1, replica_groups={{0,2,4,6,8,10,12,14},{1,3,5,7,9,11,13,15},{16,18,20,22,24,26,28,30},{17..., dimensions={0} | all-to-all | bytes 4096 | tf_op jit(solution)/shard_map/all_to_all | solution.py:468
  17.4 0.9 assign.1
  18.3 0.0 collective-permute-done.1.rows1_ref
  18.3 4.9 %pack_rows.24 = bf16[272,768]{1,0:T(8,128)(2,1)S(1)} custom-call(s32[1]{0:T(128)} %bitcast.17.me_ref, s32[1,2048]{1,0:T(1,128)S(1)} %get-tuple-element.140.owner0_ref.owner_ref, s32[1,2048]{1,0:T(1,128)S(1)} %get-tuple-element.125.owner1_ref, s32[1,2048]{1,0:T(1,128)S(1)} %get-tuple-element.126.slot0_ref.slot_ref, ...), custom_call_target="tpu_custom_call" | custom-call | flops 272 | bytes 272 | tf_op jit(solution)/shard_map/pack_rows/pallas_call | solution.py:225
  23.2 0.6 collective-permute-start.7
  23.9 1.9 %pack_rows.25 = bf16[272,768]{1,0:T(8,128)(2,1)S(1)} custom-call(s32[1]{0:T(128)} %bitcast.17.me_ref, s32[1,2048]{1,0:T(1,128)S(1)} %get-tuple-element.140.owner0_ref.owner_ref, s32[1,2048]{1,0:T(1,128)S(1)} %get-tuple-element.125.owner1_ref, s32[1,2048]{1,0:T(1,128)S(1)} %get-tuple-element.126.slot0_ref.slot_ref, ...), custom_call_target="tpu_custom_call" | custom-call | flops 272 | bytes 272 | tf_op jit(solution)/shard_map/pack_rows/pallas_call | solution.py:225
  25.8 1.9 %pack_rows.26 = bf16[272,768]{1,0:T(8,128)(2,1)S(1)} custom-call(s32[1]{0:T(128)} %bitcast.17.me_ref, s32[1,2048]{1,0:T(1,128)S(1)} %get-tuple-element.140.owner0_ref.owner_ref, s32[1,2048]{1,0:T(1,128)S(1)} %get-tuple-element.125.owner1_ref, s32[1,2048]{1,0:T(1,128)S(1)} %get-tuple-element.126.slot0_ref.slot_ref, ...), custom_call_target="tpu_custom_call" | custom-call | flops 272 | bytes 272 | tf_op jit(solution)/shard_map/pack_rows/pallas_call | solution.py:225
  27.7 1.9 %pack_rows.27 = bf16[272,768]{1,0:T(8,128)(2,1)S(1)} custom-call(s32[1]{0:T(128)} %bitcast.17.me_ref, s32[1,2048]{1,0:T(1,128)S(1)} %get-tuple-element.140.owner0_ref.owner_ref, s32[1,2048]{1,0:T(1,128)S(1)} %get-tuple-element.125.owner1_ref, s32[1,2048]{1,0:T(1,128)S(1)} %get-tuple-element.126.slot0_ref.slot_ref, ...), custom_call_target="tpu_custom_call" | custom-call | flops 272 | bytes 272 | tf_op jit(solution)/shard_map/pack_rows/pallas_call | solution.py:225
  29.6 3.3 %collective-permute-start.2 = (bf16[272,768]{1,0:T(8,128)(2,1)S(1)}, bf16[272,768]{1,0:T(8,128)(2,1)S(1)}, u32[]{:S(2)}, u32[]{:S(2)}) collective-permute-start(bf16[272,768]{1,0:T(8,128)(2,1)S(1)} %pack_rows.25), channel_id=1, source_target_pairs={{0,12},{1,13},{2,14},{3,15},{4,8},{5,9},{6,10},{7,11},{8,4},{9,5},... | collective-permute-start | bytes 1253384 | tf_op jit(solution)/shard_map/ppermute | solution.py:475
  32.9 1.9 %pack_rows.28 = bf16[272,768]{1,0:T(8,128)(2,1)S(1)} custom-call(s32[1]{0:T(128)} %bitcast.17.me_ref, s32[1,2048]{1,0:T(1,128)S(1)} %get-tuple-element.140.owner0_ref.owner_ref, s32[1,2048]{1,0:T(1,128)S(1)} %get-tuple-element.125.owner1_ref, s32[1,2048]{1,0:T(1,128)S(1)} %get-tuple-element.126.slot0_ref.slot_ref, ...), custom_call_target="tpu_custom_call" | custom-call | flops 272 | bytes 272 | tf_op jit(solution)/shard_map/pack_rows/pallas_call | solution.py:225
  34.8 1.5 %collective-permute-start.6 = (bf16[272,768]{1,0:T(8,128)(2,1)S(1)}, bf16[272,768]{1,0:T(8,128)(2,1)S(1)}, u32[]{:S(2)}, u32[]{:S(2)}) collective-permute-start(bf16[272,768]{1,0:T(8,128)(2,1)S(1)} %pack_rows.28), channel_id=1, source_target_pairs={{0,2},{1,3},{2,0},{3,1},{4,6},{5,7},{6,4},{7,5},{8,10},{9,11},{10,... | collective-permute-start | bytes 1253384 | tf_op jit(solution)/shard_map/ppermute | solution.py:475
  36.3 2.0 %collective-permute-start.4 = (bf16[272,768]{1,0:T(8,128)(2,1)S(1)}, bf16[272,768]{1,0:T(8,128)(2,1)S(1)}, u32[]{:S(2)}, u32[]{:S(2)}) collective-permute-start(bf16[272,768]{1,0:T(8,128)(2,1)S(1)} %pack_rows.26), channel_id=1, source_target_pairs={{0,6},{1,7},{2,4},{3,5},{4,2},{5,3},{6,0},{7,1},{8,14},{9,15},{10,... | collective-permute-start | bytes 1253384 | tf_op jit(solution)/shard_map/ppermute | solution.py:475
  38.4 1.9 %pack_rows.29 = bf16[272,768]{1,0:T(8,128)(2,1)S(1)} custom-call(s32[1]{0:T(128)} %bitcast.17.me_ref, s32[1,2048]{1,0:T(1,128)S(1)} %get-tuple-element.140.owner0_ref.owner_ref, s32[1,2048]{1,0:T(1,128)S(1)} %get-tuple-element.125.owner1_ref, s32[1,2048]{1,0:T(1,128)S(1)} %get-tuple-element.126.slot0_ref.slot_ref, ...), custom_call_target="tpu_custom_call" | custom-call | flops 272 | bytes 272 | tf_op jit(solution)/shard_map/pack_rows/pallas_call | solution.py:225
  40.3 13.9 %collective-permute-start.8 = (bf16[272,768]{1,0:T(8,128)(2,1)S(1)}, bf16[272,768]{1,0:T(8,128)(2,1)S(1)}, u32[]{:S(2)}, u32[]{:S(2)}) collective-permute-start(bf16[272,768]{1,0:T(8,128)(2,1)S(1)} %pack_rows.29), channel_id=1, source_target_pairs={{0,10},{1,11},{2,8},{3,9},{4,14},{5,15},{6,12},{7,13},{8,2},{9,3},... | collective-permute-start | bytes 1253384 | tf_op jit(solution)/shard_map/ppermute | solution.py:475
  54.2 1.9 %pack_rows.30 = bf16[272,768]{1,0:T(8,128)(2,1)S(1)} custom-call(s32[1]{0:T(128)} %bitcast.17.me_ref, s32[1,2048]{1,0:T(1,128)S(1)} %get-tuple-element.140.owner0_ref.owner_ref, s32[1,2048]{1,0:T(1,128)S(1)} %get-tuple-element.125.owner1_ref, s32[1,2048]{1,0:T(1,128)S(1)} %get-tuple-element.126.slot0_ref.slot_ref, ...), custom_call_target="tpu_custom_call" | custom-call | flops 272 | bytes 272 | tf_op jit(solution)/shard_map/pack_rows/pallas_call | solution.py:225
  56.1 2.1 %pack_rows.31.refs_0_ = bf16[272,768]{1,0:T(8,128)(2,1)S(1)} custom-call(s32[1]{0:T(128)} %bitcast.17.me_ref, s32[1,2048]{1,0:T(1,128)S(1)} %get-tuple-element.140.owner0_ref.owner_ref, s32[1,2048]{1,0:T(1,128)S(1)} %get-tuple-element.125.owner1_ref, s32[1,2048]{1,0:T(1,128)S(1)} %get-tuple-element.126.slot0_ref.slot_ref, ...), custom_call_target="tpu_custom_call" | custom-call | flops 272 | bytes 272 | tf_op jit(solution)/shard_map/pack_rows/pallas_call | solution.py:225
  58.2 6.2 %collective-permute-start.3 = (bf16[272,768]{1,0:T(8,128)(2,1)S(1)}, bf16[272,768]{1,0:T(8,128)(2,1)S(1)}, u32[]{:S(2)}, u32[]{:S(2)}) collective-permute-start(bf16[272,768]{1,0:T(8,128)(2,1)S(1)} %pack_rows.30), channel_id=1, source_target_pairs={{0,8},{1,9},{2,10},{3,11},{4,12},{5,13},{6,14},{7,15},{8,0},{9,1},... | collective-permute-start | bytes 1253384 | tf_op jit(solution)/shard_map/ppermute | solution.py:475
  64.4 0.9 collective-permute-done.4.refs_1_
  65.3 3.0 %score_rows.9 = (bf16[1088,768]{1,0:T(8,128)(2,1)S(1)}, f32[1088,128]{1,0:T(8,128)S(1)}, f32[1088,128]{1,0:T(8,128)S(1)}, f32[8,768]{1,0:T(8,128)S(1)}) custom-call(f32[8,128]{1,0:T(8,128)S(1)} %get-tuple-element.129.bound_ref, bf16[272,768]{1,0:T(8,128)(2,1)S(1)} %pack_rows.31.refs_0_, bf16[272,768]{1,0:T(8,128)(2,1)S(1)} %collective-permute-done.4.refs_1_, ...), custom_call_target="tpu_custom_call" | custom-call | flops 1925185536 | bytes 1671168 | tf_op jit(solution)/shard_map/score_rows/pallas_call | solution.py:346
  68.3 2.4 %score_rows.10 = (bf16[544,768]{1,0:T(8,128)(2,1)S(1)}, f32[544,128]{1,0:T(8,128)S(1)}, f32[544,128]{1,0:T(8,128)S(1)}, f32[8,768]{1,0:T(8,128)S(1)}, f32[1088,128]{1,0:T(8,128)S(1)}) custom-call(f32[8,128]{1,0:T(8,128)S(1)} %get-tuple-element.129.bound_ref, bf16[272,768]{1,0:T(8,128)(2,1)S(1)} %collective-permute-done.7.refs_0_, ...), custom_call_target="tpu_custom_call" | custom-call | flops 1604321280 | bytes 2506752 | tf_op jit(solution)/shard_map/score_rows/pallas_call | solution.py:346
  70.7 19.6 %collective-permute-done.8.refs_0_ = bf16[272,768]{1,0:T(8,128)(2,1)S(1)} collective-permute-done((bf16[272,768]{1,0:T(8,128)(2,1)S(1)}, bf16[272,768]{1,0:T(8,128)(2,1)S(1)}, u32[]{:S(2)}, u32[]{:S(2)}) %collective-permute-start.8) | collective-permute-done | bytes 417824 | tf_op jit(solution)/shard_map/ppermute | solution.py:475
  90.3 1.9 %score_rows.11 = (bf16[272,768]{1,0:T(8,128)(2,1)S(1)}, f32[272,128]{1,0:T(8,128)S(1)}, f32[272,128]{1,0:T(8,128)S(1)}, f32[8,768]{1,0:T(8,128)S(1)}, f32[1088,128]{1,0:T(8,128)S(1)}, /*index=5*/f32[544,128]{1,0:T(8,128)S(1)}) custom-call(f32[8,128]{1,0:T(8,128)S(1)} %get-tuple-element.129.bound_ref, bf16[272,768]{1,0:T(8,128)(2,1)S(1)} %collective-permute-done.8.refs_0_, ...), custom_call_target="tpu_custom_call" | custom-call | flops 1123024896 | bytes 2924544 | tf_op jit(solution)/shard_map/score_rows/pallas_call | solution.py:346
  92.2 4.2 %collective-permute-done.3.refs_0_ = bf16[272,768]{1,0:T(8,128)(2,1)S(1)} collective-permute-done((bf16[272,768]{1,0:T(8,128)(2,1)S(1)}, bf16[272,768]{1,0:T(8,128)(2,1)S(1)}, u32[]{:S(2)}, u32[]{:S(2)}) %collective-permute-start.3) | collective-permute-done | bytes 417824 | tf_op jit(solution)/shard_map/ppermute | solution.py:475
  96.4 3.1 %finish_rows.3 = f32[16,1,768]{2,1,0:T(1,128)} custom-call(s32[1]{0:T(128)} %bitcast.17.me_ref, f32[8,128]{1,0:T(8,128)S(1)} %get-tuple-element.129.bound_ref, f32[8,128]{1,0:T(8,128)S(1)} %get-tuple-element.130.total_ref, bf16[272,768]{1,0:T(8,128)(2,1)S(1)} %collective-permute-done.3.refs_0_, bf16[1088,768]{1,0:T(8,128)(2,1)S(1)} %get-tuple-element.145.refs_2_.refs_1_, ...), custom_call_target="tpu_custom_call" | custom-call | flops 2566914048 | bytes 6684672 | tf_op jit(solution)/shard_map/finish_rows/pallas_call | solution.py:411
  99.5 3.7 %all-to-all-start.3 = ((f32[16,1,768]{2,1,0:T(1,128)}), f32[16,1,768]{2,1,0:T(1,128)S(1)}, u32[]{:S(2)}, u32[]{:S(2)}) async-start(f32[16,1,768]{2,1,0:T(1,128)} %finish_rows.3), calls=%async_computation.3 | async-start | bytes 98304 | tf_op jit(solution)/shard_map/all_to_all | solution.py:462
  103.2 6.7 %all-to-all-done.3.back_ref = f32[16,1,768]{2,1,0:T(1,128)S(1)} async-done(((f32[16,1,768]{2,1,0:T(1,128)}), f32[16,1,768]{2,1,0:T(1,128)S(1)}, u32[]{:S(2)}, u32[]{:S(2)}) %all-to-all-start.3) | async-done | bytes 49184 | tf_op jit(solution)/shard_map/all_to_all | solution.py:462
  110.0 1.6 %restore_rows.3 = (f32[1,2048]{1,0:T(1,128)}, f32[1,2048]{1,0:T(1,128)}) custom-call(s32[1,2048]{1,0:T(1,128)S(1)} %get-tuple-element.140.owner0_ref.owner_ref, s32[1,2048]{1,0:T(1,128)S(1)} %get-tuple-element.126.slot0_ref.slot_ref, f32[16,1,768]{2,1,0:T(1,128)S(1)} %all-to-all-done.3.back_ref), custom_call_target="tpu_custom_call" | custom-call | tf_op jit(solution)/shard_map/restore_rows/pallas_call | solution.py:451
  (11 shorter events, 0.0 us)
Async XLA Ops:
  0.6 1.6 %collective-permute-start = (s32[1,2048]{1,0:T(1,128)}, s32[1,2048]{1,0:T(1,128)S(1)}, u32[]{:S(2)}, u32[]{:S(2)}) collective-permute-start(s32[1,2048]{1,0:T(1,128)} %bitcast.40), channel_id=1, source_target_pairs={{0,1},{1,0},{2,3},{3,2},{4,5},{5,4},{6,7},{7,6},{8,9},{9,8},{10,11... | collective-permute-start | bytes 24584 | tf_op jit(solution)/shard_map/ppermute | solution.py:487
  2.2 16.1 %collective-permute-start.1 = (bf16[2048,768]{1,0:T(8,128)(2,1)}, bf16[2048,768]{1,0:T(8,128)(2,1)S(1)}, u32[]{:S(2)}, u32[]{:S(2)}) collective-permute-start(bf16[2048,768]{1,0:T(8,128)(2,1)} %rows0_ref.15), channel_id=1, source_target_pairs={{0,1},{1,0},{2,3},{3,2},{4,5},{5,4},{6,7},{7,6},{8,9},{9,8},{10,11... | collective-permute-start | bytes 9437192 | tf_op jit(solution)/shard_map/ppermute | solution.py:487
  2.5 0.7 copy-start.3
  3.2 20.6 %copy-start.4 = (bf16[2048,768]{1,0:T(8,128)(2,1)S(1)}, bf16[2048,768]{1,0:T(8,128)(2,1)}, u32[]{:S(2)}) copy-start(bf16[2048,768]{1,0:T(8,128)(2,1)} %rows0_ref.15) | copy-start | bytes 9437188
  18.3 37.8 %copy-start.6 = (bf16[2048,768]{1,0:T(8,128)(2,1)}, bf16[2048,768]{1,0:T(8,128)(2,1)S(1)}, u32[]{:S(2)}) copy-start(bf16[2048,768]{1,0:T(8,128)(2,1)S(1)} %collective-permute-done.1.rows1_ref) | copy-start | bytes 9437188
  23.2 17.1 %collective-permute-start.7 = (bf16[272,768]{1,0:T(8,128)(2,1)S(1)}, bf16[272,768]{1,0:T(8,128)(2,1)S(1)}, u32[]{:S(2)}, u32[]{:S(2)}) collective-permute-start(bf16[272,768]{1,0:T(8,128)(2,1)S(1)} %pack_rows.24), channel_id=1, source_target_pairs={{0,14},{1,15},{2,12},{3,13},{4,10},{5,11},{6,8},{7,9},{8,6},{9,7},... | collective-permute-start | bytes 1253384 | tf_op jit(solution)/shard_map/ppermute | solution.py:475
  29.6 28.6 %collective-permute-start.2 = (bf16[272,768]{1,0:T(8,128)(2,1)S(1)}, bf16[272,768]{1,0:T(8,128)(2,1)S(1)}, u32[]{:S(2)}, u32[]{:S(2)}) collective-permute-start(bf16[272,768]{1,0:T(8,128)(2,1)S(1)} %pack_rows.25), channel_id=1, source_target_pairs={{0,12},{1,13},{2,14},{3,15},{4,8},{5,9},{6,10},{7,11},{8,4},{9,5},... | collective-permute-start | bytes 1253384 | tf_op jit(solution)/shard_map/ppermute | solution.py:475
  34.8 29.6 %collective-permute-start.6 = (bf16[272,768]{1,0:T(8,128)(2,1)S(1)}, bf16[272,768]{1,0:T(8,128)(2,1)S(1)}, u32[]{:S(2)}, u32[]{:S(2)}) collective-permute-start(bf16[272,768]{1,0:T(8,128)(2,1)S(1)} %pack_rows.28), channel_id=1, source_target_pairs={{0,2},{1,3},{2,0},{3,1},{4,6},{5,7},{6,4},{7,5},{8,10},{9,11},{10,... | collective-permute-start | bytes 1253384 | tf_op jit(solution)/shard_map/ppermute | solution.py:475
  36.3 28.1 %collective-permute-start.5 = (bf16[272,768]{1,0:T(8,128)(2,1)S(1)}, bf16[272,768]{1,0:T(8,128)(2,1)S(1)}, u32[]{:S(2)}, u32[]{:S(2)}) collective-permute-start(bf16[272,768]{1,0:T(8,128)(2,1)S(1)} %pack_rows.27), channel_id=1, source_target_pairs={{0,4},{1,5},{2,6},{3,7},{4,0},{5,1},{6,2},{7,3},{8,12},{9,13},{10,... | collective-permute-start | bytes 1253384 | tf_op jit(solution)/shard_map/ppermute | solution.py:475
  36.3 29.0 %collective-permute-start.4 = (bf16[272,768]{1,0:T(8,128)(2,1)S(1)}, bf16[272,768]{1,0:T(8,128)(2,1)S(1)}, u32[]{:S(2)}, u32[]{:S(2)}) collective-permute-start(bf16[272,768]{1,0:T(8,128)(2,1)S(1)} %pack_rows.26), channel_id=1, source_target_pairs={{0,6},{1,7},{2,4},{3,5},{4,2},{5,3},{6,0},{7,1},{8,14},{9,15},{10,... | collective-permute-start | bytes 1253384 | tf_op jit(solution)/shard_map/ppermute | solution.py:475
  40.3 50.0 %collective-permute-start.8 = (bf16[272,768]{1,0:T(8,128)(2,1)S(1)}, bf16[272,768]{1,0:T(8,128)(2,1)S(1)}, u32[]{:S(2)}, u32[]{:S(2)}) collective-permute-start(bf16[272,768]{1,0:T(8,128)(2,1)S(1)} %pack_rows.29), channel_id=1, source_target_pairs={{0,10},{1,11},{2,8},{3,9},{4,14},{5,15},{6,12},{7,13},{8,2},{9,3},... | collective-permute-start | bytes 1253384 | tf_op jit(solution)/shard_map/ppermute | solution.py:475
  58.2 38.2 %collective-permute-start.3 = (bf16[272,768]{1,0:T(8,128)(2,1)S(1)}, bf16[272,768]{1,0:T(8,128)(2,1)S(1)}, u32[]{:S(2)}, u32[]{:S(2)}) collective-permute-start(bf16[272,768]{1,0:T(8,128)(2,1)S(1)} %pack_rows.30), channel_id=1, source_target_pairs={{0,8},{1,9},{2,10},{3,11},{4,12},{5,13},{6,14},{7,15},{8,0},{9,1},... | collective-permute-start | bytes 1253384 | tf_op jit(solution)/shard_map/ppermute | solution.py:475
  99.5 10.5 %all-to-all-start.3 = ((f32[16,1,768]{2,1,0:T(1,128)}), f32[16,1,768]{2,1,0:T(1,128)S(1)}, u32[]{:S(2)}, u32[]{:S(2)}) async-start(f32[16,1,768]{2,1,0:T(1,128)} %finish_rows.3), calls=%async_computation.3 | async-start | bytes 98304 | tf_op jit(solution)/shard_map/all_to_all | solution.py:462

commit v11 on v10

--- a/solution.py
+++ b/solution.py
@@ -90,6 +90,7 @@
         in_specs=[SMEM, VMEM, VMEM],
         out_specs=(VMEM,) * 3,
         compiler_params=pltpu.CompilerParams(vmem_limit_bytes=16 * MIB),
+        cost_estimate=pl.CostEstimate(flops=8_000_000_000, bytes_accessed=1 << 20, transcendentals=0),
         name="count_rows",
     )(me, ids0, ids1)
 
@@ -351,8 +352,8 @@
         scratch_shapes=[pltpu.VMEM((padded, width), bf16)],
         compiler_params=pltpu.CompilerParams(vmem_limit_bytes=(36 if slots < 400 else 58) * MIB),
         cost_estimate=pl.CostEstimate(
-            flops=2 * (old_rows + rows) * padded * width,
-            bytes_accessed=2 * (old_rows + rows) * width,
+            flops=2 * (old_rows + rows) * padded,
+            bytes_accessed=2 * (old_rows + rows),
             transcendentals=rows,
         ),
         name="score_rows",
@@ -382,7 +383,7 @@
     results = score_group(new_ref, new_cids, old_refs, cid_row, rows)
     half = out_ref.shape[2] // 2
     group, within = rows // LANES, rows % LANES
-    eye = iota((slots, half), 0) == iota((slots, half), 1)
+    eye = iota((LANES, LANES), 0) == iota((LANES, LANES), 1)
     all_cids = [old[2][...] for old in old_refs] + [new_cids]
     for (scores, acc), cids, names in zip(results, all_cids, earlier + [partners]):
         best = jnp.max(acc, axis=1, keepdims=True)
@@ -394,10 +395,13 @@
         for i, r in enumerate(names):
             at = slice(i * slots, (i + 1) * slots)
             for j, col in enumerate((best, gap)):
-                line = jnp.sum(jnp.where(eye, col[at], 0.0), axis=0, keepdims=True)
-                for core in range(2):
-                    device = 2 * (r ^ chip) + core
-                    out_ref[device, :, j * half : (j + 1) * half] = line
+                for first in range(0, slots, LANES):
+                    size = min(LANES, slots - first)
+                    piece = col[at][first : first + size]
+                    line = jnp.sum(jnp.where(eye[:size], piece, 0.0), axis=0, keepdims=True)
+                    lanes = slice(j * half + first, j * half + first + LANES)
+                    for core in range(2):
+                        out_ref[2 * (r ^ chip) + core, :, lanes] = line
 
 
 def finish(me, bound, total, blocks, partners, earlier, state):

time: 112 us -> 109 us (0.973)
  Pallas kernels: 32 us -> 29.2 us
  waiting for transfers between devices: 32.5 us -> 30.2 us
  starting transfers between devices: 32.2 us -> 34.2 us
    pallas_call x8, Pallas kernels: 18.4 us -> 15.4 us  [pack(): pl.pallas_call(functools.partial(pack_kernel, partner), out_shape=jax.Sha...]
    ppermute x7, waiting for transfers between devices: 24.7 us -> 22.5 us  [swap(): return lax.ppermute(block, 'owner', [(s, s ^ 2 * r) for s in range(owners)])]
    ppermute x7, starting transfers between devices: 27.6 us -> 29.6 us  [swap(): return lax.ppermute(block, 'owner', [(s, s ^ 2 * r) for s in range(owners)])]
  transfers between devices with their start and end apart: 10 -> 10, of which waited for: 5 -> 4; matrix products, arithmetic and copies ran while one was open for 0% -> 0% of each run, Pallas kernels for 20% -> 21%
where the time goes in v11:
time: 109 us
  starting transfers between devices  34.2 us (31%)
  waiting for transfers between devices  30.2 us (28%)
  Pallas kernels  29.2 us (27%)
  blocking collectives  13.4 us (12%)
    ppermute x7, starting transfers between devices, swap(): return lax.ppermute(block, 'owner', [(s, s ^ 2 * r) for s in range(owners)])  29.6 us
    ppermute x7, waiting for transfers between devices, swap(): return lax.ppermute(block, 'owner', [(s, s ^ 2 * r) for s in range(owners)])  22.5 us
    pallas_call x8, Pallas kernels, pack(): pl.pallas_call(functools.partial(pack_kernel, partner), out_shape=jax.Sha...  15.4 us
    all_to_all x1, blocking collectives, exchange_chips(): lax.all_to_all(x, 'owner', split_axis=0, concat_axis=0, axis_index_groups...  13.4 us
    pallas_call x3, Pallas kernels, score(): pl.pallas_call(functools.partial(score_kernel, slots, partners, len(units...  7.5 us
    all_to_all x1, waiting for transfers between devices, exchange(): return lax.all_to_all(x, 'owner', split_axis=0, concat_axis=0, tiled=True)  6.73 us
    all_to_all x1, starting transfers between devices, exchange(): return lax.all_to_all(x, 'owner', split_axis=0, concat_axis=0, tiled=True)  3.73 us
    pallas_call x1, Pallas kernels, finish(): pl.pallas_call(functools.partial(finish_kernel, slots, partners, earlier,...  3.08 us
  transfers between devices with their start and end apart: 10, of which 4 were waited for; matrix products, arithmetic and copies ran while one was open for 0% of the time, Pallas kernels for 21%

profile of v11, /device:TPU:0, one launch (start us, length us, event | category | flops | bytes accessed | tf_op | source)
XLA Modules:
  0.0 108.5 jit_solution(9378686556264440250)
XLA Ops:
  0.6 0.5 collective-permute-start
  1.1 1.0 collective-permute-done.ids1_ref
  2.2 0.3 collective-permute-start.1
  2.5 0.7 copy-done.3
  3.2 0.8 count_rows.1
  4.0 13.4 %all_to_all.20.counts_ref = s32[8,1,64]{2,1,0:T(1,128)S(1)} all-to-all(s32[8,1,64]{2,1,0:T(1,128)S(1)} %get-tuple-element.120), channel_id=1, replica_groups={{0,2,4,6,8,10,12,14},{1,3,5,7,9,11,13,15},{16,18,20,22,24,26,28,30},{17..., dimensions={0} | all-to-all | bytes 4096 | tf_op jit(solution)/shard_map/all_to_all | solution.py:472
  17.4 0.9 assign.1
  18.3 1.9 %pack_rows.24 = bf16[272,768]{1,0:T(8,128)(2,1)S(1)} custom-call(s32[1]{0:T(128)} %bitcast.17.me_ref, s32[1,2048]{1,0:T(1,128)S(1)} %get-tuple-element.140.owner0_ref.owner_ref, s32[1,2048]{1,0:T(1,128)S(1)} %get-tuple-element.125.owner1_ref, s32[1,2048]{1,0:T(1,128)S(1)} %get-tuple-element.126.slot0_ref.slot_ref, ...), custom_call_target="tpu_custom_call" | custom-call | flops 272 | bytes 272 | tf_op jit(solution)/shard_map/pack_rows/pallas_call | solution.py:226
  20.2 0.6 collective-permute-start.7
  20.8 1.9 %pack_rows.25 = bf16[272,768]{1,0:T(8,128)(2,1)S(1)} custom-call(s32[1]{0:T(128)} %bitcast.17.me_ref, s32[1,2048]{1,0:T(1,128)S(1)} %get-tuple-element.140.owner0_ref.owner_ref, s32[1,2048]{1,0:T(1,128)S(1)} %get-tuple-element.125.owner1_ref, s32[1,2048]{1,0:T(1,128)S(1)} %get-tuple-element.126.slot0_ref.slot_ref, ...), custom_call_target="tpu_custom_call" | custom-call | flops 272 | bytes 272 | tf_op jit(solution)/shard_map/pack_rows/pallas_call | solution.py:226
  22.8 3.3 %collective-permute-start.2 = (bf16[272,768]{1,0:T(8,128)(2,1)S(1)}, bf16[272,768]{1,0:T(8,128)(2,1)S(1)}, u32[]{:S(2)}, u32[]{:S(2)}) collective-permute-start(bf16[272,768]{1,0:T(8,128)(2,1)S(1)} %pack_rows.25), channel_id=1, source_target_pairs={{0,12},{1,13},{2,14},{3,15},{4,8},{5,9},{6,10},{7,11},{8,4},{9,5},... | collective-permute-start | bytes 1253384 | tf_op jit(solution)/shard_map/ppermute | solution.py:479
  26.1 1.9 %pack_rows.26 = bf16[272,768]{1,0:T(8,128)(2,1)S(1)} custom-call(s32[1]{0:T(128)} %bitcast.17.me_ref, s32[1,2048]{1,0:T(1,128)S(1)} %get-tuple-element.140.owner0_ref.owner_ref, s32[1,2048]{1,0:T(1,128)S(1)} %get-tuple-element.125.owner1_ref, s32[1,2048]{1,0:T(1,128)S(1)} %get-tuple-element.126.slot0_ref.slot_ref, ...), custom_call_target="tpu_custom_call" | custom-call | flops 272 | bytes 272 | tf_op jit(solution)/shard_map/pack_rows/pallas_call | solution.py:226
  28.0 1.9 %pack_rows.27 = bf16[272,768]{1,0:T(8,128)(2,1)S(1)} custom-call(s32[1]{0:T(128)} %bitcast.17.me_ref, s32[1,2048]{1,0:T(1,128)S(1)} %get-tuple-element.140.owner0_ref.owner_ref, s32[1,2048]{1,0:T(1,128)S(1)} %get-tuple-element.125.owner1_ref, s32[1,2048]{1,0:T(1,128)S(1)} %get-tuple-element.126.slot0_ref.slot_ref, ...), custom_call_target="tpu_custom_call" | custom-call | flops 272 | bytes 272 | tf_op jit(solution)/shard_map/pack_rows/pallas_call | solution.py:226
  29.9 1.9 %pack_rows.28 = bf16[272,768]{1,0:T(8,128)(2,1)S(1)} custom-call(s32[1]{0:T(128)} %bitcast.17.me_ref, s32[1,2048]{1,0:T(1,128)S(1)} %get-tuple-element.140.owner0_ref.owner_ref, s32[1,2048]{1,0:T(1,128)S(1)} %get-tuple-element.125.owner1_ref, s32[1,2048]{1,0:T(1,128)S(1)} %get-tuple-element.126.slot0_ref.slot_ref, ...), custom_call_target="tpu_custom_call" | custom-call | flops 272 | bytes 272 | tf_op jit(solution)/shard_map/pack_rows/pallas_call | solution.py:226
  31.8 1.5 %collective-permute-start.6 = (bf16[272,768]{1,0:T(8,128)(2,1)S(1)}, bf16[272,768]{1,0:T(8,128)(2,1)S(1)}, u32[]{:S(2)}, u32[]{:S(2)}) collective-permute-start(bf16[272,768]{1,0:T(8,128)(2,1)S(1)} %pack_rows.28), channel_id=1, source_target_pairs={{0,2},{1,3},{2,0},{3,1},{4,6},{5,7},{6,4},{7,5},{8,10},{9,11},{10,... | collective-permute-start | bytes 1253384 | tf_op jit(solution)/shard_map/ppermute | solution.py:479
  33.3 2.0 %collective-permute-start.4 = (bf16[272,768]{1,0:T(8,128)(2,1)S(1)}, bf16[272,768]{1,0:T(8,128)(2,1)S(1)}, u32[]{:S(2)}, u32[]{:S(2)}) collective-permute-start(bf16[272,768]{1,0:T(8,128)(2,1)S(1)} %pack_rows.26), channel_id=1, source_target_pairs={{0,6},{1,7},{2,4},{3,5},{4,2},{5,3},{6,0},{7,1},{8,14},{9,15},{10,... | collective-permute-start | bytes 1253384 | tf_op jit(solution)/shard_map/ppermute | solution.py:479
  35.3 1.9 %pack_rows.29 = bf16[272,768]{1,0:T(8,128)(2,1)S(1)} custom-call(s32[1]{0:T(128)} %bitcast.17.me_ref, s32[1,2048]{1,0:T(1,128)S(1)} %get-tuple-element.140.owner0_ref.owner_ref, s32[1,2048]{1,0:T(1,128)S(1)} %get-tuple-element.125.owner1_ref, s32[1,2048]{1,0:T(1,128)S(1)} %get-tuple-element.126.slot0_ref.slot_ref, ...), custom_call_target="tpu_custom_call" | custom-call | flops 272 | bytes 272 | tf_op jit(solution)/shard_map/pack_rows/pallas_call | solution.py:226
  37.2 0.0 collective-permute-done.7.refs_0_
  37.3 13.9 %collective-permute-start.8 = (bf16[272,768]{1,0:T(8,128)(2,1)S(1)}, bf16[272,768]{1,0:T(8,128)(2,1)S(1)}, u32[]{:S(2)}, u32[]{:S(2)}) collective-permute-start(bf16[272,768]{1,0:T(8,128)(2,1)S(1)} %pack_rows.29), channel_id=1, source_target_pairs={{0,10},{1,11},{2,8},{3,9},{4,14},{5,15},{6,12},{7,13},{8,2},{9,3},... | collective-permute-start | bytes 1253384 | tf_op jit(solution)/shard_map/ppermute | solution.py:479
  51.2 1.9 %pack_rows.30 = bf16[272,768]{1,0:T(8,128)(2,1)S(1)} custom-call(s32[1]{0:T(128)} %bitcast.17.me_ref, s32[1,2048]{1,0:T(1,128)S(1)} %get-tuple-element.140.owner0_ref.owner_ref, s32[1,2048]{1,0:T(1,128)S(1)} %get-tuple-element.125.owner1_ref, s32[1,2048]{1,0:T(1,128)S(1)} %get-tuple-element.126.slot0_ref.slot_ref, ...), custom_call_target="tpu_custom_call" | custom-call | flops 272 | bytes 272 | tf_op jit(solution)/shard_map/pack_rows/pallas_call | solution.py:226
  53.1 0.0 collective-permute-done.2.refs_1_
  53.1 8.2 %collective-permute-start.3 = (bf16[272,768]{1,0:T(8,128)(2,1)S(1)}, bf16[272,768]{1,0:T(8,128)(2,1)S(1)}, u32[]{:S(2)}, u32[]{:S(2)}) collective-permute-start(bf16[272,768]{1,0:T(8,128)(2,1)S(1)} %pack_rows.30), channel_id=1, source_target_pairs={{0,8},{1,9},{2,10},{3,11},{4,12},{5,13},{6,14},{7,15},{8,0},{9,1},... | collective-permute-start | bytes 1253384 | tf_op jit(solution)/shard_map/ppermute | solution.py:479
  61.3 2.1 %pack_rows.31.refs_0_ = bf16[272,768]{1,0:T(8,128)(2,1)S(1)} custom-call(s32[1]{0:T(128)} %bitcast.17.me_ref, s32[1,2048]{1,0:T(1,128)S(1)} %get-tuple-element.140.owner0_ref.owner_ref, s32[1,2048]{1,0:T(1,128)S(1)} %get-tuple-element.125.owner1_ref, s32[1,2048]{1,0:T(1,128)S(1)} %get-tuple-element.126.slot0_ref.slot_ref, ...), custom_call_target="tpu_custom_call" | custom-call | flops 272 | bytes 272 | tf_op jit(solution)/shard_map/pack_rows/pallas_call | solution.py:226
  63.4 3.0 %score_rows.9 = (bf16[1088,768]{1,0:T(8,128)(2,1)S(1)}, f32[1088,128]{1,0:T(8,128)S(1)}, f32[1088,128]{1,0:T(8,128)S(1)}, f32[8,768]{1,0:T(8,128)S(1)}) custom-call(f32[8,128]{1,0:T(8,128)S(1)} %get-tuple-element.129.bound_ref, bf16[272,768]{1,0:T(8,128)(2,1)S(1)} %pack_rows.31.refs_0_, bf16[272,768]{1,0:T(8,128)(2,1)S(1)} %collective-permute-done.4.refs_1_, ...), custom_call_target="tpu_custom_call" | custom-call | flops 2506752 | bytes 2176 | tf_op jit(solution)/shard_map/score_rows/pallas_call | solution.py:347
  66.5 2.6 %score_rows.10 = (bf16[544,768]{1,0:T(8,128)(2,1)S(1)}, f32[544,128]{1,0:T(8,128)S(1)}, f32[544,128]{1,0:T(8,128)S(1)}, f32[8,768]{1,0:T(8,128)S(1)}, f32[1088,128]{1,0:T(8,128)S(1)}) custom-call(f32[8,128]{1,0:T(8,128)S(1)} %get-tuple-element.129.bound_ref, bf16[272,768]{1,0:T(8,128)(2,1)S(1)} %collective-permute-done.7.refs_0_, ...), custom_call_target="tpu_custom_call" | custom-call | flops 2088960 | bytes 3264 | tf_op jit(solution)/shard_map/score_rows/pallas_call | solution.py:347
  69.0 18.3 %collective-permute-done.8.refs_0_ = bf16[272,768]{1,0:T(8,128)(2,1)S(1)} collective-permute-done((bf16[272,768]{1,0:T(8,128)(2,1)S(1)}, bf16[272,768]{1,0:T(8,128)(2,1)S(1)}, u32[]{:S(2)}, u32[]{:S(2)}) %collective-permute-start.8) | collective-permute-done | bytes 417824 | tf_op jit(solution)/shard_map/ppermute | solution.py:479
  87.3 1.9 %score_rows.11 = (bf16[272,768]{1,0:T(8,128)(2,1)S(1)}, f32[272,128]{1,0:T(8,128)S(1)}, f32[272,128]{1,0:T(8,128)S(1)}, f32[8,768]{1,0:T(8,128)S(1)}, f32[1088,128]{1,0:T(8,128)S(1)}, /*index=5*/f32[544,128]{1,0:T(8,128)S(1)}) custom-call(f32[8,128]{1,0:T(8,128)S(1)} %get-tuple-element.129.bound_ref, bf16[272,768]{1,0:T(8,128)(2,1)S(1)} %collective-permute-done.8.refs_0_, ...), custom_call_target="tpu_custom_call" | custom-call | flops 1462272 | bytes 3808 | tf_op jit(solution)/shard_map/score_rows/pallas_call | solution.py:347
  89.2 4.2 %collective-permute-done.3.refs_0_ = bf16[272,768]{1,0:T(8,128)(2,1)S(1)} collective-permute-done((bf16[272,768]{1,0:T(8,128)(2,1)S(1)}, bf16[272,768]{1,0:T(8,128)(2,1)S(1)}, u32[]{:S(2)}, u32[]{:S(2)}) %collective-permute-start.3) | collective-permute-done | bytes 417824 | tf_op jit(solution)/shard_map/ppermute | solution.py:479
  93.4 3.1 %finish_rows.3 = f32[16,1,768]{2,1,0:T(1,128)} custom-call(s32[1]{0:T(128)} %bitcast.17.me_ref, f32[8,128]{1,0:T(8,128)S(1)} %get-tuple-element.129.bound_ref, f32[8,128]{1,0:T(8,128)S(1)} %get-tuple-element.130.total_ref, bf16[272,768]{1,0:T(8,128)(2,1)S(1)} %collective-permute-done.3.refs_0_, bf16[1088,768]{1,0:T(8,128)(2,1)S(1)} %get-tuple-element.145.refs_2_.refs_1_, ...), custom_call_target="tpu_custom_call" | custom-call | flops 2566914048 | bytes 6684672 | tf_op jit(solution)/shard_map/finish_rows/pallas_call | solution.py:415
  96.5 3.7 %all-to-all-start.3 = ((f32[16,1,768]{2,1,0:T(1,128)}), f32[16,1,768]{2,1,0:T(1,128)S(1)}, u32[]{:S(2)}, u32[]{:S(2)}) async-start(f32[16,1,768]{2,1,0:T(1,128)} %finish_rows.3), calls=%async_computation.3 | async-start | bytes 98304 | tf_op jit(solution)/shard_map/all_to_all | solution.py:466
  100.3 6.7 %all-to-all-done.3.back_ref = f32[16,1,768]{2,1,0:T(1,128)S(1)} async-done(((f32[16,1,768]{2,1,0:T(1,128)}), f32[16,1,768]{2,1,0:T(1,128)S(1)}, u32[]{:S(2)}, u32[]{:S(2)}) %all-to-all-start.3) | async-done | bytes 49184 | tf_op jit(solution)/shard_map/all_to_all | solution.py:466
  107.0 1.6 %restore_rows.3 = (f32[1,2048]{1,0:T(1,128)}, f32[1,2048]{1,0:T(1,128)}) custom-call(s32[1,2048]{1,0:T(1,128)S(1)} %get-tuple-element.140.owner0_ref.owner_ref, s32[1,2048]{1,0:T(1,128)S(1)} %get-tuple-element.126.slot0_ref.slot_ref, f32[16,1,768]{2,1,0:T(1,128)S(1)} %all-to-all-done.3.back_ref), custom_call_target="tpu_custom_call" | custom-call | tf_op jit(solution)/shard_map/restore_rows/pallas_call | solution.py:455
  (11 shorter events, 0.0 us)
Async XLA Ops:
  0.6 1.6 %collective-permute-start = (s32[1,2048]{1,0:T(1,128)}, s32[1,2048]{1,0:T(1,128)S(1)}, u32[]{:S(2)}, u32[]{:S(2)}) collective-permute-start(s32[1,2048]{1,0:T(1,128)} %bitcast.40), channel_id=1, source_target_pairs={{0,1},{1,0},{2,3},{3,2},{4,5},{5,4},{6,7},{7,6},{8,9},{9,8},{10,11... | collective-permute-start | bytes 24584 | tf_op jit(solution)/shard_map/ppermute | solution.py:491
  2.2 16.1 %collective-permute-start.1 = (bf16[2048,768]{1,0:T(8,128)(2,1)}, bf16[2048,768]{1,0:T(8,128)(2,1)S(1)}, u32[]{:S(2)}, u32[]{:S(2)}) collective-permute-start(bf16[2048,768]{1,0:T(8,128)(2,1)} %rows0_ref.15), channel_id=1, source_target_pairs={{0,1},{1,0},{2,3},{3,2},{4,5},{5,4},{6,7},{7,6},{8,9},{9,8},{10,11... | collective-permute-start | bytes 9437192 | tf_op jit(solution)/shard_map/ppermute | solution.py:491
  2.5 0.7 copy-start.3
  3.2 15.1 %copy-start.4 = (bf16[2048,768]{1,0:T(8,128)(2,1)S(1)}, bf16[2048,768]{1,0:T(8,128)(2,1)}, u32[]{:S(2)}) copy-start(bf16[2048,768]{1,0:T(8,128)(2,1)} %rows0_ref.15) | copy-start | bytes 9437188
  18.3 43.0 %copy-start.6 = (bf16[2048,768]{1,0:T(8,128)(2,1)}, bf16[2048,768]{1,0:T(8,128)(2,1)S(1)}, u32[]{:S(2)}) copy-start(bf16[2048,768]{1,0:T(8,128)(2,1)S(1)} %collective-permute-done.1.rows1_ref) | copy-start | bytes 9437188
  20.2 17.1 %collective-permute-start.7 = (bf16[272,768]{1,0:T(8,128)(2,1)S(1)}, bf16[272,768]{1,0:T(8,128)(2,1)S(1)}, u32[]{:S(2)}, u32[]{:S(2)}) collective-permute-start(bf16[272,768]{1,0:T(8,128)(2,1)S(1)} %pack_rows.24), channel_id=1, source_target_pairs={{0,14},{1,15},{2,12},{3,13},{4,10},{5,11},{6,8},{7,9},{8,6},{9,7},... | collective-permute-start | bytes 1253384 | tf_op jit(solution)/shard_map/ppermute | solution.py:479
  22.8 30.3 %collective-permute-start.2 = (bf16[272,768]{1,0:T(8,128)(2,1)S(1)}, bf16[272,768]{1,0:T(8,128)(2,1)S(1)}, u32[]{:S(2)}, u32[]{:S(2)}) collective-permute-start(bf16[272,768]{1,0:T(8,128)(2,1)S(1)} %pack_rows.25), channel_id=1, source_target_pairs={{0,12},{1,13},{2,14},{3,15},{4,8},{5,9},{6,10},{7,11},{8,4},{9,5},... | collective-permute-start | bytes 1253384 | tf_op jit(solution)/shard_map/ppermute | solution.py:479
  31.8 31.6 %collective-permute-start.6 = (bf16[272,768]{1,0:T(8,128)(2,1)S(1)}, bf16[272,768]{1,0:T(8,128)(2,1)S(1)}, u32[]{:S(2)}, u32[]{:S(2)}) collective-permute-start(bf16[272,768]{1,0:T(8,128)(2,1)S(1)} %pack_rows.28), channel_id=1, source_target_pairs={{0,2},{1,3},{2,0},{3,1},{4,6},{5,7},{6,4},{7,5},{8,10},{9,11},{10,... | collective-permute-start | bytes 1253384 | tf_op jit(solution)/shard_map/ppermute | solution.py:479
  33.3 30.1 %collective-permute-start.5 = (bf16[272,768]{1,0:T(8,128)(2,1)S(1)}, bf16[272,768]{1,0:T(8,128)(2,1)S(1)}, u32[]{:S(2)}, u32[]{:S(2)}) collective-permute-start(bf16[272,768]{1,0:T(8,128)(2,1)S(1)} %pack_rows.27), channel_id=1, source_target_pairs={{0,4},{1,5},{2,6},{3,7},{4,0},{5,1},{6,2},{7,3},{8,12},{9,13},{10,... | collective-permute-start | bytes 1253384 | tf_op jit(solution)/shard_map/ppermute | solution.py:479
  33.3 30.1 %collective-permute-start.4 = (bf16[272,768]{1,0:T(8,128)(2,1)S(1)}, bf16[272,768]{1,0:T(8,128)(2,1)S(1)}, u32[]{:S(2)}, u32[]{:S(2)}) collective-permute-start(bf16[272,768]{1,0:T(8,128)(2,1)S(1)} %pack_rows.26), channel_id=1, source_target_pairs={{0,6},{1,7},{2,4},{3,5},{4,2},{5,3},{6,0},{7,1},{8,14},{9,15},{10,... | collective-permute-start | bytes 1253384 | tf_op jit(solution)/shard_map/ppermute | solution.py:479
  37.3 50.0 %collective-permute-start.8 = (bf16[272,768]{1,0:T(8,128)(2,1)S(1)}, bf16[272,768]{1,0:T(8,128)(2,1)S(1)}, u32[]{:S(2)}, u32[]{:S(2)}) collective-permute-start(bf16[272,768]{1,0:T(8,128)(2,1)S(1)} %pack_rows.29), channel_id=1, source_target_pairs={{0,10},{1,11},{2,8},{3,9},{4,14},{5,15},{6,12},{7,13},{8,2},{9,3},... | collective-permute-start | bytes 1253384 | tf_op jit(solution)/shard_map/ppermute | solution.py:479
  53.1 40.3 %collective-permute-start.3 = (bf16[272,768]{1,0:T(8,128)(2,1)S(1)}, bf16[272,768]{1,0:T(8,128)(2,1)S(1)}, u32[]{:S(2)}, u32[]{:S(2)}) collective-permute-start(bf16[272,768]{1,0:T(8,128)(2,1)S(1)} %pack_rows.30), channel_id=1, source_target_pairs={{0,8},{1,9},{2,10},{3,11},{4,12},{5,13},{6,14},{7,15},{8,0},{9,1},... | collective-permute-start | bytes 1253384 | tf_op jit(solution)/shard_map/ppermute | solution.py:479
  96.5 10.5 %all-to-all-start.3 = ((f32[16,1,768]{2,1,0:T(1,128)}), f32[16,1,768]{2,1,0:T(1,128)S(1)}, u32[]{:S(2)}, u32[]{:S(2)}) async-start(f32[16,1,768]{2,1,0:T(1,128)} %finish_rows.3), calls=%async_computation.3 | async-start | bytes 98304 | tf_op jit(solution)/shard_map/all_to_all | solution.py:466

commit v12 on v11

--- a/solution.py
+++ b/solution.py
@@ -281,10 +281,10 @@
     columns = None
     results = []
     for unit_ref, acc_ref, cid_ref in olds:
-        scores = nt_dot(unit_ref[...], new)
+        scores = nt_dot(unit_ref[0 : acc_ref.shape[0], :], new)
         best, cols = folded(scores, cid_ref[...], False)
         columns = cols if columns is None else [jnp.maximum(a, b) for a, b in zip(columns, cols)]
-        results.append((scores, jnp.maximum(acc_ref[...], best)))
+        results.append(jnp.maximum(acc_ref[...], best))
     scores = nt_dot(new[0:slots_new], new)
     best, _ = folded(scores, new_cids, True)
     if columns is not None:
@@ -292,7 +292,7 @@
         lane = iota((slots_new, LANES), 1)
         for g, col in enumerate(columns):
             best = jnp.maximum(best, jnp.where(row == lane + g * LANES, col, -1.0))
-    results.append((scores, best))
+    results.append(best)
     return results
 
 
@@ -319,10 +319,10 @@
     padded = new_ref.shape[0]
     if padded > rows:
         new_ref[rows:, :] = jnp.zeros((padded - rows, new_ref.shape[1]), bf16)
-    unit_ref[...] = new_ref[0:rows, :]
+    unit_ref[...] = new_ref[...]
     cid_row = cluster_lanes(bound_ref, partners, slots, padded)
     results = score_group(new_ref, cid_ref[...], old_refs, cid_row, rows)
-    for (_, best), ref in zip(results, list(old_accs) + [acc_ref]):
+    for best, ref in zip(results, list(old_accs) + [acc_ref]):
         ref[...] = best
     sums = member_sums(cid_row, new_ref[...])
     sums_out[...] = sums + sums_ref[...] if olds else sums
@@ -334,10 +334,10 @@
     rows = len(blocks) * slots
     padded = round_up(rows, LANES)
     old = [x for group in zip(units, accs, cids) for x in group]
-    old_rows = sum(u.shape[0] for u in units)
+    old_rows = sum(a.shape[0] for a in accs)
     acc_shapes = [jax.ShapeDtypeStruct(a.shape, f32) for a in accs]
     out_shape = (
-        jax.ShapeDtypeStruct((rows, width), bf16),
+        jax.ShapeDtypeStruct((padded, width), bf16),
         jax.ShapeDtypeStruct((rows, LANES), f32),
         jax.ShapeDtypeStruct((rows, LANES), f32),
         jax.ShapeDtypeStruct((8, width), f32),
@@ -361,14 +361,48 @@
     return units + [out[0]], list(out[4:]) + [out[1]], cids + [out[2]], out[3]
 
 
-def finish_kernel(slots, partners, earlier, olds, me_ref, bound_ref, total_ref, *refs):
+def diagonal():
+    return iota((LANES, LANES), 0) == iota((LANES, LANES), 1)
+
+
+def to_line(col, first):
+    piece = col[first : first + LANES]
+    return jnp.sum(jnp.where(diagonal()[: piece.shape[0]], piece, 0.0), axis=0, keepdims=True)
+
+
+def line_kernel(slots, names, bound_ref, *refs):
+    count = len(names)
+    for i, partners in enumerate(names):
+        acc_ref, best_ref, cid_ref = refs[i], refs[count + 2 * i], refs[count + 2 * i + 1]
+        best = jnp.max(acc_ref[...], axis=1, keepdims=True)
+        for first in range(0, best_ref.shape[1], LANES):
+            best_ref[:, first : first + LANES] = to_line(best, first)
+        cid_ref[...] = cluster_lanes(bound_ref, partners, slots, cid_ref.shape[1])
+
+
+def lines(bound, names, slots, accs):
+    widths = [round_up(acc.shape[0], LANES) for acc in accs]
+    out = pl.pallas_call(
+        functools.partial(line_kernel, slots, names),
+        out_shape=tuple(jax.ShapeDtypeStruct((1, w), f32) for w in widths for _ in range(2)),
+        in_specs=[VMEM] * (1 + len(accs)),
+        out_specs=(VMEM,) * (2 * len(accs)),
+        compiler_params=pltpu.CompilerParams(vmem_limit_bytes=16 * MIB),
+        name="line_rows",
+    )(bound, *accs)
+    return out[0::2], out[1::2]
+
+
+def finish_kernel(slots, partners, earlier, me_ref, bound_ref, total_ref, *refs):
     fresh = len(partners)
+    olds = len(earlier)
     raw_refs, refs = refs[:fresh], refs[fresh:]
     old_refs = [refs[3 * i : 3 * i + 3] for i in range(olds)]
     sums_ref, out_ref, new_ref = refs[3 * olds :]
     chip = me_ref[0] >> 1
     rows = fresh * slots
     padded, width = new_ref.shape
+    half = out_ref.shape[2] // 2
     new_ref[rows:, :] = jnp.zeros((padded - rows, width), bf16)
     pieces = []
     for i, r in enumerate(partners):
@@ -380,40 +414,57 @@
     centroid = (sums / jnp.maximum(total_ref[:, 0:1], 1.0)).astype(bf16)
     centroid = jnp.concatenate([centroid, jnp.zeros_like(centroid)], axis=0)
     new_ref[rows : rows + STEP, :] = centroid
-    results = score_group(new_ref, new_cids, old_refs, cid_row, rows)
-    half = out_ref.shape[2] // 2
-    group, within = rows // LANES, rows % LANES
-    eye = iota((LANES, LANES), 0) == iota((LANES, LANES), 1)
-    all_cids = [old[2][...] for old in old_refs] + [new_cids]
-    for (scores, acc), cids, names in zip(results, all_cids, earlier + [partners]):
-        best = jnp.max(acc, axis=1, keepdims=True)
-        lane = iota(cids.shape, 1).astype(f32)
-        dots = scores[:, group * LANES : (group + 1) * LANES]
-        gap = 1.0 - jnp.sum(
-            jnp.where(lane == cids + float(within), dots, 0.0), axis=1, keepdims=True
-        )
+    left = new_ref[0 : rows + STEP, :]
+    label = iota((8, LANES), 0).astype(f32)
+    row = iota((rows, LANES), 0)
+    lane = iota((rows, LANES), 1)
+
+    def write(names, best_line, gap_line):
         for i, r in enumerate(names):
             at = slice(i * slots, (i + 1) * slots)
-            for j, col in enumerate((best, gap)):
-                for first in range(0, slots, LANES):
-                    size = min(LANES, slots - first)
-                    piece = col[at][first : first + size]
-                    line = jnp.sum(jnp.where(eye[:size], piece, 0.0), axis=0, keepdims=True)
-                    lanes = slice(j * half + first, j * half + first + LANES)
-                    for core in range(2):
-                        out_ref[2 * (r ^ chip) + core, :, lanes] = line
+            for j, line in enumerate((best_line, gap_line)):
+                piece = line[:, at]
+                for core in range(2):
+                    out_ref[2 * (r ^ chip) + core, :, j * half : j * half + slots] = piece
+
+    best_new = jnp.full((rows, LANES), -1.0, f32)
+    for names, (unit_ref, best_ref, cid_ref) in zip(earlier, old_refs):
+        scores = nt_dot(left, unit_ref[...])
+        bests, gaps = [], []
+        for first in range(0, unit_ref.shape[0], LANES):
+            at = slice(first, first + LANES)
+            cids = cid_ref[:, at]
+            part = jnp.where(new_cids == cids, scores[0:rows, at], -1.0)
+            best_new = jnp.maximum(best_new, part)
+            bests.append(jnp.maximum(best_ref[:, at], jnp.max(part, axis=0, keepdims=True)))
+            dots = jnp.where(label == cids, scores[rows : rows + 8, at], 0.0)
+            gaps.append(1.0 - jnp.sum(dots, axis=0, keepdims=True))
+        write(names, jnp.concatenate(bests, axis=1), jnp.concatenate(gaps, axis=1))
+    scores = nt_dot(left, new_ref[...])
+    gaps = []
+    for first in range(0, padded, LANES):
+        at = slice(first, first + LANES)
+        cids = cid_row[:, at]
+        allowed = (new_cids == cids) & (row != lane + first)
+        best_new = jnp.maximum(best_new, jnp.where(allowed, scores[0:rows, at], -1.0))
+        dots = jnp.where(label == cids, scores[rows : rows + 8, at], 0.0)
+        gaps.append(1.0 - jnp.sum(dots, axis=0, keepdims=True))
+    best = jnp.max(best_new, axis=1, keepdims=True)
+    bests = [to_line(best, first) for first in range(0, rows, LANES)]
+    write(partners, jnp.concatenate(bests, axis=1), jnp.concatenate(gaps, axis=1))
 
 
 def finish(me, bound, total, blocks, partners, earlier, state):
     slots, width = blocks[0].shape
     owners = 2 * bound.shape[0]
-    units, accs, cids, sums = state
+    units, accs, _, sums = state
     rows = len(blocks) * slots
     padded = round_up(rows + STEP, LANES)
-    old = [x for group in zip(units, accs, cids) for x in group]
+    best_lines, cid_lines = lines(bound, earlier, slots, accs)
+    old = [x for group in zip(units, best_lines, cid_lines) for x in group]
     args = [me, bound, total, *blocks, *old, sums]
     return pl.pallas_call(
-        functools.partial(finish_kernel, slots, partners, earlier, len(units)),
+        functools.partial(finish_kernel, slots, partners, earlier),
         out_shape=jax.ShapeDtypeStruct((owners, 1, 2 * round_up(slots, LANES)), f32),
         in_specs=[SMEM] + [VMEM] * (len(args) - 1),
         out_specs=VMEM,

time: 109 us -> 108 us (level)
    pallas_call x1 -> x2, Pallas kernels: 3.08 us -> 3.11 us  [the longest x1 2.61 us: finish(): pl.pallas_call(functools.partial(finish_kernel, slots, partners, earlier)...]
  transfers between devices with their start and end apart: 10 -> 10, of which waited for: 4 -> 4; matrix products, arithmetic and copies ran while one was open for 0% -> 0% of each run, Pallas kernels for 21% -> 22%
where the time goes in v12:
time: 108 us
  starting transfers between devices  34.2 us (32%)
  Pallas kernels  29.7 us (28%)
  waiting for transfers between devices  29.2 us (27%)
  blocking collectives  13.4 us (12%)
    ppermute x7, starting transfers between devices, swap(): return lax.ppermute(block, 'owner', [(s, s ^ 2 * r) for s in range(owners)])  29.6 us
    ppermute x7, waiting for transfers between devices, swap(): return lax.ppermute(block, 'owner', [(s, s ^ 2 * r) for s in range(owners)])  21.4 us
    pallas_call x8, Pallas kernels, pack(): pl.pallas_call(functools.partial(pack_kernel, partner), out_shape=jax.Sha...  15.4 us
    all_to_all x1, blocking collectives, exchange_chips(): lax.all_to_all(x, 'owner', split_axis=0, concat_axis=0, axis_index_groups...  13.4 us
    pallas_call x3, Pallas kernels, score(): pl.pallas_call(functools.partial(score_kernel, slots, partners, len(units...  8.02 us
    all_to_all x1, waiting for transfers between devices, exchange(): return lax.all_to_all(x, 'owner', split_axis=0, concat_axis=0, tiled=True)  6.73 us
    all_to_all x1, starting transfers between devices, exchange(): return lax.all_to_all(x, 'owner', split_axis=0, concat_axis=0, tiled=True)  3.73 us
    pallas_call x1, Pallas kernels, finish(): pl.pallas_call(functools.partial(finish_kernel, slots, partners, earlier)...  2.61 us
  transfers between devices with their start and end apart: 10, of which 4 were waited for; matrix products, arithmetic and copies ran while one was open for 0% of the time, Pallas kernels for 22%

profile of v12, /device:TPU:0, one launch (start us, length us, event | category | flops | bytes accessed | tf_op | source)
XLA Modules:
  0.0 108.1 jit_solution(8042952069335329366)
XLA Ops:
  0.6 0.5 collective-permute-start
  1.1 1.0 collective-permute-done.ids1_ref
  2.2 0.3 collective-permute-start.1
  2.5 0.7 copy-done.6
  3.2 0.8 count_rows.1
  4.0 13.4 %all_to_all.20.counts_ref = s32[8,1,64]{2,1,0:T(1,128)S(1)} all-to-all(s32[8,1,64]{2,1,0:T(1,128)S(1)} %get-tuple-element.130), channel_id=1, replica_groups={{0,2,4,6,8,10,12,14},{1,3,5,7,9,11,13,15},{16,18,20,22,24,26,28,30},{17..., dimensions={0} | all-to-all | bytes 4096 | tf_op jit(solution)/shard_map/all_to_all | solution.py:523
  17.4 0.9 assign.1
  18.3 1.9 %pack_rows.24 = bf16[272,768]{1,0:T(8,128)(2,1)S(1)} custom-call(s32[1]{0:T(128)} %bitcast.17.me_ref, s32[1,2048]{1,0:T(1,128)S(1)} %get-tuple-element.150.owner0_ref.owner_ref, s32[1,2048]{1,0:T(1,128)S(1)} %get-tuple-element.135.owner1_ref, s32[1,2048]{1,0:T(1,128)S(1)} %get-tuple-element.136.slot0_ref.slot_ref, ...), custom_call_target="tpu_custom_call" | custom-call | flops 272 | bytes 272 | tf_op jit(solution)/shard_map/pack_rows/pallas_call | solution.py:226
  20.2 0.6 collective-permute-start.7
  20.8 1.9 %pack_rows.25 = bf16[272,768]{1,0:T(8,128)(2,1)S(1)} custom-call(s32[1]{0:T(128)} %bitcast.17.me_ref, s32[1,2048]{1,0:T(1,128)S(1)} %get-tuple-element.150.owner0_ref.owner_ref, s32[1,2048]{1,0:T(1,128)S(1)} %get-tuple-element.135.owner1_ref, s32[1,2048]{1,0:T(1,128)S(1)} %get-tuple-element.136.slot0_ref.slot_ref, ...), custom_call_target="tpu_custom_call" | custom-call | flops 272 | bytes 272 | tf_op jit(solution)/shard_map/pack_rows/pallas_call | solution.py:226
  22.8 3.3 %collective-permute-start.2 = (bf16[272,768]{1,0:T(8,128)(2,1)S(1)}, bf16[272,768]{1,0:T(8,128)(2,1)S(1)}, u32[]{:S(2)}, u32[]{:S(2)}) collective-permute-start(bf16[272,768]{1,0:T(8,128)(2,1)S(1)} %pack_rows.25), channel_id=1, source_target_pairs={{0,12},{1,13},{2,14},{3,15},{4,8},{5,9},{6,10},{7,11},{8,4},{9,5},... | collective-permute-start | bytes 1253384 | tf_op jit(solution)/shard_map/ppermute | solution.py:530
  26.1 1.9 %pack_rows.26 = bf16[272,768]{1,0:T(8,128)(2,1)S(1)} custom-call(s32[1]{0:T(128)} %bitcast.17.me_ref, s32[1,2048]{1,0:T(1,128)S(1)} %get-tuple-element.150.owner0_ref.owner_ref, s32[1,2048]{1,0:T(1,128)S(1)} %get-tuple-element.135.owner1_ref, s32[1,2048]{1,0:T(1,128)S(1)} %get-tuple-element.136.slot0_ref.slot_ref, ...), custom_call_target="tpu_custom_call" | custom-call | flops 272 | bytes 272 | tf_op jit(solution)/shard_map/pack_rows/pallas_call | solution.py:226
  28.0 1.9 %pack_rows.27 = bf16[272,768]{1,0:T(8,128)(2,1)S(1)} custom-call(s32[1]{0:T(128)} %bitcast.17.me_ref, s32[1,2048]{1,0:T(1,128)S(1)} %get-tuple-element.150.owner0_ref.owner_ref, s32[1,2048]{1,0:T(1,128)S(1)} %get-tuple-element.135.owner1_ref, s32[1,2048]{1,0:T(1,128)S(1)} %get-tuple-element.136.slot0_ref.slot_ref, ...), custom_call_target="tpu_custom_call" | custom-call | flops 272 | bytes 272 | tf_op jit(solution)/shard_map/pack_rows/pallas_call | solution.py:226
  29.9 1.9 %pack_rows.28 = bf16[272,768]{1,0:T(8,128)(2,1)S(1)} custom-call(s32[1]{0:T(128)} %bitcast.17.me_ref, s32[1,2048]{1,0:T(1,128)S(1)} %get-tuple-element.150.owner0_ref.owner_ref, s32[1,2048]{1,0:T(1,128)S(1)} %get-tuple-element.135.owner1_ref, s32[1,2048]{1,0:T(1,128)S(1)} %get-tuple-element.136.slot0_ref.slot_ref, ...), custom_call_target="tpu_custom_call" | custom-call | flops 272 | bytes 272 | tf_op jit(solution)/shard_map/pack_rows/pallas_call | solution.py:226
  31.8 1.5 %collective-permute-start.6 = (bf16[272,768]{1,0:T(8,128)(2,1)S(1)}, bf16[272,768]{1,0:T(8,128)(2,1)S(1)}, u32[]{:S(2)}, u32[]{:S(2)}) collective-permute-start(bf16[272,768]{1,0:T(8,128)(2,1)S(1)} %pack_rows.28), channel_id=1, source_target_pairs={{0,2},{1,3},{2,0},{3,1},{4,6},{5,7},{6,4},{7,5},{8,10},{9,11},{10,... | collective-permute-start | bytes 1253384 | tf_op jit(solution)/shard_map/ppermute | solution.py:530
  33.3 2.0 %collective-permute-start.4 = (bf16[272,768]{1,0:T(8,128)(2,1)S(1)}, bf16[272,768]{1,0:T(8,128)(2,1)S(1)}, u32[]{:S(2)}, u32[]{:S(2)}) collective-permute-start(bf16[272,768]{1,0:T(8,128)(2,1)S(1)} %pack_rows.26), channel_id=1, source_target_pairs={{0,6},{1,7},{2,4},{3,5},{4,2},{5,3},{6,0},{7,1},{8,14},{9,15},{10,... | collective-permute-start | bytes 1253384 | tf_op jit(solution)/shard_map/ppermute | solution.py:530
  35.3 1.9 %pack_rows.29 = bf16[272,768]{1,0:T(8,128)(2,1)S(1)} custom-call(s32[1]{0:T(128)} %bitcast.17.me_ref, s32[1,2048]{1,0:T(1,128)S(1)} %get-tuple-element.150.owner0_ref.owner_ref, s32[1,2048]{1,0:T(1,128)S(1)} %get-tuple-element.135.owner1_ref, s32[1,2048]{1,0:T(1,128)S(1)} %get-tuple-element.136.slot0_ref.slot_ref, ...), custom_call_target="tpu_custom_call" | custom-call | flops 272 | bytes 272 | tf_op jit(solution)/shard_map/pack_rows/pallas_call | solution.py:226
  37.2 0.0 collective-permute-done.7.refs_0_
  37.3 13.9 %collective-permute-start.8 = (bf16[272,768]{1,0:T(8,128)(2,1)S(1)}, bf16[272,768]{1,0:T(8,128)(2,1)S(1)}, u32[]{:S(2)}, u32[]{:S(2)}) collective-permute-start(bf16[272,768]{1,0:T(8,128)(2,1)S(1)} %pack_rows.29), channel_id=1, source_target_pairs={{0,10},{1,11},{2,8},{3,9},{4,14},{5,15},{6,12},{7,13},{8,2},{9,3},... | collective-permute-start | bytes 1253384 | tf_op jit(solution)/shard_map/ppermute | solution.py:530
  51.2 1.9 %pack_rows.30 = bf16[272,768]{1,0:T(8,128)(2,1)S(1)} custom-call(s32[1]{0:T(128)} %bitcast.17.me_ref, s32[1,2048]{1,0:T(1,128)S(1)} %get-tuple-element.150.owner0_ref.owner_ref, s32[1,2048]{1,0:T(1,128)S(1)} %get-tuple-element.135.owner1_ref, s32[1,2048]{1,0:T(1,128)S(1)} %get-tuple-element.136.slot0_ref.slot_ref, ...), custom_call_target="tpu_custom_call" | custom-call | flops 272 | bytes 272 | tf_op jit(solution)/shard_map/pack_rows/pallas_call | solution.py:226
  53.1 8.2 %collective-permute-start.3 = (bf16[272,768]{1,0:T(8,128)(2,1)S(1)}, bf16[272,768]{1,0:T(8,128)(2,1)S(1)}, u32[]{:S(2)}, u32[]{:S(2)}) collective-permute-start(bf16[272,768]{1,0:T(8,128)(2,1)S(1)} %pack_rows.30), channel_id=1, source_target_pairs={{0,8},{1,9},{2,10},{3,11},{4,12},{5,13},{6,14},{7,15},{8,0},{9,1},... | collective-permute-start | bytes 1253384 | tf_op jit(solution)/shard_map/ppermute | solution.py:530
  61.3 2.1 %pack_rows.31.refs_0_ = bf16[272,768]{1,0:T(8,128)(2,1)S(1)} custom-call(s32[1]{0:T(128)} %bitcast.17.me_ref, s32[1,2048]{1,0:T(1,128)S(1)} %get-tuple-element.150.owner0_ref.owner_ref, s32[1,2048]{1,0:T(1,128)S(1)} %get-tuple-element.135.owner1_ref, s32[1,2048]{1,0:T(1,128)S(1)} %get-tuple-element.136.slot0_ref.slot_ref, ...), custom_call_target="tpu_custom_call" | custom-call | flops 272 | bytes 272 | tf_op jit(solution)/shard_map/pack_rows/pallas_call | solution.py:226
  63.4 3.0 %score_rows.9 = (bf16[1152,768]{1,0:T(8,128)(2,1)S(1)}, f32[1088,128]{1,0:T(8,128)S(1)}, f32[1088,128]{1,0:T(8,128)S(1)}, f32[8,768]{1,0:T(8,128)S(1)}) custom-call(f32[8,128]{1,0:T(8,128)S(1)} %get-tuple-element.139.bound_ref, bf16[272,768]{1,0:T(8,128)(2,1)S(1)} %pack_rows.31.refs_0_, bf16[272,768]{1,0:T(8,128)(2,1)S(1)} %collective-permute-done.4.refs_1_, ...), custom_call_target="tpu_custom_call" | custom-call | flops 2506752 | bytes 2176 | tf_op jit(solution)/shard_map/score_rows/pallas_call | solution.py:347
  66.5 2.6 %score_rows.10 = (bf16[640,768]{1,0:T(8,128)(2,1)S(1)}, f32[544,128]{1,0:T(8,128)S(1)}, f32[544,128]{1,0:T(8,128)S(1)}, f32[8,768]{1,0:T(8,128)S(1)}, f32[1088,128]{1,0:T(8,128)S(1)}) custom-call(f32[8,128]{1,0:T(8,128)S(1)} %get-tuple-element.139.bound_ref, bf16[272,768]{1,0:T(8,128)(2,1)S(1)} %collective-permute-done.7.refs_0_, ...), custom_call_target="tpu_custom_call" | custom-call | flops 2088960 | bytes 3264 | tf_op jit(solution)/shard_map/score_rows/pallas_call | solution.py:347
  69.1 18.2 %collective-permute-done.8.refs_0_ = bf16[272,768]{1,0:T(8,128)(2,1)S(1)} collective-permute-done((bf16[272,768]{1,0:T(8,128)(2,1)S(1)}, bf16[272,768]{1,0:T(8,128)(2,1)S(1)}, u32[]{:S(2)}, u32[]{:S(2)}) %collective-permute-start.8) | collective-permute-done | bytes 417824 | tf_op jit(solution)/shard_map/ppermute | solution.py:530
  87.3 2.4 %score_rows.11 = (bf16[384,768]{1,0:T(8,128)(2,1)S(1)}, f32[272,128]{1,0:T(8,128)S(1)}, f32[272,128]{1,0:T(8,128)}, f32[8,768]{1,0:T(8,128)S(1)}, f32[1088,128]{1,0:T(8,128)S(1)}, /*index=5*/f32[544,128]{1,0:T(8,128)S(1)}) custom-call(f32[8,128]{1,0:T(8,128)S(1)} %get-tuple-element.139.bound_ref, bf16[272,768]{1,0:T(8,128)(2,1)S(1)} %collective-permute-done.8.refs_0_, ...), custom_call_target="tpu_custom_call" | custom-call | flops 1462272 | bytes 3808 | tf_op jit(solution)/shard_map/score_rows/pallas_call | solution.py:347
  89.7 0.5 line_rows.3
  90.2 3.2 %collective-permute-done.3.refs_0_ = bf16[272,768]{1,0:T(8,128)(2,1)S(1)} collective-permute-done((bf16[272,768]{1,0:T(8,128)(2,1)S(1)}, bf16[272,768]{1,0:T(8,128)(2,1)S(1)}, u32[]{:S(2)}, u32[]{:S(2)}) %collective-permute-start.3) | collective-permute-done | bytes 417824 | tf_op jit(solution)/shard_map/ppermute | solution.py:530
  93.4 2.6 %finish_rows.3 = f32[16,1,768]{2,1,0:T(1,128)} custom-call(s32[1]{0:T(128)} %bitcast.17.me_ref, f32[8,128]{1,0:T(8,128)S(1)} %get-tuple-element.139.bound_ref, f32[8,128]{1,0:T(8,128)S(1)} %get-tuple-element.140.total_ref, bf16[272,768]{1,0:T(8,128)(2,1)S(1)} %collective-permute-done.3.refs_0_, bf16[1152,768]{1,0:T(8,128)(2,1)S(1)} %get-tuple-element.155.refs_2_.refs_1_, ...), custom_call_target="tpu_custom_call" | custom-call | flops 2566914048 | bytes 6684672 | tf_op jit(solution)/shard_map/finish_rows/pallas_call | solution.py:466
  96.0 3.7 %all-to-all-start.3 = ((f32[16,1,768]{2,1,0:T(1,128)}), f32[16,1,768]{2,1,0:T(1,128)S(1)}, u32[]{:S(2)}, u32[]{:S(2)}) async-start(f32[16,1,768]{2,1,0:T(1,128)} %finish_rows.3), calls=%async_computation.3 | async-start | bytes 98304 | tf_op jit(solution)/shard_map/all_to_all | solution.py:517
  99.8 6.7 %all-to-all-done.3.back_ref = f32[16,1,768]{2,1,0:T(1,128)S(1)} async-done(((f32[16,1,768]{2,1,0:T(1,128)}), f32[16,1,768]{2,1,0:T(1,128)S(1)}, u32[]{:S(2)}, u32[]{:S(2)}) %all-to-all-start.3) | async-done | bytes 49184 | tf_op jit(solution)/shard_map/all_to_all | solution.py:517
  106.5 1.6 %restore_rows.3 = (f32[1,2048]{1,0:T(1,128)}, f32[1,2048]{1,0:T(1,128)}) custom-call(s32[1,2048]{1,0:T(1,128)S(1)} %get-tuple-element.150.owner0_ref.owner_ref, s32[1,2048]{1,0:T(1,128)S(1)} %get-tuple-element.136.slot0_ref.slot_ref, f32[16,1,768]{2,1,0:T(1,128)S(1)} %all-to-all-done.3.back_ref), custom_call_target="tpu_custom_call" | custom-call | tf_op jit(solution)/shard_map/restore_rows/pallas_call | solution.py:506
  (12 shorter events, 0.0 us)
Async XLA Ops:
  0.6 1.6 %collective-permute-start = (s32[1,2048]{1,0:T(1,128)}, s32[1,2048]{1,0:T(1,128)S(1)}, u32[]{:S(2)}, u32[]{:S(2)}) collective-permute-start(s32[1,2048]{1,0:T(1,128)} %bitcast.40), channel_id=1, source_target_pairs={{0,1},{1,0},{2,3},{3,2},{4,5},{5,4},{6,7},{7,6},{8,9},{9,8},{10,11... | collective-permute-start | bytes 24584 | tf_op jit(solution)/shard_map/ppermute | solution.py:542
  2.2 16.1 %collective-permute-start.1 = (bf16[2048,768]{1,0:T(8,128)(2,1)}, bf16[2048,768]{1,0:T(8,128)(2,1)S(1)}, u32[]{:S(2)}, u32[]{:S(2)}) collective-permute-start(bf16[2048,768]{1,0:T(8,128)(2,1)} %rows0_ref.15), channel_id=1, source_target_pairs={{0,1},{1,0},{2,3},{3,2},{4,5},{5,4},{6,7},{7,6},{8,9},{9,8},{10,11... | collective-permute-start | bytes 9437192 | tf_op jit(solution)/shard_map/ppermute | solution.py:542
  2.5 0.7 copy-start.6
  3.2 15.1 %copy-start.13 = (bf16[2048,768]{1,0:T(8,128)(2,1)S(1)}, bf16[2048,768]{1,0:T(8,128)(2,1)}, u32[]{:S(2)}) copy-start(bf16[2048,768]{1,0:T(8,128)(2,1)} %rows0_ref.15) | copy-start | bytes 9437188
  18.3 43.0 %copy-start.15 = (bf16[2048,768]{1,0:T(8,128)(2,1)}, bf16[2048,768]{1,0:T(8,128)(2,1)S(1)}, u32[]{:S(2)}) copy-start(bf16[2048,768]{1,0:T(8,128)(2,1)S(1)} %collective-permute-done.1.rows1_ref) | copy-start | bytes 9437188
  20.2 17.1 %collective-permute-start.7 = (bf16[272,768]{1,0:T(8,128)(2,1)S(1)}, bf16[272,768]{1,0:T(8,128)(2,1)S(1)}, u32[]{:S(2)}, u32[]{:S(2)}) collective-permute-start(bf16[272,768]{1,0:T(8,128)(2,1)S(1)} %pack_rows.24), channel_id=1, source_target_pairs={{0,14},{1,15},{2,12},{3,13},{4,10},{5,11},{6,8},{7,9},{8,6},{9,7},... | collective-permute-start | bytes 1253384 | tf_op jit(solution)/shard_map/ppermute | solution.py:530
  22.8 30.3 %collective-permute-start.2 = (bf16[272,768]{1,0:T(8,128)(2,1)S(1)}, bf16[272,768]{1,0:T(8,128)(2,1)S(1)}, u32[]{:S(2)}, u32[]{:S(2)}) collective-permute-start(bf16[272,768]{1,0:T(8,128)(2,1)S(1)} %pack_rows.25), channel_id=1, source_target_pairs={{0,12},{1,13},{2,14},{3,15},{4,8},{5,9},{6,10},{7,11},{8,4},{9,5},... | collective-permute-start | bytes 1253384 | tf_op jit(solution)/shard_map/ppermute | solution.py:530
  31.8 31.6 %collective-permute-start.6 = (bf16[272,768]{1,0:T(8,128)(2,1)S(1)}, bf16[272,768]{1,0:T(8,128)(2,1)S(1)}, u32[]{:S(2)}, u32[]{:S(2)}) collective-permute-start(bf16[272,768]{1,0:T(8,128)(2,1)S(1)} %pack_rows.28), channel_id=1, source_target_pairs={{0,2},{1,3},{2,0},{3,1},{4,6},{5,7},{6,4},{7,5},{8,10},{9,11},{10,... | collective-permute-start | bytes 1253384 | tf_op jit(solution)/shard_map/ppermute | solution.py:530
  33.3 30.1 %collective-permute-start.5 = (bf16[272,768]{1,0:T(8,128)(2,1)S(1)}, bf16[272,768]{1,0:T(8,128)(2,1)S(1)}, u32[]{:S(2)}, u32[]{:S(2)}) collective-permute-start(bf16[272,768]{1,0:T(8,128)(2,1)S(1)} %pack_rows.27), channel_id=1, source_target_pairs={{0,4},{1,5},{2,6},{3,7},{4,0},{5,1},{6,2},{7,3},{8,12},{9,13},{10,... | collective-permute-start | bytes 1253384 | tf_op jit(solution)/shard_map/ppermute | solution.py:530
  33.3 30.1 %collective-permute-start.4 = (bf16[272,768]{1,0:T(8,128)(2,1)S(1)}, bf16[272,768]{1,0:T(8,128)(2,1)S(1)}, u32[]{:S(2)}, u32[]{:S(2)}) collective-permute-start(bf16[272,768]{1,0:T(8,128)(2,1)S(1)} %pack_rows.26), channel_id=1, source_target_pairs={{0,6},{1,7},{2,4},{3,5},{4,2},{5,3},{6,0},{7,1},{8,14},{9,15},{10,... | collective-permute-start | bytes 1253384 | tf_op jit(solution)/shard_map/ppermute | solution.py:530
  37.3 50.0 %collective-permute-start.8 = (bf16[272,768]{1,0:T(8,128)(2,1)S(1)}, bf16[272,768]{1,0:T(8,128)(2,1)S(1)}, u32[]{:S(2)}, u32[]{:S(2)}) collective-permute-start(bf16[272,768]{1,0:T(8,128)(2,1)S(1)} %pack_rows.29), channel_id=1, source_target_pairs={{0,10},{1,11},{2,8},{3,9},{4,14},{5,15},{6,12},{7,13},{8,2},{9,3},... | collective-permute-start | bytes 1253384 | tf_op jit(solution)/shard_map/ppermute | solution.py:530
  53.1 40.3 %collective-permute-start.3 = (bf16[272,768]{1,0:T(8,128)(2,1)S(1)}, bf16[272,768]{1,0:T(8,128)(2,1)S(1)}, u32[]{:S(2)}, u32[]{:S(2)}) collective-permute-start(bf16[272,768]{1,0:T(8,128)(2,1)S(1)} %pack_rows.30), channel_id=1, source_target_pairs={{0,8},{1,9},{2,10},{3,11},{4,12},{5,13},{6,14},{7,15},{8,0},{9,1},... | collective-permute-start | bytes 1253384 | tf_op jit(solution)/shard_map/ppermute | solution.py:530
  96.0 10.5 %all-to-all-start.3 = ((f32[16,1,768]{2,1,0:T(1,128)}), f32[16,1,768]{2,1,0:T(1,128)S(1)}, u32[]{:S(2)}, u32[]{:S(2)}) async-start(f32[16,1,768]{2,1,0:T(1,128)} %finish_rows.3), calls=%async_computation.3 | async-start | bytes 98304 | tf_op jit(solution)/shard_map/all_to_all | solution.py:517

commit v13 on v12

--- a/solution.py
+++ b/solution.py
@@ -44,55 +44,79 @@
     return mask.astype(f32).astype(bf16)
 
 
-def count_kernel(me_ref, ids0_ref, ids1_ref, counts_ref, rank0_ref, rank1_ref):
-    rows = ids0_ref.shape[1]
+def rank_rows(ids_ref, rank_ref, clusters):
+    label = iota((clusters, TILE), 0)
+    upto = to_bf16(iota((TILE, TILE), 0) <= iota((TILE, TILE), 1))
+    total = jnp.zeros((clusters, 1), f32)
+    for first in range(0, ids_ref.shape[1], TILE):
+        at = slice(first, first + TILE)
+        hot = ids_ref[:, at] == label
+        prefix = mm(to_bf16(hot), upto)
+        rank = jnp.sum(jnp.where(hot, prefix + total - 1.0, 0.0), axis=0, keepdims=True)
+        rank_ref[:, at] = ids_ref[:, at] * RANKS + rank.astype(i32)
+        total = total + prefix[:, TILE - 1 :]
+    return total
+
+
+def own_kernel(ids_ref, rank_ref, total_ref):
+    total = rank_rows(ids_ref, rank_ref, total_ref.shape[0])
+    total_ref[...] = jnp.broadcast_to(total, total_ref.shape)
+
+
+def rank_own(ids, clusters):
+    return pl.pallas_call(
+        own_kernel,
+        out_shape=(
+            jax.ShapeDtypeStruct(ids.shape, i32),
+            jax.ShapeDtypeStruct((clusters, LANES), f32),
+        ),
+        in_specs=[VMEM],
+        out_specs=(VMEM, VMEM),
+        compiler_params=pltpu.CompilerParams(vmem_limit_bytes=16 * MIB),
+        cost_estimate=pl.CostEstimate(flops=1_000_000_000, bytes_accessed=1 << 20, transcendentals=0),
+        name="rank_own",
+    )(ids)
+
+
+def count_kernel(
+    me_ref, ids1_ref, own_ref, total_ref, counts_ref, rank0_ref, rank1_ref
+):
+    rows = ids1_ref.shape[1]
     chips, _, clusters = counts_ref.shape
     core = me_ref[0] & 1
     label = iota((clusters, TILE), 0)
-    upto = to_bf16(iota((TILE, TILE), 0) <= iota((TILE, TILE), 1))
-    totals = []
-    for ids_ref, rank_ref in ((ids0_ref, rank0_ref), (ids1_ref, rank1_ref)):
-        total = jnp.zeros((clusters, 1), f32)
-        for b in range(rows // TILE):
-            at = slice(b * TILE, (b + 1) * TILE)
-            hot = ids_ref[:, at] == label
-            prefix = mm(to_bf16(hot), upto)
-            rank = jnp.sum(jnp.where(hot, prefix + total - 1.0, 0.0), axis=0, keepdims=True)
-            rank_ref[:, at] = ids_ref[:, at] * RANKS + rank.astype(i32)
-            total = total + prefix[:, TILE - 1 :]
-        totals.append(total)
-    ahead0 = jnp.where(core == 1, totals[1], 0.0)
-    ahead1 = jnp.where(core == 0, totals[0], 0.0)
-    for ids_ref, rank_ref, ahead in (
-        (ids0_ref, rank0_ref, ahead0),
-        (ids1_ref, rank1_ref, ahead1),
-    ):
-        for b in range(rows // TILE):
-            at = slice(b * TILE, (b + 1) * TILE)
-            more = jnp.where(ids_ref[:, at] == label, ahead, 0.0)
-            rank_ref[:, at] += jnp.sum(more, axis=0, keepdims=True).astype(i32)
+    total0 = total_ref[:, 0:1]
+    total1 = rank_rows(ids1_ref, rank1_ref, clusters)
     square = (clusters, clusters)
     eye = iota(square, 0) == iota(square, 1)
-    both = totals[0] + totals[1]
-    total_row = jnp.sum(jnp.where(eye, both, 0.0), axis=0, keepdims=True).astype(i32)
+    total_row = jnp.sum(jnp.where(eye, total0 + total1, 0.0), axis=0, keepdims=True).astype(i32)
     for chip in range(chips):
         counts_ref[chip] = total_row
-
-
-def count_rows(me, ids0, ids1, chips, clusters):
+    for from_ref, rank_ref, ahead in (
+        (own_ref, rank0_ref, jnp.where(core == 1, total1, 0.0)),
+        (rank1_ref, rank1_ref, jnp.where(core == 0, total0, 0.0)),
+    ):
+        for first in range(0, rows, TILE):
+            at = slice(first, first + TILE)
+            rank = from_ref[:, at]
+            more = jnp.where((rank // RANKS) == label, ahead, 0.0)
+            rank_ref[:, at] = rank + jnp.sum(more, axis=0, keepdims=True).astype(i32)
+
+
+def count_rows(me, ids1, own, total, chips, clusters):
     return pl.pallas_call(
         count_kernel,
         out_shape=(
             jax.ShapeDtypeStruct((chips, 1, clusters), i32),
-            jax.ShapeDtypeStruct(ids0.shape, i32),
-            jax.ShapeDtypeStruct(ids0.shape, i32),
+            jax.ShapeDtypeStruct(ids1.shape, i32),
+            jax.ShapeDtypeStruct(ids1.shape, i32),
         ),
-        in_specs=[SMEM, VMEM, VMEM],
+        in_specs=[SMEM, VMEM, VMEM, VMEM],
         out_specs=(VMEM,) * 3,
         compiler_params=pltpu.CompilerParams(vmem_limit_bytes=16 * MIB),
         cost_estimate=pl.CostEstimate(flops=8_000_000_000, bytes_accessed=1 << 20, transcendentals=0),
         name="count_rows",
-    )(me, ids0, ids1)
+    )(me, ids1, own, total)
 
 
 def assign_kernel(
@@ -126,21 +150,23 @@
     rank_col = jnp.sum(outranks_col.astype(f32), axis=1, keepdims=True).astype(i32)
     rank_row = jnp.sum(outranks_row.astype(f32), axis=0, keepdims=True).astype(i32)
 
-    def owner_of(rank, variant):
-        layer = rank >> shift
-        within = rank & (owners - 1)
-        flip = jnp.zeros_like(variant)
-        for p in range(1, CL_DEV):
-            bits = (variant >> (p - 1)) & 1
-            if p < CL_DEV - 1:
-                bits = bits + 2 * ((variant >> (p + CL_DEV - 2)) & 1)
-            flip = flip + jnp.where(layer == p, bits, 0)
-        within = within ^ flip
-        return jnp.where((layer & 1) == 1, owners - 1 - within, within)
-
-    wide = (clusters, VARIANTS * owners)
-    variant = iota(wide, 1) >> shift
-    tried = owner_of(rank_col, variant) == (iota(wide, 1) & (owners - 1))
+    layer_col, layer_row = rank_col >> shift, rank_row >> shift
+
+    def plain(rank, layer):
+        return (rank & (owners - 1)) ^ jnp.where((layer & 1) == 1, owners - 1, 0)
+
+    def flip(p, variant):
+        bits = (variant >> (p - 1)) & 1
+        if p < CL_DEV - 1:
+            bits = bits + 2 * ((variant >> (p + CL_DEV - 2)) & 1)
+        return bits
+
+    lanes = iota((1, VARIANTS * owners), 1)
+    target = lanes & (owners - 1)
+    for p in range(1, CL_DEV):
+        swapped = (lanes & (owners - 1)) ^ flip(p, lanes >> shift)
+        target = jnp.where(layer_col == p, swapped, target)
+    tried = plain(rank_col, layer_col) == target
     load = jnp.max(mm(count16, to_bf16(tried)), axis=0, keepdims=True)
     by_variant = (VARIANTS, VARIANTS * owners)
     worst = jnp.max(
@@ -152,9 +178,15 @@
     chosen = jnp.min(
         jnp.where(worst == best, iota((VARIANTS, 1), 0), VARIANTS), axis=0, keepdims=True
     )
-    owner_col = owner_of(rank_col, chosen + jnp.zeros_like(rank_col))
-    owner_row = owner_of(rank_row, chosen + jnp.zeros_like(rank_row))
-    layer_col, layer_row = rank_col >> shift, rank_row >> shift
+
+    def owner_of(rank, layer):
+        swaps = jnp.zeros_like(rank)
+        for p in range(1, CL_DEV):
+            swaps = jnp.where(layer == p, flip(p, chosen), swaps)
+        return plain(rank, layer) ^ swaps
+
+    owner_col = owner_of(rank_col, layer_col)
+    owner_row = owner_of(rank_row, layer_row)
     load_ref[...] = jnp.broadcast_to(best, load_ref.shape).astype(i32)
 
     mine = jnp.sum(jnp.where(iota(count.shape, 0) == chip, count, 0.0), axis=0, keepdims=True)
@@ -554,9 +586,10 @@
     me = lax.axis_index("owner").astype(i32).reshape(1)
     ids0 = cluster_ids.reshape(1, rows)
     ids1 = swap_cores(ids0)
-    mine, ids1 = lax.optimization_barrier((embeddings, ids1))
+    own, own_total = rank_own(ids0, clusters)
+    mine, ids1, own = lax.optimization_barrier((embeddings, ids1, own))
     other = swap_cores(mine)
-    counts, rank0, rank1 = count_rows(me, ids0, ids1, chips, clusters)
+    counts, rank0, rank1 = count_rows(me, ids1, own, own_total, chips, clusters)
     counts = exchange_chips(counts)
     both = (embeddings, other)
     *places, bound, total, load = assign(me, counts, rank0, rank1)

time: 108 us -> 107 us (level)
  waiting for transfers between devices: 29.2 us -> 28.1 us
  transfers between devices with their start and end apart: 10 -> 10, of which waited for: 4 -> 3; matrix products, arithmetic and copies ran while one was open for 0% -> 0% of each run, Pallas kernels for 22% -> 22%
where the time goes in v13:
time: 107 us
  starting transfers between devices  34.2 us (32%)
  Pallas kernels  29.8 us (28%)
  waiting for transfers between devices  28.1 us (26%)
  blocking collectives  13.5 us (13%)
    ppermute x7, starting transfers between devices, swap(): return lax.ppermute(block, 'owner', [(s, s ^ 2 * r) for s in range(owners)])  29.7 us
    ppermute x7, waiting for transfers between devices, swap(): return lax.ppermute(block, 'owner', [(s, s ^ 2 * r) for s in range(owners)])  21.3 us
    pallas_call x8, Pallas kernels, pack(): pl.pallas_call(functools.partial(pack_kernel, partner), out_shape=jax.Sha...  15.3 us
    all_to_all x1, blocking collectives, exchange_chips(): lax.all_to_all(x, 'owner', split_axis=0, concat_axis=0, axis_index_groups...  13.5 us
    pallas_call x3, Pallas kernels, score(): pl.pallas_call(functools.partial(score_kernel, slots, partners, len(units...  8.01 us
    all_to_all x1, waiting for transfers between devices, exchange(): return lax.all_to_all(x, 'owner', split_axis=0, concat_axis=0, tiled=True)  6.73 us
    all_to_all x1, starting transfers between devices, exchange(): return lax.all_to_all(x, 'owner', split_axis=0, concat_axis=0, tiled=True)  3.74 us
    pallas_call x1, Pallas kernels, finish(): pl.pallas_call(functools.partial(finish_kernel, slots, partners, earlier)...  2.6 us
  transfers between devices with their start and end apart: 10, of which 3 were waited for; matrix products, arithmetic and copies ran while one was open for 0% of the time, Pallas kernels for 22%

profile of v13, /device:TPU:0, one launch (start us, length us, event | category | flops | bytes accessed | tf_op | source)
XLA Modules:
  0.0 107.2 jit_solution(18166273141394186683)
XLA Ops:
  0.6 0.5 collective-permute-start
  1.1 0.7 copy-done.6
  1.8 0.4 rank_own.1
  2.3 0.3 collective-permute-start.1
  2.5 0.6 count_rows.1
  3.1 13.5 %all_to_all.20.counts_ref = s32[8,1,64]{2,1,0:T(1,128)S(1)} all-to-all(s32[8,1,64]{2,1,0:T(1,128)S(1)} %get-tuple-element.136), channel_id=1, replica_groups={{0,2,4,6,8,10,12,14},{1,3,5,7,9,11,13,15},{16,18,20,22,24,26,28,30},{17..., dimensions={0} | all-to-all | bytes 4096 | tf_op jit(solution)/shard_map/all_to_all | solution.py:555
  16.7 0.8 assign.1
  17.5 1.9 %pack_rows.24 = bf16[272,768]{1,0:T(8,128)(2,1)S(1)} custom-call(s32[1]{0:T(128)} %bitcast.17.me_ref, s32[1,2048]{1,0:T(1,128)S(1)} %get-tuple-element.156.owner0_ref.owner_ref, s32[1,2048]{1,0:T(1,128)S(1)} %get-tuple-element.141.owner1_ref, s32[1,2048]{1,0:T(1,128)S(1)} %get-tuple-element.142.slot0_ref.slot_ref, ...), custom_call_target="tpu_custom_call" | custom-call | flops 272 | bytes 272 | tf_op jit(solution)/shard_map/pack_rows/pallas_call | solution.py:258
  19.4 0.6 collective-permute-start.7
  20.1 1.9 %pack_rows.25 = bf16[272,768]{1,0:T(8,128)(2,1)S(1)} custom-call(s32[1]{0:T(128)} %bitcast.17.me_ref, s32[1,2048]{1,0:T(1,128)S(1)} %get-tuple-element.156.owner0_ref.owner_ref, s32[1,2048]{1,0:T(1,128)S(1)} %get-tuple-element.141.owner1_ref, s32[1,2048]{1,0:T(1,128)S(1)} %get-tuple-element.142.slot0_ref.slot_ref, ...), custom_call_target="tpu_custom_call" | custom-call | flops 272 | bytes 272 | tf_op jit(solution)/shard_map/pack_rows/pallas_call | solution.py:258
  22.0 3.3 %collective-permute-start.2 = (bf16[272,768]{1,0:T(8,128)(2,1)S(1)}, bf16[272,768]{1,0:T(8,128)(2,1)S(1)}, u32[]{:S(2)}, u32[]{:S(2)}) collective-permute-start(bf16[272,768]{1,0:T(8,128)(2,1)S(1)} %pack_rows.25), channel_id=1, source_target_pairs={{0,12},{1,13},{2,14},{3,15},{4,8},{5,9},{6,10},{7,11},{8,4},{9,5},... | collective-permute-start | bytes 1253384 | tf_op jit(solution)/shard_map/ppermute | solution.py:562
  25.3 1.9 %pack_rows.26 = bf16[272,768]{1,0:T(8,128)(2,1)S(1)} custom-call(s32[1]{0:T(128)} %bitcast.17.me_ref, s32[1,2048]{1,0:T(1,128)S(1)} %get-tuple-element.156.owner0_ref.owner_ref, s32[1,2048]{1,0:T(1,128)S(1)} %get-tuple-element.141.owner1_ref, s32[1,2048]{1,0:T(1,128)S(1)} %get-tuple-element.142.slot0_ref.slot_ref, ...), custom_call_target="tpu_custom_call" | custom-call | flops 272 | bytes 272 | tf_op jit(solution)/shard_map/pack_rows/pallas_call | solution.py:258
  27.2 1.9 %pack_rows.27 = bf16[272,768]{1,0:T(8,128)(2,1)S(1)} custom-call(s32[1]{0:T(128)} %bitcast.17.me_ref, s32[1,2048]{1,0:T(1,128)S(1)} %get-tuple-element.156.owner0_ref.owner_ref, s32[1,2048]{1,0:T(1,128)S(1)} %get-tuple-element.141.owner1_ref, s32[1,2048]{1,0:T(1,128)S(1)} %get-tuple-element.142.slot0_ref.slot_ref, ...), custom_call_target="tpu_custom_call" | custom-call | flops 272 | bytes 272 | tf_op jit(solution)/shard_map/pack_rows/pallas_call | solution.py:258
  29.1 1.9 %pack_rows.28 = bf16[272,768]{1,0:T(8,128)(2,1)S(1)} custom-call(s32[1]{0:T(128)} %bitcast.17.me_ref, s32[1,2048]{1,0:T(1,128)S(1)} %get-tuple-element.156.owner0_ref.owner_ref, s32[1,2048]{1,0:T(1,128)S(1)} %get-tuple-element.141.owner1_ref, s32[1,2048]{1,0:T(1,128)S(1)} %get-tuple-element.142.slot0_ref.slot_ref, ...), custom_call_target="tpu_custom_call" | custom-call | flops 272 | bytes 272 | tf_op jit(solution)/shard_map/pack_rows/pallas_call | solution.py:258
  31.0 1.5 %collective-permute-start.6 = (bf16[272,768]{1,0:T(8,128)(2,1)S(1)}, bf16[272,768]{1,0:T(8,128)(2,1)S(1)}, u32[]{:S(2)}, u32[]{:S(2)}) collective-permute-start(bf16[272,768]{1,0:T(8,128)(2,1)S(1)} %pack_rows.28), channel_id=1, source_target_pairs={{0,2},{1,3},{2,0},{3,1},{4,6},{5,7},{6,4},{7,5},{8,10},{9,11},{10,... | collective-permute-start | bytes 1253384 | tf_op jit(solution)/shard_map/ppermute | solution.py:562
  32.5 0.0 collective-permute-start.5
  32.5 2.0 %collective-permute-start.4 = (bf16[272,768]{1,0:T(8,128)(2,1)S(1)}, bf16[272,768]{1,0:T(8,128)(2,1)S(1)}, u32[]{:S(2)}, u32[]{:S(2)}) collective-permute-start(bf16[272,768]{1,0:T(8,128)(2,1)S(1)} %pack_rows.26), channel_id=1, source_target_pairs={{0,6},{1,7},{2,4},{3,5},{4,2},{5,3},{6,0},{7,1},{8,14},{9,15},{10,... | collective-permute-start | bytes 1253384 | tf_op jit(solution)/shard_map/ppermute | solution.py:562
  34.5 1.9 %pack_rows.29 = bf16[272,768]{1,0:T(8,128)(2,1)S(1)} custom-call(s32[1]{0:T(128)} %bitcast.17.me_ref, s32[1,2048]{1,0:T(1,128)S(1)} %get-tuple-element.156.owner0_ref.owner_ref, s32[1,2048]{1,0:T(1,128)S(1)} %get-tuple-element.141.owner1_ref, s32[1,2048]{1,0:T(1,128)S(1)} %get-tuple-element.142.slot0_ref.slot_ref, ...), custom_call_target="tpu_custom_call" | custom-call | flops 272 | bytes 272 | tf_op jit(solution)/shard_map/pack_rows/pallas_call | solution.py:258
  36.4 13.8 %collective-permute-start.8 = (bf16[272,768]{1,0:T(8,128)(2,1)S(1)}, bf16[272,768]{1,0:T(8,128)(2,1)S(1)}, u32[]{:S(2)}, u32[]{:S(2)}) collective-permute-start(bf16[272,768]{1,0:T(8,128)(2,1)S(1)} %pack_rows.29), channel_id=1, source_target_pairs={{0,10},{1,11},{2,8},{3,9},{4,14},{5,15},{6,12},{7,13},{8,2},{9,3},... | collective-permute-start | bytes 1253384 | tf_op jit(solution)/shard_map/ppermute | solution.py:562
  50.3 1.9 %pack_rows.30 = bf16[272,768]{1,0:T(8,128)(2,1)S(1)} custom-call(s32[1]{0:T(128)} %bitcast.17.me_ref, s32[1,2048]{1,0:T(1,128)S(1)} %get-tuple-element.156.owner0_ref.owner_ref, s32[1,2048]{1,0:T(1,128)S(1)} %get-tuple-element.141.owner1_ref, s32[1,2048]{1,0:T(1,128)S(1)} %get-tuple-element.142.slot0_ref.slot_ref, ...), custom_call_target="tpu_custom_call" | custom-call | flops 272 | bytes 272 | tf_op jit(solution)/shard_map/pack_rows/pallas_call | solution.py:258
  52.2 8.4 %collective-permute-start.3 = (bf16[272,768]{1,0:T(8,128)(2,1)S(1)}, bf16[272,768]{1,0:T(8,128)(2,1)S(1)}, u32[]{:S(2)}, u32[]{:S(2)}) collective-permute-start(bf16[272,768]{1,0:T(8,128)(2,1)S(1)} %pack_rows.30), channel_id=1, source_target_pairs={{0,8},{1,9},{2,10},{3,11},{4,12},{5,13},{6,14},{7,15},{8,0},{9,1},... | collective-permute-start | bytes 1253384 | tf_op jit(solution)/shard_map/ppermute | solution.py:562
  60.6 2.1 %pack_rows.31.refs_0_ = bf16[272,768]{1,0:T(8,128)(2,1)S(1)} custom-call(s32[1]{0:T(128)} %bitcast.17.me_ref, s32[1,2048]{1,0:T(1,128)S(1)} %get-tuple-element.156.owner0_ref.owner_ref, s32[1,2048]{1,0:T(1,128)S(1)} %get-tuple-element.141.owner1_ref, s32[1,2048]{1,0:T(1,128)S(1)} %get-tuple-element.142.slot0_ref.slot_ref, ...), custom_call_target="tpu_custom_call" | custom-call | flops 272 | bytes 272 | tf_op jit(solution)/shard_map/pack_rows/pallas_call | solution.py:258
  62.7 3.0 %score_rows.9 = (bf16[1152,768]{1,0:T(8,128)(2,1)S(1)}, f32[1088,128]{1,0:T(8,128)S(1)}, f32[1088,128]{1,0:T(8,128)S(1)}, f32[8,768]{1,0:T(8,128)S(1)}) custom-call(f32[8,128]{1,0:T(8,128)S(1)} %get-tuple-element.145.bound_ref, bf16[272,768]{1,0:T(8,128)(2,1)S(1)} %pack_rows.31.refs_0_, bf16[272,768]{1,0:T(8,128)(2,1)S(1)} %collective-permute-done.4.refs_1_, ...), custom_call_target="tpu_custom_call" | custom-call | flops 2506752 | bytes 2176 | tf_op jit(solution)/shard_map/score_rows/pallas_call | solution.py:379
  65.7 2.6 %score_rows.10 = (bf16[640,768]{1,0:T(8,128)(2,1)S(1)}, f32[544,128]{1,0:T(8,128)S(1)}, f32[544,128]{1,0:T(8,128)S(1)}, f32[8,768]{1,0:T(8,128)S(1)}, f32[1088,128]{1,0:T(8,128)S(1)}) custom-call(f32[8,128]{1,0:T(8,128)S(1)} %get-tuple-element.145.bound_ref, bf16[272,768]{1,0:T(8,128)(2,1)S(1)} %collective-permute-done.7.refs_0_, ...), custom_call_target="tpu_custom_call" | custom-call | flops 2088960 | bytes 3264 | tf_op jit(solution)/shard_map/score_rows/pallas_call | solution.py:379
  68.3 18.1 %collective-permute-done.8.refs_0_ = bf16[272,768]{1,0:T(8,128)(2,1)S(1)} collective-permute-done((bf16[272,768]{1,0:T(8,128)(2,1)S(1)}, bf16[272,768]{1,0:T(8,128)(2,1)S(1)}, u32[]{:S(2)}, u32[]{:S(2)}) %collective-permute-start.8) | collective-permute-done | bytes 417824 | tf_op jit(solution)/shard_map/ppermute | solution.py:562
  86.4 2.4 %score_rows.11 = (bf16[384,768]{1,0:T(8,128)(2,1)S(1)}, f32[272,128]{1,0:T(8,128)S(1)}, f32[272,128]{1,0:T(8,128)}, f32[8,768]{1,0:T(8,128)S(1)}, f32[1088,128]{1,0:T(8,128)S(1)}, /*index=5*/f32[544,128]{1,0:T(8,128)S(1)}) custom-call(f32[8,128]{1,0:T(8,128)S(1)} %get-tuple-element.145.bound_ref, bf16[272,768]{1,0:T(8,128)(2,1)S(1)} %collective-permute-done.8.refs_0_, ...), custom_call_target="tpu_custom_call" | custom-call | flops 1462272 | bytes 3808 | tf_op jit(solution)/shard_map/score_rows/pallas_call | solution.py:379
  88.8 0.5 line_rows.3
  89.3 3.2 %collective-permute-done.3.refs_0_ = bf16[272,768]{1,0:T(8,128)(2,1)S(1)} collective-permute-done((bf16[272,768]{1,0:T(8,128)(2,1)S(1)}, bf16[272,768]{1,0:T(8,128)(2,1)S(1)}, u32[]{:S(2)}, u32[]{:S(2)}) %collective-permute-start.3) | collective-permute-done | bytes 417824 | tf_op jit(solution)/shard_map/ppermute | solution.py:562
  92.5 2.6 %finish_rows.3 = f32[16,1,768]{2,1,0:T(1,128)} custom-call(s32[1]{0:T(128)} %bitcast.17.me_ref, f32[8,128]{1,0:T(8,128)S(1)} %get-tuple-element.145.bound_ref, f32[8,128]{1,0:T(8,128)S(1)} %get-tuple-element.146.total_ref, bf16[272,768]{1,0:T(8,128)(2,1)S(1)} %collective-permute-done.3.refs_0_, bf16[1152,768]{1,0:T(8,128)(2,1)S(1)} %get-tuple-element.161.refs_2_.refs_1_, ...), custom_call_target="tpu_custom_call" | custom-call | flops 2566914048 | bytes 6684672 | tf_op jit(solution)/shard_map/finish_rows/pallas_call | solution.py:498
  95.1 3.7 %all-to-all-start.3 = ((f32[16,1,768]{2,1,0:T(1,128)}), f32[16,1,768]{2,1,0:T(1,128)S(1)}, u32[]{:S(2)}, u32[]{:S(2)}) async-start(f32[16,1,768]{2,1,0:T(1,128)} %finish_rows.3), calls=%async_computation.3 | async-start | bytes 98304 | tf_op jit(solution)/shard_map/all_to_all | solution.py:549
  98.9 6.7 %all-to-all-done.3.back_ref = f32[16,1,768]{2,1,0:T(1,128)S(1)} async-done(((f32[16,1,768]{2,1,0:T(1,128)}), f32[16,1,768]{2,1,0:T(1,128)S(1)}, u32[]{:S(2)}, u32[]{:S(2)}) %all-to-all-start.3) | async-done | bytes 49184 | tf_op jit(solution)/shard_map/all_to_all | solution.py:549
  105.6 1.6 %restore_rows.3 = (f32[1,2048]{1,0:T(1,128)}, f32[1,2048]{1,0:T(1,128)}) custom-call(s32[1,2048]{1,0:T(1,128)S(1)} %get-tuple-element.156.owner0_ref.owner_ref, s32[1,2048]{1,0:T(1,128)S(1)} %get-tuple-element.142.slot0_ref.slot_ref, f32[16,1,768]{2,1,0:T(1,128)S(1)} %all-to-all-done.3.back_ref), custom_call_target="tpu_custom_call" | custom-call | tf_op jit(solution)/shard_map/restore_rows/pallas_call | solution.py:538
  (13 shorter events, 0.0 us)
Async XLA Ops:
  0.6 1.6 %collective-permute-start = (s32[1,2048]{1,0:T(1,128)}, s32[1,2048]{1,0:T(1,128)S(1)}, u32[]{:S(2)}, u32[]{:S(2)}) collective-permute-start(s32[1,2048]{1,0:T(1,128)} %bitcast.40), channel_id=1, source_target_pairs={{0,1},{1,0},{2,3},{3,2},{4,5},{5,4},{6,7},{7,6},{8,9},{9,8},{10,11... | collective-permute-start | bytes 24584 | tf_op jit(solution)/shard_map/ppermute | solution.py:574
  1.1 0.7 copy-start.6
  2.3 15.3 %collective-permute-start.1 = (bf16[2048,768]{1,0:T(8,128)(2,1)}, bf16[2048,768]{1,0:T(8,128)(2,1)S(1)}, u32[]{:S(2)}, u32[]{:S(2)}) collective-permute-start(bf16[2048,768]{1,0:T(8,128)(2,1)} %rows0_ref.15), channel_id=1, source_target_pairs={{0,1},{1,0},{2,3},{3,2},{4,5},{5,4},{6,7},{7,6},{8,9},{9,8},{10,11... | collective-permute-start | bytes 9437192 | tf_op jit(solution)/shard_map/ppermute | solution.py:574
  2.5 15.0 %copy-start.13 = (bf16[2048,768]{1,0:T(8,128)(2,1)S(1)}, bf16[2048,768]{1,0:T(8,128)(2,1)}, u32[]{:S(2)}) copy-start(bf16[2048,768]{1,0:T(8,128)(2,1)} %rows0_ref.15) | copy-start | bytes 9437188
  17.5 43.0 %copy-start.15 = (bf16[2048,768]{1,0:T(8,128)(2,1)}, bf16[2048,768]{1,0:T(8,128)(2,1)S(1)}, u32[]{:S(2)}) copy-start(bf16[2048,768]{1,0:T(8,128)(2,1)S(1)} %collective-permute-done.1.rows1_ref) | copy-start | bytes 9437188
  19.4 17.0 %collective-permute-start.7 = (bf16[272,768]{1,0:T(8,128)(2,1)S(1)}, bf16[272,768]{1,0:T(8,128)(2,1)S(1)}, u32[]{:S(2)}, u32[]{:S(2)}) collective-permute-start(bf16[272,768]{1,0:T(8,128)(2,1)S(1)} %pack_rows.24), channel_id=1, source_target_pairs={{0,14},{1,15},{2,12},{3,13},{4,10},{5,11},{6,8},{7,9},{8,6},{9,7},... | collective-permute-start | bytes 1253384 | tf_op jit(solution)/shard_map/ppermute | solution.py:562
  22.0 30.2 %collective-permute-start.2 = (bf16[272,768]{1,0:T(8,128)(2,1)S(1)}, bf16[272,768]{1,0:T(8,128)(2,1)S(1)}, u32[]{:S(2)}, u32[]{:S(2)}) collective-permute-start(bf16[272,768]{1,0:T(8,128)(2,1)S(1)} %pack_rows.25), channel_id=1, source_target_pairs={{0,12},{1,13},{2,14},{3,15},{4,8},{5,9},{6,10},{7,11},{8,4},{9,5},... | collective-permute-start | bytes 1253384 | tf_op jit(solution)/shard_map/ppermute | solution.py:562
  31.0 31.7 %collective-permute-start.6 = (bf16[272,768]{1,0:T(8,128)(2,1)S(1)}, bf16[272,768]{1,0:T(8,128)(2,1)S(1)}, u32[]{:S(2)}, u32[]{:S(2)}) collective-permute-start(bf16[272,768]{1,0:T(8,128)(2,1)S(1)} %pack_rows.28), channel_id=1, source_target_pairs={{0,2},{1,3},{2,0},{3,1},{4,6},{5,7},{6,4},{7,5},{8,10},{9,11},{10,... | collective-permute-start | bytes 1253384 | tf_op jit(solution)/shard_map/ppermute | solution.py:562
  32.5 30.1 %collective-permute-start.5 = (bf16[272,768]{1,0:T(8,128)(2,1)S(1)}, bf16[272,768]{1,0:T(8,128)(2,1)S(1)}, u32[]{:S(2)}, u32[]{:S(2)}) collective-permute-start(bf16[272,768]{1,0:T(8,128)(2,1)S(1)} %pack_rows.27), channel_id=1, source_target_pairs={{0,4},{1,5},{2,6},{3,7},{4,0},{5,1},{6,2},{7,3},{8,12},{9,13},{10,... | collective-permute-start | bytes 1253384 | tf_op jit(solution)/shard_map/ppermute | solution.py:562
  32.5 30.1 %collective-permute-start.4 = (bf16[272,768]{1,0:T(8,128)(2,1)S(1)}, bf16[272,768]{1,0:T(8,128)(2,1)S(1)}, u32[]{:S(2)}, u32[]{:S(2)}) collective-permute-start(bf16[272,768]{1,0:T(8,128)(2,1)S(1)} %pack_rows.26), channel_id=1, source_target_pairs={{0,6},{1,7},{2,4},{3,5},{4,2},{5,3},{6,0},{7,1},{8,14},{9,15},{10,... | collective-permute-start | bytes 1253384 | tf_op jit(solution)/shard_map/ppermute | solution.py:562
  36.4 50.0 %collective-permute-start.8 = (bf16[272,768]{1,0:T(8,128)(2,1)S(1)}, bf16[272,768]{1,0:T(8,128)(2,1)S(1)}, u32[]{:S(2)}, u32[]{:S(2)}) collective-permute-start(bf16[272,768]{1,0:T(8,128)(2,1)S(1)} %pack_rows.29), channel_id=1, source_target_pairs={{0,10},{1,11},{2,8},{3,9},{4,14},{5,15},{6,12},{7,13},{8,2},{9,3},... | collective-permute-start | bytes 1253384 | tf_op jit(solution)/shard_map/ppermute | solution.py:562
  52.2 40.3 %collective-permute-start.3 = (bf16[272,768]{1,0:T(8,128)(2,1)S(1)}, bf16[272,768]{1,0:T(8,128)(2,1)S(1)}, u32[]{:S(2)}, u32[]{:S(2)}) collective-permute-start(bf16[272,768]{1,0:T(8,128)(2,1)S(1)} %pack_rows.30), channel_id=1, source_target_pairs={{0,8},{1,9},{2,10},{3,11},{4,12},{5,13},{6,14},{7,15},{8,0},{9,1},... | collective-permute-start | bytes 1253384 | tf_op jit(solution)/shard_map/ppermute | solution.py:562
  95.1 10.5 %all-to-all-start.3 = ((f32[16,1,768]{2,1,0:T(1,128)}), f32[16,1,768]{2,1,0:T(1,128)S(1)}, u32[]{:S(2)}, u32[]{:S(2)}) async-start(f32[16,1,768]{2,1,0:T(1,128)} %finish_rows.3), calls=%async_computation.3 | async-start | bytes 98304 | tf_op jit(solution)/shard_map/all_to_all | solution.py:549

commit v14 on v13

--- a/solution.py
+++ b/solution.py
@@ -597,6 +597,7 @@
 
     half = chips // 2
     far = list(range(chips - 1, half - 1, -1))
+    far = far[: half // 2 : 2] + far[half // 2 :: 2] + far[1 : half // 2 : 2] + far[half // 2 + 1 :: 2]
     near = list(range(half - 1, 0, -1))
     sent = far[:2] + near + far[2:] + [0]
     share = max(half // 4, 1)

time: 107 us -> 108 us (level)
  waiting for transfers between devices: 28.1 us -> 49.7 us
  starting transfers between devices: 34.2 us -> 12.7 us
    ppermute x7, waiting for transfers between devices: 21.3 us -> 43 us  [swap(): return lax.ppermute(block, 'owner', [(s, s ^ 2 * r) for s in range(owners)])]
    ppermute x7, starting transfers between devices: 29.7 us -> 8.13 us  [swap(): return lax.ppermute(block, 'owner', [(s, s ^ 2 * r) for s in range(owners)])]
where the time goes in v14:
time: 108 us; the launch traced here: 107 us
  waiting for transfers between devices  49.7 us (46%)
  Pallas kernels  29.8 us (28%)
  blocking collectives  13.5 us (12%)
  starting transfers between devices  12.7 us (12%)
    ppermute x7, waiting for transfers between devices, swap(): return lax.ppermute(block, 'owner', [(s, s ^ 2 * r) for s in range(owners)])  43 us
    pallas_call x8, Pallas kernels, pack(): pl.pallas_call(functools.partial(pack_kernel, partner), out_shape=jax.Sha...  15.3 us
    all_to_all x1, blocking collectives, exchange_chips(): lax.all_to_all(x, 'owner', split_axis=0, concat_axis=0, axis_index_groups...  13.5 us
    ppermute x7, starting transfers between devices, swap(): return lax.ppermute(block, 'owner', [(s, s ^ 2 * r) for s in range(owners)])  8.13 us
    pallas_call x3, Pallas kernels, score(): pl.pallas_call(functools.partial(score_kernel, slots, partners, len(units...  8.01 us
    all_to_all x1, waiting for transfers between devices, exchange(): return lax.all_to_all(x, 'owner', split_axis=0, concat_axis=0, tiled=True)  6.73 us
    all_to_all x1, starting transfers between devices, exchange(): return lax.all_to_all(x, 'owner', split_axis=0, concat_axis=0, tiled=True)  3.73 us
    pallas_call x1, Pallas kernels, finish(): pl.pallas_call(functools.partial(finish_kernel, slots, partners, earlier)...  2.61 us
  transfers between devices with their start and end apart: 10, of which 3 were waited for; matrix products, arithmetic and copies ran while one was open for 0% of the time, Pallas kernels for 22%

profile of v14, /device:TPU:0, one launch (start us, length us, event | category | flops | bytes accessed | tf_op | source)
XLA Modules:
  0.0 107.3 jit_solution(637073166925324901)
XLA Ops:
  0.6 0.5 collective-permute-start
  1.1 0.7 copy-done.6
  1.8 0.4 rank_own.1
  2.2 0.0 collective-permute-done.ids1_ref
  2.3 0.3 collective-permute-start.1
  2.5 0.6 count_rows.1
  3.1 13.5 %all_to_all.20.counts_ref = s32[8,1,64]{2,1,0:T(1,128)S(1)} all-to-all(s32[8,1,64]{2,1,0:T(1,128)S(1)} %get-tuple-element.136), channel_id=1, replica_groups={{0,2,4,6,8,10,12,14},{1,3,5,7,9,11,13,15},{16,18,20,22,24,26,28,30},{17..., dimensions={0} | all-to-all | bytes 4096 | tf_op jit(solution)/shard_map/all_to_all | solution.py:555
  16.7 0.8 assign.1
  17.5 1.9 %pack_rows.24 = bf16[272,768]{1,0:T(8,128)(2,1)S(1)} custom-call(s32[1]{0:T(128)} %bitcast.17.me_ref, s32[1,2048]{1,0:T(1,128)S(1)} %get-tuple-element.156.owner0_ref.owner_ref, s32[1,2048]{1,0:T(1,128)S(1)} %get-tuple-element.141.owner1_ref, s32[1,2048]{1,0:T(1,128)S(1)} %get-tuple-element.142.slot0_ref.slot_ref, ...), custom_call_target="tpu_custom_call" | custom-call | flops 272 | bytes 272 | tf_op jit(solution)/shard_map/pack_rows/pallas_call | solution.py:258
  19.4 0.6 collective-permute-start.7
  20.1 1.9 %pack_rows.25 = bf16[272,768]{1,0:T(8,128)(2,1)S(1)} custom-call(s32[1]{0:T(128)} %bitcast.17.me_ref, s32[1,2048]{1,0:T(1,128)S(1)} %get-tuple-element.156.owner0_ref.owner_ref, s32[1,2048]{1,0:T(1,128)S(1)} %get-tuple-element.141.owner1_ref, s32[1,2048]{1,0:T(1,128)S(1)} %get-tuple-element.142.slot0_ref.slot_ref, ...), custom_call_target="tpu_custom_call" | custom-call | flops 272 | bytes 272 | tf_op jit(solution)/shard_map/pack_rows/pallas_call | solution.py:258
  22.0 2.4 %collective-permute-start.2 = (bf16[272,768]{1,0:T(8,128)(2,1)S(1)}, bf16[272,768]{1,0:T(8,128)(2,1)S(1)}, u32[]{:S(2)}, u32[]{:S(2)}) collective-permute-start(bf16[272,768]{1,0:T(8,128)(2,1)S(1)} %pack_rows.25), channel_id=1, source_target_pairs={{0,10},{1,11},{2,8},{3,9},{4,14},{5,15},{6,12},{7,13},{8,2},{9,3},... | collective-permute-start | bytes 1253384 | tf_op jit(solution)/shard_map/ppermute | solution.py:562
  24.4 1.9 %pack_rows.26 = bf16[272,768]{1,0:T(8,128)(2,1)S(1)} custom-call(s32[1]{0:T(128)} %bitcast.17.me_ref, s32[1,2048]{1,0:T(1,128)S(1)} %get-tuple-element.156.owner0_ref.owner_ref, s32[1,2048]{1,0:T(1,128)S(1)} %get-tuple-element.141.owner1_ref, s32[1,2048]{1,0:T(1,128)S(1)} %get-tuple-element.142.slot0_ref.slot_ref, ...), custom_call_target="tpu_custom_call" | custom-call | flops 272 | bytes 272 | tf_op jit(solution)/shard_map/pack_rows/pallas_call | solution.py:258
  26.3 1.9 %pack_rows.27 = bf16[272,768]{1,0:T(8,128)(2,1)S(1)} custom-call(s32[1]{0:T(128)} %bitcast.17.me_ref, s32[1,2048]{1,0:T(1,128)S(1)} %get-tuple-element.156.owner0_ref.owner_ref, s32[1,2048]{1,0:T(1,128)S(1)} %get-tuple-element.141.owner1_ref, s32[1,2048]{1,0:T(1,128)S(1)} %get-tuple-element.142.slot0_ref.slot_ref, ...), custom_call_target="tpu_custom_call" | custom-call | flops 272 | bytes 272 | tf_op jit(solution)/shard_map/pack_rows/pallas_call | solution.py:258
  28.2 1.9 %pack_rows.28 = bf16[272,768]{1,0:T(8,128)(2,1)S(1)} custom-call(s32[1]{0:T(128)} %bitcast.17.me_ref, s32[1,2048]{1,0:T(1,128)S(1)} %get-tuple-element.156.owner0_ref.owner_ref, s32[1,2048]{1,0:T(1,128)S(1)} %get-tuple-element.141.owner1_ref, s32[1,2048]{1,0:T(1,128)S(1)} %get-tuple-element.142.slot0_ref.slot_ref, ...), custom_call_target="tpu_custom_call" | custom-call | flops 272 | bytes 272 | tf_op jit(solution)/shard_map/pack_rows/pallas_call | solution.py:258
  30.1 0.7 collective-permute-start.6
  30.7 2.3 %collective-permute-start.5 = (bf16[272,768]{1,0:T(8,128)(2,1)S(1)}, bf16[272,768]{1,0:T(8,128)(2,1)S(1)}, u32[]{:S(2)}, u32[]{:S(2)}) collective-permute-start(bf16[272,768]{1,0:T(8,128)(2,1)S(1)} %pack_rows.27), channel_id=1, source_target_pairs={{0,4},{1,5},{2,6},{3,7},{4,0},{5,1},{6,2},{7,3},{8,12},{9,13},{10,... | collective-permute-start | bytes 1253384 | tf_op jit(solution)/shard_map/ppermute | solution.py:562
  33.1 0.9 collective-permute-start.4
  34.0 1.9 %pack_rows.29 = bf16[272,768]{1,0:T(8,128)(2,1)S(1)} custom-call(s32[1]{0:T(128)} %bitcast.17.me_ref, s32[1,2048]{1,0:T(1,128)S(1)} %get-tuple-element.156.owner0_ref.owner_ref, s32[1,2048]{1,0:T(1,128)S(1)} %get-tuple-element.141.owner1_ref, s32[1,2048]{1,0:T(1,128)S(1)} %get-tuple-element.142.slot0_ref.slot_ref, ...), custom_call_target="tpu_custom_call" | custom-call | flops 272 | bytes 272 | tf_op jit(solution)/shard_map/pack_rows/pallas_call | solution.py:258
  35.9 1.2 %collective-permute-start.8 = (bf16[272,768]{1,0:T(8,128)(2,1)S(1)}, bf16[272,768]{1,0:T(8,128)(2,1)S(1)}, u32[]{:S(2)}, u32[]{:S(2)}) collective-permute-start(bf16[272,768]{1,0:T(8,128)(2,1)S(1)} %pack_rows.29), channel_id=1, source_target_pairs={{0,12},{1,13},{2,14},{3,15},{4,8},{5,9},{6,10},{7,11},{8,4},{9,5},... | collective-permute-start | bytes 1253384 | tf_op jit(solution)/shard_map/ppermute | solution.py:562
  37.1 1.9 %pack_rows.30 = bf16[272,768]{1,0:T(8,128)(2,1)S(1)} custom-call(s32[1]{0:T(128)} %bitcast.17.me_ref, s32[1,2048]{1,0:T(1,128)S(1)} %get-tuple-element.156.owner0_ref.owner_ref, s32[1,2048]{1,0:T(1,128)S(1)} %get-tuple-element.141.owner1_ref, s32[1,2048]{1,0:T(1,128)S(1)} %get-tuple-element.142.slot0_ref.slot_ref, ...), custom_call_target="tpu_custom_call" | custom-call | flops 272 | bytes 272 | tf_op jit(solution)/shard_map/pack_rows/pallas_call | solution.py:258
  39.0 34.1 %collective-permute-done.2.refs_1_ = bf16[272,768]{1,0:T(8,128)(2,1)S(1)} collective-permute-done((bf16[272,768]{1,0:T(8,128)(2,1)S(1)}, bf16[272,768]{1,0:T(8,128)(2,1)S(1)}, u32[]{:S(2)}, u32[]{:S(2)}) %collective-permute-start.2) | collective-permute-done | bytes 417824 | tf_op jit(solution)/shard_map/ppermute | solution.py:562
  73.1 2.1 %pack_rows.31.refs_0_ = bf16[272,768]{1,0:T(8,128)(2,1)S(1)} custom-call(s32[1]{0:T(128)} %bitcast.17.me_ref, s32[1,2048]{1,0:T(1,128)S(1)} %get-tuple-element.156.owner0_ref.owner_ref, s32[1,2048]{1,0:T(1,128)S(1)} %get-tuple-element.141.owner1_ref, s32[1,2048]{1,0:T(1,128)S(1)} %get-tuple-element.142.slot0_ref.slot_ref, ...), custom_call_target="tpu_custom_call" | custom-call | flops 272 | bytes 272 | tf_op jit(solution)/shard_map/pack_rows/pallas_call | solution.py:258
  75.2 3.0 %score_rows.9 = (bf16[1152,768]{1,0:T(8,128)(2,1)S(1)}, f32[1088,128]{1,0:T(8,128)S(1)}, f32[1088,128]{1,0:T(8,128)S(1)}, f32[8,768]{1,0:T(8,128)S(1)}) custom-call(f32[8,128]{1,0:T(8,128)S(1)} %get-tuple-element.145.bound_ref, bf16[272,768]{1,0:T(8,128)(2,1)S(1)} %pack_rows.31.refs_0_, bf16[272,768]{1,0:T(8,128)(2,1)S(1)} %collective-permute-done.4.refs_1_, ...), custom_call_target="tpu_custom_call" | custom-call | flops 2506752 | bytes 2176 | tf_op jit(solution)/shard_map/score_rows/pallas_call | solution.py:379
  78.2 2.6 %score_rows.10 = (bf16[640,768]{1,0:T(8,128)(2,1)S(1)}, f32[544,128]{1,0:T(8,128)S(1)}, f32[544,128]{1,0:T(8,128)S(1)}, f32[8,768]{1,0:T(8,128)S(1)}, f32[1088,128]{1,0:T(8,128)S(1)}) custom-call(f32[8,128]{1,0:T(8,128)S(1)} %get-tuple-element.145.bound_ref, bf16[272,768]{1,0:T(8,128)(2,1)S(1)} %collective-permute-done.7.refs_0_, ...), custom_call_target="tpu_custom_call" | custom-call | flops 2088960 | bytes 3264 | tf_op jit(solution)/shard_map/score_rows/pallas_call | solution.py:379
  80.9 2.4 %score_rows.11 = (bf16[384,768]{1,0:T(8,128)(2,1)S(1)}, f32[272,128]{1,0:T(8,128)S(1)}, f32[272,128]{1,0:T(8,128)}, f32[8,768]{1,0:T(8,128)S(1)}, f32[1088,128]{1,0:T(8,128)S(1)}, /*index=5*/f32[544,128]{1,0:T(8,128)S(1)}) custom-call(f32[8,128]{1,0:T(8,128)S(1)} %get-tuple-element.145.bound_ref, bf16[272,768]{1,0:T(8,128)(2,1)S(1)} %collective-permute-done.8.refs_0_, ...), custom_call_target="tpu_custom_call" | custom-call | flops 1462272 | bytes 3808 | tf_op jit(solution)/shard_map/score_rows/pallas_call | solution.py:379
  83.2 0.5 line_rows.3
  83.8 8.8 %collective-permute-done.3.refs_0_ = bf16[272,768]{1,0:T(8,128)(2,1)S(1)} collective-permute-done((bf16[272,768]{1,0:T(8,128)(2,1)S(1)}, bf16[272,768]{1,0:T(8,128)(2,1)S(1)}, u32[]{:S(2)}, u32[]{:S(2)}) %collective-permute-start.3) | collective-permute-done | bytes 417824 | tf_op jit(solution)/shard_map/ppermute | solution.py:562
  92.6 2.6 %finish_rows.3 = f32[16,1,768]{2,1,0:T(1,128)} custom-call(s32[1]{0:T(128)} %bitcast.17.me_ref, f32[8,128]{1,0:T(8,128)S(1)} %get-tuple-element.145.bound_ref, f32[8,128]{1,0:T(8,128)S(1)} %get-tuple-element.146.total_ref, bf16[272,768]{1,0:T(8,128)(2,1)S(1)} %collective-permute-done.3.refs_0_, bf16[1152,768]{1,0:T(8,128)(2,1)S(1)} %get-tuple-element.161.refs_2_.refs_1_, ...), custom_call_target="tpu_custom_call" | custom-call | flops 2566914048 | bytes 6684672 | tf_op jit(solution)/shard_map/finish_rows/pallas_call | solution.py:498
  95.2 3.7 %all-to-all-start.3 = ((f32[16,1,768]{2,1,0:T(1,128)}), f32[16,1,768]{2,1,0:T(1,128)S(1)}, u32[]{:S(2)}, u32[]{:S(2)}) async-start(f32[16,1,768]{2,1,0:T(1,128)} %finish_rows.3), calls=%async_computation.3 | async-start | bytes 98304 | tf_op jit(solution)/shard_map/all_to_all | solution.py:549
  99.0 6.7 %all-to-all-done.3.back_ref = f32[16,1,768]{2,1,0:T(1,128)S(1)} async-done(((f32[16,1,768]{2,1,0:T(1,128)}), f32[16,1,768]{2,1,0:T(1,128)S(1)}, u32[]{:S(2)}, u32[]{:S(2)}) %all-to-all-start.3) | async-done | bytes 49184 | tf_op jit(solution)/shard_map/all_to_all | solution.py:549
  105.7 1.6 %restore_rows.3 = (f32[1,2048]{1,0:T(1,128)}, f32[1,2048]{1,0:T(1,128)}) custom-call(s32[1,2048]{1,0:T(1,128)S(1)} %get-tuple-element.156.owner0_ref.owner_ref, s32[1,2048]{1,0:T(1,128)S(1)} %get-tuple-element.142.slot0_ref.slot_ref, f32[16,1,768]{2,1,0:T(1,128)S(1)} %all-to-all-done.3.back_ref), custom_call_target="tpu_custom_call" | custom-call | tf_op jit(solution)/shard_map/restore_rows/pallas_call | solution.py:538
  (13 shorter events, 0.0 us)
Async XLA Ops:
  0.6 1.6 %collective-permute-start = (s32[1,2048]{1,0:T(1,128)}, s32[1,2048]{1,0:T(1,128)S(1)}, u32[]{:S(2)}, u32[]{:S(2)}) collective-permute-start(s32[1,2048]{1,0:T(1,128)} %bitcast.40), channel_id=1, source_target_pairs={{0,1},{1,0},{2,3},{3,2},{4,5},{5,4},{6,7},{7,6},{8,9},{9,8},{10,11... | collective-permute-start | bytes 24584 | tf_op jit(solution)/shard_map/ppermute | solution.py:574
  1.1 0.7 copy-start.6
  2.3 15.3 %collective-permute-start.1 = (bf16[2048,768]{1,0:T(8,128)(2,1)}, bf16[2048,768]{1,0:T(8,128)(2,1)S(1)}, u32[]{:S(2)}, u32[]{:S(2)}) collective-permute-start(bf16[2048,768]{1,0:T(8,128)(2,1)} %rows0_ref.15), channel_id=1, source_target_pairs={{0,1},{1,0},{2,3},{3,2},{4,5},{5,4},{6,7},{7,6},{8,9},{9,8},{10,11... | collective-permute-start | bytes 9437192 | tf_op jit(solution)/shard_map/ppermute | solution.py:574
  2.5 15.0 %copy-start.13 = (bf16[2048,768]{1,0:T(8,128)(2,1)S(1)}, bf16[2048,768]{1,0:T(8,128)(2,1)}, u32[]{:S(2)}) copy-start(bf16[2048,768]{1,0:T(8,128)(2,1)} %rows0_ref.15) | copy-start | bytes 9437188
  17.5 55.6 %copy-start.15 = (bf16[2048,768]{1,0:T(8,128)(2,1)}, bf16[2048,768]{1,0:T(8,128)(2,1)S(1)}, u32[]{:S(2)}) copy-start(bf16[2048,768]{1,0:T(8,128)(2,1)S(1)} %collective-permute-done.1.rows1_ref) | copy-start | bytes 9437188
  19.4 16.4 %collective-permute-start.7 = (bf16[272,768]{1,0:T(8,128)(2,1)S(1)}, bf16[272,768]{1,0:T(8,128)(2,1)S(1)}, u32[]{:S(2)}, u32[]{:S(2)}) collective-permute-start(bf16[272,768]{1,0:T(8,128)(2,1)S(1)} %pack_rows.24), channel_id=1, source_target_pairs={{0,14},{1,15},{2,12},{3,13},{4,10},{5,11},{6,8},{7,9},{8,6},{9,7},... | collective-permute-start | bytes 1253384 | tf_op jit(solution)/shard_map/ppermute | solution.py:562
  22.0 51.1 %collective-permute-start.2 = (bf16[272,768]{1,0:T(8,128)(2,1)S(1)}, bf16[272,768]{1,0:T(8,128)(2,1)S(1)}, u32[]{:S(2)}, u32[]{:S(2)}) collective-permute-start(bf16[272,768]{1,0:T(8,128)(2,1)S(1)} %pack_rows.25), channel_id=1, source_target_pairs={{0,10},{1,11},{2,8},{3,9},{4,14},{5,15},{6,12},{7,13},{8,2},{9,3},... | collective-permute-start | bytes 1253384 | tf_op jit(solution)/shard_map/ppermute | solution.py:562
  30.1 45.1 %collective-permute-start.6 = (bf16[272,768]{1,0:T(8,128)(2,1)S(1)}, bf16[272,768]{1,0:T(8,128)(2,1)S(1)}, u32[]{:S(2)}, u32[]{:S(2)}) collective-permute-start(bf16[272,768]{1,0:T(8,128)(2,1)S(1)} %pack_rows.28), channel_id=1, source_target_pairs={{0,2},{1,3},{2,0},{3,1},{4,6},{5,7},{6,4},{7,5},{8,10},{9,11},{10,... | collective-permute-start | bytes 1253384 | tf_op jit(solution)/shard_map/ppermute | solution.py:562
  30.7 44.5 %collective-permute-start.5 = (bf16[272,768]{1,0:T(8,128)(2,1)S(1)}, bf16[272,768]{1,0:T(8,128)(2,1)S(1)}, u32[]{:S(2)}, u32[]{:S(2)}) collective-permute-start(bf16[272,768]{1,0:T(8,128)(2,1)S(1)} %pack_rows.27), channel_id=1, source_target_pairs={{0,4},{1,5},{2,6},{3,7},{4,0},{5,1},{6,2},{7,3},{8,12},{9,13},{10,... | collective-permute-start | bytes 1253384 | tf_op jit(solution)/shard_map/ppermute | solution.py:562
  33.1 42.1 %collective-permute-start.4 = (bf16[272,768]{1,0:T(8,128)(2,1)S(1)}, bf16[272,768]{1,0:T(8,128)(2,1)S(1)}, u32[]{:S(2)}, u32[]{:S(2)}) collective-permute-start(bf16[272,768]{1,0:T(8,128)(2,1)S(1)} %pack_rows.26), channel_id=1, source_target_pairs={{0,6},{1,7},{2,4},{3,5},{4,2},{5,3},{6,0},{7,1},{8,14},{9,15},{10,... | collective-permute-start | bytes 1253384 | tf_op jit(solution)/shard_map/ppermute | solution.py:562
  35.9 44.9 %collective-permute-start.8 = (bf16[272,768]{1,0:T(8,128)(2,1)S(1)}, bf16[272,768]{1,0:T(8,128)(2,1)S(1)}, u32[]{:S(2)}, u32[]{:S(2)}) collective-permute-start(bf16[272,768]{1,0:T(8,128)(2,1)S(1)} %pack_rows.29), channel_id=1, source_target_pairs={{0,12},{1,13},{2,14},{3,15},{4,8},{5,9},{6,10},{7,11},{8,4},{9,5},... | collective-permute-start | bytes 1253384 | tf_op jit(solution)/shard_map/ppermute | solution.py:562
  73.1 19.5 %collective-permute-start.3 = (bf16[272,768]{1,0:T(8,128)(2,1)S(1)}, bf16[272,768]{1,0:T(8,128)(2,1)S(1)}, u32[]{:S(2)}, u32[]{:S(2)}) collective-permute-start(bf16[272,768]{1,0:T(8,128)(2,1)S(1)} %pack_rows.30), channel_id=1, source_target_pairs={{0,8},{1,9},{2,10},{3,11},{4,12},{5,13},{6,14},{7,15},{8,0},{9,1},... | collective-permute-start | bytes 1253384 | tf_op jit(solution)/shard_map/ppermute | solution.py:562
  95.2 10.5 %all-to-all-start.3 = ((f32[16,1,768]{2,1,0:T(1,128)}), f32[16,1,768]{2,1,0:T(1,128)S(1)}, u32[]{:S(2)}, u32[]{:S(2)}) async-start(f32[16,1,768]{2,1,0:T(1,128)} %finish_rows.3), calls=%async_computation.3 | async-start | bytes 98304 | tf_op jit(solution)/shard_map/all_to_all | solution.py:549

commit v15 on v13

--- a/solution.py
+++ b/solution.py
@@ -82,7 +82,7 @@
     me_ref, ids1_ref, own_ref, total_ref, counts_ref, rank0_ref, rank1_ref
 ):
     rows = ids1_ref.shape[1]
-    chips, _, clusters = counts_ref.shape
+    clusters = counts_ref.shape[2]
     core = me_ref[0] & 1
     label = iota((clusters, TILE), 0)
     total0 = total_ref[:, 0:1]
@@ -90,8 +90,7 @@
     square = (clusters, clusters)
     eye = iota(square, 0) == iota(square, 1)
     total_row = jnp.sum(jnp.where(eye, total0 + total1, 0.0), axis=0, keepdims=True).astype(i32)
-    for chip in range(chips):
-        counts_ref[chip] = total_row
+    counts_ref[0] = total_row
     for from_ref, rank_ref, ahead in (
         (own_ref, rank0_ref, jnp.where(core == 1, total1, 0.0)),
         (rank1_ref, rank1_ref, jnp.where(core == 0, total0, 0.0)),
@@ -103,11 +102,11 @@
             rank_ref[:, at] = rank + jnp.sum(more, axis=0, keepdims=True).astype(i32)
 
 
-def count_rows(me, ids1, own, total, chips, clusters):
+def count_rows(me, ids1, own, total, clusters):
     return pl.pallas_call(
         count_kernel,
         out_shape=(
-            jax.ShapeDtypeStruct((chips, 1, clusters), i32),
+            jax.ShapeDtypeStruct((1, 1, clusters), i32),
             jax.ShapeDtypeStruct(ids1.shape, i32),
             jax.ShapeDtypeStruct(ids1.shape, i32),
         ),
@@ -557,6 +556,12 @@
     )
 
 
+def gather_chips(x):
+    chips = lax.axis_size("owner") // 2
+    cores = [[2 * chip + core for chip in range(chips)] for core in range(2)]
+    return lax.all_gather(x, "owner", axis_index_groups=cores, tiled=True)
+
+
 def swap(block, r):
     owners = lax.axis_size("owner")
     return lax.ppermute(block, "owner", [(s, s ^ (2 * r)) for s in range(owners)])
@@ -589,8 +594,8 @@
     own, own_total = rank_own(ids0, clusters)
     mine, ids1, own = lax.optimization_barrier((embeddings, ids1, own))
     other = swap_cores(mine)
-    counts, rank0, rank1 = count_rows(me, ids1, own, own_total, chips, clusters)
-    counts = exchange_chips(counts)
+    counts, rank0, rank1 = count_rows(me, ids1, own, own_total, clusters)
+    counts = gather_chips(counts)
     both = (embeddings, other)
     *places, bound, total, load = assign(me, counts, rank0, rank1)
     owner_row, slot_row = places[0], places[2]

time: 107 us -> 111 us (1.037)
  blocking collectives: 13.5 us -> 22.1 us
  waiting for transfers between devices: 28.1 us -> 23.1 us
    all_gather x0 -> x1, blocking collectives: none -> 22.1 us  [gather_chips(): return lax.all_gather(x, 'owner', axis_index_groups=cores, tiled=True)]
    all_to_all x1 -> x0, blocking collectives: 13.5 us -> none  [exchange_chips(): lax.all_to_all(x, 'owner', split_axis=0, concat_axis=0, axis_index_groups...]
    ppermute x7, waiting for transfers between devices: 21.3 us -> 16.4 us  [swap(): return lax.ppermute(block, 'owner', [(s, s ^ 2 * r) for s in range(owners)])]
  transfers between devices with their start and end apart: 10 -> 10, of which waited for: 3 -> 2; matrix products, arithmetic and copies ran while one was open for 0% -> 0% of each run, Pallas kernels for 22% -> 21%
where the time goes in v15:
time: 111 us
  starting transfers between devices  34.1 us (31%)
  Pallas kernels  29.8 us (27%)
  waiting for transfers between devices  23.1 us (21%)
  blocking collectives  22.1 us (20%)
    ppermute x7, starting transfers between devices, swap(): return lax.ppermute(block, 'owner', [(s, s ^ 2 * r) for s in range(owners)])  29.1 us
    all_gather x1, blocking collectives, gather_chips(): return lax.all_gather(x, 'owner', axis_index_groups=cores, tiled=True)  22.1 us
    ppermute x7, waiting for transfers between devices, swap(): return lax.ppermute(block, 'owner', [(s, s ^ 2 * r) for s in range(owners)])  16.4 us
    pallas_call x8, Pallas kernels, pack(): pl.pallas_call(functools.partial(pack_kernel, partner), out_shape=jax.Sha...  15.3 us
    pallas_call x3, Pallas kernels, score(): pl.pallas_call(functools.partial(score_kernel, slots, partners, len(units...  8.01 us
    all_to_all x1, waiting for transfers between devices, exchange(): return lax.all_to_all(x, 'owner', split_axis=0, concat_axis=0, tiled=True)  6.73 us
    all_to_all x1, starting transfers between devices, exchange(): return lax.all_to_all(x, 'owner', split_axis=0, concat_axis=0, tiled=True)  4.23 us
    pallas_call x1, Pallas kernels, finish(): pl.pallas_call(functools.partial(finish_kernel, slots, partners, earlier)...  2.61 us
  transfers between devices with their start and end apart: 10, of which 2 were waited for; matrix products, arithmetic and copies ran while one was open for 0% of the time, Pallas kernels for 21%

profile of v15, /device:TPU:0, one launch (start us, length us, event | category | flops | bytes accessed | tf_op | source)
XLA Modules:
  0.0 110.8 jit_solution(16588049825313270550)
XLA Ops:
  0.6 0.5 collective-permute-start
  1.1 0.7 copy-done.6
  1.8 0.4 rank_own.1
  2.2 0.0 collective-permute-done.ids1_ref
  2.3 0.3 collective-permute-start.1
  2.5 0.6 count_rows.1
  3.1 22.1 %all_gather.3.counts_ref = s32[8,1,64]{2,1,0:T(1,128)S(1)} all-gather(s32[1,1,64]{2,1,0:T(1,128)S(1)} %get-tuple-element.136), channel_id=1, replica_groups={{0,2,4,6,8,10,12,14},{1,3,5,7,9,11,13,15},{16,18,20,22,24,26,28,30},{17..., dimensions={0}, use_global_device_ids=true | all-gather | bytes 2304 | tf_op jit(solution)/shard_map/all_gather | solution.py:562
  25.3 0.8 assign.1
  26.2 1.9 %pack_rows.24 = bf16[272,768]{1,0:T(8,128)(2,1)S(1)} custom-call(s32[1]{0:T(128)} %bitcast.17.me_ref, s32[1,2048]{1,0:T(1,128)S(1)} %get-tuple-element.156.owner0_ref.owner_ref, s32[1,2048]{1,0:T(1,128)S(1)} %get-tuple-element.141.owner1_ref, s32[1,2048]{1,0:T(1,128)S(1)} %get-tuple-element.142.slot0_ref.slot_ref, ...), custom_call_target="tpu_custom_call" | custom-call | flops 272 | bytes 272 | tf_op jit(solution)/shard_map/pack_rows/pallas_call | solution.py:257
  28.1 0.1 collective-permute-start.7
  28.1 1.9 %pack_rows.25 = bf16[272,768]{1,0:T(8,128)(2,1)S(1)} custom-call(s32[1]{0:T(128)} %bitcast.17.me_ref, s32[1,2048]{1,0:T(1,128)S(1)} %get-tuple-element.156.owner0_ref.owner_ref, s32[1,2048]{1,0:T(1,128)S(1)} %get-tuple-element.141.owner1_ref, s32[1,2048]{1,0:T(1,128)S(1)} %get-tuple-element.142.slot0_ref.slot_ref, ...), custom_call_target="tpu_custom_call" | custom-call | flops 272 | bytes 272 | tf_op jit(solution)/shard_map/pack_rows/pallas_call | solution.py:257
  30.0 1.1 %collective-permute-start.2 = (bf16[272,768]{1,0:T(8,128)(2,1)S(1)}, bf16[272,768]{1,0:T(8,128)(2,1)S(1)}, u32[]{:S(2)}, u32[]{:S(2)}) collective-permute-start(bf16[272,768]{1,0:T(8,128)(2,1)S(1)} %pack_rows.25), channel_id=1, source_target_pairs={{0,12},{1,13},{2,14},{3,15},{4,8},{5,9},{6,10},{7,11},{8,4},{9,5},... | collective-permute-start | bytes 1253384 | tf_op jit(solution)/shard_map/ppermute | solution.py:567
  31.2 1.9 %pack_rows.26 = bf16[272,768]{1,0:T(8,128)(2,1)S(1)} custom-call(s32[1]{0:T(128)} %bitcast.17.me_ref, s32[1,2048]{1,0:T(1,128)S(1)} %get-tuple-element.156.owner0_ref.owner_ref, s32[1,2048]{1,0:T(1,128)S(1)} %get-tuple-element.141.owner1_ref, s32[1,2048]{1,0:T(1,128)S(1)} %get-tuple-element.142.slot0_ref.slot_ref, ...), custom_call_target="tpu_custom_call" | custom-call | flops 272 | bytes 272 | tf_op jit(solution)/shard_map/pack_rows/pallas_call | solution.py:257
  33.0 1.9 %pack_rows.27 = bf16[272,768]{1,0:T(8,128)(2,1)S(1)} custom-call(s32[1]{0:T(128)} %bitcast.17.me_ref, s32[1,2048]{1,0:T(1,128)S(1)} %get-tuple-element.156.owner0_ref.owner_ref, s32[1,2048]{1,0:T(1,128)S(1)} %get-tuple-element.141.owner1_ref, s32[1,2048]{1,0:T(1,128)S(1)} %get-tuple-element.142.slot0_ref.slot_ref, ...), custom_call_target="tpu_custom_call" | custom-call | flops 272 | bytes 272 | tf_op jit(solution)/shard_map/pack_rows/pallas_call | solution.py:257
  34.9 1.9 %pack_rows.28 = bf16[272,768]{1,0:T(8,128)(2,1)S(1)} custom-call(s32[1]{0:T(128)} %bitcast.17.me_ref, s32[1,2048]{1,0:T(1,128)S(1)} %get-tuple-element.156.owner0_ref.owner_ref, s32[1,2048]{1,0:T(1,128)S(1)} %get-tuple-element.141.owner1_ref, s32[1,2048]{1,0:T(1,128)S(1)} %get-tuple-element.142.slot0_ref.slot_ref, ...), custom_call_target="tpu_custom_call" | custom-call | flops 272 | bytes 272 | tf_op jit(solution)/shard_map/pack_rows/pallas_call | solution.py:257
  36.8 4.3 %collective-permute-start.6 = (bf16[272,768]{1,0:T(8,128)(2,1)S(1)}, bf16[272,768]{1,0:T(8,128)(2,1)S(1)}, u32[]{:S(2)}, u32[]{:S(2)}) collective-permute-start(bf16[272,768]{1,0:T(8,128)(2,1)S(1)} %pack_rows.28), channel_id=1, source_target_pairs={{0,2},{1,3},{2,0},{3,1},{4,6},{5,7},{6,4},{7,5},{8,10},{9,11},{10,... | collective-permute-start | bytes 1253384 | tf_op jit(solution)/shard_map/ppermute | solution.py:567
  41.1 1.5 %collective-permute-start.4 = (bf16[272,768]{1,0:T(8,128)(2,1)S(1)}, bf16[272,768]{1,0:T(8,128)(2,1)S(1)}, u32[]{:S(2)}, u32[]{:S(2)}) collective-permute-start(bf16[272,768]{1,0:T(8,128)(2,1)S(1)} %pack_rows.26), channel_id=1, source_target_pairs={{0,6},{1,7},{2,4},{3,5},{4,2},{5,3},{6,0},{7,1},{8,14},{9,15},{10,... | collective-permute-start | bytes 1253384 | tf_op jit(solution)/shard_map/ppermute | solution.py:567
  42.7 1.9 %pack_rows.29 = bf16[272,768]{1,0:T(8,128)(2,1)S(1)} custom-call(s32[1]{0:T(128)} %bitcast.17.me_ref, s32[1,2048]{1,0:T(1,128)S(1)} %get-tuple-element.156.owner0_ref.owner_ref, s32[1,2048]{1,0:T(1,128)S(1)} %get-tuple-element.141.owner1_ref, s32[1,2048]{1,0:T(1,128)S(1)} %get-tuple-element.142.slot0_ref.slot_ref, ...), custom_call_target="tpu_custom_call" | custom-call | flops 272 | bytes 272 | tf_op jit(solution)/shard_map/pack_rows/pallas_call | solution.py:257
  44.6 0.0 collective-permute-done.7.refs_0_
  44.6 11.8 %collective-permute-start.8 = (bf16[272,768]{1,0:T(8,128)(2,1)S(1)}, bf16[272,768]{1,0:T(8,128)(2,1)S(1)}, u32[]{:S(2)}, u32[]{:S(2)}) collective-permute-start(bf16[272,768]{1,0:T(8,128)(2,1)S(1)} %pack_rows.29), channel_id=1, source_target_pairs={{0,10},{1,11},{2,8},{3,9},{4,14},{5,15},{6,12},{7,13},{8,2},{9,3},... | collective-permute-start | bytes 1253384 | tf_op jit(solution)/shard_map/ppermute | solution.py:567
  56.4 1.9 %pack_rows.30 = bf16[272,768]{1,0:T(8,128)(2,1)S(1)} custom-call(s32[1]{0:T(128)} %bitcast.17.me_ref, s32[1,2048]{1,0:T(1,128)S(1)} %get-tuple-element.156.owner0_ref.owner_ref, s32[1,2048]{1,0:T(1,128)S(1)} %get-tuple-element.141.owner1_ref, s32[1,2048]{1,0:T(1,128)S(1)} %get-tuple-element.142.slot0_ref.slot_ref, ...), custom_call_target="tpu_custom_call" | custom-call | flops 272 | bytes 272 | tf_op jit(solution)/shard_map/pack_rows/pallas_call | solution.py:257
  58.3 10.3 %collective-permute-start.3 = (bf16[272,768]{1,0:T(8,128)(2,1)S(1)}, bf16[272,768]{1,0:T(8,128)(2,1)S(1)}, u32[]{:S(2)}, u32[]{:S(2)}) collective-permute-start(bf16[272,768]{1,0:T(8,128)(2,1)S(1)} %pack_rows.30), channel_id=1, source_target_pairs={{0,8},{1,9},{2,10},{3,11},{4,12},{5,13},{6,14},{7,15},{8,0},{9,1},... | collective-permute-start | bytes 1253384 | tf_op jit(solution)/shard_map/ppermute | solution.py:567
  68.6 2.1 %pack_rows.31.refs_0_ = bf16[272,768]{1,0:T(8,128)(2,1)S(1)} custom-call(s32[1]{0:T(128)} %bitcast.17.me_ref, s32[1,2048]{1,0:T(1,128)S(1)} %get-tuple-element.156.owner0_ref.owner_ref, s32[1,2048]{1,0:T(1,128)S(1)} %get-tuple-element.141.owner1_ref, s32[1,2048]{1,0:T(1,128)S(1)} %get-tuple-element.142.slot0_ref.slot_ref, ...), custom_call_target="tpu_custom_call" | custom-call | flops 272 | bytes 272 | tf_op jit(solution)/shard_map/pack_rows/pallas_call | solution.py:257
  70.7 3.0 %score_rows.9 = (bf16[1152,768]{1,0:T(8,128)(2,1)S(1)}, f32[1088,128]{1,0:T(8,128)S(1)}, f32[1088,128]{1,0:T(8,128)S(1)}, f32[8,768]{1,0:T(8,128)S(1)}) custom-call(f32[8,128]{1,0:T(8,128)S(1)} %get-tuple-element.145.bound_ref, bf16[272,768]{1,0:T(8,128)(2,1)S(1)} %pack_rows.31.refs_0_, bf16[272,768]{1,0:T(8,128)(2,1)S(1)} %collective-permute-done.4.refs_1_, ...), custom_call_target="tpu_custom_call" | custom-call | flops 2506752 | bytes 2176 | tf_op jit(solution)/shard_map/score_rows/pallas_call | solution.py:378
  73.7 2.6 %score_rows.10 = (bf16[640,768]{1,0:T(8,128)(2,1)S(1)}, f32[544,128]{1,0:T(8,128)S(1)}, f32[544,128]{1,0:T(8,128)S(1)}, f32[8,768]{1,0:T(8,128)S(1)}, f32[1088,128]{1,0:T(8,128)S(1)}) custom-call(f32[8,128]{1,0:T(8,128)S(1)} %get-tuple-element.145.bound_ref, bf16[272,768]{1,0:T(8,128)(2,1)S(1)} %collective-permute-done.7.refs_0_, ...), custom_call_target="tpu_custom_call" | custom-call | flops 2088960 | bytes 3264 | tf_op jit(solution)/shard_map/score_rows/pallas_call | solution.py:378
  76.4 16.3 %collective-permute-done.8.refs_0_ = bf16[272,768]{1,0:T(8,128)(2,1)S(1)} collective-permute-done((bf16[272,768]{1,0:T(8,128)(2,1)S(1)}, bf16[272,768]{1,0:T(8,128)(2,1)S(1)}, u32[]{:S(2)}, u32[]{:S(2)}) %collective-permute-start.8) | collective-permute-done | bytes 417824 | tf_op jit(solution)/shard_map/ppermute | solution.py:567
  92.7 2.4 %score_rows.11 = (bf16[384,768]{1,0:T(8,128)(2,1)S(1)}, f32[272,128]{1,0:T(8,128)S(1)}, f32[272,128]{1,0:T(8,128)}, f32[8,768]{1,0:T(8,128)S(1)}, f32[1088,128]{1,0:T(8,128)S(1)}, /*index=5*/f32[544,128]{1,0:T(8,128)S(1)}) custom-call(f32[8,128]{1,0:T(8,128)S(1)} %get-tuple-element.145.bound_ref, bf16[272,768]{1,0:T(8,128)(2,1)S(1)} %collective-permute-done.8.refs_0_, ...), custom_call_target="tpu_custom_call" | custom-call | flops 1462272 | bytes 3808 | tf_op jit(solution)/shard_map/score_rows/pallas_call | solution.py:378
  95.1 0.5 line_rows.3
  95.6 2.6 %finish_rows.3 = f32[16,1,768]{2,1,0:T(1,128)} custom-call(s32[1]{0:T(128)} %bitcast.17.me_ref, f32[8,128]{1,0:T(8,128)S(1)} %get-tuple-element.145.bound_ref, f32[8,128]{1,0:T(8,128)S(1)} %get-tuple-element.146.total_ref, bf16[272,768]{1,0:T(8,128)(2,1)S(1)} %collective-permute-done.3.refs_0_, bf16[1152,768]{1,0:T(8,128)(2,1)S(1)} %get-tuple-element.161.refs_2_.refs_1_, ...), custom_call_target="tpu_custom_call" | custom-call | flops 2566914048 | bytes 6684672 | tf_op jit(solution)/shard_map/finish_rows/pallas_call | solution.py:497
  98.2 4.2 %all-to-all-start.2 = ((f32[16,1,768]{2,1,0:T(1,128)}), f32[16,1,768]{2,1,0:T(1,128)S(1)}, u32[]{:S(2)}, u32[]{:S(2)}) async-start(f32[16,1,768]{2,1,0:T(1,128)} %finish_rows.3), calls=%async_computation.2 | async-start | bytes 98304 | tf_op jit(solution)/shard_map/all_to_all | solution.py:548
  102.5 6.7 %all-to-all-done.2.back_ref = f32[16,1,768]{2,1,0:T(1,128)S(1)} async-done(((f32[16,1,768]{2,1,0:T(1,128)}), f32[16,1,768]{2,1,0:T(1,128)S(1)}, u32[]{:S(2)}, u32[]{:S(2)}) %all-to-all-start.2) | async-done | bytes 49184 | tf_op jit(solution)/shard_map/all_to_all | solution.py:548
  109.2 1.6 %restore_rows.3 = (f32[1,2048]{1,0:T(1,128)}, f32[1,2048]{1,0:T(1,128)}) custom-call(s32[1,2048]{1,0:T(1,128)S(1)} %get-tuple-element.156.owner0_ref.owner_ref, s32[1,2048]{1,0:T(1,128)S(1)} %get-tuple-element.142.slot0_ref.slot_ref, f32[16,1,768]{2,1,0:T(1,128)S(1)} %all-to-all-done.2.back_ref), custom_call_target="tpu_custom_call" | custom-call | tf_op jit(solution)/shard_map/restore_rows/pallas_call | solution.py:537
  (13 shorter events, 0.0 us)
Async XLA Ops:
  0.6 1.6 %collective-permute-start = (s32[1,2048]{1,0:T(1,128)}, s32[1,2048]{1,0:T(1,128)S(1)}, u32[]{:S(2)}, u32[]{:S(2)}) collective-permute-start(s32[1,2048]{1,0:T(1,128)} %bitcast.40), channel_id=1, source_target_pairs={{0,1},{1,0},{2,3},{3,2},{4,5},{5,4},{6,7},{7,6},{8,9},{9,8},{10,11... | collective-permute-start | bytes 24584 | tf_op jit(solution)/shard_map/ppermute | solution.py:579
  1.1 0.7 copy-start.6
  2.3 23.9 %collective-permute-start.1 = (bf16[2048,768]{1,0:T(8,128)(2,1)}, bf16[2048,768]{1,0:T(8,128)(2,1)S(1)}, u32[]{:S(2)}, u32[]{:S(2)}) collective-permute-start(bf16[2048,768]{1,0:T(8,128)(2,1)} %rows0_ref.15), channel_id=1, source_target_pairs={{0,1},{1,0},{2,3},{3,2},{4,5},{5,4},{6,7},{7,6},{8,9},{9,8},{10,11... | collective-permute-start | bytes 9437192 | tf_op jit(solution)/shard_map/ppermute | solution.py:579
  2.5 23.6 %copy-start.13 = (bf16[2048,768]{1,0:T(8,128)(2,1)S(1)}, bf16[2048,768]{1,0:T(8,128)(2,1)}, u32[]{:S(2)}) copy-start(bf16[2048,768]{1,0:T(8,128)(2,1)} %rows0_ref.15) | copy-start | bytes 9437188
  26.1 42.5 %copy-start.15 = (bf16[2048,768]{1,0:T(8,128)(2,1)}, bf16[2048,768]{1,0:T(8,128)(2,1)S(1)}, u32[]{:S(2)}) copy-start(bf16[2048,768]{1,0:T(8,128)(2,1)S(1)} %collective-permute-done.1.rows1_ref) | copy-start | bytes 9437188
  28.1 16.5 %collective-permute-start.7 = (bf16[272,768]{1,0:T(8,128)(2,1)S(1)}, bf16[272,768]{1,0:T(8,128)(2,1)S(1)}, u32[]{:S(2)}, u32[]{:S(2)}) collective-permute-start(bf16[272,768]{1,0:T(8,128)(2,1)S(1)} %pack_rows.24), channel_id=1, source_target_pairs={{0,14},{1,15},{2,12},{3,13},{4,10},{5,11},{6,8},{7,9},{8,6},{9,7},... | collective-permute-start | bytes 1253384 | tf_op jit(solution)/shard_map/ppermute | solution.py:567
  30.0 28.3 %collective-permute-start.2 = (bf16[272,768]{1,0:T(8,128)(2,1)S(1)}, bf16[272,768]{1,0:T(8,128)(2,1)S(1)}, u32[]{:S(2)}, u32[]{:S(2)}) collective-permute-start(bf16[272,768]{1,0:T(8,128)(2,1)S(1)} %pack_rows.25), channel_id=1, source_target_pairs={{0,12},{1,13},{2,14},{3,15},{4,8},{5,9},{6,10},{7,11},{8,4},{9,5},... | collective-permute-start | bytes 1253384 | tf_op jit(solution)/shard_map/ppermute | solution.py:567
  36.8 33.8 %collective-permute-start.6 = (bf16[272,768]{1,0:T(8,128)(2,1)S(1)}, bf16[272,768]{1,0:T(8,128)(2,1)S(1)}, u32[]{:S(2)}, u32[]{:S(2)}) collective-permute-start(bf16[272,768]{1,0:T(8,128)(2,1)S(1)} %pack_rows.28), channel_id=1, source_target_pairs={{0,2},{1,3},{2,0},{3,1},{4,6},{5,7},{6,4},{7,5},{8,10},{9,11},{10,... | collective-permute-start | bytes 1253384 | tf_op jit(solution)/shard_map/ppermute | solution.py:567
  41.1 29.6 %collective-permute-start.5 = (bf16[272,768]{1,0:T(8,128)(2,1)S(1)}, bf16[272,768]{1,0:T(8,128)(2,1)S(1)}, u32[]{:S(2)}, u32[]{:S(2)}) collective-permute-start(bf16[272,768]{1,0:T(8,128)(2,1)S(1)} %pack_rows.27), channel_id=1, source_target_pairs={{0,4},{1,5},{2,6},{3,7},{4,0},{5,1},{6,2},{7,3},{8,12},{9,13},{10,... | collective-permute-start | bytes 1253384 | tf_op jit(solution)/shard_map/ppermute | solution.py:567
  41.1 29.6 %collective-permute-start.4 = (bf16[272,768]{1,0:T(8,128)(2,1)S(1)}, bf16[272,768]{1,0:T(8,128)(2,1)S(1)}, u32[]{:S(2)}, u32[]{:S(2)}) collective-permute-start(bf16[272,768]{1,0:T(8,128)(2,1)S(1)} %pack_rows.26), channel_id=1, source_target_pairs={{0,6},{1,7},{2,4},{3,5},{4,2},{5,3},{6,0},{7,1},{8,14},{9,15},{10,... | collective-permute-start | bytes 1253384 | tf_op jit(solution)/shard_map/ppermute | solution.py:567
  44.6 48.1 %collective-permute-start.8 = (bf16[272,768]{1,0:T(8,128)(2,1)S(1)}, bf16[272,768]{1,0:T(8,128)(2,1)S(1)}, u32[]{:S(2)}, u32[]{:S(2)}) collective-permute-start(bf16[272,768]{1,0:T(8,128)(2,1)S(1)} %pack_rows.29), channel_id=1, source_target_pairs={{0,10},{1,11},{2,8},{3,9},{4,14},{5,15},{6,12},{7,13},{8,2},{9,3},... | collective-permute-start | bytes 1253384 | tf_op jit(solution)/shard_map/ppermute | solution.py:567
  58.3 37.3 %collective-permute-start.3 = (bf16[272,768]{1,0:T(8,128)(2,1)S(1)}, bf16[272,768]{1,0:T(8,128)(2,1)S(1)}, u32[]{:S(2)}, u32[]{:S(2)}) collective-permute-start(bf16[272,768]{1,0:T(8,128)(2,1)S(1)} %pack_rows.30), channel_id=1, source_target_pairs={{0,8},{1,9},{2,10},{3,11},{4,12},{5,13},{6,14},{7,15},{8,0},{9,1},... | collective-permute-start | bytes 1253384 | tf_op jit(solution)/shard_map/ppermute | solution.py:567
  98.2 11.0 %all-to-all-start.2 = ((f32[16,1,768]{2,1,0:T(1,128)}), f32[16,1,768]{2,1,0:T(1,128)S(1)}, u32[]{:S(2)}, u32[]{:S(2)}) async-start(f32[16,1,768]{2,1,0:T(1,128)} %finish_rows.3), calls=%async_computation.2 | async-start | bytes 98304 | tf_op jit(solution)/shard_map/all_to_all | solution.py:548
